TPU v7x, 32 devices: a whole 2x2x4 slice. The times are simulated.
32 devices in a mesh: fsdp: 16 (over z, y, core), rep: 2 (over x).
Axes of the slice: x: 2, y: 2, z: 4, core: 2. Of those that a mesh axis runs over, the one named last changes fastest.
Arguments:
- patches: bfloat16 [8192, 2048], P(('fsdp', 'rep')), may hold values from -6 to 6
- cotangent: bfloat16 [8192, 2048], P(('fsdp', 'rep')), may hold values from -0.0625 to 0.0625
- student: float32 [2048, 2048], P('fsdp'), may hold values from -6 to 6
- first_moment: float32 [2048, 2048], P('fsdp'), may hold values from -4 to 4
- second_moment: float32 [2048, 2048], P('fsdp'), may hold values from 0.0005 to 0.03
- teacher: float32 [2048, 2048], P('fsdp'), may hold values from -6 to 6
Outputs:
- features: bfloat16 [8192, 2048], P(('fsdp', 'rep'))
- new_student: float32 [2048, 2048], P('fsdp')
- new_first: float32 [2048, 2048], P('fsdp')
- new_second: float32 [2048, 2048], P('fsdp')
- new_teacher: float32 [2048, 2048], P('fsdp')
All inputs are finite; a program needn't handle non-finite values.
Results may differ from a plain program's by a relative error of at most 0.006.
Values may be sent and summed in bfloat16 or wider, within the bound.
No kernel may reach another device: no remote copies, remote signals or barrier semaphores. Data moves between devices by JAX's collectives and lax.ppermute only.
A program may use at most 128 MiB of HBM per device.

v0:
```python
import jax
import jax.numpy as jnp
from jax import lax
from jax.sharding import PartitionSpec as P

FEAT = 2048
STEP = 100


beta_one = 0.9
beta_two = 0.999
adam_eps = 1e-08
learn_rate = 0.1
decay_rate = 0.04
ema_keep = 0.994


def update_shard(gradient, student, first_moment, second_moment, teacher):
    new_first = beta_one * first_moment + (1.0 - beta_one) * gradient
    new_second = beta_two * second_moment + (1.0 - beta_two) * gradient * gradient
    corr_one = 1.0 - beta_one**STEP
    corr_two = 1.0 - beta_two**STEP
    direction = new_first / corr_one / (jnp.sqrt(new_second / corr_two) + adam_eps)
    new_student = student - learn_rate * (direction + decay_rate * student)
    new_teacher = ema_keep * teacher + (1.0 - ema_keep) * new_student
    return (new_student, new_first, new_second, new_teacher)


def per_device(patches, cotangent, student, first_moment, second_moment, teacher):
    feat_width = patches.shape[1]
    out_width = cotangent.shape[1]
    block_size = min(256, feat_width)
    block_count = feat_width // block_size

    def term_block(index_block):
        columns = lax.dynamic_slice_in_dim(patches, index_block * block_size, block_size, 1)
        return jnp.dot(columns.T, cotangent, preferred_element_type=jnp.float32).astype(
            jnp.bfloat16
        )

    terms = lax.map(term_block, jnp.arange(block_count)).reshape(1, feat_width, out_width)
    group_grad = jnp.sum(
        lax.all_to_all(terms, "fsdp", split_axis=1, concat_axis=0, tiled=True).astype(jnp.float32),
        axis=0,
    )
    columns = patches
    total = jnp.dot(
        columns,
        lax.all_gather(teacher.astype(jnp.bfloat16), "fsdp", axis=0, tiled=True),
        preferred_element_type=jnp.float32,
    )
    gradient = lax.psum(group_grad.astype(jnp.bfloat16), "rep").astype(jnp.float32)
    new_student, new_first, new_second, new_teacher = update_shard(
        gradient, student, first_moment, second_moment, teacher
    )
    features = (total * FEAT ** (-0.5)).astype(jnp.bfloat16)
    return (features, new_student, new_first, new_second, new_teacher)


def solution(mesh):
    placed = (
        P(("fsdp", "rep"), None),
        P(("fsdp", "rep"), None),
        P("fsdp", None),
        P("fsdp", None),
        P("fsdp", None),
        P("fsdp", None),
    )
    return jax.shard_map(
        per_device,
        mesh=mesh,
        in_specs=placed,
        out_specs=(
            P(("fsdp", "rep"), None),
            P("fsdp", None),
            P("fsdp", None),
            P("fsdp", None),
            P("fsdp", None),
        ),
        check_vma=False,
    )
```

profile of v0, /device:TPU:0, one launch (start us, length us, event | category | flops | bytes accessed | tf_op | source)
XLA Modules:
  0.0 469.5 jit_solution(12225440351586615972)
XLA Ops:
  7.2 0.0 all-reduce.2.cloned.1.call-start
  7.2 32.1 %while.10 = (s32[]{:T(128)}, bf16[8,256,2048]{2,1,0:T(8,128)(2,1)}, s32[8]{0:T(128)S(1)}, bf16[256,2048]{1,0:T(8,128)(2,1)}, bf16[256,2048]{1,0:T(8,128)(2,1)}, ...) while((s32[]{:T(128)}, bf16[8,256,2048]{2,1,0:T(8,128)(2,1)}, s32[8]{0:T(128)S(1)}, ...), condition=%wide.region_1.2_spmd, body=%wide.region_0.1_spmd.sunk | while | flops 268959744 | bytes 2228391 | solution.py:41
  7.2 0.6 dynamic_slice.12
  8.5 2.8 fusion.17
  11.2 0.6 dynamic_slice.12
  12.5 2.8 fusion.17
  15.3 0.6 dynamic_slice.12
  16.5 2.8 fusion.17
  19.3 0.6 dynamic_slice.12
  20.5 2.7 fusion.17
  23.3 0.6 dynamic_slice.12
  24.5 2.8 fusion.17
  27.3 0.6 dynamic_slice.12
  28.5 2.8 fusion.17
  31.3 0.6 dynamic_slice.12
  32.5 2.8 fusion.17
  35.3 0.6 dynamic_slice.12
  36.5 2.8 fusion.17
  39.3 15.5 %copy.14 = bf16[1,2048,2048]{2,0,1:T(2,128)(2,1)} copy(bf16[1,2048,2048]{2,1,0:T(8,128)(2,1)} %bitcast.23) | data formatting | bytes 16777216 | tf_op jit(solution)/shard_map/reshape | solution.py:41
  54.8 0.5 broadcast.10
  55.3 51.0 %reduce.3 = bf16[2048,2048]{1,0:T(8,128)(2,1)} reduce(bf16[2048,1,2048]{2,1,0:T(2,128)(2,1)} %bitcast.21, bf16[]{:T(256)} %broadcast.10), dimensions={1}, to_apply=%bitcast.13.reduce_sub_computation | reduce | bytes 16777218
  106.3 14.5 %reshape.19 = bf16[16,2,131072]{2,1,0:T(2,128)(2,1)} reshape(bf16[2048,2048]{1,0:T(8,128)(2,1)} %reduce.3) | data formatting | bytes 16777216
  120.8 189.6 %all_to_all.12 = bf16[16,2,131072]{2,1,0:T(2,128)(2,1)} all-to-all(bf16[16,2,131072]{2,1,0:T(2,128)(2,1)} %reshape.19), channel_id=1, replica_groups=mesh['fsdp'=16,'rep'=2] {'fsdp'}, dimensions={0} | all-to-all | bytes 16777216 | tf_op jit(solution)/shard_map/all_to_all | solution.py:43
  310.4 16.3 %reshape.20 = bf16[2048,1,2048]{2,1,0:T(2,128)(2,1)} reshape(bf16[16,2,131072]{2,1,0:T(2,128)(2,1)} %all_to_all.12) | data formatting | bytes 16777216
  326.8 13.5 %copy.12 = bf16[1,2048,2048]{2,1,0:T(8,128)(2,1)} copy(bf16[1,2048,2048]{2,0,1:T(2,128)(2,1)} %bitcast.20) | data formatting | bytes 16777216
  340.2 0.0 copy-start
  340.2 0.0 copy-start.1
  340.2 0.0 copy-start.2
  340.2 6.3 %reduce_sum.12 = bf16[128,2048]{1,0:T(8,128)(2,1)} reduce(bf16[16,128,2048]{2,1,0:T(8,128)(2,1)} %bitcast.22, bf16[]{:T(256)} %constant.7.clone.1), dimensions={0}, to_apply=%region_2.3 | reduce | flops 3932160 | bytes 8912898 | tf_op jit(solution)/shard_map/reduce_sum | solution.py:42
  346.5 0.0 all-reduce.2.cloned.1.call-update
  346.6 0.2 all-gather.2.cloned.1.call-start
  346.8 29.5 %all-reduce.2.cloned.1.call-done = bf16[128,2048]{1,0:T(8,128)(2,1)} async-done(((bf16[128,2048]{1,0:T(8,128)(2,1)}), bf16[128,2048]{1,0:T(8,128)(2,1)}) %all-reduce.2.cloned.1.call-update) | async-done | bytes 524304 | tf_op jit(solution)/shard_map/psum | solution.py:52
  376.3 0.0 copy-done
  376.3 0.0 copy-done.1
  376.3 0.0 copy-done.2
  376.3 4.3 multiply_add_fusion
  380.6 0.0 all-gather.2.cloned.1.call-update
  380.6 75.1 %all-gather.2.cloned.1.call-done = bf16[2048,2048]{1,0:T(8,128)(2,1)} async-done(((bf16[128,2048]{1,0:T(8,128)(2,1)}), bf16[2048,2048]{1,0:T(8,128)(2,1)}) %all-gather.2.cloned.1.call-update) | async-done | bytes 8388624 | tf_op jit(solution)/shard_map/all_gather | solution.py:49
  455.7 7.0 %fusion.4 = bf16[256,2048]{1,0:T(8,128)(2,1)} fusion(bf16[256,2048]{1,0:T(8,128)(2,1)} %get-tuple-element.113, bf16[2048,2048]{1,0:T(8,128)(2,1)} %all-gather.2.cloned.1.call-done), kind=kOutput, calls=%fused_computation.6 | convolution fusion | flops 2148532224 | bytes 10485760 | tf_op jit(solution)/shard_map/dot_general | solution.py:47
  (2 shorter events, 0.0 us)
Async XLA Ops:
  7.2 369.2 %all-reduce.2.cloned.1.call-start = ((), (), s32[]{:S(2)}) async-start(), calls=%async_computation.2 | async-start | bytes 1048576 | tf_op jit(solution)/shard_map/psum | solution.py:52
  340.2 36.1 %copy-start = (f32[128,2048]{1,0:T(8,128)S(1)}, f32[128,2048]{1,0:T(8,128)}, u32[]{:S(2)}) copy-start(f32[128,2048]{1,0:T(8,128)} %param.13) | copy-start | bytes 3145732
  340.2 36.1 %copy-start.1 = (f32[128,2048]{1,0:T(8,128)S(1)}, f32[128,2048]{1,0:T(8,128)}, u32[]{:S(2)}) copy-start(f32[128,2048]{1,0:T(8,128)} %param.10) | copy-start | bytes 3145732
  340.2 36.1 %copy-start.2 = (f32[128,2048]{1,0:T(8,128)S(1)}, f32[128,2048]{1,0:T(8,128)}, u32[]{:S(2)}) copy-start(f32[128,2048]{1,0:T(8,128)} %param.11) | copy-start | bytes 3145732
  346.6 109.1 %all-gather.2.cloned.1.call-start = ((), (), s32[]{:S(2)}) async-start(), calls=%async_computation.1 | async-start | bytes 8912896 | tf_op jit(solution)/shard_map/all_gather | solution.py:49
Sparse Core Ops, SparseCore 0:
  346.7 29.5 all-reduce.1
  380.7 74.8 all-gather.1
where the time goes:
time: 471 us; the launch traced here: 470 us
  blocking collectives  190 us (40%)
  waiting for transfers between devices  105 us (22%)
  local copies, waits for them, and re-layouts  65 us (14%)
  other arithmetic  61.6 us (13%)
  matrix products  29.2 us (6%)
  between operations  14.1 us (3%)
  loops' own time  5.27 us (1%)
    all_to_all x1, blocking collectives, per_device(): lax.all_to_all(terms, 'fsdp', split_axis=1, concat_axis=0, tiled=True)  190 us
    all_gather x1, waiting for transfers between devices, per_device(): lax.all_gather(teacher.astype(jnp.bfloat16), 'fsdp', axis=0, tiled=True)  75.1 us
    unnamed x1, other arithmetic  51 us
    unnamed x10, local copies, waits for them, and re-layouts  44.8 us
    psum x1, waiting for transfers between devices, per_device(): lax.psum(group_grad.astype(jnp.bfloat16), 'rep').astype(jnp.float32)  29.5 us
    dot_general x8, matrix products, term_block(): jnp.dot(columns.T, cotangent, preferred_element_type=jnp.float32)  22.1 us
    reshape x1, local copies, waits for them, and re-layouts, per_device(): lax.map(term_block, jnp.arange(block_count))  15.5 us
  transfers between devices with their start and end apart: 2, of which 2 were waited for; matrix products, arithmetic and copies ran while one was open for 0% of the time, Pallas kernels for 0%

commit v1 on v0

v1 whole, which is shorter than its diff:
```python
import math

import jax
import jax.numpy as jnp
from jax import lax
from jax.experimental import pallas as pl
from jax.experimental.pallas import tpu as pltpu
from jax.sharding import PartitionSpec as P

STEP = 100

beta_one = 0.9
beta_two = 0.999
adam_eps = 1e-08
learn_rate = 0.1
decay_rate = 0.04
ema_keep = 0.994

bf16, f32 = jnp.bfloat16, jnp.float32
VMEM = pl.BlockSpec(memory_space=pltpu.VMEM)


def call(name, body, outs, inputs, scratch=()):
    shapes = [jax.ShapeDtypeStruct(*out) for out in outs]
    moved = sum(a.size * a.dtype.itemsize for a in (*inputs, *shapes))
    held = sum(4 * math.prod(getattr(s, "shape", ())) for s in scratch)
    with jax.named_scope(name):
        return pl.pallas_call(
            body,
            out_shape=shapes,
            in_specs=[VMEM] * len(inputs),
            out_specs=[VMEM] * len(shapes),
            scratch_shapes=list(scratch),
            cost_estimate=pl.CostEstimate(flops=1, bytes_accessed=1, transcendentals=0),
            compiler_params=pltpu.CompilerParams(vmem_limit_bytes=moved + held + 4 * 2**20),
        )(*inputs)


def after(value, *others):
    return lax.optimization_barrier((value, *others))[0]


def aligned(index, size):
    return pl.ds(pl.multiple_of(index * size, size), size)


def solution(mesh):
    n, r = mesh.shape["fsdp"], mesh.shape["rep"]
    nz = 4
    ny = n // (2 * nz)
    pair_groups = r // 2

    def send(value, move):
        perm = []
        for f in range(n):
            for p in range(r):
                z, y, c = f // (2 * ny), f // 2 % ny, f % 2
                z, y, c, g, h = move(z, y, c, p // 2, p % 2)
                perm.append((f * r + p, ((z * ny + y) * 2 + c) * r + g * 2 + h))
        return lax.ppermute(value, ("fsdp", "rep"), perm)

    def sibling(z, y, c, g, h):
        return z, y, 1 - c, g, h

    def partner(z, y, c, g, h):
        return z, y, c, g, 1 - h

    def diagonal(z, y, c, g, h):
        return z, y, 1 - c, g, 1 - h

    def along_z(d):
        return lambda z, y, c, g, h: ((z + d) % nz, y, c, g, h)

    def across_z(d):
        return lambda z, y, c, g, h: (z ^ d, y, c, g, h)

    def along_y(d):
        return lambda z, y, c, g, h: (z, (y + d) % ny, c, g, h)

    def along_g(d):
        return lambda z, y, c, g, h: (z, y, c, (g + d) % pair_groups, h)

    def place():
        f = lax.axis_index("fsdp")
        core = lax.rem(f, 2)
        return f // (2 * ny), lax.rem(f // 2, ny), core, lax.rem(lax.axis_index("rep"), 2) * 2 + core

    def per_device(patches, cotangent, student, first_moment, second_moment, teacher):
        tokens, feat = patches.shape
        outw = cotangent.shape[1]
        rows = teacher.shape[0]
        part = outw // 4
        span = feat // nz
        g_order = [3, 2, 1, 0]
        lead = 2 * part

        def cut_body(p, c, first, near, c_own, *rest):
            z, y, core, q = place()
            first[:, :lead] = c[:, aligned(1 - q // 2, lead)]
            for k, dz in enumerate(g_order):
                block = p[:, aligned(z ^ dz, span)]
                near[:, k * span : (k + 1) * span] = block
                if k == 0:
                    first[:, lead:] = block
                else:
                    rest[k - 1][...] = block
            near[:, feat:] = c[:, aligned(q ^ 1, part)]
            c_own[...] = c[:, aligned(q, part)]

        def split_body(message, c_sib, c_here, block):
            z, y, core, q = place()
            c_sib[...] = message[:, aligned(1 - core, part)]
            c_here[...] = message[:, aligned(core, part)]
            block[...] = message[:, lead:]

        clock = []

        def run(name, body, outs, inputs, *scratch, **options):
            first = after(inputs[0], *clock) if clock else inputs[0]
            out = call(name, body, outs, [first, *inputs[1:]], *scratch, **options)
            clock[:] = out[:1]
            return out

        def start(value, move, *others):
            return send(after(value, *others) if others else value, move)

        def wait(*values):
            clock.extend(values)

        def cast_body(t, same, other):
            z, y, core, q = place()
            same[...] = t[:, aligned(q, part)].astype(bf16)
            other[...] = t[:, aligned(q ^ 1, part)].astype(bf16)

        def join_body(same, sib, out):
            z, y, core, q = place()
            out[aligned(core, rows), :] = same[...]
            out[aligned(1 - core, rows), :] = sib[...]

        def stack_body(*refs):
            for k, ref in enumerate(refs[:-1]):
                refs[-1][k * 2 * rows : (k + 1) * 2 * rows, :] = ref[...]

        def terms_body(k):
            def body(own, sib, par, dia, c0, c_par, c_dia, *outs):
                z, y, core, q = place()
                whole = outs[-1]
                near = slice(k * span, (k + 1) * span)
                total = None
                for p, c in (
                    (own[:, near], c0[...]),
                    (sib[:, near], sib[:, feat:]),
                    (par[...], c_par[...]),
                    (dia[...], c_dia[...]),
                ):
                    term = lax.dot_general(
                        p, c, (((0,), (0,)), ((), ())), preferred_element_type=f32
                    )
                    total = term if total is None else total + term
                whole[...] = total
                for dy in range(ny):
                    block = whole[aligned(lax.rem(y + dy, ny), 2 * rows), :]
                    outs[dy][...] = block.astype(outs[dy].dtype)

            return body

        def gradient_block(k):
            dz = g_order[k]
            terms[dz] = run(
                "gradient_block",
                terms_body(k),
                [((2 * rows, part), f32)] + [((2 * rows, part), bf16)] * (ny - 1),
                [near_own, near_sib, far_par[k], far_dia[k], c_own, c_par, c_dia],
                scratch=[pltpu.VMEM((span, part), f32)],
            )
            moved_y[dz] = [start(terms[dz][dy], along_y(dy)) for dy in others]

        def add_body(*refs):
            refs[-1][...] = sum(ref[...].astype(f32) for ref in refs[:-1]).astype(refs[-1].dtype)

        def add(values, dtype, **options):
            return run("add_blocks", add_body, [(values[0].shape, dtype)], values, **options)[0]

        def sum_body(*refs):
            z, y, core, q = place()
            for out, at in zip(refs[-2:], (aligned(core, rows), aligned(1 - core, rows))):
                out[...] = sum(ref[at, :].astype(f32) for ref in refs[:-2]).astype(bf16)

        def features_of(blocks, full, out):
            total = sum(
                jnp.dot(
                    block, full[dz * span : (dz + 1) * span, :], preferred_element_type=f32
                )
                for block, dz in zip(blocks, g_order)
            )
            out[...] = (total * feat ** (-0.5)).astype(bf16)

        def fill_body(*refs):
            z, y, core, q = place()
            for k in range(nz * ny):
                dz, dy = w_order[k // ny], k % ny
                ref, at = (refs[k], 0) if dz != 1 else (refs[-2], dy * 2 * rows)
                block = (z ^ lax.rem(z + dz, nz)) * ny + lax.rem(y + dy, ny)
                refs[-1][aligned(block, 2 * rows), :] = ref[at : at + 2 * rows, :]

        def near_body(own, sib, full, f_own, f_sib):
            for ref, out in ((own, f_own), (sib, f_sib)):
                features_of([ref[:, k * span : (k + 1) * span] for k in range(nz)], full, out)

        def far_body(*refs):
            features_of([ref[...] for ref in refs[:nz]], refs[nz], refs[nz + 1])

        def far_features(blocks):
            return run(
                "far_features", far_body, [((tokens, part), bf16)], [*blocks, w_full]
            )[0]

        def place_body(*refs):
            z, y, core, q = place()
            for j in range(4):
                refs[4][:, aligned(q ^ j, part)] = refs[j][...]

        w_order = [0, 3, 2, 1]
        others = range(1, ny)
        w_line = [None] * nz
        w_side = [None] * nz
        far_par, far_dia = [None] * nz, [None] * nz
        terms, moved_y = [None] * nz, [None] * nz

        def teacher_y(dz, *gates):
            w_side[dz] = [start(w_line[dz], along_y(-dy), *gates) for dy in others]

        def block_sum(dz, *more, **options):
            return add([terms[dz][0], *moved_y[dz], *more], bf16, **options)

        first, near_own, c_own, *rest = run(
            "cut_tokens",
            cut_body,
            [
                ((tokens, width), bf16)
                for width in (lead + span, feat + part, part, *[span] * (nz - 1))
            ],
            [patches, cotangent],
        )
        message = start(first, partner)
        near_sib = start(near_own, sibling)
        w_same, w_other = run("cast_teacher", cast_body, [((rows, part), bf16)] * 2, [teacher])
        w_sib = start(w_other, sibling)
        (w_line[0],) = run(
            "join_teacher", join_body, [((2 * rows, part), bf16)], [w_same, w_sib]
        )
        w_line[3] = start(w_line[0], along_z(1))
        teacher_y(0)
        w_line[2] = start(w_line[3], along_z(1))
        teacher_y(3, *w_side[0])
        (turn,) = run(
            "stack_teacher", stack_body, [((ny * 2 * rows, part), bf16)], [w_line[0], *w_side[0]]
        )
        turn = start(turn, along_z(-1), w_line[2])
        teacher_y(2)
        for k in range(1, nz):
            far_par[k] = start(rest[k - 1], partner, *far_par[1 : k - 1])
        c_other, c_par, far_par[0] = run(
            "split_message",
            split_body,
            [((tokens, part), bf16)] * 2 + [((tokens, span), bf16)],
            [after(message, near_sib, w_line[2], *w_side[3])],
        )
        c_dia = start(c_other, sibling)
        held = ([], [], w_side[2])
        for k in range(nz - 1):
            far_dia[k] = start(far_par[k], sibling, *held[k])
        gradient_block(0)
        gradient_block(1)
        onward = start(block_sum(3), across_z(1))
        gradient_block(2)
        far_dia[3] = start(far_par[3], sibling, turn, terms[1][0])
        (w_full,) = run(
            "fill_teacher",
            fill_body,
            [((feat, part), bf16)],
            [*(w for dz in w_order[:-1] for w in (w_line[dz], *w_side[dz])), turn],
        )
        onward = start(block_sum(2, onward), across_z(2))
        f_par = start(far_features(far_par), partner)
        gradient_block(3)
        f_dia = start(far_features(far_dia), diagonal)
        back = start(block_sum(1), across_z(1))
        f_own, f_sib = run(
            "near_features",
            near_body,
            [((tokens, part), bf16)] * 2,
            [near_own, near_sib, w_full],
        )
        f_sib = start(f_sib, sibling)
        wait(f_par, f_dia)
        pieces = [terms[0][0], *moved_y[0], onward, back]
        if pair_groups > 1:
            total = add(pieces, f32)
            sent = total.astype(bf16)
            pieces = [total] + [start(sent, along_g(dg)) for dg in range(1, pair_groups)]
        mine, other = run("sum_gradient", sum_body, [((rows, part), bf16)] * 2, pieces)
        g_par, g_dia, g_sib = (
            start(mine, partner), start(other, diagonal), start(other, sibling)
        )
        (features,) = run(
            "place_features",
            place_body,
            [((tokens, outw), bf16)],
            [f_own, f_sib, f_par, f_dia],
        )
        grads = [mine, g_sib, g_par, g_dia]

        def update_body(*refs):
            z, y, core, q = place()
            student, first, second, teach, *outs = refs[4:]
            corr_one = 1.0 - beta_one**STEP
            corr_two = 1.0 - beta_two**STEP
            for j in range(4):
                at = (slice(None), aligned(q ^ j, part))
                gradient = refs[j][...].astype(f32)
                new_first = beta_one * first[at] + (1.0 - beta_one) * gradient
                new_second = beta_two * second[at] + (1.0 - beta_two) * gradient * gradient
                direction = new_first / corr_one / (jnp.sqrt(new_second / corr_two) + adam_eps)
                weights = student[at]
                new_student = weights - learn_rate * (direction + decay_rate * weights)
                outs[0][at] = new_student
                outs[1][at] = new_first
                outs[2][at] = new_second
                outs[3][at] = ema_keep * teach[at] + (1.0 - ema_keep) * new_student

        new = run(
            "update",
            update_body,
            [((rows, outw), f32)] * 4,
            [*grads, student, first_moment, second_moment, teacher],
        )
        return (features, *new)

    tokens_placed, weights_placed = P(("fsdp", "rep"), None), P("fsdp", None)
    return jax.shard_map(
        per_device,
        mesh=mesh,
        in_specs=(tokens_placed,) * 2 + (weights_placed,) * 4,
        out_specs=(tokens_placed,) + (weights_placed,) * 4,
        check_vma=False,
    )
```

time: 471 us -> 83.9 us (0.18)
  blocking collectives: 190 us -> 0 us
  waiting for transfers between devices: 105 us -> 42.3 us
  local copies, waits for them, and re-layouts: 65 us -> 2.55 us
  other arithmetic: 61.6 us -> 0 us
  matrix products: 29.2 us -> 0 us
  starting transfers between devices: 0.26 us -> 27.2 us
  between operations: 14.1 us -> 0.84 us
  Pallas kernels: 0 us -> 10.8 us
  loops' own time: 5.27 us -> 0 us
    all_to_all x1 -> x0, blocking collectives: 190 us -> none  [per_device(): lax.all_to_all(terms, 'fsdp', split_axis=1, concat_axis=0, tiled=True)]
    all_gather x1 -> x0, waiting for transfers between devices: 75.1 us -> none  [per_device(): lax.all_gather(teacher.astype(jnp.bfloat16), 'fsdp', axis=0, tiled=True)]
    unnamed x1 -> x0, other arithmetic: 51 us -> none
    ppermute x0 -> x30, waiting for transfers between devices: none -> 42.3 us  [send(): return lax.ppermute(value, ('fsdp', 'rep'), perm)]
    unnamed x10 -> x12, local copies, waits for them, and re-layouts: 44.8 us -> 2.55 us
    psum x1 -> x0, waiting for transfers between devices: 29.5 us -> none  [per_device(): lax.psum(group_grad.astype(jnp.bfloat16), 'rep').astype(jnp.float32)]
    dot_general x9 -> x0, matrix products: 29.2 us -> none  [the longest x8 22.1 us: term_block(): jnp.dot(columns.T, cotangent, preferred_element_type=jnp.float32)]
    ppermute x0 -> x30, starting transfers between devices: none -> 27.2 us  [send(): return lax.ppermute(value, ('fsdp', 'rep'), perm)]
  transfers between devices with their start and end apart: 2 -> 30, of which waited for: 2 -> 16; matrix products, arithmetic and copies ran while one was open for 0% -> 0% of each run, Pallas kernels for 0% -> 9%
where the time goes in v1:
time: 83.9 us; the launch traced here: 83.7 us
  waiting for transfers between devices  42.3 us (50%)
  starting transfers between devices  27.2 us (32%)
  Pallas kernels  10.8 us (13%)
  local copies, waits for them, and re-layouts  2.55 us (3%)
  between operations  0.84 us (1%)
    ppermute x30, waiting for transfers between devices, send(): return lax.ppermute(value, ('fsdp', 'rep'), perm)  42.3 us
    ppermute x30, starting transfers between devices, send(): return lax.ppermute(value, ('fsdp', 'rep'), perm)  27.2 us
    pallas_call x19, Pallas kernels, call(): pl.pallas_call(body, out_shape=shapes, in_specs=[VMEM] * len(inputs), out...  10.8 us
    unnamed x12, local copies, waits for them, and re-layouts  2.55 us
  transfers between devices with their start and end apart: 30, of which 16 were waited for; matrix products, arithmetic and copies ran while one was open for 0% of the time, Pallas kernels for 9%

profile of v1, /device:TPU:0, one launch (start us, length us, event | category | flops | bytes accessed | tf_op | source)
XLA Modules:
  0.0 83.7 jit_solution(8601578125655585792)
XLA Ops:
  0.7 1.3 %copy-done.1 = bf16[256,2048]{1,0:T(8,128)(2,1)S(1)} copy-done((bf16[256,2048]{1,0:T(8,128)(2,1)S(1)}, bf16[256,2048]{1,0:T(8,128)(2,1)}, u32[]{:S(2)}) %copy-start.1) | copy-done | bytes 1048600
  2.0 1.2 %copy-done.2 = bf16[256,2048]{1,0:T(8,128)(2,1)S(1)} copy-done((bf16[256,2048]{1,0:T(8,128)(2,1)S(1)}, bf16[256,2048]{1,0:T(8,128)(2,1)}, u32[]{:S(2)}) %copy-start.2) | copy-done | bytes 1048600
  3.4 0.5 collective-permute-start.1
  3.9 2.6 %collective-permute-start = (bf16[256,1536]{1,0:T(8,128)(2,1)S(1)}, bf16[256,1536]{1,0:T(8,128)(2,1)S(1)}, u32[]{:S(2)}, u32[]{:S(2)}) collective-permute-start(bf16[256,1536]{1,0:T(8,128)(2,1)S(1)} %get-tuple-element.56), channel_id=1, source_target_pairs={{0,1},{1,0},{2,3},{3,2},{4,5},{5,4},{6,7},{7,6},{8,9},{9,8},{10,11... | collective-permute-start | bytes 2359304 | tf_op jit(solution)/shard_map/ppermute | solution.py:60
  6.7 1.2 %collective-permute-done.2.sib = bf16[128,512]{1,0:T(8,128)(2,1)S(1)} collective-permute-done((bf16[128,512]{1,0:T(8,128)(2,1)S(1)}, bf16[128,512]{1,0:T(8,128)(2,1)S(1)}, u32[]{:S(2)}, u32[]{:S(2)}) %collective-permute-start.2) | collective-permute-done | bytes 131104 | tf_op jit(solution)/shard_map/ppermute | solution.py:60
  8.0 1.8 %collective-permute-start.5 = (bf16[256,512]{1,0:T(8,128)(2,1)S(1)}, bf16[256,512]{1,0:T(8,128)(2,1)S(1)}, u32[]{:S(2)}, u32[]{:S(2)}) collective-permute-start(bf16[256,512]{1,0:T(8,128)(2,1)S(1)} %join_teacher.1.refs_0_), channel_id=1, source_target_pairs={{0,4},{1,5},{2,6},{3,7},{4,0},{5,1},{6,2},{7,3},{8,12},{9,13},{10,... | collective-permute-start | bytes 786440 | tf_op jit(solution)/shard_map/ppermute | solution.py:60
  9.8 1.6 %collective-permute-start.3 = (bf16[256,512]{1,0:T(8,128)(2,1)S(1)}, bf16[256,512]{1,0:T(8,128)(2,1)S(1)}, u32[]{:S(2)}, u32[]{:S(2)}) collective-permute-start(bf16[256,512]{1,0:T(8,128)(2,1)S(1)} %join_teacher.1.refs_0_), channel_id=1, source_target_pairs={{0,8},{1,9},{2,10},{3,11},{4,12},{5,13},{6,14},{7,15},{8,16},{9,17... | collective-permute-start | bytes 786440 | tf_op jit(solution)/shard_map/ppermute | solution.py:60
  11.3 5.1 %collective-permute-done.5.refs_1_ = bf16[256,512]{1,0:T(8,128)(2,1)S(1)} collective-permute-done((bf16[256,512]{1,0:T(8,128)(2,1)S(1)}, bf16[256,512]{1,0:T(8,128)(2,1)S(1)}, u32[]{:S(2)}, u32[]{:S(2)}) %collective-permute-start.5) | collective-permute-done | bytes 262176 | tf_op jit(solution)/shard_map/ppermute | solution.py:60
  16.4 3.3 %collective-permute-done.3.refs_2_ = bf16[256,512]{1,0:T(8,128)(2,1)S(1)} collective-permute-done((bf16[256,512]{1,0:T(8,128)(2,1)S(1)}, bf16[256,512]{1,0:T(8,128)(2,1)S(1)}, u32[]{:S(2)}, u32[]{:S(2)}) %collective-permute-start.3) | collective-permute-done | bytes 262176 | tf_op jit(solution)/shard_map/ppermute | solution.py:60
  19.7 0.5 collective-permute-start.6
  20.2 1.5 %collective-permute-start.9 = (bf16[256,512]{1,0:T(8,128)(2,1)S(1)}, bf16[256,512]{1,0:T(8,128)(2,1)S(1)}, u32[]{:S(2)}, u32[]{:S(2)}) collective-permute-start(bf16[256,512]{1,0:T(8,128)(2,1)S(1)} %get-tuple-element.71), channel_id=1, source_target_pairs={{0,1},{1,0},{2,3},{3,2},{4,5},{5,4},{6,7},{7,6},{8,9},{9,8},{10,11... | collective-permute-start | bytes 786440 | tf_op jit(solution)/shard_map/ppermute | solution.py:60
  21.7 5.2 %collective-permute-done.6.refs_3_ = bf16[256,512]{1,0:T(8,128)(2,1)S(1)} collective-permute-done((bf16[256,512]{1,0:T(8,128)(2,1)S(1)}, bf16[256,512]{1,0:T(8,128)(2,1)S(1)}, u32[]{:S(2)}, u32[]{:S(2)}) %collective-permute-start.6) | collective-permute-done | bytes 262176 | tf_op jit(solution)/shard_map/ppermute | solution.py:60
  26.9 2.3 %collective-permute-done.4.refs_4_ = bf16[256,512]{1,0:T(8,128)(2,1)S(1)} collective-permute-done((bf16[256,512]{1,0:T(8,128)(2,1)S(1)}, bf16[256,512]{1,0:T(8,128)(2,1)S(1)}, u32[]{:S(2)}, u32[]{:S(2)}) %collective-permute-start.4) | collective-permute-done | bytes 262176 | tf_op jit(solution)/shard_map/ppermute | solution.py:60
  29.3 0.5 collective-permute-start.7
  29.8 1.3 %collective-permute-start.12 = (bf16[256,512]{1,0:T(8,128)(2,1)S(1)}, bf16[256,512]{1,0:T(8,128)(2,1)S(1)}, u32[]{:S(2)}, u32[]{:S(2)}) collective-permute-start(bf16[256,512]{1,0:T(8,128)(2,1)S(1)} %get-tuple-element.76), channel_id=1, source_target_pairs={{0,1},{1,0},{2,3},{3,2},{4,5},{5,4},{6,7},{7,6},{8,9},{9,8},{10,11... | collective-permute-start | bytes 786440 | tf_op jit(solution)/shard_map/ppermute | solution.py:60
  31.1 1.5 %collective-permute-start.13 = (bf16[256,512]{1,0:T(8,128)(2,1)S(1)}, bf16[256,512]{1,0:T(8,128)(2,1)S(1)}, u32[]{:S(2)}, u32[]{:S(2)}) collective-permute-start(bf16[256,512]{1,0:T(8,128)(2,1)S(1)} %collective-permute-done.4.refs_4_), channel_id=1, source_target_pairs={{0,4},{1,5},{2,6},{3,7},{4,0},{5,1},{6,2},{7,3},{8,12},{9,13},{10,... | collective-permute-start | bytes 786440 | tf_op jit(solution)/shard_map/ppermute | solution.py:60
  32.6 1.9 %collective-permute-start.15 = (bf16[512,512]{1,0:T(8,128)(2,1)S(1)}, bf16[512,512]{1,0:T(8,128)(2,1)S(1)}, u32[]{:S(2)}, u32[]{:S(2)}) collective-permute-start(bf16[512,512]{1,0:T(8,128)(2,1)S(1)} %stack_teacher.1), channel_id=1, source_target_pairs={{0,24},{1,25},{2,26},{3,27},{4,28},{5,29},{6,30},{7,31},{8,0},{9,1... | collective-permute-start | bytes 1572872 | tf_op jit(solution)/shard_map/ppermute | solution.py:60
  34.6 0.8 %gradient_block.4 = (f32[256,512]{1,0:T(8,128)S(1)}, bf16[256,512]{1,0:T(8,128)(2,1)S(1)}) custom-call(bf16[256,2560]{1,0:T(8,128)(2,1)S(1)} %get-tuple-element.92.own, bf16[256,2560]{1,0:T(8,128)(2,1)S(1)} %collective-permute-done.1.sib, bf16[256,512]{1,0:T(8,128)(2,1)S(1)} %get-tuple-element.83.par.refs_0_, ...), custom_call_target="tpu_custom_call" | custom-call | flops 1 | bytes 1 | tf_op jit(solution)/shard_map/gradient_block/pallas_call | solution.py:28
  35.4 1.6 %collective-permute-start.11 = (bf16[256,512]{1,0:T(8,128)(2,1)S(1)}, bf16[256,512]{1,0:T(8,128)(2,1)S(1)}, u32[]{:S(2)}, u32[]{:S(2)}) collective-permute-start(bf16[256,512]{1,0:T(8,128)(2,1)S(1)} %get-tuple-element.74), channel_id=1, source_target_pairs={{0,4},{1,5},{2,6},{3,7},{4,0},{5,1},{6,2},{7,3},{8,12},{9,13},{10,... | collective-permute-start | bytes 786440 | tf_op jit(solution)/shard_map/ppermute | solution.py:60
  37.0 1.1 %collective-permute-done.12.par.refs_2_ = bf16[256,512]{1,0:T(8,128)(2,1)S(1)} collective-permute-done((bf16[256,512]{1,0:T(8,128)(2,1)S(1)}, bf16[256,512]{1,0:T(8,128)(2,1)S(1)}, u32[]{:S(2)}, u32[]{:S(2)}) %collective-permute-start.12) | collective-permute-done | bytes 262176 | tf_op jit(solution)/shard_map/ppermute | solution.py:60
  38.1 1.5 %collective-permute-done.13.refs_5_ = bf16[256,512]{1,0:T(8,128)(2,1)S(1)} collective-permute-done((bf16[256,512]{1,0:T(8,128)(2,1)S(1)}, bf16[256,512]{1,0:T(8,128)(2,1)S(1)}, u32[]{:S(2)}, u32[]{:S(2)}) %collective-permute-start.13) | collective-permute-done | bytes 262176 | tf_op jit(solution)/shard_map/ppermute | solution.py:60
  39.6 0.3 collective-permute-start.18
  39.9 0.8 gradient_block.5
  40.7 1.4 %collective-permute-start.16 = (bf16[256,512]{1,0:T(8,128)(2,1)S(1)}, bf16[256,512]{1,0:T(8,128)(2,1)S(1)}, u32[]{:S(2)}, u32[]{:S(2)}) collective-permute-start(bf16[256,512]{1,0:T(8,128)(2,1)S(1)} %get-tuple-element.82), channel_id=1, source_target_pairs={{0,4},{1,5},{2,6},{3,7},{4,0},{5,1},{6,2},{7,3},{8,12},{9,13},{10,... | collective-permute-start | bytes 786440 | tf_op jit(solution)/shard_map/ppermute | solution.py:60
  42.1 3.1 %collective-permute-done.11.refs_1_ = bf16[256,512]{1,0:T(8,128)(2,1)S(1)} collective-permute-done((bf16[256,512]{1,0:T(8,128)(2,1)S(1)}, bf16[256,512]{1,0:T(8,128)(2,1)S(1)}, u32[]{:S(2)}, u32[]{:S(2)}) %collective-permute-start.11) | collective-permute-done | bytes 262176 | tf_op jit(solution)/shard_map/ppermute | solution.py:60
  45.3 0.8 gradient_block.6
  46.2 2.1 %collective-permute-done.18.refs_3_.par = bf16[256,512]{1,0:T(8,128)(2,1)S(1)} collective-permute-done((bf16[256,512]{1,0:T(8,128)(2,1)S(1)}, bf16[256,512]{1,0:T(8,128)(2,1)S(1)}, u32[]{:S(2)}, u32[]{:S(2)}) %collective-permute-start.18) | collective-permute-done | bytes 262176 | tf_op jit(solution)/shard_map/ppermute | solution.py:60
  48.3 1.5 %collective-permute-start.20 = (bf16[256,512]{1,0:T(8,128)(2,1)S(1)}, bf16[256,512]{1,0:T(8,128)(2,1)S(1)}, u32[]{:S(2)}, u32[]{:S(2)}) collective-permute-start(bf16[256,512]{1,0:T(8,128)(2,1)S(1)} %get-tuple-element.91), channel_id=1, source_target_pairs={{0,4},{1,5},{2,6},{3,7},{4,0},{5,1},{6,2},{7,3},{8,12},{9,13},{10,... | collective-permute-start | bytes 786440 | tf_op jit(solution)/shard_map/ppermute | solution.py:60
  50.0 0.3 collective-permute-done.16.refs_1_
  50.3 2.3 %collective-permute-done.17.refs_2_ = bf16[256,512]{1,0:T(8,128)(2,1)S(1)} collective-permute-done((bf16[256,512]{1,0:T(8,128)(2,1)S(1)}, bf16[256,512]{1,0:T(8,128)(2,1)S(1)}, u32[]{:S(2)}, u32[]{:S(2)}) %collective-permute-start.17) | collective-permute-done | bytes 262176 | tf_op jit(solution)/shard_map/ppermute | solution.py:60
  52.8 0.7 far_features.2
  53.5 1.1 %collective-permute-start.21 = (bf16[256,512]{1,0:T(8,128)(2,1)S(1)}, bf16[256,512]{1,0:T(8,128)(2,1)S(1)}, u32[]{:S(2)}, u32[]{:S(2)}) collective-permute-start(bf16[256,512]{1,0:T(8,128)(2,1)S(1)} %far_features.2), channel_id=1, source_target_pairs={{0,1},{1,0},{2,3},{3,2},{4,5},{5,4},{6,7},{7,6},{8,9},{9,8},{10,11... | collective-permute-start | bytes 786440 | tf_op jit(solution)/shard_map/ppermute | solution.py:60
  54.6 0.9 %collective-permute-start.24 = (bf16[256,512]{1,0:T(8,128)(2,1)S(1)}, bf16[256,512]{1,0:T(8,128)(2,1)S(1)}, u32[]{:S(2)}, u32[]{:S(2)}) collective-permute-start(bf16[256,512]{1,0:T(8,128)(2,1)S(1)} %add_blocks.4), channel_id=1, source_target_pairs={{0,16},{1,17},{2,18},{3,19},{4,20},{5,21},{6,22},{7,23},{8,24},{9,... | collective-permute-start | bytes 786440 | tf_op jit(solution)/shard_map/ppermute | solution.py:60
  55.4 0.8 gradient_block.7
  56.3 0.7 far_features.3
  57.1 1.6 %collective-permute-start.23 = (bf16[256,512]{1,0:T(8,128)(2,1)S(1)}, bf16[256,512]{1,0:T(8,128)(2,1)S(1)}, u32[]{:S(2)}, u32[]{:S(2)}) collective-permute-start(bf16[256,512]{1,0:T(8,128)(2,1)S(1)} %get-tuple-element.95), channel_id=1, source_target_pairs={{0,4},{1,5},{2,6},{3,7},{4,0},{5,1},{6,2},{7,3},{8,12},{9,13},{10,... | collective-permute-start | bytes 786440 | tf_op jit(solution)/shard_map/ppermute | solution.py:60
  58.7 2.6 %collective-permute-start.25 = (bf16[256,512]{1,0:T(8,128)(2,1)S(1)}, bf16[256,512]{1,0:T(8,128)(2,1)S(1)}, u32[]{:S(2)}, u32[]{:S(2)}) collective-permute-start(bf16[256,512]{1,0:T(8,128)(2,1)S(1)} %add_blocks.5), channel_id=1, source_target_pairs={{0,8},{1,9},{2,10},{3,11},{4,12},{5,13},{6,14},{7,15},{8,0},{9,1},... | collective-permute-start | bytes 786440 | tf_op jit(solution)/shard_map/ppermute | solution.py:60
  61.3 1.2 %near_features.1 = (bf16[256,512]{1,0:T(8,128)(2,1)S(1)}, bf16[256,512]{1,0:T(8,128)(2,1)S(1)}) custom-call(bf16[256,2560]{1,0:T(8,128)(2,1)S(1)} %get-tuple-element.92.own, bf16[256,2560]{1,0:T(8,128)(2,1)S(1)} %collective-permute-done.1.sib, bf16[2048,512]{1,0:T(8,128)(2,1)S(1)} %fill_teacher.1.refs_4_.full), custom_call_target="tpu_custom_call" | custom-call | flops 1 | bytes 1 | tf_op jit(solution)/shard_map/near_features/pallas_call | solution.py:28
  62.6 3.0 %collective-permute-done.22.refs_3_ = bf16[256,512]{1,0:T(8,128)(2,1)S(1)} collective-permute-done((bf16[256,512]{1,0:T(8,128)(2,1)S(1)}, bf16[256,512]{1,0:T(8,128)(2,1)S(1)}, u32[]{:S(2)}, u32[]{:S(2)}) %collective-permute-start.22) | collective-permute-done | bytes 262176 | tf_op jit(solution)/shard_map/ppermute | solution.py:60
  65.6 2.1 %collective-permute-done.24.refs_2_ = bf16[256,512]{1,0:T(8,128)(2,1)S(1)} collective-permute-done((bf16[256,512]{1,0:T(8,128)(2,1)S(1)}, bf16[256,512]{1,0:T(8,128)(2,1)S(1)}, u32[]{:S(2)}, u32[]{:S(2)}) %collective-permute-start.24) | collective-permute-done | bytes 262176 | tf_op jit(solution)/shard_map/ppermute | solution.py:60
  67.7 4.3 %collective-permute-done.25.refs_3_ = bf16[256,512]{1,0:T(8,128)(2,1)S(1)} collective-permute-done((bf16[256,512]{1,0:T(8,128)(2,1)S(1)}, bf16[256,512]{1,0:T(8,128)(2,1)S(1)}, u32[]{:S(2)}, u32[]{:S(2)}) %collective-permute-start.25) | collective-permute-done | bytes 262176 | tf_op jit(solution)/shard_map/ppermute | solution.py:60
  72.1 1.3 %collective-permute-start.29 = (bf16[128,512]{1,0:T(8,128)(2,1)S(1)}, bf16[128,512]{1,0:T(8,128)(2,1)S(1)}, u32[]{:S(2)}, u32[]{:S(2)}) collective-permute-start(bf16[128,512]{1,0:T(8,128)(2,1)S(1)} %get-tuple-element.100), channel_id=1, source_target_pairs={{0,3},{1,2},{2,1},{3,0},{4,7},{5,6},{6,5},{7,4},{8,11},{9,10},{10,... | collective-permute-start | bytes 393224 | tf_op jit(solution)/shard_map/ppermute | solution.py:60
  73.3 0.4 collective-permute-start.27
  73.7 0.6 collective-permute-start.28
  74.3 1.1 %place_features.1 = bf16[256,2048]{1,0:T(8,128)(2,1)} custom-call(bf16[256,512]{1,0:T(8,128)(2,1)S(1)} %get-tuple-element.97.refs_0_, bf16[256,512]{1,0:T(8,128)(2,1)S(1)} %collective-permute-done.26.refs_1_, bf16[256,512]{1,0:T(8,128)(2,1)S(1)} %collective-permute-done.21.refs_2_, bf16[256,512]{1,0:T(8,128)(2,1)S(1)} %collective-permute-done.22.refs_3_), custom_call_target="tpu_custom_call" | custom-call | flops 1 | bytes 1 | tf_op jit(solution)/shard_map/place_features/pallas_call | solution.py:28
  75.4 2.6 %collective-permute-done.29.refs_3_ = bf16[128,512]{1,0:T(8,128)(2,1)S(1)} collective-permute-done((bf16[128,512]{1,0:T(8,128)(2,1)S(1)}, bf16[128,512]{1,0:T(8,128)(2,1)S(1)}, u32[]{:S(2)}, u32[]{:S(2)}) %collective-permute-start.29) | collective-permute-done | bytes 131104 | tf_op jit(solution)/shard_map/ppermute | solution.py:60
  77.9 2.8 %collective-permute-done.28.refs_2_ = bf16[128,512]{1,0:T(8,128)(2,1)S(1)} collective-permute-done((bf16[128,512]{1,0:T(8,128)(2,1)S(1)}, bf16[128,512]{1,0:T(8,128)(2,1)S(1)}, u32[]{:S(2)}, u32[]{:S(2)}) %collective-permute-start.28) | collective-permute-done | bytes 131104 | tf_op jit(solution)/shard_map/ppermute | solution.py:60
  80.8 3.0 %update.1 = (f32[128,2048]{1,0:T(8,128)}, f32[128,2048]{1,0:T(8,128)}, f32[128,2048]{1,0:T(8,128)}, f32[128,2048]{1,0:T(8,128)}) custom-call(bf16[128,512]{1,0:T(8,128)(2,1)S(1)} %get-tuple-element.99.refs_0_, bf16[128,512]{1,0:T(8,128)(2,1)S(1)} %collective-permute-done.27.refs_1_, bf16[128,512]{1,0:T(8,128)(2,1)S(1)} %collective-permute-done.28.refs_2_, ...), custom_call_target="tpu_custom_call" | custom-call | flops 1 | bytes 1 | tf_op jit(solution)/shard_map/update/pallas_call | solution.py:28
  (43 shorter events, 1.4 us)
Async XLA Ops:
  0.6 5.8 %copy-start = (f32[128,2048]{1,0:T(8,128)S(1)}, f32[128,2048]{1,0:T(8,128)}, u32[]{:S(2)}) copy-start(f32[128,2048]{1,0:T(8,128)} %refs_7_.1) | copy-start | bytes 3145732
  0.6 1.3 %copy-start.1 = (bf16[256,2048]{1,0:T(8,128)(2,1)S(1)}, bf16[256,2048]{1,0:T(8,128)(2,1)}, u32[]{:S(2)}) copy-start(bf16[256,2048]{1,0:T(8,128)(2,1)} %p.1) | copy-start | bytes 3145732
  2.0 1.2 %copy-start.2 = (bf16[256,2048]{1,0:T(8,128)(2,1)S(1)}, bf16[256,2048]{1,0:T(8,128)(2,1)}, u32[]{:S(2)}) copy-start(bf16[256,2048]{1,0:T(8,128)(2,1)} %c.1) | copy-start | bytes 3145732
  3.4 25.8 %collective-permute-start.1 = (bf16[256,2560]{1,0:T(8,128)(2,1)S(1)}, bf16[256,2560]{1,0:T(8,128)(2,1)S(1)}, u32[]{:S(2)}, u32[]{:S(2)}) collective-permute-start(bf16[256,2560]{1,0:T(8,128)(2,1)S(1)} %get-tuple-element.92.own), channel_id=1, source_target_pairs={{0,2},{1,3},{2,0},{3,1},{4,6},{5,7},{6,4},{7,5},{8,10},{9,11},{10,... | collective-permute-start | bytes 3932168 | tf_op jit(solution)/shard_map/ppermute | solution.py:60
  3.9 25.3 %collective-permute-start = (bf16[256,1536]{1,0:T(8,128)(2,1)S(1)}, bf16[256,1536]{1,0:T(8,128)(2,1)S(1)}, u32[]{:S(2)}, u32[]{:S(2)}) collective-permute-start(bf16[256,1536]{1,0:T(8,128)(2,1)S(1)} %get-tuple-element.56), channel_id=1, source_target_pairs={{0,1},{1,0},{2,3},{3,2},{4,5},{5,4},{6,7},{7,6},{8,9},{9,8},{10,11... | collective-permute-start | bytes 2359304 | tf_op jit(solution)/shard_map/ppermute | solution.py:60
  6.5 1.4 %collective-permute-start.2 = (bf16[128,512]{1,0:T(8,128)(2,1)S(1)}, bf16[128,512]{1,0:T(8,128)(2,1)S(1)}, u32[]{:S(2)}, u32[]{:S(2)}) collective-permute-start(bf16[128,512]{1,0:T(8,128)(2,1)S(1)} %get-tuple-element.59), channel_id=1, source_target_pairs={{0,2},{1,3},{2,0},{3,1},{4,6},{5,7},{6,4},{7,5},{8,10},{9,11},{10,... | collective-permute-start | bytes 393224 | tf_op jit(solution)/shard_map/ppermute | solution.py:60
  8.0 8.4 %collective-permute-start.5 = (bf16[256,512]{1,0:T(8,128)(2,1)S(1)}, bf16[256,512]{1,0:T(8,128)(2,1)S(1)}, u32[]{:S(2)}, u32[]{:S(2)}) collective-permute-start(bf16[256,512]{1,0:T(8,128)(2,1)S(1)} %join_teacher.1.refs_0_), channel_id=1, source_target_pairs={{0,4},{1,5},{2,6},{3,7},{4,0},{5,1},{6,2},{7,3},{8,12},{9,13},{10,... | collective-permute-start | bytes 786440 | tf_op jit(solution)/shard_map/ppermute | solution.py:60
  9.8 9.9 %collective-permute-start.3 = (bf16[256,512]{1,0:T(8,128)(2,1)S(1)}, bf16[256,512]{1,0:T(8,128)(2,1)S(1)}, u32[]{:S(2)}, u32[]{:S(2)}) collective-permute-start(bf16[256,512]{1,0:T(8,128)(2,1)S(1)} %join_teacher.1.refs_0_), channel_id=1, source_target_pairs={{0,8},{1,9},{2,10},{3,11},{4,12},{5,13},{6,14},{7,15},{8,16},{9,17... | collective-permute-start | bytes 786440 | tf_op jit(solution)/shard_map/ppermute | solution.py:60
  19.7 7.3 %collective-permute-start.6 = (bf16[256,512]{1,0:T(8,128)(2,1)S(1)}, bf16[256,512]{1,0:T(8,128)(2,1)S(1)}, u32[]{:S(2)}, u32[]{:S(2)}) collective-permute-start(bf16[256,512]{1,0:T(8,128)(2,1)S(1)} %collective-permute-done.3.refs_2_), channel_id=1, source_target_pairs={{0,4},{1,5},{2,6},{3,7},{4,0},{5,1},{6,2},{7,3},{8,12},{9,13},{10,... | collective-permute-start | bytes 786440 | tf_op jit(solution)/shard_map/ppermute | solution.py:60
  20.2 9.0 %collective-permute-start.4 = (bf16[256,512]{1,0:T(8,128)(2,1)S(1)}, bf16[256,512]{1,0:T(8,128)(2,1)S(1)}, u32[]{:S(2)}, u32[]{:S(2)}) collective-permute-start(bf16[256,512]{1,0:T(8,128)(2,1)S(1)} %collective-permute-done.3.refs_2_), channel_id=1, source_target_pairs={{0,8},{1,9},{2,10},{3,11},{4,12},{5,13},{6,14},{7,15},{8,16},{9,17... | collective-permute-start | bytes 786440 | tf_op jit(solution)/shard_map/ppermute | solution.py:60
  20.2 12.4 %collective-permute-start.9 = (bf16[256,512]{1,0:T(8,128)(2,1)S(1)}, bf16[256,512]{1,0:T(8,128)(2,1)S(1)}, u32[]{:S(2)}, u32[]{:S(2)}) collective-permute-start(bf16[256,512]{1,0:T(8,128)(2,1)S(1)} %get-tuple-element.71), channel_id=1, source_target_pairs={{0,1},{1,0},{2,3},{3,2},{4,5},{5,4},{6,7},{7,6},{8,9},{9,8},{10,11... | collective-permute-start | bytes 786440 | tf_op jit(solution)/shard_map/ppermute | solution.py:60
  29.3 5.3 %collective-permute-start.8 = (bf16[256,512]{1,0:T(8,128)(2,1)S(1)}, bf16[256,512]{1,0:T(8,128)(2,1)S(1)}, u32[]{:S(2)}, u32[]{:S(2)}) collective-permute-start(bf16[256,512]{1,0:T(8,128)(2,1)S(1)} %get-tuple-element.64), channel_id=1, source_target_pairs={{0,2},{1,3},{2,0},{3,1},{4,6},{5,7},{6,4},{7,5},{8,10},{9,11},{10,... | collective-permute-start | bytes 786440 | tf_op jit(solution)/shard_map/ppermute | solution.py:60
  29.3 5.2 %collective-permute-start.7 = (bf16[256,512]{1,0:T(8,128)(2,1)S(1)}, bf16[256,512]{1,0:T(8,128)(2,1)S(1)}, u32[]{:S(2)}, u32[]{:S(2)}) collective-permute-start(bf16[256,512]{1,0:T(8,128)(2,1)S(1)} %get-tuple-element.83.par.refs_0_), channel_id=1, source_target_pairs={{0,2},{1,3},{2,0},{3,1},{4,6},{5,7},{6,4},{7,5},{8,10},{9,11},{10,... | collective-permute-start | bytes 786440 | tf_op jit(solution)/shard_map/ppermute | solution.py:60
  29.8 8.3 %collective-permute-start.12 = (bf16[256,512]{1,0:T(8,128)(2,1)S(1)}, bf16[256,512]{1,0:T(8,128)(2,1)S(1)}, u32[]{:S(2)}, u32[]{:S(2)}) collective-permute-start(bf16[256,512]{1,0:T(8,128)(2,1)S(1)} %get-tuple-element.76), channel_id=1, source_target_pairs={{0,1},{1,0},{2,3},{3,2},{4,5},{5,4},{6,7},{7,6},{8,9},{9,8},{10,11... | collective-permute-start | bytes 786440 | tf_op jit(solution)/shard_map/ppermute | solution.py:60
  31.1 8.5 %collective-permute-start.13 = (bf16[256,512]{1,0:T(8,128)(2,1)S(1)}, bf16[256,512]{1,0:T(8,128)(2,1)S(1)}, u32[]{:S(2)}, u32[]{:S(2)}) collective-permute-start(bf16[256,512]{1,0:T(8,128)(2,1)S(1)} %collective-permute-done.4.refs_4_), channel_id=1, source_target_pairs={{0,4},{1,5},{2,6},{3,7},{4,0},{5,1},{6,2},{7,3},{8,12},{9,13},{10,... | collective-permute-start | bytes 786440 | tf_op jit(solution)/shard_map/ppermute | solution.py:60
  32.6 15.7 %collective-permute-start.15 = (bf16[512,512]{1,0:T(8,128)(2,1)S(1)}, bf16[512,512]{1,0:T(8,128)(2,1)S(1)}, u32[]{:S(2)}, u32[]{:S(2)}) collective-permute-start(bf16[512,512]{1,0:T(8,128)(2,1)S(1)} %stack_teacher.1), channel_id=1, source_target_pairs={{0,24},{1,25},{2,26},{3,27},{4,28},{5,29},{6,30},{7,31},{8,0},{9,1... | collective-permute-start | bytes 1572872 | tf_op jit(solution)/shard_map/ppermute | solution.py:60
  34.6 5.3 %collective-permute-start.10 = (bf16[256,512]{1,0:T(8,128)(2,1)S(1)}, bf16[256,512]{1,0:T(8,128)(2,1)S(1)}, u32[]{:S(2)}, u32[]{:S(2)}) collective-permute-start(bf16[256,512]{1,0:T(8,128)(2,1)S(1)} %collective-permute-done.9.par.refs_1_), channel_id=1, source_target_pairs={{0,2},{1,3},{2,0},{3,1},{4,6},{5,7},{6,4},{7,5},{8,10},{9,11},{10,... | collective-permute-start | bytes 786440 | tf_op jit(solution)/shard_map/ppermute | solution.py:60
  35.4 9.8 %collective-permute-start.11 = (bf16[256,512]{1,0:T(8,128)(2,1)S(1)}, bf16[256,512]{1,0:T(8,128)(2,1)S(1)}, u32[]{:S(2)}, u32[]{:S(2)}) collective-permute-start(bf16[256,512]{1,0:T(8,128)(2,1)S(1)} %get-tuple-element.74), channel_id=1, source_target_pairs={{0,4},{1,5},{2,6},{3,7},{4,0},{5,1},{6,2},{7,3},{8,12},{9,13},{10,... | collective-permute-start | bytes 786440 | tf_op jit(solution)/shard_map/ppermute | solution.py:60
  39.6 5.7 %collective-permute-start.14 = (bf16[256,512]{1,0:T(8,128)(2,1)S(1)}, bf16[256,512]{1,0:T(8,128)(2,1)S(1)}, u32[]{:S(2)}, u32[]{:S(2)}) collective-permute-start(bf16[256,512]{1,0:T(8,128)(2,1)S(1)} %collective-permute-done.12.par.refs_2_), channel_id=1, source_target_pairs={{0,2},{1,3},{2,0},{3,1},{4,6},{5,7},{6,4},{7,5},{8,10},{9,11},{10,... | collective-permute-start | bytes 786440 | tf_op jit(solution)/shard_map/ppermute | solution.py:60
  39.6 8.7 %collective-permute-start.18 = (bf16[256,512]{1,0:T(8,128)(2,1)S(1)}, bf16[256,512]{1,0:T(8,128)(2,1)S(1)}, u32[]{:S(2)}, u32[]{:S(2)}) collective-permute-start(bf16[256,512]{1,0:T(8,128)(2,1)S(1)} %get-tuple-element.85), channel_id=1, source_target_pairs={{0,1},{1,0},{2,3},{3,2},{4,5},{5,4},{6,7},{7,6},{8,9},{9,8},{10,11... | collective-permute-start | bytes 786440 | tf_op jit(solution)/shard_map/ppermute | solution.py:60
  40.7 9.6 %collective-permute-start.16 = (bf16[256,512]{1,0:T(8,128)(2,1)S(1)}, bf16[256,512]{1,0:T(8,128)(2,1)S(1)}, u32[]{:S(2)}, u32[]{:S(2)}) collective-permute-start(bf16[256,512]{1,0:T(8,128)(2,1)S(1)} %get-tuple-element.82), channel_id=1, source_target_pairs={{0,4},{1,5},{2,6},{3,7},{4,0},{5,1},{6,2},{7,3},{8,12},{9,13},{10,... | collective-permute-start | bytes 786440 | tf_op jit(solution)/shard_map/ppermute | solution.py:60
  45.3 7.4 %collective-permute-start.17 = (bf16[256,512]{1,0:T(8,128)(2,1)S(1)}, bf16[256,512]{1,0:T(8,128)(2,1)S(1)}, u32[]{:S(2)}, u32[]{:S(2)}) collective-permute-start(bf16[256,512]{1,0:T(8,128)(2,1)S(1)} %add_blocks.3), channel_id=1, source_target_pairs={{0,8},{1,9},{2,10},{3,11},{4,12},{5,13},{6,14},{7,15},{8,0},{9,1},... | collective-permute-start | bytes 786440 | tf_op jit(solution)/shard_map/ppermute | solution.py:60
  48.3 7.1 %collective-permute-start.19 = (bf16[256,512]{1,0:T(8,128)(2,1)S(1)}, bf16[256,512]{1,0:T(8,128)(2,1)S(1)}, u32[]{:S(2)}, u32[]{:S(2)}) collective-permute-start(bf16[256,512]{1,0:T(8,128)(2,1)S(1)} %collective-permute-done.18.refs_3_.par), channel_id=1, source_target_pairs={{0,2},{1,3},{2,0},{3,1},{4,6},{5,7},{6,4},{7,5},{8,10},{9,11},{10,... | collective-permute-start | bytes 786440 | tf_op jit(solution)/shard_map/ppermute | solution.py:60
  48.3 10.3 %collective-permute-start.20 = (bf16[256,512]{1,0:T(8,128)(2,1)S(1)}, bf16[256,512]{1,0:T(8,128)(2,1)S(1)}, u32[]{:S(2)}, u32[]{:S(2)}) collective-permute-start(bf16[256,512]{1,0:T(8,128)(2,1)S(1)} %get-tuple-element.91), channel_id=1, source_target_pairs={{0,4},{1,5},{2,6},{3,7},{4,0},{5,1},{6,2},{7,3},{8,12},{9,13},{10,... | collective-permute-start | bytes 786440 | tf_op jit(solution)/shard_map/ppermute | solution.py:60
  53.5 9.0 %collective-permute-start.21 = (bf16[256,512]{1,0:T(8,128)(2,1)S(1)}, bf16[256,512]{1,0:T(8,128)(2,1)S(1)}, u32[]{:S(2)}, u32[]{:S(2)}) collective-permute-start(bf16[256,512]{1,0:T(8,128)(2,1)S(1)} %far_features.2), channel_id=1, source_target_pairs={{0,1},{1,0},{2,3},{3,2},{4,5},{5,4},{6,7},{7,6},{8,9},{9,8},{10,11... | collective-permute-start | bytes 786440 | tf_op jit(solution)/shard_map/ppermute | solution.py:60
  54.6 13.1 %collective-permute-start.24 = (bf16[256,512]{1,0:T(8,128)(2,1)S(1)}, bf16[256,512]{1,0:T(8,128)(2,1)S(1)}, u32[]{:S(2)}, u32[]{:S(2)}) collective-permute-start(bf16[256,512]{1,0:T(8,128)(2,1)S(1)} %add_blocks.4), channel_id=1, source_target_pairs={{0,16},{1,17},{2,18},{3,19},{4,20},{5,21},{6,22},{7,23},{8,24},{9,... | collective-permute-start | bytes 786440 | tf_op jit(solution)/shard_map/ppermute | solution.py:60
  57.0 8.6 %collective-permute-start.22 = (bf16[256,512]{1,0:T(8,128)(2,1)S(1)}, bf16[256,512]{1,0:T(8,128)(2,1)S(1)}, u32[]{:S(2)}, u32[]{:S(2)}) collective-permute-start(bf16[256,512]{1,0:T(8,128)(2,1)S(1)} %far_features.3), channel_id=1, source_target_pairs={{0,3},{1,2},{2,1},{3,0},{4,7},{5,6},{6,5},{7,4},{8,11},{9,10},{10,... | collective-permute-start | bytes 786440 | tf_op jit(solution)/shard_map/ppermute | solution.py:60
  57.1 10.6 %collective-permute-start.23 = (bf16[256,512]{1,0:T(8,128)(2,1)S(1)}, bf16[256,512]{1,0:T(8,128)(2,1)S(1)}, u32[]{:S(2)}, u32[]{:S(2)}) collective-permute-start(bf16[256,512]{1,0:T(8,128)(2,1)S(1)} %get-tuple-element.95), channel_id=1, source_target_pairs={{0,4},{1,5},{2,6},{3,7},{4,0},{5,1},{6,2},{7,3},{8,12},{9,13},{10,... | collective-permute-start | bytes 786440 | tf_op jit(solution)/shard_map/ppermute | solution.py:60
  58.7 13.2 %collective-permute-start.25 = (bf16[256,512]{1,0:T(8,128)(2,1)S(1)}, bf16[256,512]{1,0:T(8,128)(2,1)S(1)}, u32[]{:S(2)}, u32[]{:S(2)}) collective-permute-start(bf16[256,512]{1,0:T(8,128)(2,1)S(1)} %add_blocks.5), channel_id=1, source_target_pairs={{0,8},{1,9},{2,10},{3,11},{4,12},{5,13},{6,14},{7,15},{8,0},{9,1},... | collective-permute-start | bytes 786440 | tf_op jit(solution)/shard_map/ppermute | solution.py:60
  62.5 11.8 %collective-permute-start.26 = (bf16[256,512]{1,0:T(8,128)(2,1)S(1)}, bf16[256,512]{1,0:T(8,128)(2,1)S(1)}, u32[]{:S(2)}, u32[]{:S(2)}) collective-permute-start(bf16[256,512]{1,0:T(8,128)(2,1)S(1)} %get-tuple-element.98), channel_id=1, source_target_pairs={{0,2},{1,3},{2,0},{3,1},{4,6},{5,7},{6,4},{7,5},{8,10},{9,11},{10,... | collective-permute-start | bytes 786440 | tf_op jit(solution)/shard_map/ppermute | solution.py:60
  71.9 8.8 %copy-start.5 = (f32[128,2048]{1,0:T(8,128)S(1)}, f32[128,2048]{1,0:T(8,128)}, u32[]{:S(2)}) copy-start(f32[128,2048]{1,0:T(8,128)} %refs_6_.1) | copy-start | bytes 3145732
  72.1 8.7 %copy-start.3 = (f32[128,2048]{1,0:T(8,128)S(1)}, f32[128,2048]{1,0:T(8,128)}, u32[]{:S(2)}) copy-start(f32[128,2048]{1,0:T(8,128)} %refs_4_.1) | copy-start | bytes 3145732
  72.1 8.7 %copy-start.4 = (f32[128,2048]{1,0:T(8,128)S(1)}, f32[128,2048]{1,0:T(8,128)}, u32[]{:S(2)}) copy-start(f32[128,2048]{1,0:T(8,128)} %refs_5_.1) | copy-start | bytes 3145732
  72.1 5.8 %collective-permute-start.29 = (bf16[128,512]{1,0:T(8,128)(2,1)S(1)}, bf16[128,512]{1,0:T(8,128)(2,1)S(1)}, u32[]{:S(2)}, u32[]{:S(2)}) collective-permute-start(bf16[128,512]{1,0:T(8,128)(2,1)S(1)} %get-tuple-element.100), channel_id=1, source_target_pairs={{0,3},{1,2},{2,1},{3,0},{4,7},{5,6},{6,5},{7,4},{8,11},{9,10},{10,... | collective-permute-start | bytes 393224 | tf_op jit(solution)/shard_map/ppermute | solution.py:60
  73.3 4.6 %collective-permute-start.27 = (bf16[128,512]{1,0:T(8,128)(2,1)S(1)}, bf16[128,512]{1,0:T(8,128)(2,1)S(1)}, u32[]{:S(2)}, u32[]{:S(2)}) collective-permute-start(bf16[128,512]{1,0:T(8,128)(2,1)S(1)} %get-tuple-element.100), channel_id=1, source_target_pairs={{0,2},{1,3},{2,0},{3,1},{4,6},{5,7},{6,4},{7,5},{8,10},{9,11},{10,... | collective-permute-start | bytes 393224 | tf_op jit(solution)/shard_map/ppermute | solution.py:60
  73.7 7.0 %collective-permute-start.28 = (bf16[128,512]{1,0:T(8,128)(2,1)S(1)}, bf16[128,512]{1,0:T(8,128)(2,1)S(1)}, u32[]{:S(2)}, u32[]{:S(2)}) collective-permute-start(bf16[128,512]{1,0:T(8,128)(2,1)S(1)} %get-tuple-element.99.refs_0_), channel_id=1, source_target_pairs={{0,1},{1,0},{2,3},{3,2},{4,5},{5,4},{6,7},{7,6},{8,9},{9,8},{10,11... | collective-permute-start | bytes 393224 | tf_op jit(solution)/shard_map/ppermute | solution.py:60

commit v2 on v1

--- a/solution.py
+++ b/solution.py
@@ -18,6 +18,7 @@
 
 bf16, f32 = jnp.bfloat16, jnp.float32
 VMEM = pl.BlockSpec(memory_space=pltpu.VMEM)
+ANY = pl.BlockSpec(memory_space=pl.ANY)
 
 
 def call(name, body, outs, inputs, scratch=()):
@@ -68,8 +69,12 @@
     def diagonal(z, y, c, g, h):
         return z, y, 1 - c, g, 1 - h
 
+    def turned(z, d):
+        p = ((z ^ (z >> 1)) + d) & 3
+        return p ^ (p >> 1)
+
     def along_z(d):
-        return lambda z, y, c, g, h: ((z + d) % nz, y, c, g, h)
+        return lambda z, y, c, g, h: (turned(z, d), y, c, g, h)
 
     def across_z(d):
         return lambda z, y, c, g, h: (z ^ d, y, c, g, h)
@@ -94,7 +99,7 @@
         g_order = [3, 2, 1, 0]
         lead = 2 * part
 
-        def cut_body(p, c, first, near, c_own, *rest):
+        def cut_body(p, c, first, near, c_own, second, third):
             z, y, core, q = place()
             first[:, :lead] = c[:, aligned(1 - q // 2, lead)]
             for k, dz in enumerate(g_order):
@@ -102,8 +107,10 @@
                 near[:, k * span : (k + 1) * span] = block
                 if k == 0:
                     first[:, lead:] = block
+                elif k < 3:
+                    second[:, (k - 1) * span : k * span] = block
                 else:
-                    rest[k - 1][...] = block
+                    third[...] = block
             near[:, feat:] = c[:, aligned(q ^ 1, part)]
             c_own[...] = c[:, aligned(q, part)]
 
@@ -112,6 +119,10 @@
             c_sib[...] = message[:, aligned(1 - core, part)]
             c_here[...] = message[:, aligned(core, part)]
             block[...] = message[:, lead:]
+
+        def halve_body(message, *blocks):
+            for k, out in enumerate(blocks):
+                out[...] = message[:, k * span : (k + 1) * span]
 
         clock = []
 
@@ -160,7 +171,10 @@
                 whole[...] = total
                 for dy in range(ny):
                     block = whole[aligned(lax.rem(y + dy, ny), 2 * rows), :]
-                    outs[dy][...] = block.astype(outs[dy].dtype)
+                    outs[dy][: 2 * rows, :] = block.astype(outs[dy].dtype)
+                    if outs[dy].shape[0] > 2 * rows:
+                        rest = (outs[dy].shape[0] - 2 * rows, part)
+                        outs[dy][2 * rows :, :] = jnp.zeros(rest, outs[dy].dtype)
 
             return body
 
@@ -169,14 +183,17 @@
             terms[dz] = run(
                 "gradient_block",
                 terms_body(k),
-                [((2 * rows, part), f32)] + [((2 * rows, part), bf16)] * (ny - 1),
+                [((2 * rows, part), f32)] + [((2 * rows + 16 * (k == 0), part), bf16)] * (ny - 1),
                 [near_own, near_sib, far_par[k], far_dia[k], c_own, c_par, c_dia],
                 scratch=[pltpu.VMEM((span, part), f32)],
             )
-            moved_y[dz] = [start(terms[dz][dy], along_y(dy)) for dy in others]
+            gates = () if k else w_side[2]
+            moved_y[dz] = [start(terms[dz][dy], along_y(dy), *gates) for dy in others]
 
         def add_body(*refs):
-            refs[-1][...] = sum(ref[...].astype(f32) for ref in refs[:-1]).astype(refs[-1].dtype)
+            count = refs[-1].shape[0]
+            total = sum(ref[:count, :].astype(f32) for ref in refs[:-1])
+            refs[-1][...] = total.astype(refs[-1].dtype)
 
         def add(values, dtype, **options):
             return run("add_blocks", add_body, [(values[0].shape, dtype)], values, **options)[0]
@@ -200,7 +217,7 @@
             for k in range(nz * ny):
                 dz, dy = w_order[k // ny], k % ny
                 ref, at = (refs[k], 0) if dz != 1 else (refs[-2], dy * 2 * rows)
-                block = (z ^ lax.rem(z + dz, nz)) * ny + lax.rem(y + dy, ny)
+                block = (z ^ turned(z, dz)) * ny + lax.rem(y + dy, ny)
                 refs[-1][aligned(block, 2 * rows), :] = ref[at : at + 2 * rows, :]
 
         def near_body(own, sib, full, f_own, f_sib):
@@ -233,18 +250,18 @@
         def block_sum(dz, *more, **options):
             return add([terms[dz][0], *moved_y[dz], *more], bf16, **options)
 
-        first, near_own, c_own, *rest = run(
+        first, near_own, c_own, second, third = run(
             "cut_tokens",
             cut_body,
             [
                 ((tokens, width), bf16)
-                for width in (lead + span, feat + part, part, *[span] * (nz - 1))
+                for width in (lead + span, feat + part, part, 2 * span, span)
             ],
             [patches, cotangent],
         )
         message = start(first, partner)
         near_sib = start(near_own, sibling)
-        w_same, w_other = run("cast_teacher", cast_body, [((rows, part), bf16)] * 2, [teacher])
+        w_same, w_other = run("cast_teacher", cast_body, [((rows, part), bf16)] * 2, [after(teacher, first)])
         w_sib = start(w_other, sibling)
         (w_line[0],) = run(
             "join_teacher", join_body, [((2 * rows, part), bf16)], [w_same, w_sib]
@@ -256,10 +273,8 @@
         (turn,) = run(
             "stack_teacher", stack_body, [((ny * 2 * rows, part), bf16)], [w_line[0], *w_side[0]]
         )
-        turn = start(turn, along_z(-1), w_line[2])
         teacher_y(2)
-        for k in range(1, nz):
-            far_par[k] = start(rest[k - 1], partner, *far_par[1 : k - 1])
+        second = start(second, partner)
         c_other, c_par, far_par[0] = run(
             "split_message",
             split_body,
@@ -267,12 +282,18 @@
             [after(message, near_sib, w_line[2], *w_side[3])],
         )
         c_dia = start(c_other, sibling)
-        held = ([], [], w_side[2])
-        for k in range(nz - 1):
-            far_dia[k] = start(far_par[k], sibling, *held[k])
+        far_dia[0] = start(far_par[0], sibling)
         gradient_block(0)
+        begun = terms[3][0]
+        far_par[3] = start(third, partner, begun)
+        turn = start(turn, along_z(-1), begun)
+        far_par[1:3] = run(
+            "halve_message", halve_body, [((tokens, span), bf16)] * 2, [second]
+        )
+        far_dia[1] = start(far_par[1], sibling)
         gradient_block(1)
         onward = start(block_sum(3), across_z(1))
+        far_dia[2] = start(far_par[2], sibling)
         gradient_block(2)
         far_dia[3] = start(far_par[3], sibling, turn, terms[1][0])
         (w_full,) = run(
@@ -281,8 +302,8 @@
             [((feat, part), bf16)],
             [*(w for dz in w_order[:-1] for w in (w_line[dz], *w_side[dz])), turn],
         )
+        f_par = start(far_features(far_par), partner)
         onward = start(block_sum(2, onward), across_z(2))
-        f_par = start(far_features(far_par), partner)
         gradient_block(3)
         f_dia = start(far_features(far_dia), diagonal)
         back = start(block_sum(1), across_z(1))
@@ -303,38 +324,63 @@
         g_par, g_dia, g_sib = (
             start(mine, partner), start(other, diagonal), start(other, sibling)
         )
+        def update_body(quarters):
+            def body(*refs):
+                z, y, core, q = place()
+                student, first, second, teach = refs[2:6]
+                outs, held, sems = refs[-6:-2], refs[-2], refs[-1]
+                corr_one = 1.0 - beta_one**STEP
+                corr_two = 1.0 - beta_two**STEP
+                copies = []
+                for i, j in enumerate(quarters):
+                    at = (slice(None), aligned(q ^ j, part))
+                    gradient = refs[i][...].astype(f32)
+                    new_first = beta_one * first[at] + (1.0 - beta_one) * gradient
+                    new_second = beta_two * second[at] + (1.0 - beta_two) * gradient * gradient
+                    direction = new_first / corr_one / (jnp.sqrt(new_second / corr_two) + adam_eps)
+                    weights = student[at]
+                    new_student = weights - learn_rate * (direction + decay_rate * weights)
+                    new_teacher = ema_keep * teach[at] + (1.0 - ema_keep) * new_student
+                    for k, new in enumerate((new_student, new_first, new_second, new_teacher)):
+                        held[4 * i + k] = new
+                        copies.append(
+                            pltpu.make_async_copy(
+                                held.at[4 * i + k], outs[k].at[at], sems.at[4 * i + k]
+                            )
+                        )
+                        copies[-1].start()
+                for copy in copies:
+                    copy.wait()
+
+            return body
+
+        def update(name, quarters, grads, begun):
+            inputs = [after(grads[0], *clock), *grads[1:]]
+            inputs += [student, first_moment, second_moment, teacher]
+            with jax.named_scope(name):
+                out = pl.pallas_call(
+                    update_body(quarters),
+                    out_shape=[jax.ShapeDtypeStruct((rows, outw), f32)] * 4,
+                    in_specs=[VMEM] * 6 + [ANY] * len(begun),
+                    out_specs=[ANY] * 4,
+                    input_output_aliases={6 + k: k for k in range(len(begun))},
+                    scratch_shapes=[
+                        pltpu.VMEM((8, rows, part), f32), pltpu.SemaphoreType.DMA((8,))
+                    ],
+                    cost_estimate=pl.CostEstimate(flops=1, bytes_accessed=1, transcendentals=0),
+                    compiler_params=pltpu.CompilerParams(vmem_limit_bytes=16 * 2**20),
+                )(*inputs, *begun)
+            clock[:] = out[:1]
+            return out
+
+        new = update("update_near", (0, 1), [mine, g_sib], [])
         (features,) = run(
             "place_features",
             place_body,
             [((tokens, outw), bf16)],
             [f_own, f_sib, f_par, f_dia],
         )
-        grads = [mine, g_sib, g_par, g_dia]
-
-        def update_body(*refs):
-            z, y, core, q = place()
-            student, first, second, teach, *outs = refs[4:]
-            corr_one = 1.0 - beta_one**STEP
-            corr_two = 1.0 - beta_two**STEP
-            for j in range(4):
-                at = (slice(None), aligned(q ^ j, part))
-                gradient = refs[j][...].astype(f32)
-                new_first = beta_one * first[at] + (1.0 - beta_one) * gradient
-                new_second = beta_two * second[at] + (1.0 - beta_two) * gradient * gradient
-                direction = new_first / corr_one / (jnp.sqrt(new_second / corr_two) + adam_eps)
-                weights = student[at]
-                new_student = weights - learn_rate * (direction + decay_rate * weights)
-                outs[0][at] = new_student
-                outs[1][at] = new_first
-                outs[2][at] = new_second
-                outs[3][at] = ema_keep * teach[at] + (1.0 - ema_keep) * new_student
-
-        new = run(
-            "update",
-            update_body,
-            [((rows, outw), f32)] * 4,
-            [*grads, student, first_moment, second_moment, teacher],
-        )
+        new = update("update_far", (2, 3), [g_par, g_dia], new)
         return (features, *new)
 
     tokens_placed, weights_placed = P(("fsdp", "rep"), None), P("fsdp", None)

time: 83.9 us -> 82.3 us (0.981)
  waiting for transfers between devices: 42.3 us -> 36.3 us
  starting transfers between devices: 27.2 us -> 31.2 us
    ppermute x30 -> x29, waiting for transfers between devices: 42.3 us -> 36.3 us  [send(): return lax.ppermute(value, ('fsdp', 'rep'), perm)]
    ppermute x30 -> x29, starting transfers between devices: 27.2 us -> 31.2 us  [send(): return lax.ppermute(value, ('fsdp', 'rep'), perm)]
    pallas_call x0 -> x2, Pallas kernels: none -> 3.33 us  [update(): pl.pallas_call(update_body(quarters), out_shape=[jax.ShapeDtypeStruct((ro...]
    pallas_call x19, Pallas kernels: 10.8 us -> 7.91 us  [call(): pl.pallas_call(body, out_shape=shapes, in_specs=[VMEM] * len(inputs), out...]
  transfers between devices with their start and end apart: 30 -> 29, of which waited for: 16 -> 14; matrix products, arithmetic and copies ran while one was open for 0% -> 0% of each run, Pallas kernels for 9% -> 11%
where the time goes in v2:
time: 82.3 us; the launch traced here: 82.2 us
  waiting for transfers between devices  36.3 us (44%)
  starting transfers between devices  31.2 us (38%)
  Pallas kernels  11.2 us (14%)
  local copies, waits for them, and re-layouts  2.55 us (3%)
  between operations  0.86 us (1%)
    ppermute x29, waiting for transfers between devices, send(): return lax.ppermute(value, ('fsdp', 'rep'), perm)  36.3 us
    ppermute x29, starting transfers between devices, send(): return lax.ppermute(value, ('fsdp', 'rep'), perm)  31.2 us
    pallas_call x19, Pallas kernels, call(): pl.pallas_call(body, out_shape=shapes, in_specs=[VMEM] * len(inputs), out...  7.91 us
    pallas_call x2, Pallas kernels, update(): pl.pallas_call(update_body(quarters), out_shape=[jax.ShapeDtypeStruct((ro...  3.33 us
    unnamed x12, local copies, waits for them, and re-layouts  2.55 us
  transfers between devices with their start and end apart: 29, of which 14 were waited for; matrix products, arithmetic and copies ran while one was open for 0% of the time, Pallas kernels for 11%

profile of v2, /device:TPU:0, one launch (start us, length us, event | category | flops | bytes accessed | tf_op | source)
XLA Modules:
  0.0 82.2 jit_solution(11307194663897586200)
XLA Ops:
  0.7 1.3 %copy-done.4 = bf16[256,2048]{1,0:T(8,128)(2,1)S(1)} copy-done((bf16[256,2048]{1,0:T(8,128)(2,1)S(1)}, bf16[256,2048]{1,0:T(8,128)(2,1)}, u32[]{:S(2)}) %copy-start.4) | copy-done | bytes 1048600
  2.0 1.2 %copy-done.5 = bf16[256,2048]{1,0:T(8,128)(2,1)S(1)} copy-done((bf16[256,2048]{1,0:T(8,128)(2,1)S(1)}, bf16[256,2048]{1,0:T(8,128)(2,1)}, u32[]{:S(2)}) %copy-start.5) | copy-done | bytes 1048600
  3.4 0.5 collective-permute-start.1
  3.9 2.6 %collective-permute-start = (bf16[256,1536]{1,0:T(8,128)(2,1)S(1)}, bf16[256,1536]{1,0:T(8,128)(2,1)S(1)}, u32[]{:S(2)}, u32[]{:S(2)}) collective-permute-start(bf16[256,1536]{1,0:T(8,128)(2,1)S(1)} %get-tuple-element.64), channel_id=1, source_target_pairs={{0,1},{1,0},{2,3},{3,2},{4,5},{5,4},{6,7},{7,6},{8,9},{9,8},{10,11... | collective-permute-start | bytes 2359304 | tf_op jit(solution)/shard_map/ppermute | solution.py:61
  6.5 0.2 collective-permute-start.2
  6.7 1.2 %collective-permute-done.2.sib = bf16[128,512]{1,0:T(8,128)(2,1)S(1)} collective-permute-done((bf16[128,512]{1,0:T(8,128)(2,1)S(1)}, bf16[128,512]{1,0:T(8,128)(2,1)S(1)}, u32[]{:S(2)}, u32[]{:S(2)}) %collective-permute-start.2) | collective-permute-done | bytes 131104 | tf_op jit(solution)/shard_map/ppermute | solution.py:61
  8.0 1.8 %collective-permute-start.5 = (bf16[256,512]{1,0:T(8,128)(2,1)S(1)}, bf16[256,512]{1,0:T(8,128)(2,1)S(1)}, u32[]{:S(2)}, u32[]{:S(2)}) collective-permute-start(bf16[256,512]{1,0:T(8,128)(2,1)S(1)} %join_teacher.1.refs_0_), channel_id=1, source_target_pairs={{0,4},{1,5},{2,6},{3,7},{4,0},{5,1},{6,2},{7,3},{8,12},{9,13},{10,... | collective-permute-start | bytes 786440 | tf_op jit(solution)/shard_map/ppermute | solution.py:61
  9.8 1.6 %collective-permute-start.3 = (bf16[256,512]{1,0:T(8,128)(2,1)S(1)}, bf16[256,512]{1,0:T(8,128)(2,1)S(1)}, u32[]{:S(2)}, u32[]{:S(2)}) collective-permute-start(bf16[256,512]{1,0:T(8,128)(2,1)S(1)} %join_teacher.1.refs_0_), channel_id=1, source_target_pairs={{0,8},{1,9},{2,10},{3,11},{4,12},{5,13},{6,14},{7,15},{8,24},{9,25... | collective-permute-start | bytes 786440 | tf_op jit(solution)/shard_map/ppermute | solution.py:61
  11.3 5.1 %collective-permute-done.5.refs_1_ = bf16[256,512]{1,0:T(8,128)(2,1)S(1)} collective-permute-done((bf16[256,512]{1,0:T(8,128)(2,1)S(1)}, bf16[256,512]{1,0:T(8,128)(2,1)S(1)}, u32[]{:S(2)}, u32[]{:S(2)}) %collective-permute-start.5) | collective-permute-done | bytes 262176 | tf_op jit(solution)/shard_map/ppermute | solution.py:61
  16.4 2.3 %collective-permute-done.3.refs_2_ = bf16[256,512]{1,0:T(8,128)(2,1)S(1)} collective-permute-done((bf16[256,512]{1,0:T(8,128)(2,1)S(1)}, bf16[256,512]{1,0:T(8,128)(2,1)S(1)}, u32[]{:S(2)}, u32[]{:S(2)}) %collective-permute-start.3) | collective-permute-done | bytes 262176 | tf_op jit(solution)/shard_map/ppermute | solution.py:61
  18.7 0.5 collective-permute-start.6
  19.2 0.8 %collective-permute-start.4 = (bf16[256,512]{1,0:T(8,128)(2,1)S(1)}, bf16[256,512]{1,0:T(8,128)(2,1)S(1)}, u32[]{:S(2)}, u32[]{:S(2)}) collective-permute-start(bf16[256,512]{1,0:T(8,128)(2,1)S(1)} %collective-permute-done.3.refs_2_), channel_id=1, source_target_pairs={{0,8},{1,9},{2,10},{3,11},{4,12},{5,13},{6,14},{7,15},{8,24},{9,25... | collective-permute-start | bytes 786440 | tf_op jit(solution)/shard_map/ppermute | solution.py:61
  20.0 1.5 %collective-permute-start.9 = (bf16[256,1024]{1,0:T(8,128)(2,1)S(1)}, bf16[256,1024]{1,0:T(8,128)(2,1)S(1)}, u32[]{:S(2)}, u32[]{:S(2)}) collective-permute-start(bf16[256,1024]{1,0:T(8,128)(2,1)S(1)} %get-tuple-element.79), channel_id=1, source_target_pairs={{0,1},{1,0},{2,3},{3,2},{4,5},{5,4},{6,7},{7,6},{8,9},{9,8},{10,11... | collective-permute-start | bytes 1572872 | tf_op jit(solution)/shard_map/ppermute | solution.py:61
  21.5 4.4 %collective-permute-done.6.refs_3_ = bf16[256,512]{1,0:T(8,128)(2,1)S(1)} collective-permute-done((bf16[256,512]{1,0:T(8,128)(2,1)S(1)}, bf16[256,512]{1,0:T(8,128)(2,1)S(1)}, u32[]{:S(2)}, u32[]{:S(2)}) %collective-permute-start.6) | collective-permute-done | bytes 262176 | tf_op jit(solution)/shard_map/ppermute | solution.py:61
  25.9 1.2 %collective-permute-done.4.refs_4_ = bf16[256,512]{1,0:T(8,128)(2,1)S(1)} collective-permute-done((bf16[256,512]{1,0:T(8,128)(2,1)S(1)}, bf16[256,512]{1,0:T(8,128)(2,1)S(1)}, u32[]{:S(2)}, u32[]{:S(2)}) %collective-permute-start.4) | collective-permute-done | bytes 262176 | tf_op jit(solution)/shard_map/ppermute | solution.py:61
  27.3 0.5 collective-permute-start.7
  27.8 1.4 %collective-permute-start.11 = (bf16[256,512]{1,0:T(8,128)(2,1)S(1)}, bf16[256,512]{1,0:T(8,128)(2,1)S(1)}, u32[]{:S(2)}, u32[]{:S(2)}) collective-permute-start(bf16[256,512]{1,0:T(8,128)(2,1)S(1)} %collective-permute-done.4.refs_4_), channel_id=1, source_target_pairs={{0,4},{1,5},{2,6},{3,7},{4,0},{5,1},{6,2},{7,3},{8,12},{9,13},{10,... | collective-permute-start | bytes 786440 | tf_op jit(solution)/shard_map/ppermute | solution.py:61
  29.2 0.8 %gradient_block.4 = (f32[256,512]{1,0:T(8,128)S(1)}, bf16[272,512]{1,0:T(8,128)(2,1)S(1)}) custom-call(bf16[256,2560]{1,0:T(8,128)(2,1)S(1)} %get-tuple-element.103.own, bf16[256,2560]{1,0:T(8,128)(2,1)S(1)} %collective-permute-done.1.sib, bf16[256,512]{1,0:T(8,128)(2,1)S(1)} %get-tuple-element.92.par.refs_0_, ...), custom_call_target="tpu_custom_call" | custom-call | flops 1 | bytes 1 | tf_op jit(solution)/shard_map/gradient_block/pallas_call | solution.py:29
  30.1 1.6 %collective-permute-start.14 = (bf16[512,512]{1,0:T(8,128)(2,1)S(1)}, bf16[512,512]{1,0:T(8,128)(2,1)S(1)}, u32[]{:S(2)}, u32[]{:S(2)}) collective-permute-start(bf16[512,512]{1,0:T(8,128)(2,1)S(1)} %stack_teacher.1), channel_id=1, source_target_pairs={{0,16},{1,17},{2,18},{3,19},{4,20},{5,21},{6,22},{7,23},{8,0},{9,1... | collective-permute-start | bytes 1572872 | tf_op jit(solution)/shard_map/ppermute | solution.py:61
  31.6 4.5 %collective-permute-done.11.refs_5_ = bf16[256,512]{1,0:T(8,128)(2,1)S(1)} collective-permute-done((bf16[256,512]{1,0:T(8,128)(2,1)S(1)}, bf16[256,512]{1,0:T(8,128)(2,1)S(1)}, u32[]{:S(2)}, u32[]{:S(2)}) %collective-permute-start.11) | collective-permute-done | bytes 262176 | tf_op jit(solution)/shard_map/ppermute | solution.py:61
  36.1 1.4 %collective-permute-start.12 = (bf16[272,512]{1,0:T(8,128)(2,1)S(1)}, bf16[272,512]{1,0:T(8,128)(2,1)S(1)}, u32[]{:S(2)}, u32[]{:S(2)}) collective-permute-start(bf16[272,512]{1,0:T(8,128)(2,1)S(1)} %get-tuple-element.86), channel_id=1, source_target_pairs={{0,4},{1,5},{2,6},{3,7},{4,0},{5,1},{6,2},{7,3},{8,12},{9,13},{10,... | collective-permute-start | bytes 835592 | tf_op jit(solution)/shard_map/ppermute | solution.py:61
  37.6 0.5 collective-permute-start.13
  38.1 1.5 %collective-permute-start.15 = (bf16[256,512]{1,0:T(8,128)(2,1)S(1)}, bf16[256,512]{1,0:T(8,128)(2,1)S(1)}, u32[]{:S(2)}, u32[]{:S(2)}) collective-permute-start(bf16[256,512]{1,0:T(8,128)(2,1)S(1)} %get-tuple-element.94), channel_id=1, source_target_pairs={{0,1},{1,0},{2,3},{3,2},{4,5},{5,4},{6,7},{7,6},{8,9},{9,8},{10,11... | collective-permute-start | bytes 786440 | tf_op jit(solution)/shard_map/ppermute | solution.py:61
  39.6 0.8 %gradient_block.5 = (f32[256,512]{1,0:T(8,128)S(1)}, bf16[256,512]{1,0:T(8,128)(2,1)S(1)}) custom-call(bf16[256,2560]{1,0:T(8,128)(2,1)S(1)} %get-tuple-element.103.own, bf16[256,2560]{1,0:T(8,128)(2,1)S(1)} %collective-permute-done.1.sib, bf16[256,512]{1,0:T(8,128)(2,1)S(1)} %get-tuple-element.81.par.refs_1_, ...), custom_call_target="tpu_custom_call" | custom-call | flops 1 | bytes 1 | tf_op jit(solution)/shard_map/gradient_block/pallas_call | solution.py:29
  40.4 0.6 collective-permute-start.16
  41.0 3.8 %collective-permute-done.12.refs_1_ = bf16[272,512]{1,0:T(8,128)(2,1)S(1)} collective-permute-done((bf16[272,512]{1,0:T(8,128)(2,1)S(1)}, bf16[272,512]{1,0:T(8,128)(2,1)S(1)}, u32[]{:S(2)}, u32[]{:S(2)}) %collective-permute-start.12) | collective-permute-done | bytes 278560 | tf_op jit(solution)/shard_map/ppermute | solution.py:61
  44.9 0.6 collective-permute-start.17
  45.5 0.8 %gradient_block.6 = (f32[256,512]{1,0:T(8,128)S(1)}, bf16[256,512]{1,0:T(8,128)(2,1)S(1)}) custom-call(bf16[256,2560]{1,0:T(8,128)(2,1)S(1)} %get-tuple-element.103.own, bf16[256,2560]{1,0:T(8,128)(2,1)S(1)} %collective-permute-done.1.sib, bf16[256,512]{1,0:T(8,128)(2,1)S(1)} %get-tuple-element.88.par.refs_2_, ...), custom_call_target="tpu_custom_call" | custom-call | flops 1 | bytes 1 | tf_op jit(solution)/shard_map/gradient_block/pallas_call | solution.py:29
  46.4 2.2 %collective-permute-start.19 = (bf16[256,512]{1,0:T(8,128)(2,1)S(1)}, bf16[256,512]{1,0:T(8,128)(2,1)S(1)}, u32[]{:S(2)}, u32[]{:S(2)}) collective-permute-start(bf16[256,512]{1,0:T(8,128)(2,1)S(1)} %get-tuple-element.102), channel_id=1, source_target_pairs={{0,4},{1,5},{2,6},{3,7},{4,0},{5,1},{6,2},{7,3},{8,12},{9,13},{10,... | collective-permute-start | bytes 786440 | tf_op jit(solution)/shard_map/ppermute | solution.py:61
  48.8 0.7 far_features.2
  49.5 1.7 %collective-permute-start.20 = (bf16[256,512]{1,0:T(8,128)(2,1)S(1)}, bf16[256,512]{1,0:T(8,128)(2,1)S(1)}, u32[]{:S(2)}, u32[]{:S(2)}) collective-permute-start(bf16[256,512]{1,0:T(8,128)(2,1)S(1)} %far_features.2), channel_id=1, source_target_pairs={{0,1},{1,0},{2,3},{3,2},{4,5},{5,4},{6,7},{7,6},{8,9},{9,8},{10,11... | collective-permute-start | bytes 786440 | tf_op jit(solution)/shard_map/ppermute | solution.py:61
  51.4 3.6 %collective-permute-start.23 = (bf16[256,512]{1,0:T(8,128)(2,1)S(1)}, bf16[256,512]{1,0:T(8,128)(2,1)S(1)}, u32[]{:S(2)}, u32[]{:S(2)}) collective-permute-start(bf16[256,512]{1,0:T(8,128)(2,1)S(1)} %add_blocks.4), channel_id=1, source_target_pairs={{0,16},{1,17},{2,18},{3,19},{4,20},{5,21},{6,22},{7,23},{8,24},{9,... | collective-permute-start | bytes 786440 | tf_op jit(solution)/shard_map/ppermute | solution.py:61
  55.0 0.8 %gradient_block.7 = (f32[256,512]{1,0:T(8,128)S(1)}, bf16[256,512]{1,0:T(8,128)(2,1)S(1)}) custom-call(bf16[256,2560]{1,0:T(8,128)(2,1)S(1)} %get-tuple-element.103.own, bf16[256,2560]{1,0:T(8,128)(2,1)S(1)} %collective-permute-done.1.sib, bf16[256,512]{1,0:T(8,128)(2,1)S(1)} %collective-permute-done.15.refs_3_.par, ...), custom_call_target="tpu_custom_call" | custom-call | flops 1 | bytes 1 | tf_op jit(solution)/shard_map/gradient_block/pallas_call | solution.py:29
  55.8 0.7 far_features.3
  56.6 0.9 %collective-permute-start.22 = (bf16[256,512]{1,0:T(8,128)(2,1)S(1)}, bf16[256,512]{1,0:T(8,128)(2,1)S(1)}, u32[]{:S(2)}, u32[]{:S(2)}) collective-permute-start(bf16[256,512]{1,0:T(8,128)(2,1)S(1)} %get-tuple-element.106), channel_id=1, source_target_pairs={{0,4},{1,5},{2,6},{3,7},{4,0},{5,1},{6,2},{7,3},{8,12},{9,13},{10,... | collective-permute-start | bytes 786440 | tf_op jit(solution)/shard_map/ppermute | solution.py:61
  57.6 2.1 %collective-permute-start.24 = (bf16[256,512]{1,0:T(8,128)(2,1)S(1)}, bf16[256,512]{1,0:T(8,128)(2,1)S(1)}, u32[]{:S(2)}, u32[]{:S(2)}) collective-permute-start(bf16[256,512]{1,0:T(8,128)(2,1)S(1)} %add_blocks.5), channel_id=1, source_target_pairs={{0,8},{1,9},{2,10},{3,11},{4,12},{5,13},{6,14},{7,15},{8,0},{9,1},... | collective-permute-start | bytes 786440 | tf_op jit(solution)/shard_map/ppermute | solution.py:61
  59.7 1.2 %near_features.1 = (bf16[256,512]{1,0:T(8,128)(2,1)S(1)}, bf16[256,512]{1,0:T(8,128)(2,1)S(1)}) custom-call(bf16[256,2560]{1,0:T(8,128)(2,1)S(1)} %get-tuple-element.103.own, bf16[256,2560]{1,0:T(8,128)(2,1)S(1)} %collective-permute-done.1.sib, bf16[2048,512]{1,0:T(8,128)(2,1)S(1)} %fill_teacher.1.refs_4_.full), custom_call_target="tpu_custom_call" | custom-call | flops 1 | bytes 1 | tf_op jit(solution)/shard_map/near_features/pallas_call | solution.py:29
  61.0 1.0 %collective-permute-start.26 = (bf16[256,512]{1,0:T(8,128)(2,1)S(1)}, bf16[256,512]{1,0:T(8,128)(2,1)S(1)}, u32[]{:S(2)}, u32[]{:S(2)}) collective-permute-start(bf16[256,512]{1,0:T(8,128)(2,1)S(1)} %get-tuple-element.112), channel_id=1, source_target_pairs={{0,2},{1,3},{2,0},{3,1},{4,6},{5,7},{6,4},{7,5},{8,10},{9,11},{10,... | collective-permute-start | bytes 786440 | tf_op jit(solution)/shard_map/ppermute | solution.py:61
  62.0 3.0 %collective-permute-done.21.refs_3_ = bf16[256,512]{1,0:T(8,128)(2,1)S(1)} collective-permute-done((bf16[256,512]{1,0:T(8,128)(2,1)S(1)}, bf16[256,512]{1,0:T(8,128)(2,1)S(1)}, u32[]{:S(2)}, u32[]{:S(2)}) %collective-permute-start.21) | collective-permute-done | bytes 262176 | tf_op jit(solution)/shard_map/ppermute | solution.py:61
  65.0 2.0 %collective-permute-done.23.refs_2_ = bf16[256,512]{1,0:T(8,128)(2,1)S(1)} collective-permute-done((bf16[256,512]{1,0:T(8,128)(2,1)S(1)}, bf16[256,512]{1,0:T(8,128)(2,1)S(1)}, u32[]{:S(2)}, u32[]{:S(2)}) %collective-permute-start.23) | collective-permute-done | bytes 262176 | tf_op jit(solution)/shard_map/ppermute | solution.py:61
  67.0 5.2 %collective-permute-done.24.refs_3_ = bf16[256,512]{1,0:T(8,128)(2,1)S(1)} collective-permute-done((bf16[256,512]{1,0:T(8,128)(2,1)S(1)}, bf16[256,512]{1,0:T(8,128)(2,1)S(1)}, u32[]{:S(2)}, u32[]{:S(2)}) %collective-permute-start.24) | collective-permute-done | bytes 262176 | tf_op jit(solution)/shard_map/ppermute | solution.py:61
  72.5 0.8 %collective-permute-start.27 = (bf16[128,512]{1,0:T(8,128)(2,1)S(1)}, bf16[128,512]{1,0:T(8,128)(2,1)S(1)}, u32[]{:S(2)}, u32[]{:S(2)}) collective-permute-start(bf16[128,512]{1,0:T(8,128)(2,1)S(1)} %get-tuple-element.108.refs_0_), channel_id=1, source_target_pairs={{0,1},{1,0},{2,3},{3,2},{4,5},{5,4},{6,7},{7,6},{8,9},{9,8},{10,11... | collective-permute-start | bytes 393224 | tf_op jit(solution)/shard_map/ppermute | solution.py:61
  73.3 0.9 %collective-permute-start.28 = (bf16[128,512]{1,0:T(8,128)(2,1)S(1)}, bf16[128,512]{1,0:T(8,128)(2,1)S(1)}, u32[]{:S(2)}, u32[]{:S(2)}) collective-permute-start(bf16[128,512]{1,0:T(8,128)(2,1)S(1)} %get-tuple-element.109), channel_id=1, source_target_pairs={{0,3},{1,2},{2,1},{3,0},{4,7},{5,6},{6,5},{7,4},{8,11},{9,10},{10,... | collective-permute-start | bytes 393224 | tf_op jit(solution)/shard_map/ppermute | solution.py:61
  74.2 1.7 %update_near.1 = (f32[128,2048]{1,0:T(8,128)}, f32[128,2048]{1,0:T(8,128)}, f32[128,2048]{1,0:T(8,128)}, f32[128,2048]{1,0:T(8,128)}) custom-call(bf16[128,512]{1,0:T(8,128)(2,1)S(1)} %get-tuple-element.108.refs_0_, bf16[128,512]{1,0:T(8,128)(2,1)S(1)} %collective-permute-done.25.refs_1_, f32[128,2048]{1,0:T(8,128)S(1)} %copy-done.1, ...), custom_call_target="tpu_custom_call" | custom-call | flops 1 | bytes 1 | tf_op jit(solution)/shard_map/update_near/pallas_call | solution.py:361
  75.9 1.1 %place_features.1 = bf16[256,2048]{1,0:T(8,128)(2,1)} custom-call(bf16[256,512]{1,0:T(8,128)(2,1)S(1)} %get-tuple-element.111.refs_0_, bf16[256,512]{1,0:T(8,128)(2,1)S(1)} %collective-permute-done.26.refs_1_, bf16[256,512]{1,0:T(8,128)(2,1)S(1)} %collective-permute-done.20.refs_2_, bf16[256,512]{1,0:T(8,128)(2,1)S(1)} %collective-permute-done.21.refs_3_), custom_call_target="tpu_custom_call" | custom-call | flops 1 | bytes 1 | tf_op jit(solution)/shard_map/place_features/pallas_call | solution.py:29
  77.0 1.8 %collective-permute-done.27.refs_0_ = bf16[128,512]{1,0:T(8,128)(2,1)S(1)} collective-permute-done((bf16[128,512]{1,0:T(8,128)(2,1)S(1)}, bf16[128,512]{1,0:T(8,128)(2,1)S(1)}, u32[]{:S(2)}, u32[]{:S(2)}) %collective-permute-start.27) | collective-permute-done | bytes 131104 | tf_op jit(solution)/shard_map/ppermute | solution.py:61
  78.8 1.7 %collective-permute-done.28.refs_1_ = bf16[128,512]{1,0:T(8,128)(2,1)S(1)} collective-permute-done((bf16[128,512]{1,0:T(8,128)(2,1)S(1)}, bf16[128,512]{1,0:T(8,128)(2,1)S(1)}, u32[]{:S(2)}, u32[]{:S(2)}) %collective-permute-start.28) | collective-permute-done | bytes 131104 | tf_op jit(solution)/shard_map/ppermute | solution.py:61
  80.5 1.7 %update_far.1 = (f32[128,2048]{1,0:T(8,128)}, f32[128,2048]{1,0:T(8,128)}, f32[128,2048]{1,0:T(8,128)}, f32[128,2048]{1,0:T(8,128)}) custom-call(bf16[128,512]{1,0:T(8,128)(2,1)S(1)} %collective-permute-done.27.refs_0_, ...), custom_call_target="tpu_custom_call", output_to_operand_aliasing={{0}: (6, {}), {1}: (7, {}), {2}: (8, {}), {3}: (9, {})} | custom-call | flops 1 | bytes 1 | tf_op jit(solution)/shard_map/update_far/pallas_call | solution.py:361
  (43 shorter events, 1.5 us)
Async XLA Ops:
  0.6 5.8 %copy-start = (f32[128,2048]{1,0:T(8,128)S(1)}, f32[128,2048]{1,0:T(8,128)}, u32[]{:S(2)}) copy-start(f32[128,2048]{1,0:T(8,128)} %refs_5_.3) | copy-start | bytes 3145732
  0.6 1.3 %copy-start.4 = (bf16[256,2048]{1,0:T(8,128)(2,1)S(1)}, bf16[256,2048]{1,0:T(8,128)(2,1)}, u32[]{:S(2)}) copy-start(bf16[256,2048]{1,0:T(8,128)(2,1)} %p.1) | copy-start | bytes 3145732
  2.0 1.2 %copy-start.5 = (bf16[256,2048]{1,0:T(8,128)(2,1)S(1)}, bf16[256,2048]{1,0:T(8,128)(2,1)}, u32[]{:S(2)}) copy-start(bf16[256,2048]{1,0:T(8,128)(2,1)} %c.1) | copy-start | bytes 3145732
  3.4 23.8 %collective-permute-start.1 = (bf16[256,2560]{1,0:T(8,128)(2,1)S(1)}, bf16[256,2560]{1,0:T(8,128)(2,1)S(1)}, u32[]{:S(2)}, u32[]{:S(2)}) collective-permute-start(bf16[256,2560]{1,0:T(8,128)(2,1)S(1)} %get-tuple-element.103.own), channel_id=1, source_target_pairs={{0,2},{1,3},{2,0},{3,1},{4,6},{5,7},{6,4},{7,5},{8,10},{9,11},{10,... | collective-permute-start | bytes 3932168 | tf_op jit(solution)/shard_map/ppermute | solution.py:61
  3.9 23.2 %collective-permute-start = (bf16[256,1536]{1,0:T(8,128)(2,1)S(1)}, bf16[256,1536]{1,0:T(8,128)(2,1)S(1)}, u32[]{:S(2)}, u32[]{:S(2)}) collective-permute-start(bf16[256,1536]{1,0:T(8,128)(2,1)S(1)} %get-tuple-element.64), channel_id=1, source_target_pairs={{0,1},{1,0},{2,3},{3,2},{4,5},{5,4},{6,7},{7,6},{8,9},{9,8},{10,11... | collective-permute-start | bytes 2359304 | tf_op jit(solution)/shard_map/ppermute | solution.py:61
  6.5 1.4 %collective-permute-start.2 = (bf16[128,512]{1,0:T(8,128)(2,1)S(1)}, bf16[128,512]{1,0:T(8,128)(2,1)S(1)}, u32[]{:S(2)}, u32[]{:S(2)}) collective-permute-start(bf16[128,512]{1,0:T(8,128)(2,1)S(1)} %get-tuple-element.68), channel_id=1, source_target_pairs={{0,2},{1,3},{2,0},{3,1},{4,6},{5,7},{6,4},{7,5},{8,10},{9,11},{10,... | collective-permute-start | bytes 393224 | tf_op jit(solution)/shard_map/ppermute | solution.py:61
  8.0 8.4 %collective-permute-start.5 = (bf16[256,512]{1,0:T(8,128)(2,1)S(1)}, bf16[256,512]{1,0:T(8,128)(2,1)S(1)}, u32[]{:S(2)}, u32[]{:S(2)}) collective-permute-start(bf16[256,512]{1,0:T(8,128)(2,1)S(1)} %join_teacher.1.refs_0_), channel_id=1, source_target_pairs={{0,4},{1,5},{2,6},{3,7},{4,0},{5,1},{6,2},{7,3},{8,12},{9,13},{10,... | collective-permute-start | bytes 786440 | tf_op jit(solution)/shard_map/ppermute | solution.py:61
  9.8 9.0 %collective-permute-start.3 = (bf16[256,512]{1,0:T(8,128)(2,1)S(1)}, bf16[256,512]{1,0:T(8,128)(2,1)S(1)}, u32[]{:S(2)}, u32[]{:S(2)}) collective-permute-start(bf16[256,512]{1,0:T(8,128)(2,1)S(1)} %join_teacher.1.refs_0_), channel_id=1, source_target_pairs={{0,8},{1,9},{2,10},{3,11},{4,12},{5,13},{6,14},{7,15},{8,24},{9,25... | collective-permute-start | bytes 786440 | tf_op jit(solution)/shard_map/ppermute | solution.py:61
  18.7 7.2 %collective-permute-start.6 = (bf16[256,512]{1,0:T(8,128)(2,1)S(1)}, bf16[256,512]{1,0:T(8,128)(2,1)S(1)}, u32[]{:S(2)}, u32[]{:S(2)}) collective-permute-start(bf16[256,512]{1,0:T(8,128)(2,1)S(1)} %collective-permute-done.3.refs_2_), channel_id=1, source_target_pairs={{0,4},{1,5},{2,6},{3,7},{4,0},{5,1},{6,2},{7,3},{8,12},{9,13},{10,... | collective-permute-start | bytes 786440 | tf_op jit(solution)/shard_map/ppermute | solution.py:61
  19.2 8.0 %collective-permute-start.4 = (bf16[256,512]{1,0:T(8,128)(2,1)S(1)}, bf16[256,512]{1,0:T(8,128)(2,1)S(1)}, u32[]{:S(2)}, u32[]{:S(2)}) collective-permute-start(bf16[256,512]{1,0:T(8,128)(2,1)S(1)} %collective-permute-done.3.refs_2_), channel_id=1, source_target_pairs={{0,8},{1,9},{2,10},{3,11},{4,12},{5,13},{6,14},{7,15},{8,24},{9,25... | collective-permute-start | bytes 786440 | tf_op jit(solution)/shard_map/ppermute | solution.py:61
  20.0 17.5 %collective-permute-start.9 = (bf16[256,1024]{1,0:T(8,128)(2,1)S(1)}, bf16[256,1024]{1,0:T(8,128)(2,1)S(1)}, u32[]{:S(2)}, u32[]{:S(2)}) collective-permute-start(bf16[256,1024]{1,0:T(8,128)(2,1)S(1)} %get-tuple-element.79), channel_id=1, source_target_pairs={{0,1},{1,0},{2,3},{3,2},{4,5},{5,4},{6,7},{7,6},{8,9},{9,8},{10,11... | collective-permute-start | bytes 1572872 | tf_op jit(solution)/shard_map/ppermute | solution.py:61
  27.2 2.0 %collective-permute-start.8 = (bf16[256,512]{1,0:T(8,128)(2,1)S(1)}, bf16[256,512]{1,0:T(8,128)(2,1)S(1)}, u32[]{:S(2)}, u32[]{:S(2)}) collective-permute-start(bf16[256,512]{1,0:T(8,128)(2,1)S(1)} %get-tuple-element.73), channel_id=1, source_target_pairs={{0,2},{1,3},{2,0},{3,1},{4,6},{5,7},{6,4},{7,5},{8,10},{9,11},{10,... | collective-permute-start | bytes 786440 | tf_op jit(solution)/shard_map/ppermute | solution.py:61
  27.3 1.9 %collective-permute-start.7 = (bf16[256,512]{1,0:T(8,128)(2,1)S(1)}, bf16[256,512]{1,0:T(8,128)(2,1)S(1)}, u32[]{:S(2)}, u32[]{:S(2)}) collective-permute-start(bf16[256,512]{1,0:T(8,128)(2,1)S(1)} %get-tuple-element.92.par.refs_0_), channel_id=1, source_target_pairs={{0,2},{1,3},{2,0},{3,1},{4,6},{5,7},{6,4},{7,5},{8,10},{9,11},{10,... | collective-permute-start | bytes 786440 | tf_op jit(solution)/shard_map/ppermute | solution.py:61
  27.8 8.3 %collective-permute-start.11 = (bf16[256,512]{1,0:T(8,128)(2,1)S(1)}, bf16[256,512]{1,0:T(8,128)(2,1)S(1)}, u32[]{:S(2)}, u32[]{:S(2)}) collective-permute-start(bf16[256,512]{1,0:T(8,128)(2,1)S(1)} %collective-permute-done.4.refs_4_), channel_id=1, source_target_pairs={{0,4},{1,5},{2,6},{3,7},{4,0},{5,1},{6,2},{7,3},{8,12},{9,13},{10,... | collective-permute-start | bytes 786440 | tf_op jit(solution)/shard_map/ppermute | solution.py:61
  30.1 16.4 %collective-permute-start.14 = (bf16[512,512]{1,0:T(8,128)(2,1)S(1)}, bf16[512,512]{1,0:T(8,128)(2,1)S(1)}, u32[]{:S(2)}, u32[]{:S(2)}) collective-permute-start(bf16[512,512]{1,0:T(8,128)(2,1)S(1)} %stack_teacher.1), channel_id=1, source_target_pairs={{0,16},{1,17},{2,18},{3,19},{4,20},{5,21},{6,22},{7,23},{8,0},{9,1... | collective-permute-start | bytes 1572872 | tf_op jit(solution)/shard_map/ppermute | solution.py:61
  36.1 8.7 %collective-permute-start.12 = (bf16[272,512]{1,0:T(8,128)(2,1)S(1)}, bf16[272,512]{1,0:T(8,128)(2,1)S(1)}, u32[]{:S(2)}, u32[]{:S(2)}) collective-permute-start(bf16[272,512]{1,0:T(8,128)(2,1)S(1)} %get-tuple-element.86), channel_id=1, source_target_pairs={{0,4},{1,5},{2,6},{3,7},{4,0},{5,1},{6,2},{7,3},{8,12},{9,13},{10,... | collective-permute-start | bytes 835592 | tf_op jit(solution)/shard_map/ppermute | solution.py:61
  37.5 2.1 %collective-permute-start.10 = (bf16[256,512]{1,0:T(8,128)(2,1)S(1)}, bf16[256,512]{1,0:T(8,128)(2,1)S(1)}, u32[]{:S(2)}, u32[]{:S(2)}) collective-permute-start(bf16[256,512]{1,0:T(8,128)(2,1)S(1)} %get-tuple-element.81.par.refs_1_), channel_id=1, source_target_pairs={{0,2},{1,3},{2,0},{3,1},{4,6},{5,7},{6,4},{7,5},{8,10},{9,11},{10,... | collective-permute-start | bytes 786440 | tf_op jit(solution)/shard_map/ppermute | solution.py:61
  37.6 7.9 %collective-permute-start.13 = (bf16[256,512]{1,0:T(8,128)(2,1)S(1)}, bf16[256,512]{1,0:T(8,128)(2,1)S(1)}, u32[]{:S(2)}, u32[]{:S(2)}) collective-permute-start(bf16[256,512]{1,0:T(8,128)(2,1)S(1)} %get-tuple-element.88.par.refs_2_), channel_id=1, source_target_pairs={{0,2},{1,3},{2,0},{3,1},{4,6},{5,7},{6,4},{7,5},{8,10},{9,11},{10,... | collective-permute-start | bytes 786440 | tf_op jit(solution)/shard_map/ppermute | solution.py:61
  38.1 8.3 %collective-permute-start.15 = (bf16[256,512]{1,0:T(8,128)(2,1)S(1)}, bf16[256,512]{1,0:T(8,128)(2,1)S(1)}, u32[]{:S(2)}, u32[]{:S(2)}) collective-permute-start(bf16[256,512]{1,0:T(8,128)(2,1)S(1)} %get-tuple-element.94), channel_id=1, source_target_pairs={{0,1},{1,0},{2,3},{3,2},{4,5},{5,4},{6,7},{7,6},{8,9},{9,8},{10,11... | collective-permute-start | bytes 786440 | tf_op jit(solution)/shard_map/ppermute | solution.py:61
  40.4 10.7 %collective-permute-start.16 = (bf16[256,512]{1,0:T(8,128)(2,1)S(1)}, bf16[256,512]{1,0:T(8,128)(2,1)S(1)}, u32[]{:S(2)}, u32[]{:S(2)}) collective-permute-start(bf16[256,512]{1,0:T(8,128)(2,1)S(1)} %get-tuple-element.96), channel_id=1, source_target_pairs={{0,4},{1,5},{2,6},{3,7},{4,0},{5,1},{6,2},{7,3},{8,12},{9,13},{10,... | collective-permute-start | bytes 786440 | tf_op jit(solution)/shard_map/ppermute | solution.py:61
  44.9 6.4 %collective-permute-start.17 = (bf16[256,512]{1,0:T(8,128)(2,1)S(1)}, bf16[256,512]{1,0:T(8,128)(2,1)S(1)}, u32[]{:S(2)}, u32[]{:S(2)}) collective-permute-start(bf16[256,512]{1,0:T(8,128)(2,1)S(1)} %add_blocks.3), channel_id=1, source_target_pairs={{0,8},{1,9},{2,10},{3,11},{4,12},{5,13},{6,14},{7,15},{8,0},{9,1},... | collective-permute-start | bytes 786440 | tf_op jit(solution)/shard_map/ppermute | solution.py:61
  46.4 8.6 %collective-permute-start.18 = (bf16[256,512]{1,0:T(8,128)(2,1)S(1)}, bf16[256,512]{1,0:T(8,128)(2,1)S(1)}, u32[]{:S(2)}, u32[]{:S(2)}) collective-permute-start(bf16[256,512]{1,0:T(8,128)(2,1)S(1)} %collective-permute-done.15.refs_3_.par), channel_id=1, source_target_pairs={{0,2},{1,3},{2,0},{3,1},{4,6},{5,7},{6,4},{7,5},{8,10},{9,11},{10,... | collective-permute-start | bytes 786440 | tf_op jit(solution)/shard_map/ppermute | solution.py:61
  46.4 11.2 %collective-permute-start.19 = (bf16[256,512]{1,0:T(8,128)(2,1)S(1)}, bf16[256,512]{1,0:T(8,128)(2,1)S(1)}, u32[]{:S(2)}, u32[]{:S(2)}) collective-permute-start(bf16[256,512]{1,0:T(8,128)(2,1)S(1)} %get-tuple-element.102), channel_id=1, source_target_pairs={{0,4},{1,5},{2,6},{3,7},{4,0},{5,1},{6,2},{7,3},{8,12},{9,13},{10,... | collective-permute-start | bytes 786440 | tf_op jit(solution)/shard_map/ppermute | solution.py:61
  49.5 11.5 %collective-permute-start.20 = (bf16[256,512]{1,0:T(8,128)(2,1)S(1)}, bf16[256,512]{1,0:T(8,128)(2,1)S(1)}, u32[]{:S(2)}, u32[]{:S(2)}) collective-permute-start(bf16[256,512]{1,0:T(8,128)(2,1)S(1)} %far_features.2), channel_id=1, source_target_pairs={{0,1},{1,0},{2,3},{3,2},{4,5},{5,4},{6,7},{7,6},{8,9},{9,8},{10,11... | collective-permute-start | bytes 786440 | tf_op jit(solution)/shard_map/ppermute | solution.py:61
  51.4 15.6 %collective-permute-start.23 = (bf16[256,512]{1,0:T(8,128)(2,1)S(1)}, bf16[256,512]{1,0:T(8,128)(2,1)S(1)}, u32[]{:S(2)}, u32[]{:S(2)}) collective-permute-start(bf16[256,512]{1,0:T(8,128)(2,1)S(1)} %add_blocks.4), channel_id=1, source_target_pairs={{0,16},{1,17},{2,18},{3,19},{4,20},{5,21},{6,22},{7,23},{8,24},{9,... | collective-permute-start | bytes 786440 | tf_op jit(solution)/shard_map/ppermute | solution.py:61
  56.5 8.5 %collective-permute-start.21 = (bf16[256,512]{1,0:T(8,128)(2,1)S(1)}, bf16[256,512]{1,0:T(8,128)(2,1)S(1)}, u32[]{:S(2)}, u32[]{:S(2)}) collective-permute-start(bf16[256,512]{1,0:T(8,128)(2,1)S(1)} %far_features.3), channel_id=1, source_target_pairs={{0,3},{1,2},{2,1},{3,0},{4,7},{5,6},{6,5},{7,4},{8,11},{9,10},{10,... | collective-permute-start | bytes 786440 | tf_op jit(solution)/shard_map/ppermute | solution.py:61
  56.6 10.4 %collective-permute-start.22 = (bf16[256,512]{1,0:T(8,128)(2,1)S(1)}, bf16[256,512]{1,0:T(8,128)(2,1)S(1)}, u32[]{:S(2)}, u32[]{:S(2)}) collective-permute-start(bf16[256,512]{1,0:T(8,128)(2,1)S(1)} %get-tuple-element.106), channel_id=1, source_target_pairs={{0,4},{1,5},{2,6},{3,7},{4,0},{5,1},{6,2},{7,3},{8,12},{9,13},{10,... | collective-permute-start | bytes 786440 | tf_op jit(solution)/shard_map/ppermute | solution.py:61
  57.6 14.5 %collective-permute-start.24 = (bf16[256,512]{1,0:T(8,128)(2,1)S(1)}, bf16[256,512]{1,0:T(8,128)(2,1)S(1)}, u32[]{:S(2)}, u32[]{:S(2)}) collective-permute-start(bf16[256,512]{1,0:T(8,128)(2,1)S(1)} %add_blocks.5), channel_id=1, source_target_pairs={{0,8},{1,9},{2,10},{3,11},{4,12},{5,13},{6,14},{7,15},{8,0},{9,1},... | collective-permute-start | bytes 786440 | tf_op jit(solution)/shard_map/ppermute | solution.py:61
  59.7 14.5 %copy-start.2 = (f32[128,2048]{1,0:T(8,128)S(1)}, f32[128,2048]{1,0:T(8,128)}, u32[]{:S(2)}) copy-start(f32[128,2048]{1,0:T(8,128)} %refs_3_.3) | copy-start | bytes 3145732
  59.7 14.5 %copy-start.3 = (f32[128,2048]{1,0:T(8,128)S(1)}, f32[128,2048]{1,0:T(8,128)}, u32[]{:S(2)}) copy-start(f32[128,2048]{1,0:T(8,128)} %refs_4_.3) | copy-start | bytes 3145732
  61.0 13.3 %copy-start.1 = (f32[128,2048]{1,0:T(8,128)S(1)}, f32[128,2048]{1,0:T(8,128)}, u32[]{:S(2)}) copy-start(f32[128,2048]{1,0:T(8,128)} %refs_2_.3) | copy-start | bytes 3145732
  61.0 14.9 %collective-permute-start.26 = (bf16[256,512]{1,0:T(8,128)(2,1)S(1)}, bf16[256,512]{1,0:T(8,128)(2,1)S(1)}, u32[]{:S(2)}, u32[]{:S(2)}) collective-permute-start(bf16[256,512]{1,0:T(8,128)(2,1)S(1)} %get-tuple-element.112), channel_id=1, source_target_pairs={{0,2},{1,3},{2,0},{3,1},{4,6},{5,7},{6,4},{7,5},{8,10},{9,11},{10,... | collective-permute-start | bytes 786440 | tf_op jit(solution)/shard_map/ppermute | solution.py:61
  72.3 1.9 %collective-permute-start.25 = (bf16[128,512]{1,0:T(8,128)(2,1)S(1)}, bf16[128,512]{1,0:T(8,128)(2,1)S(1)}, u32[]{:S(2)}, u32[]{:S(2)}) collective-permute-start(bf16[128,512]{1,0:T(8,128)(2,1)S(1)} %get-tuple-element.109), channel_id=1, source_target_pairs={{0,2},{1,3},{2,0},{3,1},{4,6},{5,7},{6,4},{7,5},{8,10},{9,11},{10,... | collective-permute-start | bytes 393224 | tf_op jit(solution)/shard_map/ppermute | solution.py:61
  72.5 6.3 %collective-permute-start.27 = (bf16[128,512]{1,0:T(8,128)(2,1)S(1)}, bf16[128,512]{1,0:T(8,128)(2,1)S(1)}, u32[]{:S(2)}, u32[]{:S(2)}) collective-permute-start(bf16[128,512]{1,0:T(8,128)(2,1)S(1)} %get-tuple-element.108.refs_0_), channel_id=1, source_target_pairs={{0,1},{1,0},{2,3},{3,2},{4,5},{5,4},{6,7},{7,6},{8,9},{9,8},{10,11... | collective-permute-start | bytes 393224 | tf_op jit(solution)/shard_map/ppermute | solution.py:61
  73.3 7.2 %collective-permute-start.28 = (bf16[128,512]{1,0:T(8,128)(2,1)S(1)}, bf16[128,512]{1,0:T(8,128)(2,1)S(1)}, u32[]{:S(2)}, u32[]{:S(2)}) collective-permute-start(bf16[128,512]{1,0:T(8,128)(2,1)S(1)} %get-tuple-element.109), channel_id=1, source_target_pairs={{0,3},{1,2},{2,1},{3,0},{4,7},{5,6},{6,5},{7,4},{8,11},{9,10},{10,... | collective-permute-start | bytes 393224 | tf_op jit(solution)/shard_map/ppermute | solution.py:61

commit v3 on v2

--- a/solution.py
+++ b/solution.py
@@ -98,19 +98,22 @@
         span = feat // nz
         g_order = [3, 2, 1, 0]
         lead = 2 * part
-
-        def cut_body(p, c, first, near, c_own, second, third):
-            z, y, core, q = place()
+        extra = 16
+
+        def cut_body(p, c, first, near, c_own, second, third, mark):
+            z, y, core, q = place()
+            mark[...] = c[: mark.shape[0], :part]
             first[:, :lead] = c[:, aligned(1 - q // 2, lead)]
             for k, dz in enumerate(g_order):
                 block = p[:, aligned(z ^ dz, span)]
                 near[:, k * span : (k + 1) * span] = block
                 if k == 0:
                     first[:, lead:] = block
-                elif k < 3:
-                    second[:, (k - 1) * span : k * span] = block
+                elif k == 1:
+                    second[:tokens, :] = block
+                    second[tokens:, :] = block[: second.shape[0] - tokens, :]
                 else:
-                    third[...] = block
+                    third[:, (k - 2) * span : (k - 1) * span] = block
             near[:, feat:] = c[:, aligned(q ^ 1, part)]
             c_own[...] = c[:, aligned(q, part)]
 
@@ -122,7 +125,7 @@
 
         def halve_body(message, *blocks):
             for k, out in enumerate(blocks):
-                out[...] = message[:, k * span : (k + 1) * span]
+                out[...] = message[:tokens, k * span : (k + 1) * span]
 
         clock = []
 
@@ -151,6 +154,7 @@
         def stack_body(*refs):
             for k, ref in enumerate(refs[:-1]):
                 refs[-1][k * 2 * rows : (k + 1) * 2 * rows, :] = ref[...]
+            refs[-1][ny * 2 * rows :, :] = refs[0][: 2 * extra, :]
 
         def terms_body(k):
             def body(own, sib, par, dia, c0, c_par, c_dia, *outs):
@@ -183,25 +187,27 @@
             terms[dz] = run(
                 "gradient_block",
                 terms_body(k),
-                [((2 * rows, part), f32)] + [((2 * rows + 16 * (k == 0), part), bf16)] * (ny - 1),
+                [((2 * rows, part), f32)]
+                + [((2 * rows + (extra, 2 * extra, 0, 0)[k], part), bf16)] * (ny - 1),
                 [near_own, near_sib, far_par[k], far_dia[k], c_own, c_par, c_dia],
                 scratch=[pltpu.VMEM((span, part), f32)],
             )
-            gates = () if k else w_side[2]
-            moved_y[dz] = [start(terms[dz][dy], along_y(dy), *gates) for dy in others]
+            moved_y[dz] = [start(terms[dz][dy], along_y(dy)) for dy in others]
 
         def add_body(*refs):
-            count = refs[-1].shape[0]
-            total = sum(ref[:count, :].astype(f32) for ref in refs[:-1])
-            refs[-1][...] = total.astype(refs[-1].dtype)
-
-        def add(values, dtype, **options):
-            return run("add_blocks", add_body, [(values[0].shape, dtype)], values, **options)[0]
+            total = sum(ref[: 2 * rows, :].astype(f32) for ref in refs[:-1])
+            refs[-1][: 2 * rows, :] = total.astype(refs[-1].dtype)
+            if refs[-1].shape[0] > 2 * rows:
+                rest = (refs[-1].shape[0] - 2 * rows, part)
+                refs[-1][2 * rows :, :] = jnp.zeros(rest, refs[-1].dtype)
+
+        def add(values, dtype, more=0):
+            return run("add_blocks", add_body, [((2 * rows + more, part), dtype)], values)[0]
 
         def sum_body(*refs):
             z, y, core, q = place()
             for out, at in zip(refs[-2:], (aligned(core, rows), aligned(1 - core, rows))):
-                out[...] = sum(ref[at, :].astype(f32) for ref in refs[:-2]).astype(bf16)
+                out[...] = sum(ref[at, :].astype(f32) for ref in refs[:-3]).astype(bf16)
 
         def features_of(blocks, full, out):
             total = sum(
@@ -247,15 +253,18 @@
         def teacher_y(dz, *gates):
             w_side[dz] = [start(w_line[dz], along_y(-dy), *gates) for dy in others]
 
-        def block_sum(dz, *more, **options):
-            return add([terms[dz][0], *moved_y[dz], *more], bf16, **options)
-
-        first, near_own, c_own, second, third = run(
+        def block_sum(dz, *parts, more=0):
+            return add([terms[dz][0], *moved_y[dz], *parts], bf16, more)
+
+        first, near_own, c_own, second, third, mark = run(
             "cut_tokens",
             cut_body,
             [
-                ((tokens, width), bf16)
-                for width in (lead + span, feat + part, part, 2 * span, span)
+                ((count, width), bf16)
+                for count, width in (
+                    (tokens, lead + span), (tokens, feat + part), (tokens, part),
+                    (tokens + 2 * extra, span), (tokens, 2 * span), (tokens - extra, part),
+                )
             ],
             [patches, cotangent],
         )
@@ -268,34 +277,40 @@
         )
         w_line[3] = start(w_line[0], along_z(1))
         teacher_y(0)
-        w_line[2] = start(w_line[3], along_z(1))
         teacher_y(3, *w_side[0])
         (turn,) = run(
-            "stack_teacher", stack_body, [((ny * 2 * rows, part), bf16)], [w_line[0], *w_side[0]]
-        )
-        teacher_y(2)
-        second = start(second, partner)
+            "stack_teacher",
+            stack_body,
+            [((ny * 2 * rows + 2 * extra, part), bf16)],
+            [after(w_line[0], near_sib), *w_side[0]],
+        )
+        turn = start(turn, along_z(-1))
+        w_line[2] = start(w_line[3], along_z(1), turn)
+        block = start(second, partner)
         c_other, c_par, far_par[0] = run(
             "split_message",
             split_body,
             [((tokens, part), bf16)] * 2 + [((tokens, span), bf16)],
-            [after(message, near_sib, w_line[2], *w_side[3])],
+            [after(message, near_sib, *w_side[3])],
         )
         c_dia = start(c_other, sibling)
         far_dia[0] = start(far_par[0], sibling)
         gradient_block(0)
-        begun = terms[3][0]
-        far_par[3] = start(third, partner, begun)
-        turn = start(turn, along_z(-1), begun)
-        far_par[1:3] = run(
-            "halve_message", halve_body, [((tokens, span), bf16)] * 2, [second]
-        )
+        both = start(third, partner)
+        (far_par[1],) = run("take_block", halve_body, [((tokens, span), bf16)], [block])
         far_dia[1] = start(far_par[1], sibling)
+        wait(turn)
         gradient_block(1)
-        onward = start(block_sum(3), across_z(1))
+        onward = block_sum(3, more=2 * extra)
+        teacher_y(2, onward)
+        onward = start(onward, across_z(1))
+        far_par[2:] = run(
+            "halve_message", halve_body, [((tokens, span), bf16)] * 2, [after(both, w_line[2])]
+        )
         far_dia[2] = start(far_par[2], sibling)
         gradient_block(2)
-        far_dia[3] = start(far_par[3], sibling, turn, terms[1][0])
+        onward = start(block_sum(2, onward), across_z(2))
+        far_dia[3] = start(far_par[3], sibling, terms[1][0])
         (w_full,) = run(
             "fill_teacher",
             fill_body,
@@ -303,7 +318,6 @@
             [*(w for dz in w_order[:-1] for w in (w_line[dz], *w_side[dz])), turn],
         )
         f_par = start(far_features(far_par), partner)
-        onward = start(block_sum(2, onward), across_z(2))
         gradient_block(3)
         f_dia = start(far_features(far_dia), diagonal)
         back = start(block_sum(1), across_z(1))
@@ -316,11 +330,12 @@
         f_sib = start(f_sib, sibling)
         wait(f_par, f_dia)
         pieces = [terms[0][0], *moved_y[0], onward, back]
+        spacer = start(mark, sibling, onward)
         if pair_groups > 1:
             total = add(pieces, f32)
             sent = total.astype(bf16)
             pieces = [total] + [start(sent, along_g(dg)) for dg in range(1, pair_groups)]
-        mine, other = run("sum_gradient", sum_body, [((rows, part), bf16)] * 2, pieces)
+        mine, other = run("sum_gradient", sum_body, [((rows, part), bf16)] * 2, [*pieces, spacer])
         g_par, g_dia, g_sib = (
             start(mine, partner), start(other, diagonal), start(other, sibling)
         )

time: 82.3 us -> 78 us (0.948)
  waiting for transfers between devices: 36.3 us -> 28.3 us
  starting transfers between devices: 31.2 us -> 34.8 us
    ppermute x29 -> x30, waiting for transfers between devices: 36.3 us -> 28.3 us  [send(): return lax.ppermute(value, ('fsdp', 'rep'), perm)]
    ppermute x29 -> x30, starting transfers between devices: 31.2 us -> 34.8 us  [send(): return lax.ppermute(value, ('fsdp', 'rep'), perm)]
    pallas_call x19 -> x20, Pallas kernels: 7.91 us -> 7.96 us  [call(): pl.pallas_call(body, out_shape=shapes, in_specs=[VMEM] * len(inputs), out...]
  transfers between devices with their start and end apart: 29 -> 30, of which waited for: 14 -> 14; matrix products, arithmetic and copies ran while one was open for 0% -> 0% of each run, Pallas kernels for 11% -> 12%
where the time goes in v3:
time: 78 us; the launch traced here: 77.8 us
  starting transfers between devices  34.8 us (45%)
  waiting for transfers between devices  28.3 us (36%)
  Pallas kernels  11.3 us (14%)
  local copies, waits for them, and re-layouts  2.55 us (3%)
  between operations  0.88 us (1%)
    ppermute x30, starting transfers between devices, send(): return lax.ppermute(value, ('fsdp', 'rep'), perm)  34.8 us
    ppermute x30, waiting for transfers between devices, send(): return lax.ppermute(value, ('fsdp', 'rep'), perm)  28.3 us
    pallas_call x20, Pallas kernels, call(): pl.pallas_call(body, out_shape=shapes, in_specs=[VMEM] * len(inputs), out...  7.96 us
    pallas_call x2, Pallas kernels, update(): pl.pallas_call(update_body(quarters), out_shape=[jax.ShapeDtypeStruct((ro...  3.33 us
    unnamed x12, local copies, waits for them, and re-layouts  2.55 us
  transfers between devices with their start and end apart: 30, of which 14 were waited for; matrix products, arithmetic and copies ran while one was open for 0% of the time, Pallas kernels for 12%

profile of v3, /device:TPU:0, one launch (start us, length us, event | category | flops | bytes accessed | tf_op | source)
XLA Modules:
  0.0 77.8 jit_solution(6426982564760899061)
XLA Ops:
  0.7 1.3 %copy-done.4 = bf16[256,2048]{1,0:T(8,128)(2,1)S(1)} copy-done((bf16[256,2048]{1,0:T(8,128)(2,1)S(1)}, bf16[256,2048]{1,0:T(8,128)(2,1)}, u32[]{:S(2)}) %copy-start.4) | copy-done | bytes 1048600
  2.0 1.2 %copy-done.5 = bf16[256,2048]{1,0:T(8,128)(2,1)S(1)} copy-done((bf16[256,2048]{1,0:T(8,128)(2,1)S(1)}, bf16[256,2048]{1,0:T(8,128)(2,1)}, u32[]{:S(2)}) %copy-start.5) | copy-done | bytes 1048600
  3.2 0.2 cut_tokens.1
  3.4 0.5 collective-permute-start.3
  3.9 2.6 %collective-permute-start.7 = (bf16[256,1536]{1,0:T(8,128)(2,1)S(1)}, bf16[256,1536]{1,0:T(8,128)(2,1)S(1)}, u32[]{:S(2)}, u32[]{:S(2)}) collective-permute-start(bf16[256,1536]{1,0:T(8,128)(2,1)S(1)} %get-tuple-element.69), channel_id=1, source_target_pairs={{0,1},{1,0},{2,3},{3,2},{4,5},{5,4},{6,7},{7,6},{8,9},{9,8},{10,11... | collective-permute-start | bytes 2359304 | tf_op jit(solution)/shard_map/ppermute | solution.py:61
  6.5 0.2 collective-permute-start.1
  6.8 1.2 %collective-permute-done.1.sib = bf16[128,512]{1,0:T(8,128)(2,1)S(1)} collective-permute-done((bf16[128,512]{1,0:T(8,128)(2,1)S(1)}, bf16[128,512]{1,0:T(8,128)(2,1)S(1)}, u32[]{:S(2)}, u32[]{:S(2)}) %collective-permute-start.1) | collective-permute-done | bytes 131104 | tf_op jit(solution)/shard_map/ppermute | solution.py:61
  8.0 1.8 %collective-permute-start.4 = (bf16[256,512]{1,0:T(8,128)(2,1)S(1)}, bf16[256,512]{1,0:T(8,128)(2,1)S(1)}, u32[]{:S(2)}, u32[]{:S(2)}) collective-permute-start(bf16[256,512]{1,0:T(8,128)(2,1)S(1)} %join_teacher.1.refs_0_), channel_id=1, source_target_pairs={{0,4},{1,5},{2,6},{3,7},{4,0},{5,1},{6,2},{7,3},{8,12},{9,13},{10,... | collective-permute-start | bytes 786440 | tf_op jit(solution)/shard_map/ppermute | solution.py:61
  9.8 1.6 %collective-permute-start.2 = (bf16[256,512]{1,0:T(8,128)(2,1)S(1)}, bf16[256,512]{1,0:T(8,128)(2,1)S(1)}, u32[]{:S(2)}, u32[]{:S(2)}) collective-permute-start(bf16[256,512]{1,0:T(8,128)(2,1)S(1)} %join_teacher.1.refs_0_), channel_id=1, source_target_pairs={{0,8},{1,9},{2,10},{3,11},{4,12},{5,13},{6,14},{7,15},{8,24},{9,25... | collective-permute-start | bytes 786440 | tf_op jit(solution)/shard_map/ppermute | solution.py:61
  11.4 5.1 %collective-permute-done.4.refs_1_ = bf16[256,512]{1,0:T(8,128)(2,1)S(1)} collective-permute-done((bf16[256,512]{1,0:T(8,128)(2,1)S(1)}, bf16[256,512]{1,0:T(8,128)(2,1)S(1)}, u32[]{:S(2)}, u32[]{:S(2)}) %collective-permute-start.4) | collective-permute-done | bytes 262176 | tf_op jit(solution)/shard_map/ppermute | solution.py:61
  16.5 2.8 %collective-permute-start.5 = (bf16[544,512]{1,0:T(8,128)(2,1)S(1)}, bf16[544,512]{1,0:T(8,128)(2,1)S(1)}, u32[]{:S(2)}, u32[]{:S(2)}) collective-permute-start(bf16[544,512]{1,0:T(8,128)(2,1)S(1)} %stack_teacher.1), channel_id=1, source_target_pairs={{0,16},{1,17},{2,18},{3,19},{4,20},{5,21},{6,22},{7,23},{8,0},{9,1... | collective-permute-start | bytes 1671176 | tf_op jit(solution)/shard_map/ppermute | solution.py:61
  19.3 1.5 %collective-permute-start.8 = (bf16[256,512]{1,0:T(8,128)(2,1)S(1)}, bf16[256,512]{1,0:T(8,128)(2,1)S(1)}, u32[]{:S(2)}, u32[]{:S(2)}) collective-permute-start(bf16[256,512]{1,0:T(8,128)(2,1)S(1)} %collective-permute-done.2.refs_2_), channel_id=1, source_target_pairs={{0,4},{1,5},{2,6},{3,7},{4,0},{5,1},{6,2},{7,3},{8,12},{9,13},{10,... | collective-permute-start | bytes 786440 | tf_op jit(solution)/shard_map/ppermute | solution.py:61
  20.8 1.5 %collective-permute-start.11 = (bf16[288,512]{1,0:T(8,128)(2,1)S(1)}, bf16[288,512]{1,0:T(8,128)(2,1)S(1)}, u32[]{:S(2)}, u32[]{:S(2)}) collective-permute-start(bf16[288,512]{1,0:T(8,128)(2,1)S(1)} %get-tuple-element.87), channel_id=1, source_target_pairs={{0,1},{1,0},{2,3},{3,2},{4,5},{5,4},{6,7},{7,6},{8,9},{9,8},{10,11... | collective-permute-start | bytes 884744 | tf_op jit(solution)/shard_map/ppermute | solution.py:61
  22.3 4.2 %collective-permute-done.8.refs_3_ = bf16[256,512]{1,0:T(8,128)(2,1)S(1)} collective-permute-done((bf16[256,512]{1,0:T(8,128)(2,1)S(1)}, bf16[256,512]{1,0:T(8,128)(2,1)S(1)}, u32[]{:S(2)}, u32[]{:S(2)}) %collective-permute-start.8) | collective-permute-done | bytes 262176 | tf_op jit(solution)/shard_map/ppermute | solution.py:61
  26.7 0.5 collective-permute-start.9
  27.2 1.5 %collective-permute-start = (bf16[256,1024]{1,0:T(8,128)(2,1)S(1)}, bf16[256,1024]{1,0:T(8,128)(2,1)S(1)}, u32[]{:S(2)}, u32[]{:S(2)}) collective-permute-start(bf16[256,1024]{1,0:T(8,128)(2,1)S(1)} %get-tuple-element.68), channel_id=1, source_target_pairs={{0,1},{1,0},{2,3},{3,2},{4,5},{5,4},{6,7},{7,6},{8,9},{9,8},{10,11... | collective-permute-start | bytes 1572872 | tf_op jit(solution)/shard_map/ppermute | solution.py:61
  28.7 0.8 %gradient_block.4 = (f32[256,512]{1,0:T(8,128)S(1)}, bf16[272,512]{1,0:T(8,128)(2,1)S(1)}) custom-call(bf16[256,2560]{1,0:T(8,128)(2,1)S(1)} %get-tuple-element.109.own, bf16[256,2560]{1,0:T(8,128)(2,1)S(1)} %collective-permute-done.3.sib, bf16[256,512]{1,0:T(8,128)(2,1)S(1)} %get-tuple-element.101.par.refs_0_, ...), custom_call_target="tpu_custom_call" | custom-call | flops 1 | bytes 1 | tf_op jit(solution)/shard_map/gradient_block/pallas_call | solution.py:29
  29.5 1.6 %collective-permute-start.13 = (bf16[272,512]{1,0:T(8,128)(2,1)S(1)}, bf16[272,512]{1,0:T(8,128)(2,1)S(1)}, u32[]{:S(2)}, u32[]{:S(2)}) collective-permute-start(bf16[272,512]{1,0:T(8,128)(2,1)S(1)} %get-tuple-element.92), channel_id=1, source_target_pairs={{0,4},{1,5},{2,6},{3,7},{4,0},{5,1},{6,2},{7,3},{8,12},{9,13},{10,... | collective-permute-start | bytes 835592 | tf_op jit(solution)/shard_map/ppermute | solution.py:61
  31.3 2.1 %collective-permute-start.6 = (bf16[256,512]{1,0:T(8,128)(2,1)S(1)}, bf16[256,512]{1,0:T(8,128)(2,1)S(1)}, u32[]{:S(2)}, u32[]{:S(2)}) collective-permute-start(bf16[256,512]{1,0:T(8,128)(2,1)S(1)} %collective-permute-done.2.refs_2_), channel_id=1, source_target_pairs={{0,8},{1,9},{2,10},{3,11},{4,12},{5,13},{6,14},{7,15},{8,24},{9,25... | collective-permute-start | bytes 786440 | tf_op jit(solution)/shard_map/ppermute | solution.py:61
  33.4 0.8 %gradient_block.5 = (f32[256,512]{1,0:T(8,128)S(1)}, bf16[288,512]{1,0:T(8,128)(2,1)S(1)}) custom-call(bf16[256,2560]{1,0:T(8,128)(2,1)S(1)} %get-tuple-element.109.own, bf16[256,2560]{1,0:T(8,128)(2,1)S(1)} %collective-permute-done.3.sib, bf16[256,512]{1,0:T(8,128)(2,1)S(1)} %take_block.1.par.refs_1_, ...), custom_call_target="tpu_custom_call" | custom-call | flops 1 | bytes 1 | tf_op jit(solution)/shard_map/gradient_block/pallas_call | solution.py:29
  34.3 3.9 %collective-permute-done.13.refs_1_ = bf16[272,512]{1,0:T(8,128)(2,1)S(1)} collective-permute-done((bf16[272,512]{1,0:T(8,128)(2,1)S(1)}, bf16[272,512]{1,0:T(8,128)(2,1)S(1)}, u32[]{:S(2)}, u32[]{:S(2)}) %collective-permute-start.13) | collective-permute-done | bytes 278560 | tf_op jit(solution)/shard_map/ppermute | solution.py:61
  38.2 0.5 collective-permute-start.16
  38.7 1.5 %collective-permute-start.15 = (bf16[288,512]{1,0:T(8,128)(2,1)S(1)}, bf16[288,512]{1,0:T(8,128)(2,1)S(1)}, u32[]{:S(2)}, u32[]{:S(2)}) collective-permute-start(bf16[288,512]{1,0:T(8,128)(2,1)S(1)} %get-tuple-element.98), channel_id=1, source_target_pairs={{0,4},{1,5},{2,6},{3,7},{4,0},{5,1},{6,2},{7,3},{8,12},{9,13},{10,... | collective-permute-start | bytes 884744 | tf_op jit(solution)/shard_map/ppermute | solution.py:61
  40.2 2.0 %collective-permute-done.message = bf16[256,1024]{1,0:T(8,128)(2,1)S(1)} collective-permute-done((bf16[256,1024]{1,0:T(8,128)(2,1)S(1)}, bf16[256,1024]{1,0:T(8,128)(2,1)S(1)}, u32[]{:S(2)}, u32[]{:S(2)}) %collective-permute-start) | collective-permute-done | bytes 524320 | tf_op jit(solution)/shard_map/ppermute | solution.py:61
  42.3 1.9 %collective-permute-start.17 = (bf16[256,512]{1,0:T(8,128)(2,1)S(1)}, bf16[256,512]{1,0:T(8,128)(2,1)S(1)}, u32[]{:S(2)}, u32[]{:S(2)}) collective-permute-start(bf16[256,512]{1,0:T(8,128)(2,1)S(1)} %collective-permute-done.6.refs_4_), channel_id=1, source_target_pairs={{0,4},{1,5},{2,6},{3,7},{4,0},{5,1},{6,2},{7,3},{8,12},{9,13},{10,... | collective-permute-start | bytes 786440 | tf_op jit(solution)/shard_map/ppermute | solution.py:61
  44.2 0.8 %gradient_block.6 = (f32[256,512]{1,0:T(8,128)S(1)}, bf16[256,512]{1,0:T(8,128)(2,1)S(1)}) custom-call(bf16[256,2560]{1,0:T(8,128)(2,1)S(1)} %get-tuple-element.109.own, bf16[256,2560]{1,0:T(8,128)(2,1)S(1)} %collective-permute-done.3.sib, bf16[256,512]{1,0:T(8,128)(2,1)S(1)} %get-tuple-element.94.par.refs_2_, ...), custom_call_target="tpu_custom_call" | custom-call | flops 1 | bytes 1 | tf_op jit(solution)/shard_map/gradient_block/pallas_call | solution.py:29
  45.0 0.2 collective-permute-start.18
  45.2 1.4 %collective-permute-start.19 = (bf16[256,512]{1,0:T(8,128)(2,1)S(1)}, bf16[256,512]{1,0:T(8,128)(2,1)S(1)}, u32[]{:S(2)}, u32[]{:S(2)}) collective-permute-start(bf16[256,512]{1,0:T(8,128)(2,1)S(1)} %get-tuple-element.108), channel_id=1, source_target_pairs={{0,4},{1,5},{2,6},{3,7},{4,0},{5,1},{6,2},{7,3},{8,12},{9,13},{10,... | collective-permute-start | bytes 786440 | tf_op jit(solution)/shard_map/ppermute | solution.py:61
  46.7 1.0 %collective-permute-done.16.refs_2_ = bf16[288,512]{1,0:T(8,128)(2,1)S(1)} collective-permute-done((bf16[288,512]{1,0:T(8,128)(2,1)S(1)}, bf16[288,512]{1,0:T(8,128)(2,1)S(1)}, u32[]{:S(2)}, u32[]{:S(2)}) %collective-permute-start.16) | collective-permute-done | bytes 294944 | tf_op jit(solution)/shard_map/ppermute | solution.py:61
  47.7 3.4 %collective-permute-start.23 = (bf16[256,512]{1,0:T(8,128)(2,1)S(1)}, bf16[256,512]{1,0:T(8,128)(2,1)S(1)}, u32[]{:S(2)}, u32[]{:S(2)}) collective-permute-start(bf16[256,512]{1,0:T(8,128)(2,1)S(1)} %add_blocks.4), channel_id=1, source_target_pairs={{0,16},{1,17},{2,18},{3,19},{4,20},{5,21},{6,22},{7,23},{8,24},{9,... | collective-permute-start | bytes 786440 | tf_op jit(solution)/shard_map/ppermute | solution.py:61
  51.2 1.9 %collective-permute-done.17.refs_5_ = bf16[256,512]{1,0:T(8,128)(2,1)S(1)} collective-permute-done((bf16[256,512]{1,0:T(8,128)(2,1)S(1)}, bf16[256,512]{1,0:T(8,128)(2,1)S(1)}, u32[]{:S(2)}, u32[]{:S(2)}) %collective-permute-start.17) | collective-permute-done | bytes 262176 | tf_op jit(solution)/shard_map/ppermute | solution.py:61
  53.3 0.7 far_features.2
  54.0 1.6 %collective-permute-start.20 = (bf16[256,512]{1,0:T(8,128)(2,1)S(1)}, bf16[256,512]{1,0:T(8,128)(2,1)S(1)}, u32[]{:S(2)}, u32[]{:S(2)}) collective-permute-start(bf16[256,512]{1,0:T(8,128)(2,1)S(1)} %far_features.2), channel_id=1, source_target_pairs={{0,1},{1,0},{2,3},{3,2},{4,5},{5,4},{6,7},{7,6},{8,9},{9,8},{10,11... | collective-permute-start | bytes 786440 | tf_op jit(solution)/shard_map/ppermute | solution.py:61
  55.5 0.8 %gradient_block.7 = (f32[256,512]{1,0:T(8,128)S(1)}, bf16[256,512]{1,0:T(8,128)(2,1)S(1)}) custom-call(bf16[256,2560]{1,0:T(8,128)(2,1)S(1)} %get-tuple-element.109.own, bf16[256,2560]{1,0:T(8,128)(2,1)S(1)} %collective-permute-done.3.sib, bf16[256,512]{1,0:T(8,128)(2,1)S(1)} %get-tuple-element.104.refs_3_.par, ...), custom_call_target="tpu_custom_call" | custom-call | flops 1 | bytes 1 | tf_op jit(solution)/shard_map/gradient_block/pallas_call | solution.py:29
  56.4 0.7 far_features.3
  57.2 1.6 %collective-permute-start.22 = (bf16[256,512]{1,0:T(8,128)(2,1)S(1)}, bf16[256,512]{1,0:T(8,128)(2,1)S(1)}, u32[]{:S(2)}, u32[]{:S(2)}) collective-permute-start(bf16[256,512]{1,0:T(8,128)(2,1)S(1)} %get-tuple-element.112), channel_id=1, source_target_pairs={{0,4},{1,5},{2,6},{3,7},{4,0},{5,1},{6,2},{7,3},{8,12},{9,13},{10,... | collective-permute-start | bytes 786440 | tf_op jit(solution)/shard_map/ppermute | solution.py:61
  58.8 1.8 %collective-permute-start.24 = (bf16[256,512]{1,0:T(8,128)(2,1)S(1)}, bf16[256,512]{1,0:T(8,128)(2,1)S(1)}, u32[]{:S(2)}, u32[]{:S(2)}) collective-permute-start(bf16[256,512]{1,0:T(8,128)(2,1)S(1)} %add_blocks.5), channel_id=1, source_target_pairs={{0,8},{1,9},{2,10},{3,11},{4,12},{5,13},{6,14},{7,15},{8,0},{9,1},... | collective-permute-start | bytes 786440 | tf_op jit(solution)/shard_map/ppermute | solution.py:61
  60.6 1.5 %collective-permute-done.23.refs_2_ = bf16[256,512]{1,0:T(8,128)(2,1)S(1)} collective-permute-done((bf16[256,512]{1,0:T(8,128)(2,1)S(1)}, bf16[256,512]{1,0:T(8,128)(2,1)S(1)}, u32[]{:S(2)}, u32[]{:S(2)}) %collective-permute-start.23) | collective-permute-done | bytes 262176 | tf_op jit(solution)/shard_map/ppermute | solution.py:61
  62.1 1.2 %near_features.1 = (bf16[256,512]{1,0:T(8,128)(2,1)S(1)}, bf16[256,512]{1,0:T(8,128)(2,1)S(1)}) custom-call(bf16[256,2560]{1,0:T(8,128)(2,1)S(1)} %get-tuple-element.109.own, bf16[256,2560]{1,0:T(8,128)(2,1)S(1)} %collective-permute-done.3.sib, bf16[2048,512]{1,0:T(8,128)(2,1)S(1)} %fill_teacher.1.refs_4_.full), custom_call_target="tpu_custom_call" | custom-call | flops 1 | bytes 1 | tf_op jit(solution)/shard_map/near_features/pallas_call | solution.py:29
  63.4 0.6 collective-permute-start.27
  64.0 1.9 %collective-permute-done.21.refs_3_ = bf16[256,512]{1,0:T(8,128)(2,1)S(1)} collective-permute-done((bf16[256,512]{1,0:T(8,128)(2,1)S(1)}, bf16[256,512]{1,0:T(8,128)(2,1)S(1)}, u32[]{:S(2)}, u32[]{:S(2)}) %collective-permute-start.21) | collective-permute-done | bytes 262176 | tf_op jit(solution)/shard_map/ppermute | solution.py:61
  66.0 1.7 %collective-permute-done.24.refs_3_ = bf16[256,512]{1,0:T(8,128)(2,1)S(1)} collective-permute-done((bf16[256,512]{1,0:T(8,128)(2,1)S(1)}, bf16[256,512]{1,0:T(8,128)(2,1)S(1)}, u32[]{:S(2)}, u32[]{:S(2)}) %collective-permute-start.24) | collective-permute-done | bytes 262176 | tf_op jit(solution)/shard_map/ppermute | solution.py:61
  67.9 1.7 %collective-permute-start.28 = (bf16[128,512]{1,0:T(8,128)(2,1)S(1)}, bf16[128,512]{1,0:T(8,128)(2,1)S(1)}, u32[]{:S(2)}, u32[]{:S(2)}) collective-permute-start(bf16[128,512]{1,0:T(8,128)(2,1)S(1)} %get-tuple-element.116.refs_0_), channel_id=1, source_target_pairs={{0,1},{1,0},{2,3},{3,2},{4,5},{5,4},{6,7},{7,6},{8,9},{9,8},{10,11... | collective-permute-start | bytes 393224 | tf_op jit(solution)/shard_map/ppermute | solution.py:61
  69.8 1.7 %update_near.1 = (f32[128,2048]{1,0:T(8,128)}, f32[128,2048]{1,0:T(8,128)}, f32[128,2048]{1,0:T(8,128)}, f32[128,2048]{1,0:T(8,128)}) custom-call(bf16[128,512]{1,0:T(8,128)(2,1)S(1)} %get-tuple-element.116.refs_0_, bf16[128,512]{1,0:T(8,128)(2,1)S(1)} %collective-permute-done.26.refs_1_, f32[128,2048]{1,0:T(8,128)S(1)} %copy-done.1, ...), custom_call_target="tpu_custom_call" | custom-call | flops 1 | bytes 1 | tf_op jit(solution)/shard_map/update_near/pallas_call | solution.py:376
  71.5 1.1 %place_features.1 = bf16[256,2048]{1,0:T(8,128)(2,1)} custom-call(bf16[256,512]{1,0:T(8,128)(2,1)S(1)} %get-tuple-element.119.refs_0_, bf16[256,512]{1,0:T(8,128)(2,1)S(1)} %collective-permute-done.27.refs_1_, bf16[256,512]{1,0:T(8,128)(2,1)S(1)} %collective-permute-done.20.refs_2_, bf16[256,512]{1,0:T(8,128)(2,1)S(1)} %collective-permute-done.21.refs_3_), custom_call_target="tpu_custom_call" | custom-call | flops 1 | bytes 1 | tf_op jit(solution)/shard_map/place_features/pallas_call | solution.py:29
  72.5 1.7 %collective-permute-done.28.refs_0_ = bf16[128,512]{1,0:T(8,128)(2,1)S(1)} collective-permute-done((bf16[128,512]{1,0:T(8,128)(2,1)S(1)}, bf16[128,512]{1,0:T(8,128)(2,1)S(1)}, u32[]{:S(2)}, u32[]{:S(2)}) %collective-permute-start.28) | collective-permute-done | bytes 131104 | tf_op jit(solution)/shard_map/ppermute | solution.py:61
  74.2 1.9 %collective-permute-done.29.refs_1_ = bf16[128,512]{1,0:T(8,128)(2,1)S(1)} collective-permute-done((bf16[128,512]{1,0:T(8,128)(2,1)S(1)}, bf16[128,512]{1,0:T(8,128)(2,1)S(1)}, u32[]{:S(2)}, u32[]{:S(2)}) %collective-permute-start.29) | collective-permute-done | bytes 131104 | tf_op jit(solution)/shard_map/ppermute | solution.py:61
  76.1 1.7 %update_far.1 = (f32[128,2048]{1,0:T(8,128)}, f32[128,2048]{1,0:T(8,128)}, f32[128,2048]{1,0:T(8,128)}, f32[128,2048]{1,0:T(8,128)}) custom-call(bf16[128,512]{1,0:T(8,128)(2,1)S(1)} %collective-permute-done.28.refs_0_, ...), custom_call_target="tpu_custom_call", output_to_operand_aliasing={{0}: (6, {}), {1}: (7, {}), {2}: (8, {}), {3}: (9, {})} | custom-call | flops 1 | bytes 1 | tf_op jit(solution)/shard_map/update_far/pallas_call | solution.py:376
  (46 shorter events, 1.5 us)
Async XLA Ops:
  0.6 5.9 %copy-start = (f32[128,2048]{1,0:T(8,128)S(1)}, f32[128,2048]{1,0:T(8,128)}, u32[]{:S(2)}) copy-start(f32[128,2048]{1,0:T(8,128)} %refs_5_.3) | copy-start | bytes 3145732
  0.6 1.3 %copy-start.4 = (bf16[256,2048]{1,0:T(8,128)(2,1)S(1)}, bf16[256,2048]{1,0:T(8,128)(2,1)}, u32[]{:S(2)}) copy-start(bf16[256,2048]{1,0:T(8,128)(2,1)} %p.1) | copy-start | bytes 3145732
  2.0 1.2 %copy-start.5 = (bf16[256,2048]{1,0:T(8,128)(2,1)S(1)}, bf16[256,2048]{1,0:T(8,128)(2,1)}, u32[]{:S(2)}) copy-start(bf16[256,2048]{1,0:T(8,128)(2,1)} %c.1) | copy-start | bytes 3145732
  3.4 7.9 %collective-permute-start.3 = (bf16[256,2560]{1,0:T(8,128)(2,1)S(1)}, bf16[256,2560]{1,0:T(8,128)(2,1)S(1)}, u32[]{:S(2)}, u32[]{:S(2)}) collective-permute-start(bf16[256,2560]{1,0:T(8,128)(2,1)S(1)} %get-tuple-element.109.own), channel_id=1, source_target_pairs={{0,2},{1,3},{2,0},{3,1},{4,6},{5,7},{6,4},{7,5},{8,10},{9,11},{10,... | collective-permute-start | bytes 3932168 | tf_op jit(solution)/shard_map/ppermute | solution.py:61
  3.9 22.6 %collective-permute-start.7 = (bf16[256,1536]{1,0:T(8,128)(2,1)S(1)}, bf16[256,1536]{1,0:T(8,128)(2,1)S(1)}, u32[]{:S(2)}, u32[]{:S(2)}) collective-permute-start(bf16[256,1536]{1,0:T(8,128)(2,1)S(1)} %get-tuple-element.69), channel_id=1, source_target_pairs={{0,1},{1,0},{2,3},{3,2},{4,5},{5,4},{6,7},{7,6},{8,9},{9,8},{10,11... | collective-permute-start | bytes 2359304 | tf_op jit(solution)/shard_map/ppermute | solution.py:61
  6.5 1.4 %collective-permute-start.1 = (bf16[128,512]{1,0:T(8,128)(2,1)S(1)}, bf16[128,512]{1,0:T(8,128)(2,1)S(1)}, u32[]{:S(2)}, u32[]{:S(2)}) collective-permute-start(bf16[128,512]{1,0:T(8,128)(2,1)S(1)} %get-tuple-element.73), channel_id=1, source_target_pairs={{0,2},{1,3},{2,0},{3,1},{4,6},{5,7},{6,4},{7,5},{8,10},{9,11},{10,... | collective-permute-start | bytes 393224 | tf_op jit(solution)/shard_map/ppermute | solution.py:61
  8.0 8.4 %collective-permute-start.4 = (bf16[256,512]{1,0:T(8,128)(2,1)S(1)}, bf16[256,512]{1,0:T(8,128)(2,1)S(1)}, u32[]{:S(2)}, u32[]{:S(2)}) collective-permute-start(bf16[256,512]{1,0:T(8,128)(2,1)S(1)} %join_teacher.1.refs_0_), channel_id=1, source_target_pairs={{0,4},{1,5},{2,6},{3,7},{4,0},{5,1},{6,2},{7,3},{8,12},{9,13},{10,... | collective-permute-start | bytes 786440 | tf_op jit(solution)/shard_map/ppermute | solution.py:61
  9.8 9.5 %collective-permute-start.2 = (bf16[256,512]{1,0:T(8,128)(2,1)S(1)}, bf16[256,512]{1,0:T(8,128)(2,1)S(1)}, u32[]{:S(2)}, u32[]{:S(2)}) collective-permute-start(bf16[256,512]{1,0:T(8,128)(2,1)S(1)} %join_teacher.1.refs_0_), channel_id=1, source_target_pairs={{0,8},{1,9},{2,10},{3,11},{4,12},{5,13},{6,14},{7,15},{8,24},{9,25... | collective-permute-start | bytes 786440 | tf_op jit(solution)/shard_map/ppermute | solution.py:61
  16.5 14.8 %collective-permute-start.5 = (bf16[544,512]{1,0:T(8,128)(2,1)S(1)}, bf16[544,512]{1,0:T(8,128)(2,1)S(1)}, u32[]{:S(2)}, u32[]{:S(2)}) collective-permute-start(bf16[544,512]{1,0:T(8,128)(2,1)S(1)} %stack_teacher.1), channel_id=1, source_target_pairs={{0,16},{1,17},{2,18},{3,19},{4,20},{5,21},{6,22},{7,23},{8,0},{9,1... | collective-permute-start | bytes 1671176 | tf_op jit(solution)/shard_map/ppermute | solution.py:61
  19.3 7.2 %collective-permute-start.8 = (bf16[256,512]{1,0:T(8,128)(2,1)S(1)}, bf16[256,512]{1,0:T(8,128)(2,1)S(1)}, u32[]{:S(2)}, u32[]{:S(2)}) collective-permute-start(bf16[256,512]{1,0:T(8,128)(2,1)S(1)} %collective-permute-done.2.refs_2_), channel_id=1, source_target_pairs={{0,4},{1,5},{2,6},{3,7},{4,0},{5,1},{6,2},{7,3},{8,12},{9,13},{10,... | collective-permute-start | bytes 786440 | tf_op jit(solution)/shard_map/ppermute | solution.py:61
  20.8 10.4 %collective-permute-start.11 = (bf16[288,512]{1,0:T(8,128)(2,1)S(1)}, bf16[288,512]{1,0:T(8,128)(2,1)S(1)}, u32[]{:S(2)}, u32[]{:S(2)}) collective-permute-start(bf16[288,512]{1,0:T(8,128)(2,1)S(1)} %get-tuple-element.87), channel_id=1, source_target_pairs={{0,1},{1,0},{2,3},{3,2},{4,5},{5,4},{6,7},{7,6},{8,9},{9,8},{10,11... | collective-permute-start | bytes 884744 | tf_op jit(solution)/shard_map/ppermute | solution.py:61
  26.6 2.1 %collective-permute-start.10 = (bf16[256,512]{1,0:T(8,128)(2,1)S(1)}, bf16[256,512]{1,0:T(8,128)(2,1)S(1)}, u32[]{:S(2)}, u32[]{:S(2)}) collective-permute-start(bf16[256,512]{1,0:T(8,128)(2,1)S(1)} %get-tuple-element.81), channel_id=1, source_target_pairs={{0,2},{1,3},{2,0},{3,1},{4,6},{5,7},{6,4},{7,5},{8,10},{9,11},{10,... | collective-permute-start | bytes 786440 | tf_op jit(solution)/shard_map/ppermute | solution.py:61
  26.7 2.0 %collective-permute-start.9 = (bf16[256,512]{1,0:T(8,128)(2,1)S(1)}, bf16[256,512]{1,0:T(8,128)(2,1)S(1)}, u32[]{:S(2)}, u32[]{:S(2)}) collective-permute-start(bf16[256,512]{1,0:T(8,128)(2,1)S(1)} %get-tuple-element.101.par.refs_0_), channel_id=1, source_target_pairs={{0,2},{1,3},{2,0},{3,1},{4,6},{5,7},{6,4},{7,5},{8,10},{9,11},{10,... | collective-permute-start | bytes 786440 | tf_op jit(solution)/shard_map/ppermute | solution.py:61
  27.2 15.0 %collective-permute-start = (bf16[256,1024]{1,0:T(8,128)(2,1)S(1)}, bf16[256,1024]{1,0:T(8,128)(2,1)S(1)}, u32[]{:S(2)}, u32[]{:S(2)}) collective-permute-start(bf16[256,1024]{1,0:T(8,128)(2,1)S(1)} %get-tuple-element.68), channel_id=1, source_target_pairs={{0,1},{1,0},{2,3},{3,2},{4,5},{5,4},{6,7},{7,6},{8,9},{9,8},{10,11... | collective-permute-start | bytes 1572872 | tf_op jit(solution)/shard_map/ppermute | solution.py:61
  29.5 8.7 %collective-permute-start.13 = (bf16[272,512]{1,0:T(8,128)(2,1)S(1)}, bf16[272,512]{1,0:T(8,128)(2,1)S(1)}, u32[]{:S(2)}, u32[]{:S(2)}) collective-permute-start(bf16[272,512]{1,0:T(8,128)(2,1)S(1)} %get-tuple-element.92), channel_id=1, source_target_pairs={{0,4},{1,5},{2,6},{3,7},{4,0},{5,1},{6,2},{7,3},{8,12},{9,13},{10,... | collective-permute-start | bytes 835592 | tf_op jit(solution)/shard_map/ppermute | solution.py:61
  31.2 2.2 %collective-permute-start.12 = (bf16[256,512]{1,0:T(8,128)(2,1)S(1)}, bf16[256,512]{1,0:T(8,128)(2,1)S(1)}, u32[]{:S(2)}, u32[]{:S(2)}) collective-permute-start(bf16[256,512]{1,0:T(8,128)(2,1)S(1)} %take_block.1.par.refs_1_), channel_id=1, source_target_pairs={{0,2},{1,3},{2,0},{3,1},{4,6},{5,7},{6,4},{7,5},{8,10},{9,11},{10,... | collective-permute-start | bytes 786440 | tf_op jit(solution)/shard_map/ppermute | solution.py:61
  31.3 10.9 %collective-permute-start.6 = (bf16[256,512]{1,0:T(8,128)(2,1)S(1)}, bf16[256,512]{1,0:T(8,128)(2,1)S(1)}, u32[]{:S(2)}, u32[]{:S(2)}) collective-permute-start(bf16[256,512]{1,0:T(8,128)(2,1)S(1)} %collective-permute-done.2.refs_2_), channel_id=1, source_target_pairs={{0,8},{1,9},{2,10},{3,11},{4,12},{5,13},{6,14},{7,15},{8,24},{9,25... | collective-permute-start | bytes 786440 | tf_op jit(solution)/shard_map/ppermute | solution.py:61
  38.2 9.4 %collective-permute-start.16 = (bf16[288,512]{1,0:T(8,128)(2,1)S(1)}, bf16[288,512]{1,0:T(8,128)(2,1)S(1)}, u32[]{:S(2)}, u32[]{:S(2)}) collective-permute-start(bf16[288,512]{1,0:T(8,128)(2,1)S(1)} %add_blocks.3), channel_id=1, source_target_pairs={{0,8},{1,9},{2,10},{3,11},{4,12},{5,13},{6,14},{7,15},{8,0},{9,1},... | collective-permute-start | bytes 884744 | tf_op jit(solution)/shard_map/ppermute | solution.py:61
  38.7 9.0 %collective-permute-start.15 = (bf16[288,512]{1,0:T(8,128)(2,1)S(1)}, bf16[288,512]{1,0:T(8,128)(2,1)S(1)}, u32[]{:S(2)}, u32[]{:S(2)}) collective-permute-start(bf16[288,512]{1,0:T(8,128)(2,1)S(1)} %get-tuple-element.98), channel_id=1, source_target_pairs={{0,4},{1,5},{2,6},{3,7},{4,0},{5,1},{6,2},{7,3},{8,12},{9,13},{10,... | collective-permute-start | bytes 884744 | tf_op jit(solution)/shard_map/ppermute | solution.py:61
  42.2 1.9 %collective-permute-start.14 = (bf16[256,512]{1,0:T(8,128)(2,1)S(1)}, bf16[256,512]{1,0:T(8,128)(2,1)S(1)}, u32[]{:S(2)}, u32[]{:S(2)}) collective-permute-start(bf16[256,512]{1,0:T(8,128)(2,1)S(1)} %get-tuple-element.94.par.refs_2_), channel_id=1, source_target_pairs={{0,2},{1,3},{2,0},{3,1},{4,6},{5,7},{6,4},{7,5},{8,10},{9,11},{10,... | collective-permute-start | bytes 786440 | tf_op jit(solution)/shard_map/ppermute | solution.py:61
  42.3 10.8 %collective-permute-start.17 = (bf16[256,512]{1,0:T(8,128)(2,1)S(1)}, bf16[256,512]{1,0:T(8,128)(2,1)S(1)}, u32[]{:S(2)}, u32[]{:S(2)}) collective-permute-start(bf16[256,512]{1,0:T(8,128)(2,1)S(1)} %collective-permute-done.6.refs_4_), channel_id=1, source_target_pairs={{0,4},{1,5},{2,6},{3,7},{4,0},{5,1},{6,2},{7,3},{8,12},{9,13},{10,... | collective-permute-start | bytes 786440 | tf_op jit(solution)/shard_map/ppermute | solution.py:61
  45.0 10.5 %collective-permute-start.18 = (bf16[256,512]{1,0:T(8,128)(2,1)S(1)}, bf16[256,512]{1,0:T(8,128)(2,1)S(1)}, u32[]{:S(2)}, u32[]{:S(2)}) collective-permute-start(bf16[256,512]{1,0:T(8,128)(2,1)S(1)} %get-tuple-element.104.refs_3_.par), channel_id=1, source_target_pairs={{0,2},{1,3},{2,0},{3,1},{4,6},{5,7},{6,4},{7,5},{8,10},{9,11},{10,... | collective-permute-start | bytes 786440 | tf_op jit(solution)/shard_map/ppermute | solution.py:61
  45.2 13.5 %collective-permute-start.19 = (bf16[256,512]{1,0:T(8,128)(2,1)S(1)}, bf16[256,512]{1,0:T(8,128)(2,1)S(1)}, u32[]{:S(2)}, u32[]{:S(2)}) collective-permute-start(bf16[256,512]{1,0:T(8,128)(2,1)S(1)} %get-tuple-element.108), channel_id=1, source_target_pairs={{0,4},{1,5},{2,6},{3,7},{4,0},{5,1},{6,2},{7,3},{8,12},{9,13},{10,... | collective-permute-start | bytes 786440 | tf_op jit(solution)/shard_map/ppermute | solution.py:61
  47.7 14.4 %collective-permute-start.23 = (bf16[256,512]{1,0:T(8,128)(2,1)S(1)}, bf16[256,512]{1,0:T(8,128)(2,1)S(1)}, u32[]{:S(2)}, u32[]{:S(2)}) collective-permute-start(bf16[256,512]{1,0:T(8,128)(2,1)S(1)} %add_blocks.4), channel_id=1, source_target_pairs={{0,16},{1,17},{2,18},{3,19},{4,20},{5,21},{6,22},{7,23},{8,24},{9,... | collective-permute-start | bytes 786440 | tf_op jit(solution)/shard_map/ppermute | solution.py:61
  54.0 9.4 %collective-permute-start.20 = (bf16[256,512]{1,0:T(8,128)(2,1)S(1)}, bf16[256,512]{1,0:T(8,128)(2,1)S(1)}, u32[]{:S(2)}, u32[]{:S(2)}) collective-permute-start(bf16[256,512]{1,0:T(8,128)(2,1)S(1)} %far_features.2), channel_id=1, source_target_pairs={{0,1},{1,0},{2,3},{3,2},{4,5},{5,4},{6,7},{7,6},{8,9},{9,8},{10,11... | collective-permute-start | bytes 786440 | tf_op jit(solution)/shard_map/ppermute | solution.py:61
  57.1 8.7 %collective-permute-start.21 = (bf16[256,512]{1,0:T(8,128)(2,1)S(1)}, bf16[256,512]{1,0:T(8,128)(2,1)S(1)}, u32[]{:S(2)}, u32[]{:S(2)}) collective-permute-start(bf16[256,512]{1,0:T(8,128)(2,1)S(1)} %far_features.3), channel_id=1, source_target_pairs={{0,3},{1,2},{2,1},{3,0},{4,7},{5,6},{6,5},{7,4},{8,11},{9,10},{10,... | collective-permute-start | bytes 786440 | tf_op jit(solution)/shard_map/ppermute | solution.py:61
  57.2 8.8 %collective-permute-start.22 = (bf16[256,512]{1,0:T(8,128)(2,1)S(1)}, bf16[256,512]{1,0:T(8,128)(2,1)S(1)}, u32[]{:S(2)}, u32[]{:S(2)}) collective-permute-start(bf16[256,512]{1,0:T(8,128)(2,1)S(1)} %get-tuple-element.112), channel_id=1, source_target_pairs={{0,4},{1,5},{2,6},{3,7},{4,0},{5,1},{6,2},{7,3},{8,12},{9,13},{10,... | collective-permute-start | bytes 786440 | tf_op jit(solution)/shard_map/ppermute | solution.py:61
  58.8 8.8 %collective-permute-start.24 = (bf16[256,512]{1,0:T(8,128)(2,1)S(1)}, bf16[256,512]{1,0:T(8,128)(2,1)S(1)}, u32[]{:S(2)}, u32[]{:S(2)}) collective-permute-start(bf16[256,512]{1,0:T(8,128)(2,1)S(1)} %add_blocks.5), channel_id=1, source_target_pairs={{0,8},{1,9},{2,10},{3,11},{4,12},{5,13},{6,14},{7,15},{8,0},{9,1},... | collective-permute-start | bytes 786440 | tf_op jit(solution)/shard_map/ppermute | solution.py:61
  62.1 3.7 %collective-permute-start.25 = (bf16[240,512]{1,0:T(8,128)(2,1)S(1)}, bf16[240,512]{1,0:T(8,128)(2,1)S(1)}, u32[]{:S(2)}, u32[]{:S(2)}) collective-permute-start(bf16[240,512]{1,0:T(8,128)(2,1)S(1)} %get-tuple-element.114), channel_id=1, source_target_pairs={{0,2},{1,3},{2,0},{3,1},{4,6},{5,7},{6,4},{7,5},{8,10},{9,11},{10,... | collective-permute-start | bytes 737288 | tf_op jit(solution)/shard_map/ppermute | solution.py:61
  62.1 7.6 %copy-start.2 = (f32[128,2048]{1,0:T(8,128)S(1)}, f32[128,2048]{1,0:T(8,128)}, u32[]{:S(2)}) copy-start(f32[128,2048]{1,0:T(8,128)} %refs_3_.3) | copy-start | bytes 3145732
  62.1 7.6 %copy-start.3 = (f32[128,2048]{1,0:T(8,128)S(1)}, f32[128,2048]{1,0:T(8,128)}, u32[]{:S(2)}) copy-start(f32[128,2048]{1,0:T(8,128)} %refs_4_.3) | copy-start | bytes 3145732
  63.4 6.4 %copy-start.1 = (f32[128,2048]{1,0:T(8,128)S(1)}, f32[128,2048]{1,0:T(8,128)}, u32[]{:S(2)}) copy-start(f32[128,2048]{1,0:T(8,128)} %refs_2_.3) | copy-start | bytes 3145732
  63.4 8.0 %collective-permute-start.27 = (bf16[256,512]{1,0:T(8,128)(2,1)S(1)}, bf16[256,512]{1,0:T(8,128)(2,1)S(1)}, u32[]{:S(2)}, u32[]{:S(2)}) collective-permute-start(bf16[256,512]{1,0:T(8,128)(2,1)S(1)} %get-tuple-element.120), channel_id=1, source_target_pairs={{0,2},{1,3},{2,0},{3,1},{4,6},{5,7},{6,4},{7,5},{8,10},{9,11},{10,... | collective-permute-start | bytes 786440 | tf_op jit(solution)/shard_map/ppermute | solution.py:61
  67.8 1.9 %collective-permute-start.26 = (bf16[128,512]{1,0:T(8,128)(2,1)S(1)}, bf16[128,512]{1,0:T(8,128)(2,1)S(1)}, u32[]{:S(2)}, u32[]{:S(2)}) collective-permute-start(bf16[128,512]{1,0:T(8,128)(2,1)S(1)} %get-tuple-element.117), channel_id=1, source_target_pairs={{0,2},{1,3},{2,0},{3,1},{4,6},{5,7},{6,4},{7,5},{8,10},{9,11},{10,... | collective-permute-start | bytes 393224 | tf_op jit(solution)/shard_map/ppermute | solution.py:61
  67.9 6.4 %collective-permute-start.28 = (bf16[128,512]{1,0:T(8,128)(2,1)S(1)}, bf16[128,512]{1,0:T(8,128)(2,1)S(1)}, u32[]{:S(2)}, u32[]{:S(2)}) collective-permute-start(bf16[128,512]{1,0:T(8,128)(2,1)S(1)} %get-tuple-element.116.refs_0_), channel_id=1, source_target_pairs={{0,1},{1,0},{2,3},{3,2},{4,5},{5,4},{6,7},{7,6},{8,9},{9,8},{10,11... | collective-permute-start | bytes 393224 | tf_op jit(solution)/shard_map/ppermute | solution.py:61
  69.6 6.6 %collective-permute-start.29 = (bf16[128,512]{1,0:T(8,128)(2,1)S(1)}, bf16[128,512]{1,0:T(8,128)(2,1)S(1)}, u32[]{:S(2)}, u32[]{:S(2)}) collective-permute-start(bf16[128,512]{1,0:T(8,128)(2,1)S(1)} %get-tuple-element.117), channel_id=1, source_target_pairs={{0,3},{1,2},{2,1},{3,0},{4,7},{5,6},{6,5},{7,4},{8,11},{9,10},{10,... | collective-permute-start | bytes 393224 | tf_op jit(solution)/shard_map/ppermute | solution.py:61

commit v4 on v3

--- a/solution.py
+++ b/solution.py
@@ -123,9 +123,18 @@
             c_here[...] = message[:, aligned(core, part)]
             block[...] = message[:, lead:]
 
-        def halve_body(message, *blocks):
-            for k, out in enumerate(blocks):
-                out[...] = message[:tokens, k * span : (k + 1) * span]
+        def first_body(message, block):
+            block[...] = message[:tokens, :]
+
+        def take_body(message, upper, lower, first, second):
+            first[...] = message[:, :span]
+            second[...] = message[:, span:]
+            upper[...] = message[: tokens // 2, :span]
+            lower[...] = message[tokens // 2 :, :span]
+
+        def pieces_body(upper, lower, block):
+            block[: tokens // 2, :] = upper[...]
+            block[tokens // 2 :, :] = lower[...]
 
         clock = []
 
@@ -144,12 +153,13 @@
         def cast_body(t, same, other):
             z, y, core, q = place()
             same[...] = t[:, aligned(q, part)].astype(bf16)
-            other[...] = t[:, aligned(q ^ 1, part)].astype(bf16)
+            other[:rows, :] = t[:, aligned(q ^ 1, part)].astype(bf16)
+            other[rows:, :] = jnp.zeros((other.shape[0] - rows, part), bf16)
 
         def join_body(same, sib, out):
             z, y, core, q = place()
             out[aligned(core, rows), :] = same[...]
-            out[aligned(1 - core, rows), :] = sib[...]
+            out[aligned(1 - core, rows), :] = sib[:rows, :]
 
         def stack_body(*refs):
             for k, ref in enumerate(refs[:-1]):
@@ -188,7 +198,7 @@
                 "gradient_block",
                 terms_body(k),
                 [((2 * rows, part), f32)]
-                + [((2 * rows + (extra, 2 * extra, 0, 0)[k], part), bf16)] * (ny - 1),
+                + [((2 * rows + extra * (k == 0), part), bf16)] * (ny - 1),
                 [near_own, near_sib, far_par[k], far_dia[k], c_own, c_par, c_dia],
                 scratch=[pltpu.VMEM((span, part), f32)],
             )
@@ -256,6 +266,13 @@
         def block_sum(dz, *parts, more=0):
             return add([terms[dz][0], *moved_y[dz], *parts], bf16, more)
 
+        w_same, w_other = run(
+            "cast_teacher",
+            cast_body,
+            [((rows, part), bf16), ((4 * rows + 2 * extra, part), bf16)],
+            [teacher],
+        )
+        w_sib = start(w_other, sibling)
         first, near_own, c_own, second, third, mark = run(
             "cut_tokens",
             cut_body,
@@ -270,8 +287,6 @@
         )
         message = start(first, partner)
         near_sib = start(near_own, sibling)
-        w_same, w_other = run("cast_teacher", cast_body, [((rows, part), bf16)] * 2, [after(teacher, first)])
-        w_sib = start(w_other, sibling)
         (w_line[0],) = run(
             "join_teacher", join_body, [((2 * rows, part), bf16)], [w_same, w_sib]
         )
@@ -291,23 +306,28 @@
             "split_message",
             split_body,
             [((tokens, part), bf16)] * 2 + [((tokens, span), bf16)],
-            [after(message, near_sib, *w_side[3])],
+            [after(message, near_sib)],
         )
         c_dia = start(c_other, sibling)
         far_dia[0] = start(far_par[0], sibling)
+        wait(*w_side[3])
         gradient_block(0)
         both = start(third, partner)
-        (far_par[1],) = run("take_block", halve_body, [((tokens, span), bf16)], [block])
+        (far_par[1],) = run("take_block", first_body, [((tokens, span), bf16)], [block])
         far_dia[1] = start(far_par[1], sibling)
         wait(turn)
         gradient_block(1)
-        onward = block_sum(3, more=2 * extra)
+        onward = block_sum(3)
         teacher_y(2, onward)
         onward = start(onward, across_z(1))
-        far_par[2:] = run(
-            "halve_message", halve_body, [((tokens, span), bf16)] * 2, [after(both, w_line[2])]
-        )
-        far_dia[2] = start(far_par[2], sibling)
+        *pieces, far_par[2], far_par[3] = run(
+            "take_blocks",
+            take_body,
+            [((tokens // 2, span), bf16)] * 2 + [((tokens, span), bf16)] * 2,
+            [after(both, w_line[2])],
+        )
+        pieces = [start(piece, sibling) for piece in pieces]
+        (far_dia[2],) = run("join_pieces", pieces_body, [((tokens, span), bf16)], pieces)
         gradient_block(2)
         onward = start(block_sum(2, onward), across_z(2))
         far_dia[3] = start(far_par[3], sibling, terms[1][0])
@@ -342,7 +362,7 @@
         def update_body(quarters):
             def body(*refs):
                 z, y, core, q = place()
-                student, first, second, teach = refs[2:6]
+                student, first, second, teach = refs[len(quarters) :][:4]
                 outs, held, sems = refs[-6:-2], refs[-2], refs[-1]
                 corr_one = 1.0 - beta_one**STEP
                 corr_two = 1.0 - beta_two**STEP
@@ -376,11 +396,12 @@
                 out = pl.pallas_call(
                     update_body(quarters),
                     out_shape=[jax.ShapeDtypeStruct((rows, outw), f32)] * 4,
-                    in_specs=[VMEM] * 6 + [ANY] * len(begun),
+                    in_specs=[VMEM] * len(inputs) + [ANY] * len(begun),
                     out_specs=[ANY] * 4,
-                    input_output_aliases={6 + k: k for k in range(len(begun))},
+                    input_output_aliases={len(inputs) + k: k for k in range(len(begun))},
                     scratch_shapes=[
-                        pltpu.VMEM((8, rows, part), f32), pltpu.SemaphoreType.DMA((8,))
+                        pltpu.VMEM((4 * len(quarters), rows, part), f32),
+                        pltpu.SemaphoreType.DMA((4 * len(quarters),)),
                     ],
                     cost_estimate=pl.CostEstimate(flops=1, bytes_accessed=1, transcendentals=0),
                     compiler_params=pltpu.CompilerParams(vmem_limit_bytes=16 * 2**20),
@@ -395,7 +416,8 @@
             [((tokens, outw), bf16)],
             [f_own, f_sib, f_par, f_dia],
         )
-        new = update("update_far", (2, 3), [g_par, g_dia], new)
+        new = update("update_partner", (2,), [g_par], new)
+        new = update("update_diagonal", (3,), [g_dia], new)
         return (features, *new)
 
     tokens_placed, weights_placed = P(("fsdp", "rep"), None), P("fsdp", None)

time: 78 us -> 79.1 us (1.014)
  waiting for transfers between devices: 28.3 us -> 25.8 us
  starting transfers between devices: 34.8 us -> 36.3 us
  local copies, waits for them, and re-layouts: 2.55 us -> 3.63 us
  Pallas kernels: 11.3 us -> 12.2 us
    ppermute x30 -> x31, waiting for transfers between devices: 28.3 us -> 25.8 us  [send(): return lax.ppermute(value, ('fsdp', 'rep'), perm)]
    ppermute x30 -> x31, starting transfers between devices: 34.8 us -> 36.3 us  [send(): return lax.ppermute(value, ('fsdp', 'rep'), perm)]
    unnamed x12 -> x14, local copies, waits for them, and re-layouts: 2.55 us -> 3.63 us
    pallas_call x2 -> x3, Pallas kernels: 3.33 us -> 4.22 us  [update(): pl.pallas_call(update_body(quarters), out_shape=[jax.ShapeDtypeStruct((ro...]
    pallas_call x20 -> x21, Pallas kernels: 7.96 us -> 8.02 us  [call(): pl.pallas_call(body, out_shape=shapes, in_specs=[VMEM] * len(inputs), out...]
  transfers between devices with their start and end apart: 30 -> 31, of which waited for: 14 -> 14; matrix products, arithmetic and copies ran while one was open for 0% -> 0% of each run, Pallas kernels for 12% -> 14%
where the time goes in v4:
time: 79.1 us; the launch traced here: 78.8 us
  starting transfers between devices  36.3 us (46%)
  waiting for transfers between devices  25.8 us (33%)
  Pallas kernels  12.2 us (15%)
  local copies, waits for them, and re-layouts  3.63 us (5%)
  between operations  0.89 us (1%)
    ppermute x31, starting transfers between devices, send(): return lax.ppermute(value, ('fsdp', 'rep'), perm)  36.3 us
    ppermute x31, waiting for transfers between devices, send(): return lax.ppermute(value, ('fsdp', 'rep'), perm)  25.8 us
    pallas_call x21, Pallas kernels, call(): pl.pallas_call(body, out_shape=shapes, in_specs=[VMEM] * len(inputs), out...  8.02 us
    pallas_call x3, Pallas kernels, update(): pl.pallas_call(update_body(quarters), out_shape=[jax.ShapeDtypeStruct((ro...  4.22 us
    unnamed x14, local copies, waits for them, and re-layouts  3.63 us
  transfers between devices with their start and end apart: 31, of which 14 were waited for; matrix products, arithmetic and copies ran while one was open for 0% of the time, Pallas kernels for 14%

profile of v4, /device:TPU:0, one launch (start us, length us, event | category | flops | bytes accessed | tf_op | source)
XLA Modules:
  0.0 78.8 jit_solution(16672779293842372238)
XLA Ops:
  0.6 1.2 %copy-done = f32[128,2048]{1,0:T(8,128)S(1)} copy-done((f32[128,2048]{1,0:T(8,128)S(1)}, f32[128,2048]{1,0:T(8,128)}, u32[]{:S(2)}) %copy-start) | copy-done | bytes 1048600
  1.9 1.2 %copy-done.5 = bf16[256,2048]{1,0:T(8,128)(2,1)S(1)} copy-done((bf16[256,2048]{1,0:T(8,128)(2,1)S(1)}, bf16[256,2048]{1,0:T(8,128)(2,1)}, u32[]{:S(2)}) %copy-start.5) | copy-done | bytes 1048600
  3.1 1.2 %copy-done.6 = bf16[256,2048]{1,0:T(8,128)(2,1)S(1)} copy-done((bf16[256,2048]{1,0:T(8,128)(2,1)S(1)}, bf16[256,2048]{1,0:T(8,128)(2,1)}, u32[]{:S(2)}) %copy-start.6) | copy-done | bytes 1048600
  4.5 0.5 collective-permute-start.3
  5.1 2.9 %collective-permute-start.7 = (bf16[256,1536]{1,0:T(8,128)(2,1)S(1)}, bf16[256,1536]{1,0:T(8,128)(2,1)S(1)}, u32[]{:S(2)}, u32[]{:S(2)}) collective-permute-start(bf16[256,1536]{1,0:T(8,128)(2,1)S(1)} %get-tuple-element.79), channel_id=1, source_target_pairs={{0,1},{1,0},{2,3},{3,2},{4,5},{5,4},{6,7},{7,6},{8,9},{9,8},{10,11... | collective-permute-start | bytes 2359304 | tf_op jit(solution)/shard_map/ppermute | solution.py:61
  8.6 3.0 %collective-permute-start.4 = (bf16[256,512]{1,0:T(8,128)(2,1)S(1)}, bf16[256,512]{1,0:T(8,128)(2,1)S(1)}, u32[]{:S(2)}, u32[]{:S(2)}) collective-permute-start(bf16[256,512]{1,0:T(8,128)(2,1)S(1)} %join_teacher.1.refs_0_), channel_id=1, source_target_pairs={{0,4},{1,5},{2,6},{3,7},{4,0},{5,1},{6,2},{7,3},{8,12},{9,13},{10,... | collective-permute-start | bytes 786440 | tf_op jit(solution)/shard_map/ppermute | solution.py:61
  11.5 1.6 %collective-permute-start.2 = (bf16[256,512]{1,0:T(8,128)(2,1)S(1)}, bf16[256,512]{1,0:T(8,128)(2,1)S(1)}, u32[]{:S(2)}, u32[]{:S(2)}) collective-permute-start(bf16[256,512]{1,0:T(8,128)(2,1)S(1)} %join_teacher.1.refs_0_), channel_id=1, source_target_pairs={{0,8},{1,9},{2,10},{3,11},{4,12},{5,13},{6,14},{7,15},{8,24},{9,25... | collective-permute-start | bytes 786440 | tf_op jit(solution)/shard_map/ppermute | solution.py:61
  13.1 5.0 %collective-permute-done.4.refs_1_ = bf16[256,512]{1,0:T(8,128)(2,1)S(1)} collective-permute-done((bf16[256,512]{1,0:T(8,128)(2,1)S(1)}, bf16[256,512]{1,0:T(8,128)(2,1)S(1)}, u32[]{:S(2)}, u32[]{:S(2)}) %collective-permute-start.4) | collective-permute-done | bytes 262176 | tf_op jit(solution)/shard_map/ppermute | solution.py:61
  18.2 2.9 %collective-permute-start.5 = (bf16[544,512]{1,0:T(8,128)(2,1)S(1)}, bf16[544,512]{1,0:T(8,128)(2,1)S(1)}, u32[]{:S(2)}, u32[]{:S(2)}) collective-permute-start(bf16[544,512]{1,0:T(8,128)(2,1)S(1)} %stack_teacher.1), channel_id=1, source_target_pairs={{0,16},{1,17},{2,18},{3,19},{4,20},{5,21},{6,22},{7,23},{8,0},{9,1... | collective-permute-start | bytes 1671176 | tf_op jit(solution)/shard_map/ppermute | solution.py:61
  21.0 1.5 %collective-permute-start.8 = (bf16[256,512]{1,0:T(8,128)(2,1)S(1)}, bf16[256,512]{1,0:T(8,128)(2,1)S(1)}, u32[]{:S(2)}, u32[]{:S(2)}) collective-permute-start(bf16[256,512]{1,0:T(8,128)(2,1)S(1)} %collective-permute-done.2.refs_2_), channel_id=1, source_target_pairs={{0,4},{1,5},{2,6},{3,7},{4,0},{5,1},{6,2},{7,3},{8,12},{9,13},{10,... | collective-permute-start | bytes 786440 | tf_op jit(solution)/shard_map/ppermute | solution.py:61
  22.5 1.5 %collective-permute-start.11 = (bf16[288,512]{1,0:T(8,128)(2,1)S(1)}, bf16[288,512]{1,0:T(8,128)(2,1)S(1)}, u32[]{:S(2)}, u32[]{:S(2)}) collective-permute-start(bf16[288,512]{1,0:T(8,128)(2,1)S(1)} %get-tuple-element.95), channel_id=1, source_target_pairs={{0,1},{1,0},{2,3},{3,2},{4,5},{5,4},{6,7},{7,6},{8,9},{9,8},{10,11... | collective-permute-start | bytes 884744 | tf_op jit(solution)/shard_map/ppermute | solution.py:61
  24.0 2.4 %collective-permute-done.7.message = bf16[256,1536]{1,0:T(8,128)(2,1)S(1)} collective-permute-done((bf16[256,1536]{1,0:T(8,128)(2,1)S(1)}, bf16[256,1536]{1,0:T(8,128)(2,1)S(1)}, u32[]{:S(2)}, u32[]{:S(2)}) %collective-permute-start.7) | collective-permute-done | bytes 786464 | tf_op jit(solution)/shard_map/ppermute | solution.py:61
  26.5 0.5 collective-permute-start.9
  27.0 1.2 %collective-permute-done.8.refs_3_ = bf16[256,512]{1,0:T(8,128)(2,1)S(1)} collective-permute-done((bf16[256,512]{1,0:T(8,128)(2,1)S(1)}, bf16[256,512]{1,0:T(8,128)(2,1)S(1)}, u32[]{:S(2)}, u32[]{:S(2)}) %collective-permute-start.8) | collective-permute-done | bytes 262176 | tf_op jit(solution)/shard_map/ppermute | solution.py:61
  28.3 1.5 %collective-permute-start = (bf16[256,1024]{1,0:T(8,128)(2,1)S(1)}, bf16[256,1024]{1,0:T(8,128)(2,1)S(1)}, u32[]{:S(2)}, u32[]{:S(2)}) collective-permute-start(bf16[256,1024]{1,0:T(8,128)(2,1)S(1)} %get-tuple-element.78), channel_id=1, source_target_pairs={{0,1},{1,0},{2,3},{3,2},{4,5},{5,4},{6,7},{7,6},{8,9},{9,8},{10,11... | collective-permute-start | bytes 1572872 | tf_op jit(solution)/shard_map/ppermute | solution.py:61
  29.8 0.8 %gradient_block.4 = (f32[256,512]{1,0:T(8,128)S(1)}, bf16[272,512]{1,0:T(8,128)(2,1)S(1)}) custom-call(bf16[256,2560]{1,0:T(8,128)(2,1)S(1)} %get-tuple-element.120.own, bf16[256,2560]{1,0:T(8,128)(2,1)S(1)} %collective-permute-done.3.sib, bf16[256,512]{1,0:T(8,128)(2,1)S(1)} %get-tuple-element.112.par.refs_0_, ...), custom_call_target="tpu_custom_call" | custom-call | flops 1 | bytes 1 | tf_op jit(solution)/shard_map/gradient_block/pallas_call | solution.py:29
  30.6 1.6 %collective-permute-start.13 = (bf16[272,512]{1,0:T(8,128)(2,1)S(1)}, bf16[272,512]{1,0:T(8,128)(2,1)S(1)}, u32[]{:S(2)}, u32[]{:S(2)}) collective-permute-start(bf16[272,512]{1,0:T(8,128)(2,1)S(1)} %get-tuple-element.100), channel_id=1, source_target_pairs={{0,4},{1,5},{2,6},{3,7},{4,0},{5,1},{6,2},{7,3},{8,12},{9,13},{10,... | collective-permute-start | bytes 835592 | tf_op jit(solution)/shard_map/ppermute | solution.py:61
  32.2 0.5 collective-permute-done.11.message
  32.8 2.2 %collective-permute-start.6 = (bf16[256,512]{1,0:T(8,128)(2,1)S(1)}, bf16[256,512]{1,0:T(8,128)(2,1)S(1)}, u32[]{:S(2)}, u32[]{:S(2)}) collective-permute-start(bf16[256,512]{1,0:T(8,128)(2,1)S(1)} %collective-permute-done.2.refs_2_), channel_id=1, source_target_pairs={{0,8},{1,9},{2,10},{3,11},{4,12},{5,13},{6,14},{7,15},{8,24},{9,25... | collective-permute-start | bytes 786440 | tf_op jit(solution)/shard_map/ppermute | solution.py:61
  35.0 0.8 %gradient_block.5 = (f32[256,512]{1,0:T(8,128)S(1)}, bf16[256,512]{1,0:T(8,128)(2,1)S(1)}) custom-call(bf16[256,2560]{1,0:T(8,128)(2,1)S(1)} %get-tuple-element.120.own, bf16[256,2560]{1,0:T(8,128)(2,1)S(1)} %collective-permute-done.3.sib, bf16[256,512]{1,0:T(8,128)(2,1)S(1)} %take_block.1.par.refs_1_, ...), custom_call_target="tpu_custom_call" | custom-call | flops 1 | bytes 1 | tf_op jit(solution)/shard_map/gradient_block/pallas_call | solution.py:29
  35.9 2.5 %collective-permute-done.13.refs_1_ = bf16[272,512]{1,0:T(8,128)(2,1)S(1)} collective-permute-done((bf16[272,512]{1,0:T(8,128)(2,1)S(1)}, bf16[272,512]{1,0:T(8,128)(2,1)S(1)}, u32[]{:S(2)}, u32[]{:S(2)}) %collective-permute-start.13) | collective-permute-done | bytes 278560 | tf_op jit(solution)/shard_map/ppermute | solution.py:61
  38.4 1.9 %collective-permute-start.17 = (bf16[256,512]{1,0:T(8,128)(2,1)S(1)}, bf16[256,512]{1,0:T(8,128)(2,1)S(1)}, u32[]{:S(2)}, u32[]{:S(2)}) collective-permute-start(bf16[256,512]{1,0:T(8,128)(2,1)S(1)} %add_blocks.3), channel_id=1, source_target_pairs={{0,8},{1,9},{2,10},{3,11},{4,12},{5,13},{6,14},{7,15},{8,0},{9,1},... | collective-permute-start | bytes 786440 | tf_op jit(solution)/shard_map/ppermute | solution.py:61
  40.3 1.5 %collective-permute-start.16 = (bf16[256,512]{1,0:T(8,128)(2,1)S(1)}, bf16[256,512]{1,0:T(8,128)(2,1)S(1)}, u32[]{:S(2)}, u32[]{:S(2)}) collective-permute-start(bf16[256,512]{1,0:T(8,128)(2,1)S(1)} %get-tuple-element.109), channel_id=1, source_target_pairs={{0,4},{1,5},{2,6},{3,7},{4,0},{5,1},{6,2},{7,3},{8,12},{9,13},{10,... | collective-permute-start | bytes 786440 | tf_op jit(solution)/shard_map/ppermute | solution.py:61
  41.8 1.6 %collective-permute-done.message = bf16[256,1024]{1,0:T(8,128)(2,1)S(1)} collective-permute-done((bf16[256,1024]{1,0:T(8,128)(2,1)S(1)}, bf16[256,1024]{1,0:T(8,128)(2,1)S(1)}, u32[]{:S(2)}, u32[]{:S(2)}) %collective-permute-start) | collective-permute-done | bytes 524320 | tf_op jit(solution)/shard_map/ppermute | solution.py:61
  43.5 0.5 collective-permute-start.15
  44.0 1.8 %collective-permute-start.18 = (bf16[256,512]{1,0:T(8,128)(2,1)S(1)}, bf16[256,512]{1,0:T(8,128)(2,1)S(1)}, u32[]{:S(2)}, u32[]{:S(2)}) collective-permute-start(bf16[256,512]{1,0:T(8,128)(2,1)S(1)} %collective-permute-done.6.refs_4_), channel_id=1, source_target_pairs={{0,4},{1,5},{2,6},{3,7},{4,0},{5,1},{6,2},{7,3},{8,12},{9,13},{10,... | collective-permute-start | bytes 786440 | tf_op jit(solution)/shard_map/ppermute | solution.py:61
  45.8 0.8 %gradient_block.6 = (f32[256,512]{1,0:T(8,128)S(1)}, bf16[256,512]{1,0:T(8,128)(2,1)S(1)}) custom-call(bf16[256,2560]{1,0:T(8,128)(2,1)S(1)} %get-tuple-element.120.own, bf16[256,2560]{1,0:T(8,128)(2,1)S(1)} %collective-permute-done.3.sib, bf16[256,512]{1,0:T(8,128)(2,1)S(1)} %get-tuple-element.106.par.refs_2_, bf16[256,512]{1,0:T(8,128)(2,1)S(1)} %join_pieces.1.dia.refs_2_, ...), custom_call_target="tpu_custom_call" | custom-call | flops 1 | bytes 1 | tf_op jit(solution)/shard_map/gradient_block/pallas_call | solution.py:29
  46.8 1.3 %collective-permute-start.20 = (bf16[256,512]{1,0:T(8,128)(2,1)S(1)}, bf16[256,512]{1,0:T(8,128)(2,1)S(1)}, u32[]{:S(2)}, u32[]{:S(2)}) collective-permute-start(bf16[256,512]{1,0:T(8,128)(2,1)S(1)} %get-tuple-element.119), channel_id=1, source_target_pairs={{0,4},{1,5},{2,6},{3,7},{4,0},{5,1},{6,2},{7,3},{8,12},{9,13},{10,... | collective-permute-start | bytes 786440 | tf_op jit(solution)/shard_map/ppermute | solution.py:61
  48.7 2.2 %collective-permute-start.24 = (bf16[256,512]{1,0:T(8,128)(2,1)S(1)}, bf16[256,512]{1,0:T(8,128)(2,1)S(1)}, u32[]{:S(2)}, u32[]{:S(2)}) collective-permute-start(bf16[256,512]{1,0:T(8,128)(2,1)S(1)} %add_blocks.4), channel_id=1, source_target_pairs={{0,16},{1,17},{2,18},{3,19},{4,20},{5,21},{6,22},{7,23},{8,24},{9,... | collective-permute-start | bytes 786440 | tf_op jit(solution)/shard_map/ppermute | solution.py:61
  50.8 2.8 %collective-permute-done.18.refs_5_ = bf16[256,512]{1,0:T(8,128)(2,1)S(1)} collective-permute-done((bf16[256,512]{1,0:T(8,128)(2,1)S(1)}, bf16[256,512]{1,0:T(8,128)(2,1)S(1)}, u32[]{:S(2)}, u32[]{:S(2)}) %collective-permute-start.18) | collective-permute-done | bytes 262176 | tf_op jit(solution)/shard_map/ppermute | solution.py:61
  53.8 0.7 far_features.2
  54.5 1.6 %collective-permute-start.21 = (bf16[256,512]{1,0:T(8,128)(2,1)S(1)}, bf16[256,512]{1,0:T(8,128)(2,1)S(1)}, u32[]{:S(2)}, u32[]{:S(2)}) collective-permute-start(bf16[256,512]{1,0:T(8,128)(2,1)S(1)} %far_features.2), channel_id=1, source_target_pairs={{0,1},{1,0},{2,3},{3,2},{4,5},{5,4},{6,7},{7,6},{8,9},{9,8},{10,11... | collective-permute-start | bytes 786440 | tf_op jit(solution)/shard_map/ppermute | solution.py:61
  56.1 0.8 %gradient_block.7 = (f32[256,512]{1,0:T(8,128)S(1)}, bf16[256,512]{1,0:T(8,128)(2,1)S(1)}) custom-call(bf16[256,2560]{1,0:T(8,128)(2,1)S(1)} %get-tuple-element.120.own, bf16[256,2560]{1,0:T(8,128)(2,1)S(1)} %collective-permute-done.3.sib, bf16[256,512]{1,0:T(8,128)(2,1)S(1)} %get-tuple-element.115.refs_3_.par, ...), custom_call_target="tpu_custom_call" | custom-call | flops 1 | bytes 1 | tf_op jit(solution)/shard_map/gradient_block/pallas_call | solution.py:29
  57.0 0.7 far_features.3
  57.8 1.6 %collective-permute-start.23 = (bf16[256,512]{1,0:T(8,128)(2,1)S(1)}, bf16[256,512]{1,0:T(8,128)(2,1)S(1)}, u32[]{:S(2)}, u32[]{:S(2)}) collective-permute-start(bf16[256,512]{1,0:T(8,128)(2,1)S(1)} %get-tuple-element.123), channel_id=1, source_target_pairs={{0,4},{1,5},{2,6},{3,7},{4,0},{5,1},{6,2},{7,3},{8,12},{9,13},{10,... | collective-permute-start | bytes 786440 | tf_op jit(solution)/shard_map/ppermute | solution.py:61
  59.4 1.4 %collective-permute-start.25 = (bf16[256,512]{1,0:T(8,128)(2,1)S(1)}, bf16[256,512]{1,0:T(8,128)(2,1)S(1)}, u32[]{:S(2)}, u32[]{:S(2)}) collective-permute-start(bf16[256,512]{1,0:T(8,128)(2,1)S(1)} %add_blocks.5), channel_id=1, source_target_pairs={{0,8},{1,9},{2,10},{3,11},{4,12},{5,13},{6,14},{7,15},{8,0},{9,1},... | collective-permute-start | bytes 786440 | tf_op jit(solution)/shard_map/ppermute | solution.py:61
  60.8 2.8 %collective-permute-done.24.refs_2_ = bf16[256,512]{1,0:T(8,128)(2,1)S(1)} collective-permute-done((bf16[256,512]{1,0:T(8,128)(2,1)S(1)}, bf16[256,512]{1,0:T(8,128)(2,1)S(1)}, u32[]{:S(2)}, u32[]{:S(2)}) %collective-permute-start.24) | collective-permute-done | bytes 262176 | tf_op jit(solution)/shard_map/ppermute | solution.py:61
  63.6 1.2 %near_features.1 = (bf16[256,512]{1,0:T(8,128)(2,1)S(1)}, bf16[256,512]{1,0:T(8,128)(2,1)S(1)}) custom-call(bf16[256,2560]{1,0:T(8,128)(2,1)S(1)} %get-tuple-element.120.own, bf16[256,2560]{1,0:T(8,128)(2,1)S(1)} %collective-permute-done.3.sib, bf16[2048,512]{1,0:T(8,128)(2,1)S(1)} %fill_teacher.1.refs_4_.full), custom_call_target="tpu_custom_call" | custom-call | flops 1 | bytes 1 | tf_op jit(solution)/shard_map/near_features/pallas_call | solution.py:29
  64.9 0.6 collective-permute-start.28
  65.4 1.1 %collective-permute-done.22.refs_3_ = bf16[256,512]{1,0:T(8,128)(2,1)S(1)} collective-permute-done((bf16[256,512]{1,0:T(8,128)(2,1)S(1)}, bf16[256,512]{1,0:T(8,128)(2,1)S(1)}, u32[]{:S(2)}, u32[]{:S(2)}) %collective-permute-start.22) | collective-permute-done | bytes 262176 | tf_op jit(solution)/shard_map/ppermute | solution.py:61
  66.6 2.5 %collective-permute-done.25.refs_3_ = bf16[256,512]{1,0:T(8,128)(2,1)S(1)} collective-permute-done((bf16[256,512]{1,0:T(8,128)(2,1)S(1)}, bf16[256,512]{1,0:T(8,128)(2,1)S(1)}, u32[]{:S(2)}, u32[]{:S(2)}) %collective-permute-start.25) | collective-permute-done | bytes 262176 | tf_op jit(solution)/shard_map/ppermute | solution.py:61
  69.3 1.6 %collective-permute-start.30 = (bf16[128,512]{1,0:T(8,128)(2,1)S(1)}, bf16[128,512]{1,0:T(8,128)(2,1)S(1)}, u32[]{:S(2)}, u32[]{:S(2)}) collective-permute-start(bf16[128,512]{1,0:T(8,128)(2,1)S(1)} %get-tuple-element.127.refs_0_), channel_id=1, source_target_pairs={{0,1},{1,0},{2,3},{3,2},{4,5},{5,4},{6,7},{7,6},{8,9},{9,8},{10,11... | collective-permute-start | bytes 393224 | tf_op jit(solution)/shard_map/ppermute | solution.py:61
  71.2 1.7 %update_near.1 = (f32[128,2048]{1,0:T(8,128)}, f32[128,2048]{1,0:T(8,128)}, f32[128,2048]{1,0:T(8,128)}, f32[128,2048]{1,0:T(8,128)}) custom-call(bf16[128,512]{1,0:T(8,128)(2,1)S(1)} %get-tuple-element.127.refs_0_, bf16[128,512]{1,0:T(8,128)(2,1)S(1)} %collective-permute-done.27.refs_1_, f32[128,2048]{1,0:T(8,128)S(1)} %copy-done.2, ...), custom_call_target="tpu_custom_call" | custom-call | flops 1 | bytes 1 | tf_op jit(solution)/shard_map/update_near/pallas_call | solution.py:396
  72.9 1.1 %place_features.1 = bf16[256,2048]{1,0:T(8,128)(2,1)} custom-call(bf16[256,512]{1,0:T(8,128)(2,1)S(1)} %get-tuple-element.130.refs_0_, bf16[256,512]{1,0:T(8,128)(2,1)S(1)} %collective-permute-done.28.refs_1_, bf16[256,512]{1,0:T(8,128)(2,1)S(1)} %collective-permute-done.21.refs_2_, bf16[256,512]{1,0:T(8,128)(2,1)S(1)} %collective-permute-done.22.refs_3_), custom_call_target="tpu_custom_call" | custom-call | flops 1 | bytes 1 | tf_op jit(solution)/shard_map/place_features/pallas_call | solution.py:29
  73.9 1.7 %collective-permute-done.30.refs_0_ = bf16[128,512]{1,0:T(8,128)(2,1)S(1)} collective-permute-done((bf16[128,512]{1,0:T(8,128)(2,1)S(1)}, bf16[128,512]{1,0:T(8,128)(2,1)S(1)}, u32[]{:S(2)}, u32[]{:S(2)}) %collective-permute-start.30) | collective-permute-done | bytes 131104 | tf_op jit(solution)/shard_map/ppermute | solution.py:61
  75.6 1.3 %update_partner.1 = (f32[128,2048]{1,0:T(8,128)}, f32[128,2048]{1,0:T(8,128)}, f32[128,2048]{1,0:T(8,128)}, f32[128,2048]{1,0:T(8,128)}) custom-call(bf16[128,512]{1,0:T(8,128)(2,1)S(1)} %collective-permute-done.30.refs_0_, f32[128,2048]{1,0:T(8,128)S(1)} %copy-done.2, ...), custom_call_target="tpu_custom_call", output_to_operand_aliasing={{0}: (5, {}), {1}: (6, {}), {2}: (7, {}), {3}: (8, {})} | custom-call | flops 1 | bytes 1 | tf_op jit(solution)/shard_map/update_partner/pallas_call | solution.py:396
  76.9 0.6 collective-permute-done.29.refs_0_
  77.5 1.3 %update_diagonal.1 = (f32[128,2048]{1,0:T(8,128)}, f32[128,2048]{1,0:T(8,128)}, f32[128,2048]{1,0:T(8,128)}, f32[128,2048]{1,0:T(8,128)}) custom-call(bf16[128,512]{1,0:T(8,128)(2,1)S(1)} %collective-permute-done.29.refs_0_, f32[128,2048]{1,0:T(8,128)S(1)} %copy-done.2, ...), custom_call_target="tpu_custom_call", output_to_operand_aliasing={{0}: (5, {}), {1}: (6, {}), {2}: (7, {}), {3}: (8, {})} | custom-call | flops 1 | bytes 1 | tf_op jit(solution)/shard_map/update_diagonal/pallas_call | solution.py:396
  (52 shorter events, 2.7 us)
Async XLA Ops:
  0.6 1.2 %copy-start = (f32[128,2048]{1,0:T(8,128)S(1)}, f32[128,2048]{1,0:T(8,128)}, u32[]{:S(2)}) copy-start(f32[128,2048]{1,0:T(8,128)} %refs_4_.5) | copy-start | bytes 3145732
  1.9 1.2 %copy-start.5 = (bf16[256,2048]{1,0:T(8,128)(2,1)S(1)}, bf16[256,2048]{1,0:T(8,128)(2,1)}, u32[]{:S(2)}) copy-start(bf16[256,2048]{1,0:T(8,128)(2,1)} %p) | copy-start | bytes 3145732
  3.1 1.2 %copy-start.6 = (bf16[256,2048]{1,0:T(8,128)(2,1)S(1)}, bf16[256,2048]{1,0:T(8,128)(2,1)}, u32[]{:S(2)}) copy-start(bf16[256,2048]{1,0:T(8,128)(2,1)} %c.1) | copy-start | bytes 3145732
  4.5 8.5 %collective-permute-start.3 = (bf16[256,2560]{1,0:T(8,128)(2,1)S(1)}, bf16[256,2560]{1,0:T(8,128)(2,1)S(1)}, u32[]{:S(2)}, u32[]{:S(2)}) collective-permute-start(bf16[256,2560]{1,0:T(8,128)(2,1)S(1)} %get-tuple-element.120.own), channel_id=1, source_target_pairs={{0,2},{1,3},{2,0},{3,1},{4,6},{5,7},{6,4},{7,5},{8,10},{9,11},{10,... | collective-permute-start | bytes 3932168 | tf_op jit(solution)/shard_map/ppermute | solution.py:61
  5.1 3.5 %collective-permute-start.1 = (bf16[544,512]{1,0:T(8,128)(2,1)S(1)}, bf16[544,512]{1,0:T(8,128)(2,1)S(1)}, u32[]{:S(2)}, u32[]{:S(2)}) collective-permute-start(bf16[544,512]{1,0:T(8,128)(2,1)S(1)} %get-tuple-element.81), channel_id=1, source_target_pairs={{0,2},{1,3},{2,0},{3,1},{4,6},{5,7},{6,4},{7,5},{8,10},{9,11},{10,... | collective-permute-start | bytes 1671176 | tf_op jit(solution)/shard_map/ppermute | solution.py:61
  5.1 21.3 %collective-permute-start.7 = (bf16[256,1536]{1,0:T(8,128)(2,1)S(1)}, bf16[256,1536]{1,0:T(8,128)(2,1)S(1)}, u32[]{:S(2)}, u32[]{:S(2)}) collective-permute-start(bf16[256,1536]{1,0:T(8,128)(2,1)S(1)} %get-tuple-element.79), channel_id=1, source_target_pairs={{0,1},{1,0},{2,3},{3,2},{4,5},{5,4},{6,7},{7,6},{8,9},{9,8},{10,11... | collective-permute-start | bytes 2359304 | tf_op jit(solution)/shard_map/ppermute | solution.py:61
  8.6 9.6 %collective-permute-start.4 = (bf16[256,512]{1,0:T(8,128)(2,1)S(1)}, bf16[256,512]{1,0:T(8,128)(2,1)S(1)}, u32[]{:S(2)}, u32[]{:S(2)}) collective-permute-start(bf16[256,512]{1,0:T(8,128)(2,1)S(1)} %join_teacher.1.refs_0_), channel_id=1, source_target_pairs={{0,4},{1,5},{2,6},{3,7},{4,0},{5,1},{6,2},{7,3},{8,12},{9,13},{10,... | collective-permute-start | bytes 786440 | tf_op jit(solution)/shard_map/ppermute | solution.py:61
  11.5 9.5 %collective-permute-start.2 = (bf16[256,512]{1,0:T(8,128)(2,1)S(1)}, bf16[256,512]{1,0:T(8,128)(2,1)S(1)}, u32[]{:S(2)}, u32[]{:S(2)}) collective-permute-start(bf16[256,512]{1,0:T(8,128)(2,1)S(1)} %join_teacher.1.refs_0_), channel_id=1, source_target_pairs={{0,8},{1,9},{2,10},{3,11},{4,12},{5,13},{6,14},{7,15},{8,24},{9,25... | collective-permute-start | bytes 786440 | tf_op jit(solution)/shard_map/ppermute | solution.py:61
  18.2 14.7 %collective-permute-start.5 = (bf16[544,512]{1,0:T(8,128)(2,1)S(1)}, bf16[544,512]{1,0:T(8,128)(2,1)S(1)}, u32[]{:S(2)}, u32[]{:S(2)}) collective-permute-start(bf16[544,512]{1,0:T(8,128)(2,1)S(1)} %stack_teacher.1), channel_id=1, source_target_pairs={{0,16},{1,17},{2,18},{3,19},{4,20},{5,21},{6,22},{7,23},{8,0},{9,1... | collective-permute-start | bytes 1671176 | tf_op jit(solution)/shard_map/ppermute | solution.py:61
  21.0 7.2 %collective-permute-start.8 = (bf16[256,512]{1,0:T(8,128)(2,1)S(1)}, bf16[256,512]{1,0:T(8,128)(2,1)S(1)}, u32[]{:S(2)}, u32[]{:S(2)}) collective-permute-start(bf16[256,512]{1,0:T(8,128)(2,1)S(1)} %collective-permute-done.2.refs_2_), channel_id=1, source_target_pairs={{0,4},{1,5},{2,6},{3,7},{4,0},{5,1},{6,2},{7,3},{8,12},{9,13},{10,... | collective-permute-start | bytes 786440 | tf_op jit(solution)/shard_map/ppermute | solution.py:61
  22.5 10.2 %collective-permute-start.11 = (bf16[288,512]{1,0:T(8,128)(2,1)S(1)}, bf16[288,512]{1,0:T(8,128)(2,1)S(1)}, u32[]{:S(2)}, u32[]{:S(2)}) collective-permute-start(bf16[288,512]{1,0:T(8,128)(2,1)S(1)} %get-tuple-element.95), channel_id=1, source_target_pairs={{0,1},{1,0},{2,3},{3,2},{4,5},{5,4},{6,7},{7,6},{8,9},{9,8},{10,11... | collective-permute-start | bytes 884744 | tf_op jit(solution)/shard_map/ppermute | solution.py:61
  26.5 3.3 %collective-permute-start.10 = (bf16[256,512]{1,0:T(8,128)(2,1)S(1)}, bf16[256,512]{1,0:T(8,128)(2,1)S(1)}, u32[]{:S(2)}, u32[]{:S(2)}) collective-permute-start(bf16[256,512]{1,0:T(8,128)(2,1)S(1)} %get-tuple-element.88), channel_id=1, source_target_pairs={{0,2},{1,3},{2,0},{3,1},{4,6},{5,7},{6,4},{7,5},{8,10},{9,11},{10,... | collective-permute-start | bytes 786440 | tf_op jit(solution)/shard_map/ppermute | solution.py:61
  26.5 3.2 %collective-permute-start.9 = (bf16[256,512]{1,0:T(8,128)(2,1)S(1)}, bf16[256,512]{1,0:T(8,128)(2,1)S(1)}, u32[]{:S(2)}, u32[]{:S(2)}) collective-permute-start(bf16[256,512]{1,0:T(8,128)(2,1)S(1)} %get-tuple-element.112.par.refs_0_), channel_id=1, source_target_pairs={{0,2},{1,3},{2,0},{3,1},{4,6},{5,7},{6,4},{7,5},{8,10},{9,11},{10,... | collective-permute-start | bytes 786440 | tf_op jit(solution)/shard_map/ppermute | solution.py:61
  28.3 15.1 %collective-permute-start = (bf16[256,1024]{1,0:T(8,128)(2,1)S(1)}, bf16[256,1024]{1,0:T(8,128)(2,1)S(1)}, u32[]{:S(2)}, u32[]{:S(2)}) collective-permute-start(bf16[256,1024]{1,0:T(8,128)(2,1)S(1)} %get-tuple-element.78), channel_id=1, source_target_pairs={{0,1},{1,0},{2,3},{3,2},{4,5},{5,4},{6,7},{7,6},{8,9},{9,8},{10,11... | collective-permute-start | bytes 1572872 | tf_op jit(solution)/shard_map/ppermute | solution.py:61
  30.6 7.8 %collective-permute-start.13 = (bf16[272,512]{1,0:T(8,128)(2,1)S(1)}, bf16[272,512]{1,0:T(8,128)(2,1)S(1)}, u32[]{:S(2)}, u32[]{:S(2)}) collective-permute-start(bf16[272,512]{1,0:T(8,128)(2,1)S(1)} %get-tuple-element.100), channel_id=1, source_target_pairs={{0,4},{1,5},{2,6},{3,7},{4,0},{5,1},{6,2},{7,3},{8,12},{9,13},{10,... | collective-permute-start | bytes 835592 | tf_op jit(solution)/shard_map/ppermute | solution.py:61
  32.7 2.3 %collective-permute-start.12 = (bf16[256,512]{1,0:T(8,128)(2,1)S(1)}, bf16[256,512]{1,0:T(8,128)(2,1)S(1)}, u32[]{:S(2)}, u32[]{:S(2)}) collective-permute-start(bf16[256,512]{1,0:T(8,128)(2,1)S(1)} %take_block.1.par.refs_1_), channel_id=1, source_target_pairs={{0,2},{1,3},{2,0},{3,1},{4,6},{5,7},{6,4},{7,5},{8,10},{9,11},{10,... | collective-permute-start | bytes 786440 | tf_op jit(solution)/shard_map/ppermute | solution.py:61
  32.8 10.6 %collective-permute-start.6 = (bf16[256,512]{1,0:T(8,128)(2,1)S(1)}, bf16[256,512]{1,0:T(8,128)(2,1)S(1)}, u32[]{:S(2)}, u32[]{:S(2)}) collective-permute-start(bf16[256,512]{1,0:T(8,128)(2,1)S(1)} %collective-permute-done.2.refs_2_), channel_id=1, source_target_pairs={{0,8},{1,9},{2,10},{3,11},{4,12},{5,13},{6,14},{7,15},{8,24},{9,25... | collective-permute-start | bytes 786440 | tf_op jit(solution)/shard_map/ppermute | solution.py:61
  38.4 10.1 %collective-permute-start.17 = (bf16[256,512]{1,0:T(8,128)(2,1)S(1)}, bf16[256,512]{1,0:T(8,128)(2,1)S(1)}, u32[]{:S(2)}, u32[]{:S(2)}) collective-permute-start(bf16[256,512]{1,0:T(8,128)(2,1)S(1)} %add_blocks.3), channel_id=1, source_target_pairs={{0,8},{1,9},{2,10},{3,11},{4,12},{5,13},{6,14},{7,15},{8,0},{9,1},... | collective-permute-start | bytes 786440 | tf_op jit(solution)/shard_map/ppermute | solution.py:61
  40.3 8.3 %collective-permute-start.16 = (bf16[256,512]{1,0:T(8,128)(2,1)S(1)}, bf16[256,512]{1,0:T(8,128)(2,1)S(1)}, u32[]{:S(2)}, u32[]{:S(2)}) collective-permute-start(bf16[256,512]{1,0:T(8,128)(2,1)S(1)} %get-tuple-element.109), channel_id=1, source_target_pairs={{0,4},{1,5},{2,6},{3,7},{4,0},{5,1},{6,2},{7,3},{8,12},{9,13},{10,... | collective-permute-start | bytes 786440 | tf_op jit(solution)/shard_map/ppermute | solution.py:61
  43.5 2.4 %collective-permute-start.14 = (bf16[128,512]{1,0:T(8,128)(2,1)S(1)}, bf16[128,512]{1,0:T(8,128)(2,1)S(1)}, u32[]{:S(2)}, u32[]{:S(2)}) collective-permute-start(bf16[128,512]{1,0:T(8,128)(2,1)S(1)} %get-tuple-element.102), channel_id=1, source_target_pairs={{0,2},{1,3},{2,0},{3,1},{4,6},{5,7},{6,4},{7,5},{8,10},{9,11},{10,... | collective-permute-start | bytes 393224 | tf_op jit(solution)/shard_map/ppermute | solution.py:61
  43.5 2.3 %collective-permute-start.15 = (bf16[128,512]{1,0:T(8,128)(2,1)S(1)}, bf16[128,512]{1,0:T(8,128)(2,1)S(1)}, u32[]{:S(2)}, u32[]{:S(2)}) collective-permute-start(bf16[128,512]{1,0:T(8,128)(2,1)S(1)} %get-tuple-element.104), channel_id=1, source_target_pairs={{0,2},{1,3},{2,0},{3,1},{4,6},{5,7},{6,4},{7,5},{8,10},{9,11},{10,... | collective-permute-start | bytes 393224 | tf_op jit(solution)/shard_map/ppermute | solution.py:61
  44.0 9.6 %collective-permute-start.18 = (bf16[256,512]{1,0:T(8,128)(2,1)S(1)}, bf16[256,512]{1,0:T(8,128)(2,1)S(1)}, u32[]{:S(2)}, u32[]{:S(2)}) collective-permute-start(bf16[256,512]{1,0:T(8,128)(2,1)S(1)} %collective-permute-done.6.refs_4_), channel_id=1, source_target_pairs={{0,4},{1,5},{2,6},{3,7},{4,0},{5,1},{6,2},{7,3},{8,12},{9,13},{10,... | collective-permute-start | bytes 786440 | tf_op jit(solution)/shard_map/ppermute | solution.py:61
  46.7 9.4 %collective-permute-start.19 = (bf16[256,512]{1,0:T(8,128)(2,1)S(1)}, bf16[256,512]{1,0:T(8,128)(2,1)S(1)}, u32[]{:S(2)}, u32[]{:S(2)}) collective-permute-start(bf16[256,512]{1,0:T(8,128)(2,1)S(1)} %get-tuple-element.115.refs_3_.par), channel_id=1, source_target_pairs={{0,2},{1,3},{2,0},{3,1},{4,6},{5,7},{6,4},{7,5},{8,10},{9,11},{10,... | collective-permute-start | bytes 786440 | tf_op jit(solution)/shard_map/ppermute | solution.py:61
  46.8 12.6 %collective-permute-start.20 = (bf16[256,512]{1,0:T(8,128)(2,1)S(1)}, bf16[256,512]{1,0:T(8,128)(2,1)S(1)}, u32[]{:S(2)}, u32[]{:S(2)}) collective-permute-start(bf16[256,512]{1,0:T(8,128)(2,1)S(1)} %get-tuple-element.119), channel_id=1, source_target_pairs={{0,4},{1,5},{2,6},{3,7},{4,0},{5,1},{6,2},{7,3},{8,12},{9,13},{10,... | collective-permute-start | bytes 786440 | tf_op jit(solution)/shard_map/ppermute | solution.py:61
  48.7 14.9 %collective-permute-start.24 = (bf16[256,512]{1,0:T(8,128)(2,1)S(1)}, bf16[256,512]{1,0:T(8,128)(2,1)S(1)}, u32[]{:S(2)}, u32[]{:S(2)}) collective-permute-start(bf16[256,512]{1,0:T(8,128)(2,1)S(1)} %add_blocks.4), channel_id=1, source_target_pairs={{0,16},{1,17},{2,18},{3,19},{4,20},{5,21},{6,22},{7,23},{8,24},{9,... | collective-permute-start | bytes 786440 | tf_op jit(solution)/shard_map/ppermute | solution.py:61
  54.5 10.3 %collective-permute-start.21 = (bf16[256,512]{1,0:T(8,128)(2,1)S(1)}, bf16[256,512]{1,0:T(8,128)(2,1)S(1)}, u32[]{:S(2)}, u32[]{:S(2)}) collective-permute-start(bf16[256,512]{1,0:T(8,128)(2,1)S(1)} %far_features.2), channel_id=1, source_target_pairs={{0,1},{1,0},{2,3},{3,2},{4,5},{5,4},{6,7},{7,6},{8,9},{9,8},{10,11... | collective-permute-start | bytes 786440 | tf_op jit(solution)/shard_map/ppermute | solution.py:61
  57.7 8.9 %collective-permute-start.22 = (bf16[256,512]{1,0:T(8,128)(2,1)S(1)}, bf16[256,512]{1,0:T(8,128)(2,1)S(1)}, u32[]{:S(2)}, u32[]{:S(2)}) collective-permute-start(bf16[256,512]{1,0:T(8,128)(2,1)S(1)} %far_features.3), channel_id=1, source_target_pairs={{0,3},{1,2},{2,1},{3,0},{4,7},{5,6},{6,5},{7,4},{8,11},{9,10},{10,... | collective-permute-start | bytes 786440 | tf_op jit(solution)/shard_map/ppermute | solution.py:61
  57.8 8.8 %collective-permute-start.23 = (bf16[256,512]{1,0:T(8,128)(2,1)S(1)}, bf16[256,512]{1,0:T(8,128)(2,1)S(1)}, u32[]{:S(2)}, u32[]{:S(2)}) collective-permute-start(bf16[256,512]{1,0:T(8,128)(2,1)S(1)} %get-tuple-element.123), channel_id=1, source_target_pairs={{0,4},{1,5},{2,6},{3,7},{4,0},{5,1},{6,2},{7,3},{8,12},{9,13},{10,... | collective-permute-start | bytes 786440 | tf_op jit(solution)/shard_map/ppermute | solution.py:61
  59.4 9.7 %collective-permute-start.25 = (bf16[256,512]{1,0:T(8,128)(2,1)S(1)}, bf16[256,512]{1,0:T(8,128)(2,1)S(1)}, u32[]{:S(2)}, u32[]{:S(2)}) collective-permute-start(bf16[256,512]{1,0:T(8,128)(2,1)S(1)} %add_blocks.5), channel_id=1, source_target_pairs={{0,8},{1,9},{2,10},{3,11},{4,12},{5,13},{6,14},{7,15},{8,0},{9,1},... | collective-permute-start | bytes 786440 | tf_op jit(solution)/shard_map/ppermute | solution.py:61
  63.6 3.0 %collective-permute-start.26 = (bf16[240,512]{1,0:T(8,128)(2,1)S(1)}, bf16[240,512]{1,0:T(8,128)(2,1)S(1)}, u32[]{:S(2)}, u32[]{:S(2)}) collective-permute-start(bf16[240,512]{1,0:T(8,128)(2,1)S(1)} %get-tuple-element.125), channel_id=1, source_target_pairs={{0,2},{1,3},{2,0},{3,1},{4,6},{5,7},{6,4},{7,5},{8,10},{9,11},{10,... | collective-permute-start | bytes 737288 | tf_op jit(solution)/shard_map/ppermute | solution.py:61
  63.6 7.6 %copy-start.2 = (f32[128,2048]{1,0:T(8,128)S(1)}, f32[128,2048]{1,0:T(8,128)}, u32[]{:S(2)}) copy-start(f32[128,2048]{1,0:T(8,128)} %refs_1_.3) | copy-start | bytes 3145732
  63.6 7.6 %copy-start.3 = (f32[128,2048]{1,0:T(8,128)S(1)}, f32[128,2048]{1,0:T(8,128)}, u32[]{:S(2)}) copy-start(f32[128,2048]{1,0:T(8,128)} %refs_2_.5) | copy-start | bytes 3145732
  63.6 7.6 %copy-start.4 = (f32[128,2048]{1,0:T(8,128)S(1)}, f32[128,2048]{1,0:T(8,128)}, u32[]{:S(2)}) copy-start(f32[128,2048]{1,0:T(8,128)} %refs_3_.5) | copy-start | bytes 3145732
  64.8 6.3 %copy-start.1 = (f32[128,2048]{1,0:T(8,128)S(1)}, f32[128,2048]{1,0:T(8,128)}, u32[]{:S(2)}) copy-start(f32[128,2048]{1,0:T(8,128)} %refs_4_.5) | copy-start | bytes 3145732
  64.9 8.0 %collective-permute-start.28 = (bf16[256,512]{1,0:T(8,128)(2,1)S(1)}, bf16[256,512]{1,0:T(8,128)(2,1)S(1)}, u32[]{:S(2)}, u32[]{:S(2)}) collective-permute-start(bf16[256,512]{1,0:T(8,128)(2,1)S(1)} %get-tuple-element.131), channel_id=1, source_target_pairs={{0,2},{1,3},{2,0},{3,1},{4,6},{5,7},{6,4},{7,5},{8,10},{9,11},{10,... | collective-permute-start | bytes 786440 | tf_op jit(solution)/shard_map/ppermute | solution.py:61
  69.2 1.9 %collective-permute-start.27 = (bf16[128,512]{1,0:T(8,128)(2,1)S(1)}, bf16[128,512]{1,0:T(8,128)(2,1)S(1)}, u32[]{:S(2)}, u32[]{:S(2)}) collective-permute-start(bf16[128,512]{1,0:T(8,128)(2,1)S(1)} %get-tuple-element.128), channel_id=1, source_target_pairs={{0,2},{1,3},{2,0},{3,1},{4,6},{5,7},{6,4},{7,5},{8,10},{9,11},{10,... | collective-permute-start | bytes 393224 | tf_op jit(solution)/shard_map/ppermute | solution.py:61
  69.3 6.3 %collective-permute-start.30 = (bf16[128,512]{1,0:T(8,128)(2,1)S(1)}, bf16[128,512]{1,0:T(8,128)(2,1)S(1)}, u32[]{:S(2)}, u32[]{:S(2)}) collective-permute-start(bf16[128,512]{1,0:T(8,128)(2,1)S(1)} %get-tuple-element.127.refs_0_), channel_id=1, source_target_pairs={{0,1},{1,0},{2,3},{3,2},{4,5},{5,4},{6,7},{7,6},{8,9},{9,8},{10,11... | collective-permute-start | bytes 393224 | tf_op jit(solution)/shard_map/ppermute | solution.py:61
  70.9 6.6 %collective-permute-start.29 = (bf16[128,512]{1,0:T(8,128)(2,1)S(1)}, bf16[128,512]{1,0:T(8,128)(2,1)S(1)}, u32[]{:S(2)}, u32[]{:S(2)}) collective-permute-start(bf16[128,512]{1,0:T(8,128)(2,1)S(1)} %get-tuple-element.128), channel_id=1, source_target_pairs={{0,3},{1,2},{2,1},{3,0},{4,7},{5,6},{6,5},{7,4},{8,11},{9,10},{10,... | collective-permute-start | bytes 393224 | tf_op jit(solution)/shard_map/ppermute | solution.py:61

commit v5 on v4

--- a/solution.py
+++ b/solution.py
@@ -198,7 +198,7 @@
                 "gradient_block",
                 terms_body(k),
                 [((2 * rows, part), f32)]
-                + [((2 * rows + extra * (k == 0), part), bf16)] * (ny - 1),
+                + [((2 * rows + (2 * extra, extra, 0, 0)[k], part), bf16)] * (ny - 1),
                 [near_own, near_sib, far_par[k], far_dia[k], c_own, c_par, c_dia],
                 scratch=[pltpu.VMEM((span, part), f32)],
             )
@@ -266,13 +266,6 @@
         def block_sum(dz, *parts, more=0):
             return add([terms[dz][0], *moved_y[dz], *parts], bf16, more)
 
-        w_same, w_other = run(
-            "cast_teacher",
-            cast_body,
-            [((rows, part), bf16), ((4 * rows + 2 * extra, part), bf16)],
-            [teacher],
-        )
-        w_sib = start(w_other, sibling)
         first, near_own, c_own, second, third, mark = run(
             "cut_tokens",
             cut_body,
@@ -285,6 +278,13 @@
             ],
             [patches, cotangent],
         )
+        w_same, w_other = run(
+            "cast_teacher",
+            cast_body,
+            [((rows, part), bf16), ((4 * rows + 2 * extra, part), bf16)],
+            [after(teacher, first)],
+        )
+        w_sib = start(w_other, sibling)
         message = start(first, partner)
         near_sib = start(near_own, sibling)
         (w_line[0],) = run(
@@ -299,8 +299,8 @@
             [((ny * 2 * rows + 2 * extra, part), bf16)],
             [after(w_line[0], near_sib), *w_side[0]],
         )
-        turn = start(turn, along_z(-1))
-        w_line[2] = start(w_line[3], along_z(1), turn)
+        w_line[2] = start(w_line[3], along_z(1))
+        turn = start(turn, along_z(-1), w_line[2])
         block = start(second, partner)
         c_other, c_par, far_par[0] = run(
             "split_message",
@@ -315,7 +315,6 @@
         both = start(third, partner)
         (far_par[1],) = run("take_block", first_body, [((tokens, span), bf16)], [block])
         far_dia[1] = start(far_par[1], sibling)
-        wait(turn)
         gradient_block(1)
         onward = block_sum(3)
         teacher_y(2, onward)
@@ -324,7 +323,7 @@
             "take_blocks",
             take_body,
             [((tokens // 2, span), bf16)] * 2 + [((tokens, span), bf16)] * 2,
-            [after(both, w_line[2])],
+            [after(both, turn)],
         )
         pieces = [start(piece, sibling) for piece in pieces]
         (far_dia[2],) = run("join_pieces", pieces_body, [((tokens, span), bf16)], pieces)

time: 79.1 us -> 77.7 us (0.982)
  starting transfers between devices: 36.3 us -> 31.8 us
  waiting for transfers between devices: 25.8 us -> 30.1 us
  local copies, waits for them, and re-layouts: 3.63 us -> 2.55 us
    ppermute x31, starting transfers between devices: 36.3 us -> 31.8 us  [send(): return lax.ppermute(value, ('fsdp', 'rep'), perm)]
    ppermute x31, waiting for transfers between devices: 25.8 us -> 30.1 us  [send(): return lax.ppermute(value, ('fsdp', 'rep'), perm)]
    unnamed x14 -> x12, local copies, waits for them, and re-layouts: 3.63 us -> 2.55 us
  transfers between devices with their start and end apart: 31 -> 31, of which waited for: 14 -> 15; matrix products, arithmetic and copies ran while one was open for 0% -> 0% of each run, Pallas kernels for 14% -> 14%
where the time goes in v5:
time: 77.7 us; the launch traced here: 77.5 us
  starting transfers between devices  31.8 us (41%)
  waiting for transfers between devices  30.1 us (39%)
  Pallas kernels  12.2 us (16%)
  local copies, waits for them, and re-layouts  2.55 us (3%)
  between operations  0.89 us (1%)
    ppermute x31, starting transfers between devices, send(): return lax.ppermute(value, ('fsdp', 'rep'), perm)  31.8 us
    ppermute x31, waiting for transfers between devices, send(): return lax.ppermute(value, ('fsdp', 'rep'), perm)  30.1 us
    pallas_call x21, Pallas kernels, call(): pl.pallas_call(body, out_shape=shapes, in_specs=[VMEM] * len(inputs), out...  8.02 us
    pallas_call x3, Pallas kernels, update(): pl.pallas_call(update_body(quarters), out_shape=[jax.ShapeDtypeStruct((ro...  4.22 us
    unnamed x12, local copies, waits for them, and re-layouts  2.55 us
  transfers between devices with their start and end apart: 31, of which 15 were waited for; matrix products, arithmetic and copies ran while one was open for 0% of the time, Pallas kernels for 14%

profile of v5, /device:TPU:0, one launch (start us, length us, event | category | flops | bytes accessed | tf_op | source)
XLA Modules:
  0.0 77.5 jit_solution(15513866567492948106)
XLA Ops:
  0.7 1.3 %copy-done.4 = bf16[256,2048]{1,0:T(8,128)(2,1)S(1)} copy-done((bf16[256,2048]{1,0:T(8,128)(2,1)S(1)}, bf16[256,2048]{1,0:T(8,128)(2,1)}, u32[]{:S(2)}) %copy-start.4) | copy-done | bytes 1048600
  2.0 1.2 %copy-done.5 = bf16[256,2048]{1,0:T(8,128)(2,1)S(1)} copy-done((bf16[256,2048]{1,0:T(8,128)(2,1)S(1)}, bf16[256,2048]{1,0:T(8,128)(2,1)}, u32[]{:S(2)}) %copy-start.5) | copy-done | bytes 1048600
  3.4 0.5 collective-permute-start.2
  4.1 2.9 %collective-permute-start.7 = (bf16[256,1536]{1,0:T(8,128)(2,1)S(1)}, bf16[256,1536]{1,0:T(8,128)(2,1)S(1)}, u32[]{:S(2)}, u32[]{:S(2)}) collective-permute-start(bf16[256,1536]{1,0:T(8,128)(2,1)S(1)} %get-tuple-element.77), channel_id=1, source_target_pairs={{0,1},{1,0},{2,3},{3,2},{4,5},{5,4},{6,7},{7,6},{8,9},{9,8},{10,11... | collective-permute-start | bytes 2359304 | tf_op jit(solution)/shard_map/ppermute | solution.py:61
  7.1 0.3 collective-permute-done.1.sib
  7.4 3.0 %collective-permute-start.4 = (bf16[256,512]{1,0:T(8,128)(2,1)S(1)}, bf16[256,512]{1,0:T(8,128)(2,1)S(1)}, u32[]{:S(2)}, u32[]{:S(2)}) collective-permute-start(bf16[256,512]{1,0:T(8,128)(2,1)S(1)} %join_teacher.1.refs_0_), channel_id=1, source_target_pairs={{0,8},{1,9},{2,10},{3,11},{4,12},{5,13},{6,14},{7,15},{8,24},{9,25... | collective-permute-start | bytes 786440 | tf_op jit(solution)/shard_map/ppermute | solution.py:61
  10.4 1.5 %collective-permute-start.3 = (bf16[256,512]{1,0:T(8,128)(2,1)S(1)}, bf16[256,512]{1,0:T(8,128)(2,1)S(1)}, u32[]{:S(2)}, u32[]{:S(2)}) collective-permute-start(bf16[256,512]{1,0:T(8,128)(2,1)S(1)} %join_teacher.1.refs_0_), channel_id=1, source_target_pairs={{0,4},{1,5},{2,6},{3,7},{4,0},{5,1},{6,2},{7,3},{8,12},{9,13},{10,... | collective-permute-start | bytes 786440 | tf_op jit(solution)/shard_map/ppermute | solution.py:61
  11.9 6.1 %collective-permute-done.4.refs_2_ = bf16[256,512]{1,0:T(8,128)(2,1)S(1)} collective-permute-done((bf16[256,512]{1,0:T(8,128)(2,1)S(1)}, bf16[256,512]{1,0:T(8,128)(2,1)S(1)}, u32[]{:S(2)}, u32[]{:S(2)}) %collective-permute-start.4) | collective-permute-done | bytes 262176 | tf_op jit(solution)/shard_map/ppermute | solution.py:61
  18.0 0.8 %collective-permute-start.5 = (bf16[256,512]{1,0:T(8,128)(2,1)S(1)}, bf16[256,512]{1,0:T(8,128)(2,1)S(1)}, u32[]{:S(2)}, u32[]{:S(2)}) collective-permute-start(bf16[256,512]{1,0:T(8,128)(2,1)S(1)} %collective-permute-done.4.refs_2_), channel_id=1, source_target_pairs={{0,8},{1,9},{2,10},{3,11},{4,12},{5,13},{6,14},{7,15},{8,24},{9,25... | collective-permute-start | bytes 786440 | tf_op jit(solution)/shard_map/ppermute | solution.py:61
  18.9 1.5 %collective-permute-start.8 = (bf16[256,512]{1,0:T(8,128)(2,1)S(1)}, bf16[256,512]{1,0:T(8,128)(2,1)S(1)}, u32[]{:S(2)}, u32[]{:S(2)}) collective-permute-start(bf16[256,512]{1,0:T(8,128)(2,1)S(1)} %collective-permute-done.4.refs_2_), channel_id=1, source_target_pairs={{0,4},{1,5},{2,6},{3,7},{4,0},{5,1},{6,2},{7,3},{8,12},{9,13},{10,... | collective-permute-start | bytes 786440 | tf_op jit(solution)/shard_map/ppermute | solution.py:61
  20.4 1.5 %collective-permute-start.11 = (bf16[288,512]{1,0:T(8,128)(2,1)S(1)}, bf16[288,512]{1,0:T(8,128)(2,1)S(1)}, u32[]{:S(2)}, u32[]{:S(2)}) collective-permute-start(bf16[288,512]{1,0:T(8,128)(2,1)S(1)} %get-tuple-element.95), channel_id=1, source_target_pairs={{0,1},{1,0},{2,3},{3,2},{4,5},{5,4},{6,7},{7,6},{8,9},{9,8},{10,11... | collective-permute-start | bytes 884744 | tf_op jit(solution)/shard_map/ppermute | solution.py:61
  21.9 3.4 %collective-permute-done.7.message = bf16[256,1536]{1,0:T(8,128)(2,1)S(1)} collective-permute-done((bf16[256,1536]{1,0:T(8,128)(2,1)S(1)}, bf16[256,1536]{1,0:T(8,128)(2,1)S(1)}, u32[]{:S(2)}, u32[]{:S(2)}) %collective-permute-start.7) | collective-permute-done | bytes 786464 | tf_op jit(solution)/shard_map/ppermute | solution.py:61
  25.5 0.5 collective-permute-start.9
  26.0 0.8 collective-permute-done.5.refs_4_
  26.8 2.4 %collective-permute-start.6 = (bf16[544,512]{1,0:T(8,128)(2,1)S(1)}, bf16[544,512]{1,0:T(8,128)(2,1)S(1)}, u32[]{:S(2)}, u32[]{:S(2)}) collective-permute-start(bf16[544,512]{1,0:T(8,128)(2,1)S(1)} %stack_teacher.1), channel_id=1, source_target_pairs={{0,16},{1,17},{2,18},{3,19},{4,20},{5,21},{6,22},{7,23},{8,0},{9,1... | collective-permute-start | bytes 1671176 | tf_op jit(solution)/shard_map/ppermute | solution.py:61
  29.2 1.5 %collective-permute-start = (bf16[256,1024]{1,0:T(8,128)(2,1)S(1)}, bf16[256,1024]{1,0:T(8,128)(2,1)S(1)}, u32[]{:S(2)}, u32[]{:S(2)}) collective-permute-start(bf16[256,1024]{1,0:T(8,128)(2,1)S(1)} %get-tuple-element.76), channel_id=1, source_target_pairs={{0,1},{1,0},{2,3},{3,2},{4,5},{5,4},{6,7},{7,6},{8,9},{9,8},{10,11... | collective-permute-start | bytes 1572872 | tf_op jit(solution)/shard_map/ppermute | solution.py:61
  30.7 0.8 %gradient_block.4 = (f32[256,512]{1,0:T(8,128)S(1)}, bf16[288,512]{1,0:T(8,128)(2,1)S(1)}) custom-call(bf16[256,2560]{1,0:T(8,128)(2,1)S(1)} %get-tuple-element.120.own, bf16[256,2560]{1,0:T(8,128)(2,1)S(1)} %collective-permute-done.2.sib, bf16[256,512]{1,0:T(8,128)(2,1)S(1)} %get-tuple-element.112.par.refs_0_, ...), custom_call_target="tpu_custom_call" | custom-call | flops 1 | bytes 1 | tf_op jit(solution)/shard_map/gradient_block/pallas_call | solution.py:29
  31.5 1.6 %collective-permute-start.13 = (bf16[288,512]{1,0:T(8,128)(2,1)S(1)}, bf16[288,512]{1,0:T(8,128)(2,1)S(1)}, u32[]{:S(2)}, u32[]{:S(2)}) collective-permute-start(bf16[288,512]{1,0:T(8,128)(2,1)S(1)} %get-tuple-element.100), channel_id=1, source_target_pairs={{0,4},{1,5},{2,6},{3,7},{4,0},{5,1},{6,2},{7,3},{8,12},{9,13},{10,... | collective-permute-start | bytes 884744 | tf_op jit(solution)/shard_map/ppermute | solution.py:61
  33.2 1.5 %collective-permute-done.12.dia.refs_1_ = bf16[256,512]{1,0:T(8,128)(2,1)S(1)} collective-permute-done((bf16[256,512]{1,0:T(8,128)(2,1)S(1)}, bf16[256,512]{1,0:T(8,128)(2,1)S(1)}, u32[]{:S(2)}, u32[]{:S(2)}) %collective-permute-start.12) | collective-permute-done | bytes 262176 | tf_op jit(solution)/shard_map/ppermute | solution.py:61
  34.7 0.8 %gradient_block.5 = (f32[256,512]{1,0:T(8,128)S(1)}, bf16[272,512]{1,0:T(8,128)(2,1)S(1)}) custom-call(bf16[256,2560]{1,0:T(8,128)(2,1)S(1)} %get-tuple-element.120.own, bf16[256,2560]{1,0:T(8,128)(2,1)S(1)} %collective-permute-done.2.sib, bf16[256,512]{1,0:T(8,128)(2,1)S(1)} %take_block.1.par.refs_1_, ...), custom_call_target="tpu_custom_call" | custom-call | flops 1 | bytes 1 | tf_op jit(solution)/shard_map/gradient_block/pallas_call | solution.py:29
  35.6 0.6 collective-permute-start.16
  36.2 5.4 %collective-permute-done.13.refs_1_ = bf16[288,512]{1,0:T(8,128)(2,1)S(1)} collective-permute-done((bf16[288,512]{1,0:T(8,128)(2,1)S(1)}, bf16[288,512]{1,0:T(8,128)(2,1)S(1)}, u32[]{:S(2)}, u32[]{:S(2)}) %collective-permute-start.13) | collective-permute-done | bytes 294944 | tf_op jit(solution)/shard_map/ppermute | solution.py:61
  41.7 1.1 %collective-permute-done.message = bf16[256,1024]{1,0:T(8,128)(2,1)S(1)} collective-permute-done((bf16[256,1024]{1,0:T(8,128)(2,1)S(1)}, bf16[256,1024]{1,0:T(8,128)(2,1)S(1)}, u32[]{:S(2)}, u32[]{:S(2)}) %collective-permute-start) | collective-permute-done | bytes 524320 | tf_op jit(solution)/shard_map/ppermute | solution.py:61
  43.0 0.5 collective-permute-start.15
  43.5 1.5 %collective-permute-start.18 = (bf16[256,512]{1,0:T(8,128)(2,1)S(1)}, bf16[256,512]{1,0:T(8,128)(2,1)S(1)}, u32[]{:S(2)}, u32[]{:S(2)}) collective-permute-start(bf16[256,512]{1,0:T(8,128)(2,1)S(1)} %collective-permute-done.5.refs_4_), channel_id=1, source_target_pairs={{0,4},{1,5},{2,6},{3,7},{4,0},{5,1},{6,2},{7,3},{8,12},{9,13},{10,... | collective-permute-start | bytes 786440 | tf_op jit(solution)/shard_map/ppermute | solution.py:61
  45.0 0.8 %gradient_block.6 = (f32[256,512]{1,0:T(8,128)S(1)}, bf16[256,512]{1,0:T(8,128)(2,1)S(1)}) custom-call(bf16[256,2560]{1,0:T(8,128)(2,1)S(1)} %get-tuple-element.120.own, bf16[256,2560]{1,0:T(8,128)(2,1)S(1)} %collective-permute-done.2.sib, bf16[256,512]{1,0:T(8,128)(2,1)S(1)} %get-tuple-element.106.par.refs_2_, bf16[256,512]{1,0:T(8,128)(2,1)S(1)} %join_pieces.1.dia.refs_2_, ...), custom_call_target="tpu_custom_call" | custom-call | flops 1 | bytes 1 | tf_op jit(solution)/shard_map/gradient_block/pallas_call | solution.py:29
  45.9 1.3 %collective-permute-start.20 = (bf16[256,512]{1,0:T(8,128)(2,1)S(1)}, bf16[256,512]{1,0:T(8,128)(2,1)S(1)}, u32[]{:S(2)}, u32[]{:S(2)}) collective-permute-start(bf16[256,512]{1,0:T(8,128)(2,1)S(1)} %get-tuple-element.119), channel_id=1, source_target_pairs={{0,4},{1,5},{2,6},{3,7},{4,0},{5,1},{6,2},{7,3},{8,12},{9,13},{10,... | collective-permute-start | bytes 786440 | tf_op jit(solution)/shard_map/ppermute | solution.py:61
  47.3 0.8 collective-permute-done.17.refs_2_
  48.1 2.0 %collective-permute-start.24 = (bf16[256,512]{1,0:T(8,128)(2,1)S(1)}, bf16[256,512]{1,0:T(8,128)(2,1)S(1)}, u32[]{:S(2)}, u32[]{:S(2)}) collective-permute-start(bf16[256,512]{1,0:T(8,128)(2,1)S(1)} %add_blocks.4), channel_id=1, source_target_pairs={{0,16},{1,17},{2,18},{3,19},{4,20},{5,21},{6,22},{7,23},{8,24},{9,... | collective-permute-start | bytes 786440 | tf_op jit(solution)/shard_map/ppermute | solution.py:61
  50.2 2.5 %collective-permute-done.18.refs_5_ = bf16[256,512]{1,0:T(8,128)(2,1)S(1)} collective-permute-done((bf16[256,512]{1,0:T(8,128)(2,1)S(1)}, bf16[256,512]{1,0:T(8,128)(2,1)S(1)}, u32[]{:S(2)}, u32[]{:S(2)}) %collective-permute-start.18) | collective-permute-done | bytes 262176 | tf_op jit(solution)/shard_map/ppermute | solution.py:61
  52.8 0.7 far_features.2
  53.5 1.6 %collective-permute-start.21 = (bf16[256,512]{1,0:T(8,128)(2,1)S(1)}, bf16[256,512]{1,0:T(8,128)(2,1)S(1)}, u32[]{:S(2)}, u32[]{:S(2)}) collective-permute-start(bf16[256,512]{1,0:T(8,128)(2,1)S(1)} %far_features.2), channel_id=1, source_target_pairs={{0,1},{1,0},{2,3},{3,2},{4,5},{5,4},{6,7},{7,6},{8,9},{9,8},{10,11... | collective-permute-start | bytes 786440 | tf_op jit(solution)/shard_map/ppermute | solution.py:61
  55.1 0.8 %gradient_block.7 = (f32[256,512]{1,0:T(8,128)S(1)}, bf16[256,512]{1,0:T(8,128)(2,1)S(1)}) custom-call(bf16[256,2560]{1,0:T(8,128)(2,1)S(1)} %get-tuple-element.120.own, bf16[256,2560]{1,0:T(8,128)(2,1)S(1)} %collective-permute-done.2.sib, bf16[256,512]{1,0:T(8,128)(2,1)S(1)} %get-tuple-element.115.refs_3_.par, ...), custom_call_target="tpu_custom_call" | custom-call | flops 1 | bytes 1 | tf_op jit(solution)/shard_map/gradient_block/pallas_call | solution.py:29
  55.9 0.7 far_features.3
  56.7 1.6 %collective-permute-start.23 = (bf16[256,512]{1,0:T(8,128)(2,1)S(1)}, bf16[256,512]{1,0:T(8,128)(2,1)S(1)}, u32[]{:S(2)}, u32[]{:S(2)}) collective-permute-start(bf16[256,512]{1,0:T(8,128)(2,1)S(1)} %get-tuple-element.123), channel_id=1, source_target_pairs={{0,4},{1,5},{2,6},{3,7},{4,0},{5,1},{6,2},{7,3},{8,12},{9,13},{10,... | collective-permute-start | bytes 786440 | tf_op jit(solution)/shard_map/ppermute | solution.py:61
  58.3 1.8 %collective-permute-start.25 = (bf16[256,512]{1,0:T(8,128)(2,1)S(1)}, bf16[256,512]{1,0:T(8,128)(2,1)S(1)}, u32[]{:S(2)}, u32[]{:S(2)}) collective-permute-start(bf16[256,512]{1,0:T(8,128)(2,1)S(1)} %add_blocks.5), channel_id=1, source_target_pairs={{0,8},{1,9},{2,10},{3,11},{4,12},{5,13},{6,14},{7,15},{8,0},{9,1},... | collective-permute-start | bytes 786440 | tf_op jit(solution)/shard_map/ppermute | solution.py:61
  60.2 2.1 %collective-permute-done.24.refs_2_ = bf16[256,512]{1,0:T(8,128)(2,1)S(1)} collective-permute-done((bf16[256,512]{1,0:T(8,128)(2,1)S(1)}, bf16[256,512]{1,0:T(8,128)(2,1)S(1)}, u32[]{:S(2)}, u32[]{:S(2)}) %collective-permute-start.24) | collective-permute-done | bytes 262176 | tf_op jit(solution)/shard_map/ppermute | solution.py:61
  62.3 1.2 %near_features.1 = (bf16[256,512]{1,0:T(8,128)(2,1)S(1)}, bf16[256,512]{1,0:T(8,128)(2,1)S(1)}) custom-call(bf16[256,2560]{1,0:T(8,128)(2,1)S(1)} %get-tuple-element.120.own, bf16[256,2560]{1,0:T(8,128)(2,1)S(1)} %collective-permute-done.2.sib, bf16[2048,512]{1,0:T(8,128)(2,1)S(1)} %fill_teacher.1.refs_4_.full), custom_call_target="tpu_custom_call" | custom-call | flops 1 | bytes 1 | tf_op jit(solution)/shard_map/near_features/pallas_call | solution.py:29
  63.5 0.6 collective-permute-start.28
  64.1 1.3 %collective-permute-done.22.refs_3_ = bf16[256,512]{1,0:T(8,128)(2,1)S(1)} collective-permute-done((bf16[256,512]{1,0:T(8,128)(2,1)S(1)}, bf16[256,512]{1,0:T(8,128)(2,1)S(1)}, u32[]{:S(2)}, u32[]{:S(2)}) %collective-permute-start.22) | collective-permute-done | bytes 262176 | tf_op jit(solution)/shard_map/ppermute | solution.py:61
  65.5 2.2 %collective-permute-done.25.refs_3_ = bf16[256,512]{1,0:T(8,128)(2,1)S(1)} collective-permute-done((bf16[256,512]{1,0:T(8,128)(2,1)S(1)}, bf16[256,512]{1,0:T(8,128)(2,1)S(1)}, u32[]{:S(2)}, u32[]{:S(2)}) %collective-permute-start.25) | collective-permute-done | bytes 262176 | tf_op jit(solution)/shard_map/ppermute | solution.py:61
  68.0 1.6 %collective-permute-start.30 = (bf16[128,512]{1,0:T(8,128)(2,1)S(1)}, bf16[128,512]{1,0:T(8,128)(2,1)S(1)}, u32[]{:S(2)}, u32[]{:S(2)}) collective-permute-start(bf16[128,512]{1,0:T(8,128)(2,1)S(1)} %get-tuple-element.127.refs_0_), channel_id=1, source_target_pairs={{0,1},{1,0},{2,3},{3,2},{4,5},{5,4},{6,7},{7,6},{8,9},{9,8},{10,11... | collective-permute-start | bytes 393224 | tf_op jit(solution)/shard_map/ppermute | solution.py:61
  69.9 1.7 %update_near.1 = (f32[128,2048]{1,0:T(8,128)}, f32[128,2048]{1,0:T(8,128)}, f32[128,2048]{1,0:T(8,128)}, f32[128,2048]{1,0:T(8,128)}) custom-call(bf16[128,512]{1,0:T(8,128)(2,1)S(1)} %get-tuple-element.127.refs_0_, bf16[128,512]{1,0:T(8,128)(2,1)S(1)} %collective-permute-done.27.refs_1_, f32[128,2048]{1,0:T(8,128)S(1)} %copy-done.1, ...), custom_call_target="tpu_custom_call" | custom-call | flops 1 | bytes 1 | tf_op jit(solution)/shard_map/update_near/pallas_call | solution.py:395
  71.5 1.1 %place_features.1 = bf16[256,2048]{1,0:T(8,128)(2,1)} custom-call(bf16[256,512]{1,0:T(8,128)(2,1)S(1)} %get-tuple-element.130.refs_0_, bf16[256,512]{1,0:T(8,128)(2,1)S(1)} %collective-permute-done.28.refs_1_, bf16[256,512]{1,0:T(8,128)(2,1)S(1)} %collective-permute-done.21.refs_2_, bf16[256,512]{1,0:T(8,128)(2,1)S(1)} %collective-permute-done.22.refs_3_), custom_call_target="tpu_custom_call" | custom-call | flops 1 | bytes 1 | tf_op jit(solution)/shard_map/place_features/pallas_call | solution.py:29
  72.6 1.7 %collective-permute-done.30.refs_0_ = bf16[128,512]{1,0:T(8,128)(2,1)S(1)} collective-permute-done((bf16[128,512]{1,0:T(8,128)(2,1)S(1)}, bf16[128,512]{1,0:T(8,128)(2,1)S(1)}, u32[]{:S(2)}, u32[]{:S(2)}) %collective-permute-start.30) | collective-permute-done | bytes 131104 | tf_op jit(solution)/shard_map/ppermute | solution.py:61
  74.3 1.3 %update_partner.1 = (f32[128,2048]{1,0:T(8,128)}, f32[128,2048]{1,0:T(8,128)}, f32[128,2048]{1,0:T(8,128)}, f32[128,2048]{1,0:T(8,128)}) custom-call(bf16[128,512]{1,0:T(8,128)(2,1)S(1)} %collective-permute-done.30.refs_0_, f32[128,2048]{1,0:T(8,128)S(1)} %copy-done.1, ...), custom_call_target="tpu_custom_call", output_to_operand_aliasing={{0}: (5, {}), {1}: (6, {}), {2}: (7, {}), {3}: (8, {})} | custom-call | flops 1 | bytes 1 | tf_op jit(solution)/shard_map/update_partner/pallas_call | solution.py:395
  75.6 0.6 collective-permute-done.29.refs_0_
  76.2 1.3 %update_diagonal.1 = (f32[128,2048]{1,0:T(8,128)}, f32[128,2048]{1,0:T(8,128)}, f32[128,2048]{1,0:T(8,128)}, f32[128,2048]{1,0:T(8,128)}) custom-call(bf16[128,512]{1,0:T(8,128)(2,1)S(1)} %collective-permute-done.29.refs_0_, f32[128,2048]{1,0:T(8,128)S(1)} %copy-done.1, ...), custom_call_target="tpu_custom_call", output_to_operand_aliasing={{0}: (5, {}), {1}: (6, {}), {2}: (7, {}), {3}: (8, {})} | custom-call | flops 1 | bytes 1 | tf_op jit(solution)/shard_map/update_diagonal/pallas_call | solution.py:395
  (50 shorter events, 2.1 us)
Async XLA Ops:
  0.6 3.3 %copy-start = (f32[128,2048]{1,0:T(8,128)S(1)}, f32[128,2048]{1,0:T(8,128)}, u32[]{:S(2)}) copy-start(f32[128,2048]{1,0:T(8,128)} %refs_4_.5) | copy-start | bytes 3145732
  0.6 1.3 %copy-start.4 = (bf16[256,2048]{1,0:T(8,128)(2,1)S(1)}, bf16[256,2048]{1,0:T(8,128)(2,1)}, u32[]{:S(2)}) copy-start(bf16[256,2048]{1,0:T(8,128)(2,1)} %p.1) | copy-start | bytes 3145732
  2.0 1.2 %copy-start.5 = (bf16[256,2048]{1,0:T(8,128)(2,1)S(1)}, bf16[256,2048]{1,0:T(8,128)(2,1)}, u32[]{:S(2)}) copy-start(bf16[256,2048]{1,0:T(8,128)(2,1)} %c.1) | copy-start | bytes 3145732
  3.4 18.5 %collective-permute-start.2 = (bf16[256,2560]{1,0:T(8,128)(2,1)S(1)}, bf16[256,2560]{1,0:T(8,128)(2,1)S(1)}, u32[]{:S(2)}, u32[]{:S(2)}) collective-permute-start(bf16[256,2560]{1,0:T(8,128)(2,1)S(1)} %get-tuple-element.120.own), channel_id=1, source_target_pairs={{0,2},{1,3},{2,0},{3,1},{4,6},{5,7},{6,4},{7,5},{8,10},{9,11},{10,... | collective-permute-start | bytes 3932168 | tf_op jit(solution)/shard_map/ppermute | solution.py:61
  4.0 3.4 %collective-permute-start.1 = (bf16[544,512]{1,0:T(8,128)(2,1)S(1)}, bf16[544,512]{1,0:T(8,128)(2,1)S(1)}, u32[]{:S(2)}, u32[]{:S(2)}) collective-permute-start(bf16[544,512]{1,0:T(8,128)(2,1)S(1)} %get-tuple-element.81), channel_id=1, source_target_pairs={{0,2},{1,3},{2,0},{3,1},{4,6},{5,7},{6,4},{7,5},{8,10},{9,11},{10,... | collective-permute-start | bytes 1671176 | tf_op jit(solution)/shard_map/ppermute | solution.py:61
  4.1 21.3 %collective-permute-start.7 = (bf16[256,1536]{1,0:T(8,128)(2,1)S(1)}, bf16[256,1536]{1,0:T(8,128)(2,1)S(1)}, u32[]{:S(2)}, u32[]{:S(2)}) collective-permute-start(bf16[256,1536]{1,0:T(8,128)(2,1)S(1)} %get-tuple-element.77), channel_id=1, source_target_pairs={{0,1},{1,0},{2,3},{3,2},{4,5},{5,4},{6,7},{7,6},{8,9},{9,8},{10,11... | collective-permute-start | bytes 2359304 | tf_op jit(solution)/shard_map/ppermute | solution.py:61
  7.4 10.6 %collective-permute-start.4 = (bf16[256,512]{1,0:T(8,128)(2,1)S(1)}, bf16[256,512]{1,0:T(8,128)(2,1)S(1)}, u32[]{:S(2)}, u32[]{:S(2)}) collective-permute-start(bf16[256,512]{1,0:T(8,128)(2,1)S(1)} %join_teacher.1.refs_0_), channel_id=1, source_target_pairs={{0,8},{1,9},{2,10},{3,11},{4,12},{5,13},{6,14},{7,15},{8,24},{9,25... | collective-permute-start | bytes 786440 | tf_op jit(solution)/shard_map/ppermute | solution.py:61
  10.4 8.5 %collective-permute-start.3 = (bf16[256,512]{1,0:T(8,128)(2,1)S(1)}, bf16[256,512]{1,0:T(8,128)(2,1)S(1)}, u32[]{:S(2)}, u32[]{:S(2)}) collective-permute-start(bf16[256,512]{1,0:T(8,128)(2,1)S(1)} %join_teacher.1.refs_0_), channel_id=1, source_target_pairs={{0,4},{1,5},{2,6},{3,7},{4,0},{5,1},{6,2},{7,3},{8,12},{9,13},{10,... | collective-permute-start | bytes 786440 | tf_op jit(solution)/shard_map/ppermute | solution.py:61
  18.0 8.7 %collective-permute-start.5 = (bf16[256,512]{1,0:T(8,128)(2,1)S(1)}, bf16[256,512]{1,0:T(8,128)(2,1)S(1)}, u32[]{:S(2)}, u32[]{:S(2)}) collective-permute-start(bf16[256,512]{1,0:T(8,128)(2,1)S(1)} %collective-permute-done.4.refs_2_), channel_id=1, source_target_pairs={{0,8},{1,9},{2,10},{3,11},{4,12},{5,13},{6,14},{7,15},{8,24},{9,25... | collective-permute-start | bytes 786440 | tf_op jit(solution)/shard_map/ppermute | solution.py:61
  18.9 10.3 %collective-permute-start.8 = (bf16[256,512]{1,0:T(8,128)(2,1)S(1)}, bf16[256,512]{1,0:T(8,128)(2,1)S(1)}, u32[]{:S(2)}, u32[]{:S(2)}) collective-permute-start(bf16[256,512]{1,0:T(8,128)(2,1)S(1)} %collective-permute-done.4.refs_2_), channel_id=1, source_target_pairs={{0,4},{1,5},{2,6},{3,7},{4,0},{5,1},{6,2},{7,3},{8,12},{9,13},{10,... | collective-permute-start | bytes 786440 | tf_op jit(solution)/shard_map/ppermute | solution.py:61
  20.4 12.7 %collective-permute-start.11 = (bf16[288,512]{1,0:T(8,128)(2,1)S(1)}, bf16[288,512]{1,0:T(8,128)(2,1)S(1)}, u32[]{:S(2)}, u32[]{:S(2)}) collective-permute-start(bf16[288,512]{1,0:T(8,128)(2,1)S(1)} %get-tuple-element.95), channel_id=1, source_target_pairs={{0,1},{1,0},{2,3},{3,2},{4,5},{5,4},{6,7},{7,6},{8,9},{9,8},{10,11... | collective-permute-start | bytes 884744 | tf_op jit(solution)/shard_map/ppermute | solution.py:61
  25.4 5.2 %collective-permute-start.10 = (bf16[256,512]{1,0:T(8,128)(2,1)S(1)}, bf16[256,512]{1,0:T(8,128)(2,1)S(1)}, u32[]{:S(2)}, u32[]{:S(2)}) collective-permute-start(bf16[256,512]{1,0:T(8,128)(2,1)S(1)} %get-tuple-element.88), channel_id=1, source_target_pairs={{0,2},{1,3},{2,0},{3,1},{4,6},{5,7},{6,4},{7,5},{8,10},{9,11},{10,... | collective-permute-start | bytes 786440 | tf_op jit(solution)/shard_map/ppermute | solution.py:61
  25.5 5.2 %collective-permute-start.9 = (bf16[256,512]{1,0:T(8,128)(2,1)S(1)}, bf16[256,512]{1,0:T(8,128)(2,1)S(1)}, u32[]{:S(2)}, u32[]{:S(2)}) collective-permute-start(bf16[256,512]{1,0:T(8,128)(2,1)S(1)} %get-tuple-element.112.par.refs_0_), channel_id=1, source_target_pairs={{0,2},{1,3},{2,0},{3,1},{4,6},{5,7},{6,4},{7,5},{8,10},{9,11},{10,... | collective-permute-start | bytes 786440 | tf_op jit(solution)/shard_map/ppermute | solution.py:61
  26.8 16.0 %collective-permute-start.6 = (bf16[544,512]{1,0:T(8,128)(2,1)S(1)}, bf16[544,512]{1,0:T(8,128)(2,1)S(1)}, u32[]{:S(2)}, u32[]{:S(2)}) collective-permute-start(bf16[544,512]{1,0:T(8,128)(2,1)S(1)} %stack_teacher.1), channel_id=1, source_target_pairs={{0,16},{1,17},{2,18},{3,19},{4,20},{5,21},{6,22},{7,23},{8,0},{9,1... | collective-permute-start | bytes 1671176 | tf_op jit(solution)/shard_map/ppermute | solution.py:61
  29.2 13.6 %collective-permute-start = (bf16[256,1024]{1,0:T(8,128)(2,1)S(1)}, bf16[256,1024]{1,0:T(8,128)(2,1)S(1)}, u32[]{:S(2)}, u32[]{:S(2)}) collective-permute-start(bf16[256,1024]{1,0:T(8,128)(2,1)S(1)} %get-tuple-element.76), channel_id=1, source_target_pairs={{0,1},{1,0},{2,3},{3,2},{4,5},{5,4},{6,7},{7,6},{8,9},{9,8},{10,11... | collective-permute-start | bytes 1572872 | tf_op jit(solution)/shard_map/ppermute | solution.py:61
  31.5 10.0 %collective-permute-start.13 = (bf16[288,512]{1,0:T(8,128)(2,1)S(1)}, bf16[288,512]{1,0:T(8,128)(2,1)S(1)}, u32[]{:S(2)}, u32[]{:S(2)}) collective-permute-start(bf16[288,512]{1,0:T(8,128)(2,1)S(1)} %get-tuple-element.100), channel_id=1, source_target_pairs={{0,4},{1,5},{2,6},{3,7},{4,0},{5,1},{6,2},{7,3},{8,12},{9,13},{10,... | collective-permute-start | bytes 884744 | tf_op jit(solution)/shard_map/ppermute | solution.py:61
  33.1 1.6 %collective-permute-start.12 = (bf16[256,512]{1,0:T(8,128)(2,1)S(1)}, bf16[256,512]{1,0:T(8,128)(2,1)S(1)}, u32[]{:S(2)}, u32[]{:S(2)}) collective-permute-start(bf16[256,512]{1,0:T(8,128)(2,1)S(1)} %take_block.1.par.refs_1_), channel_id=1, source_target_pairs={{0,2},{1,3},{2,0},{3,1},{4,6},{5,7},{6,4},{7,5},{8,10},{9,11},{10,... | collective-permute-start | bytes 786440 | tf_op jit(solution)/shard_map/ppermute | solution.py:61
  35.6 11.7 %collective-permute-start.16 = (bf16[272,512]{1,0:T(8,128)(2,1)S(1)}, bf16[272,512]{1,0:T(8,128)(2,1)S(1)}, u32[]{:S(2)}, u32[]{:S(2)}) collective-permute-start(bf16[272,512]{1,0:T(8,128)(2,1)S(1)} %get-tuple-element.109), channel_id=1, source_target_pairs={{0,4},{1,5},{2,6},{3,7},{4,0},{5,1},{6,2},{7,3},{8,12},{9,13},{10,... | collective-permute-start | bytes 835592 | tf_op jit(solution)/shard_map/ppermute | solution.py:61
  41.6 6.4 %collective-permute-start.17 = (bf16[256,512]{1,0:T(8,128)(2,1)S(1)}, bf16[256,512]{1,0:T(8,128)(2,1)S(1)}, u32[]{:S(2)}, u32[]{:S(2)}) collective-permute-start(bf16[256,512]{1,0:T(8,128)(2,1)S(1)} %add_blocks.3), channel_id=1, source_target_pairs={{0,8},{1,9},{2,10},{3,11},{4,12},{5,13},{6,14},{7,15},{8,0},{9,1},... | collective-permute-start | bytes 786440 | tf_op jit(solution)/shard_map/ppermute | solution.py:61
  42.9 2.1 %collective-permute-start.14 = (bf16[128,512]{1,0:T(8,128)(2,1)S(1)}, bf16[128,512]{1,0:T(8,128)(2,1)S(1)}, u32[]{:S(2)}, u32[]{:S(2)}) collective-permute-start(bf16[128,512]{1,0:T(8,128)(2,1)S(1)} %get-tuple-element.102), channel_id=1, source_target_pairs={{0,2},{1,3},{2,0},{3,1},{4,6},{5,7},{6,4},{7,5},{8,10},{9,11},{10,... | collective-permute-start | bytes 393224 | tf_op jit(solution)/shard_map/ppermute | solution.py:61
  43.0 2.0 %collective-permute-start.15 = (bf16[128,512]{1,0:T(8,128)(2,1)S(1)}, bf16[128,512]{1,0:T(8,128)(2,1)S(1)}, u32[]{:S(2)}, u32[]{:S(2)}) collective-permute-start(bf16[128,512]{1,0:T(8,128)(2,1)S(1)} %get-tuple-element.104), channel_id=1, source_target_pairs={{0,2},{1,3},{2,0},{3,1},{4,6},{5,7},{6,4},{7,5},{8,10},{9,11},{10,... | collective-permute-start | bytes 393224 | tf_op jit(solution)/shard_map/ppermute | solution.py:61
  43.5 9.2 %collective-permute-start.18 = (bf16[256,512]{1,0:T(8,128)(2,1)S(1)}, bf16[256,512]{1,0:T(8,128)(2,1)S(1)}, u32[]{:S(2)}, u32[]{:S(2)}) collective-permute-start(bf16[256,512]{1,0:T(8,128)(2,1)S(1)} %collective-permute-done.5.refs_4_), channel_id=1, source_target_pairs={{0,4},{1,5},{2,6},{3,7},{4,0},{5,1},{6,2},{7,3},{8,12},{9,13},{10,... | collective-permute-start | bytes 786440 | tf_op jit(solution)/shard_map/ppermute | solution.py:61
  45.9 9.2 %collective-permute-start.19 = (bf16[256,512]{1,0:T(8,128)(2,1)S(1)}, bf16[256,512]{1,0:T(8,128)(2,1)S(1)}, u32[]{:S(2)}, u32[]{:S(2)}) collective-permute-start(bf16[256,512]{1,0:T(8,128)(2,1)S(1)} %get-tuple-element.115.refs_3_.par), channel_id=1, source_target_pairs={{0,2},{1,3},{2,0},{3,1},{4,6},{5,7},{6,4},{7,5},{8,10},{9,11},{10,... | collective-permute-start | bytes 786440 | tf_op jit(solution)/shard_map/ppermute | solution.py:61
  45.9 12.4 %collective-permute-start.20 = (bf16[256,512]{1,0:T(8,128)(2,1)S(1)}, bf16[256,512]{1,0:T(8,128)(2,1)S(1)}, u32[]{:S(2)}, u32[]{:S(2)}) collective-permute-start(bf16[256,512]{1,0:T(8,128)(2,1)S(1)} %get-tuple-element.119), channel_id=1, source_target_pairs={{0,4},{1,5},{2,6},{3,7},{4,0},{5,1},{6,2},{7,3},{8,12},{9,13},{10,... | collective-permute-start | bytes 786440 | tf_op jit(solution)/shard_map/ppermute | solution.py:61
  48.1 14.1 %collective-permute-start.24 = (bf16[256,512]{1,0:T(8,128)(2,1)S(1)}, bf16[256,512]{1,0:T(8,128)(2,1)S(1)}, u32[]{:S(2)}, u32[]{:S(2)}) collective-permute-start(bf16[256,512]{1,0:T(8,128)(2,1)S(1)} %add_blocks.4), channel_id=1, source_target_pairs={{0,16},{1,17},{2,18},{3,19},{4,20},{5,21},{6,22},{7,23},{8,24},{9,... | collective-permute-start | bytes 786440 | tf_op jit(solution)/shard_map/ppermute | solution.py:61
  53.5 10.0 %collective-permute-start.21 = (bf16[256,512]{1,0:T(8,128)(2,1)S(1)}, bf16[256,512]{1,0:T(8,128)(2,1)S(1)}, u32[]{:S(2)}, u32[]{:S(2)}) collective-permute-start(bf16[256,512]{1,0:T(8,128)(2,1)S(1)} %far_features.2), channel_id=1, source_target_pairs={{0,1},{1,0},{2,3},{3,2},{4,5},{5,4},{6,7},{7,6},{8,9},{9,8},{10,11... | collective-permute-start | bytes 786440 | tf_op jit(solution)/shard_map/ppermute | solution.py:61
  56.6 8.7 %collective-permute-start.22 = (bf16[256,512]{1,0:T(8,128)(2,1)S(1)}, bf16[256,512]{1,0:T(8,128)(2,1)S(1)}, u32[]{:S(2)}, u32[]{:S(2)}) collective-permute-start(bf16[256,512]{1,0:T(8,128)(2,1)S(1)} %far_features.3), channel_id=1, source_target_pairs={{0,3},{1,2},{2,1},{3,0},{4,7},{5,6},{6,5},{7,4},{8,11},{9,10},{10,... | collective-permute-start | bytes 786440 | tf_op jit(solution)/shard_map/ppermute | solution.py:61
  56.7 8.8 %collective-permute-start.23 = (bf16[256,512]{1,0:T(8,128)(2,1)S(1)}, bf16[256,512]{1,0:T(8,128)(2,1)S(1)}, u32[]{:S(2)}, u32[]{:S(2)}) collective-permute-start(bf16[256,512]{1,0:T(8,128)(2,1)S(1)} %get-tuple-element.123), channel_id=1, source_target_pairs={{0,4},{1,5},{2,6},{3,7},{4,0},{5,1},{6,2},{7,3},{8,12},{9,13},{10,... | collective-permute-start | bytes 786440 | tf_op jit(solution)/shard_map/ppermute | solution.py:61
  58.3 9.4 %collective-permute-start.25 = (bf16[256,512]{1,0:T(8,128)(2,1)S(1)}, bf16[256,512]{1,0:T(8,128)(2,1)S(1)}, u32[]{:S(2)}, u32[]{:S(2)}) collective-permute-start(bf16[256,512]{1,0:T(8,128)(2,1)S(1)} %add_blocks.5), channel_id=1, source_target_pairs={{0,8},{1,9},{2,10},{3,11},{4,12},{5,13},{6,14},{7,15},{8,0},{9,1},... | collective-permute-start | bytes 786440 | tf_op jit(solution)/shard_map/ppermute | solution.py:61
  62.2 5.5 %collective-permute-start.26 = (bf16[240,512]{1,0:T(8,128)(2,1)S(1)}, bf16[240,512]{1,0:T(8,128)(2,1)S(1)}, u32[]{:S(2)}, u32[]{:S(2)}) collective-permute-start(bf16[240,512]{1,0:T(8,128)(2,1)S(1)} %get-tuple-element.125), channel_id=1, source_target_pairs={{0,2},{1,3},{2,0},{3,1},{4,6},{5,7},{6,4},{7,5},{8,10},{9,11},{10,... | collective-permute-start | bytes 737288 | tf_op jit(solution)/shard_map/ppermute | solution.py:61
  62.2 7.6 %copy-start.2 = (f32[128,2048]{1,0:T(8,128)S(1)}, f32[128,2048]{1,0:T(8,128)}, u32[]{:S(2)}) copy-start(f32[128,2048]{1,0:T(8,128)} %refs_2_.5) | copy-start | bytes 3145732
  62.2 7.6 %copy-start.3 = (f32[128,2048]{1,0:T(8,128)S(1)}, f32[128,2048]{1,0:T(8,128)}, u32[]{:S(2)}) copy-start(f32[128,2048]{1,0:T(8,128)} %refs_3_.5) | copy-start | bytes 3145732
  63.5 6.3 %copy-start.1 = (f32[128,2048]{1,0:T(8,128)S(1)}, f32[128,2048]{1,0:T(8,128)}, u32[]{:S(2)}) copy-start(f32[128,2048]{1,0:T(8,128)} %refs_1_.3) | copy-start | bytes 3145732
  63.5 8.0 %collective-permute-start.28 = (bf16[256,512]{1,0:T(8,128)(2,1)S(1)}, bf16[256,512]{1,0:T(8,128)(2,1)S(1)}, u32[]{:S(2)}, u32[]{:S(2)}) collective-permute-start(bf16[256,512]{1,0:T(8,128)(2,1)S(1)} %get-tuple-element.131), channel_id=1, source_target_pairs={{0,2},{1,3},{2,0},{3,1},{4,6},{5,7},{6,4},{7,5},{8,10},{9,11},{10,... | collective-permute-start | bytes 786440 | tf_op jit(solution)/shard_map/ppermute | solution.py:61
  67.9 1.9 %collective-permute-start.27 = (bf16[128,512]{1,0:T(8,128)(2,1)S(1)}, bf16[128,512]{1,0:T(8,128)(2,1)S(1)}, u32[]{:S(2)}, u32[]{:S(2)}) collective-permute-start(bf16[128,512]{1,0:T(8,128)(2,1)S(1)} %get-tuple-element.128), channel_id=1, source_target_pairs={{0,2},{1,3},{2,0},{3,1},{4,6},{5,7},{6,4},{7,5},{8,10},{9,11},{10,... | collective-permute-start | bytes 393224 | tf_op jit(solution)/shard_map/ppermute | solution.py:61
  68.0 6.3 %collective-permute-start.30 = (bf16[128,512]{1,0:T(8,128)(2,1)S(1)}, bf16[128,512]{1,0:T(8,128)(2,1)S(1)}, u32[]{:S(2)}, u32[]{:S(2)}) collective-permute-start(bf16[128,512]{1,0:T(8,128)(2,1)S(1)} %get-tuple-element.127.refs_0_), channel_id=1, source_target_pairs={{0,1},{1,0},{2,3},{3,2},{4,5},{5,4},{6,7},{7,6},{8,9},{9,8},{10,11... | collective-permute-start | bytes 393224 | tf_op jit(solution)/shard_map/ppermute | solution.py:61
  69.6 6.7 %collective-permute-start.29 = (bf16[128,512]{1,0:T(8,128)(2,1)S(1)}, bf16[128,512]{1,0:T(8,128)(2,1)S(1)}, u32[]{:S(2)}, u32[]{:S(2)}) collective-permute-start(bf16[128,512]{1,0:T(8,128)(2,1)S(1)} %get-tuple-element.128), channel_id=1, source_target_pairs={{0,3},{1,2},{2,1},{3,0},{4,7},{5,6},{6,5},{7,4},{8,11},{9,10},{10,... | collective-permute-start | bytes 393224 | tf_op jit(solution)/shard_map/ppermute | solution.py:61

commit v6 on v5

--- a/solution.py
+++ b/solution.py
@@ -192,17 +192,19 @@
 
             return body
 
+        def block_y(dz, *gates):
+            moved_y[dz] = [start(terms[dz][dy], along_y(dy), *gates) for dy in others]
+
         def gradient_block(k):
             dz = g_order[k]
             terms[dz] = run(
                 "gradient_block",
                 terms_body(k),
                 [((2 * rows, part), f32)]
-                + [((2 * rows + (2 * extra, extra, 0, 0)[k], part), bf16)] * (ny - 1),
+                + [((2 * rows + extra * (k == 0), part), bf16)] * (ny - 1),
                 [near_own, near_sib, far_par[k], far_dia[k], c_own, c_par, c_dia],
                 scratch=[pltpu.VMEM((span, part), f32)],
             )
-            moved_y[dz] = [start(terms[dz][dy], along_y(dy)) for dy in others]
 
         def add_body(*refs):
             total = sum(ref[: 2 * rows, :].astype(f32) for ref in refs[:-1])
@@ -312,11 +314,13 @@
         far_dia[0] = start(far_par[0], sibling)
         wait(*w_side[3])
         gradient_block(0)
+        block_y(3)
         both = start(third, partner)
         (far_par[1],) = run("take_block", first_body, [((tokens, span), bf16)], [block])
         far_dia[1] = start(far_par[1], sibling)
         gradient_block(1)
         onward = block_sum(3)
+        block_y(2, onward)
         teacher_y(2, onward)
         onward = start(onward, across_z(1))
         *pieces, far_par[2], far_par[3] = run(
@@ -328,6 +332,7 @@
         pieces = [start(piece, sibling) for piece in pieces]
         (far_dia[2],) = run("join_pieces", pieces_body, [((tokens, span), bf16)], pieces)
         gradient_block(2)
+        block_y(1)
         onward = start(block_sum(2, onward), across_z(2))
         far_dia[3] = start(far_par[3], sibling, terms[1][0])
         (w_full,) = run(
@@ -338,6 +343,7 @@
         )
         f_par = start(far_features(far_par), partner)
         gradient_block(3)
+        block_y(0)
         f_dia = start(far_features(far_dia), diagonal)
         back = start(block_sum(1), across_z(1))
         f_own, f_sib = run(

time: 77.7 us -> 77.7 us (level)
  waiting for transfers between devices: 30.1 us -> 29 us
  starting transfers between devices: 31.8 us -> 32.9 us
    ppermute x31, starting transfers between devices: 31.8 us -> 32.9 us  [send(): return lax.ppermute(value, ('fsdp', 'rep'), perm)]
    ppermute x31, waiting for transfers between devices: 30.1 us -> 29 us  [send(): return lax.ppermute(value, ('fsdp', 'rep'), perm)]
where the time goes in v6:
time: 77.7 us; the launch traced here: 77.5 us
  starting transfers between devices  32.9 us (42%)
  waiting for transfers between devices  29 us (37%)
  Pallas kernels  12.2 us (16%)
  local copies, waits for them, and re-layouts  2.55 us (3%)
  between operations  0.88 us (1%)
    ppermute x31, starting transfers between devices, send(): return lax.ppermute(value, ('fsdp', 'rep'), perm)  32.9 us
    ppermute x31, waiting for transfers between devices, send(): return lax.ppermute(value, ('fsdp', 'rep'), perm)  29 us
    pallas_call x21, Pallas kernels, call(): pl.pallas_call(body, out_shape=shapes, in_specs=[VMEM] * len(inputs), out...  8.02 us
    pallas_call x3, Pallas kernels, update(): pl.pallas_call(update_body(quarters), out_shape=[jax.ShapeDtypeStruct((ro...  4.22 us
    unnamed x12, local copies, waits for them, and re-layouts  2.55 us
  transfers between devices with their start and end apart: 31, of which 15 were waited for; matrix products, arithmetic and copies ran while one was open for 0% of the time, Pallas kernels for 14%

profile of v6, /device:TPU:0, one launch (start us, length us, event | category | flops | bytes accessed | tf_op | source)
XLA Modules:
  0.0 77.5 jit_solution(6928644978823453013)
XLA Ops:
  0.7 1.3 %copy-done.4 = bf16[256,2048]{1,0:T(8,128)(2,1)S(1)} copy-done((bf16[256,2048]{1,0:T(8,128)(2,1)S(1)}, bf16[256,2048]{1,0:T(8,128)(2,1)}, u32[]{:S(2)}) %copy-start.4) | copy-done | bytes 1048600
  2.0 1.2 %copy-done.5 = bf16[256,2048]{1,0:T(8,128)(2,1)S(1)} copy-done((bf16[256,2048]{1,0:T(8,128)(2,1)S(1)}, bf16[256,2048]{1,0:T(8,128)(2,1)}, u32[]{:S(2)}) %copy-start.5) | copy-done | bytes 1048600
  3.4 0.5 collective-permute-start.2
  4.1 2.9 %collective-permute-start.7 = (bf16[256,1536]{1,0:T(8,128)(2,1)S(1)}, bf16[256,1536]{1,0:T(8,128)(2,1)S(1)}, u32[]{:S(2)}, u32[]{:S(2)}) collective-permute-start(bf16[256,1536]{1,0:T(8,128)(2,1)S(1)} %get-tuple-element.78), channel_id=1, source_target_pairs={{0,1},{1,0},{2,3},{3,2},{4,5},{5,4},{6,7},{7,6},{8,9},{9,8},{10,11... | collective-permute-start | bytes 2359304 | tf_op jit(solution)/shard_map/ppermute | solution.py:61
  7.1 0.3 collective-permute-done.1.sib
  7.4 3.0 %collective-permute-start.4 = (bf16[256,512]{1,0:T(8,128)(2,1)S(1)}, bf16[256,512]{1,0:T(8,128)(2,1)S(1)}, u32[]{:S(2)}, u32[]{:S(2)}) collective-permute-start(bf16[256,512]{1,0:T(8,128)(2,1)S(1)} %join_teacher.1.refs_0_), channel_id=1, source_target_pairs={{0,8},{1,9},{2,10},{3,11},{4,12},{5,13},{6,14},{7,15},{8,24},{9,25... | collective-permute-start | bytes 786440 | tf_op jit(solution)/shard_map/ppermute | solution.py:61
  10.4 1.5 %collective-permute-start.3 = (bf16[256,512]{1,0:T(8,128)(2,1)S(1)}, bf16[256,512]{1,0:T(8,128)(2,1)S(1)}, u32[]{:S(2)}, u32[]{:S(2)}) collective-permute-start(bf16[256,512]{1,0:T(8,128)(2,1)S(1)} %join_teacher.1.refs_0_), channel_id=1, source_target_pairs={{0,4},{1,5},{2,6},{3,7},{4,0},{5,1},{6,2},{7,3},{8,12},{9,13},{10,... | collective-permute-start | bytes 786440 | tf_op jit(solution)/shard_map/ppermute | solution.py:61
  11.9 6.1 %collective-permute-done.4.refs_2_ = bf16[256,512]{1,0:T(8,128)(2,1)S(1)} collective-permute-done((bf16[256,512]{1,0:T(8,128)(2,1)S(1)}, bf16[256,512]{1,0:T(8,128)(2,1)S(1)}, u32[]{:S(2)}, u32[]{:S(2)}) %collective-permute-start.4) | collective-permute-done | bytes 262176 | tf_op jit(solution)/shard_map/ppermute | solution.py:61
  18.0 0.8 %collective-permute-start.5 = (bf16[256,512]{1,0:T(8,128)(2,1)S(1)}, bf16[256,512]{1,0:T(8,128)(2,1)S(1)}, u32[]{:S(2)}, u32[]{:S(2)}) collective-permute-start(bf16[256,512]{1,0:T(8,128)(2,1)S(1)} %collective-permute-done.4.refs_2_), channel_id=1, source_target_pairs={{0,8},{1,9},{2,10},{3,11},{4,12},{5,13},{6,14},{7,15},{8,24},{9,25... | collective-permute-start | bytes 786440 | tf_op jit(solution)/shard_map/ppermute | solution.py:61
  18.9 1.5 %collective-permute-start.8 = (bf16[256,512]{1,0:T(8,128)(2,1)S(1)}, bf16[256,512]{1,0:T(8,128)(2,1)S(1)}, u32[]{:S(2)}, u32[]{:S(2)}) collective-permute-start(bf16[256,512]{1,0:T(8,128)(2,1)S(1)} %collective-permute-done.4.refs_2_), channel_id=1, source_target_pairs={{0,4},{1,5},{2,6},{3,7},{4,0},{5,1},{6,2},{7,3},{8,12},{9,13},{10,... | collective-permute-start | bytes 786440 | tf_op jit(solution)/shard_map/ppermute | solution.py:61
  20.4 1.5 %collective-permute-start.11 = (bf16[288,512]{1,0:T(8,128)(2,1)S(1)}, bf16[288,512]{1,0:T(8,128)(2,1)S(1)}, u32[]{:S(2)}, u32[]{:S(2)}) collective-permute-start(bf16[288,512]{1,0:T(8,128)(2,1)S(1)} %get-tuple-element.96), channel_id=1, source_target_pairs={{0,1},{1,0},{2,3},{3,2},{4,5},{5,4},{6,7},{7,6},{8,9},{9,8},{10,11... | collective-permute-start | bytes 884744 | tf_op jit(solution)/shard_map/ppermute | solution.py:61
  21.9 3.4 %collective-permute-done.7.message = bf16[256,1536]{1,0:T(8,128)(2,1)S(1)} collective-permute-done((bf16[256,1536]{1,0:T(8,128)(2,1)S(1)}, bf16[256,1536]{1,0:T(8,128)(2,1)S(1)}, u32[]{:S(2)}, u32[]{:S(2)}) %collective-permute-start.7) | collective-permute-done | bytes 786464 | tf_op jit(solution)/shard_map/ppermute | solution.py:61
  25.5 0.5 collective-permute-start.9
  26.0 0.8 collective-permute-done.5.refs_4_
  26.8 2.4 %collective-permute-start.6 = (bf16[544,512]{1,0:T(8,128)(2,1)S(1)}, bf16[544,512]{1,0:T(8,128)(2,1)S(1)}, u32[]{:S(2)}, u32[]{:S(2)}) collective-permute-start(bf16[544,512]{1,0:T(8,128)(2,1)S(1)} %stack_teacher.1), channel_id=1, source_target_pairs={{0,16},{1,17},{2,18},{3,19},{4,20},{5,21},{6,22},{7,23},{8,0},{9,1... | collective-permute-start | bytes 1671176 | tf_op jit(solution)/shard_map/ppermute | solution.py:61
  29.2 1.5 %collective-permute-start = (bf16[256,1024]{1,0:T(8,128)(2,1)S(1)}, bf16[256,1024]{1,0:T(8,128)(2,1)S(1)}, u32[]{:S(2)}, u32[]{:S(2)}) collective-permute-start(bf16[256,1024]{1,0:T(8,128)(2,1)S(1)} %get-tuple-element.77), channel_id=1, source_target_pairs={{0,1},{1,0},{2,3},{3,2},{4,5},{5,4},{6,7},{7,6},{8,9},{9,8},{10,11... | collective-permute-start | bytes 1572872 | tf_op jit(solution)/shard_map/ppermute | solution.py:61
  30.7 0.8 %gradient_block.4 = (f32[256,512]{1,0:T(8,128)S(1)}, bf16[272,512]{1,0:T(8,128)(2,1)S(1)}) custom-call(bf16[256,2560]{1,0:T(8,128)(2,1)S(1)} %get-tuple-element.122.own, bf16[256,2560]{1,0:T(8,128)(2,1)S(1)} %collective-permute-done.2.sib, bf16[256,512]{1,0:T(8,128)(2,1)S(1)} %get-tuple-element.114.par.refs_0_, ...), custom_call_target="tpu_custom_call" | custom-call | flops 1 | bytes 1 | tf_op jit(solution)/shard_map/gradient_block/pallas_call | solution.py:29
  31.5 1.6 %collective-permute-start.13 = (bf16[272,512]{1,0:T(8,128)(2,1)S(1)}, bf16[272,512]{1,0:T(8,128)(2,1)S(1)}, u32[]{:S(2)}, u32[]{:S(2)}) collective-permute-start(bf16[272,512]{1,0:T(8,128)(2,1)S(1)} %get-tuple-element.101), channel_id=1, source_target_pairs={{0,4},{1,5},{2,6},{3,7},{4,0},{5,1},{6,2},{7,3},{8,12},{9,13},{10,... | collective-permute-start | bytes 835592 | tf_op jit(solution)/shard_map/ppermute | solution.py:61
  33.2 1.5 %collective-permute-done.12.dia.refs_1_ = bf16[256,512]{1,0:T(8,128)(2,1)S(1)} collective-permute-done((bf16[256,512]{1,0:T(8,128)(2,1)S(1)}, bf16[256,512]{1,0:T(8,128)(2,1)S(1)}, u32[]{:S(2)}, u32[]{:S(2)}) %collective-permute-start.12) | collective-permute-done | bytes 262176 | tf_op jit(solution)/shard_map/ppermute | solution.py:61
  34.7 0.8 %gradient_block.5 = (f32[256,512]{1,0:T(8,128)S(1)}, bf16[256,512]{1,0:T(8,128)(2,1)S(1)}) custom-call(bf16[256,2560]{1,0:T(8,128)(2,1)S(1)} %get-tuple-element.122.own, bf16[256,2560]{1,0:T(8,128)(2,1)S(1)} %collective-permute-done.2.sib, bf16[256,512]{1,0:T(8,128)(2,1)S(1)} %take_block.1.par.refs_1_, ...), custom_call_target="tpu_custom_call" | custom-call | flops 1 | bytes 1 | tf_op jit(solution)/shard_map/gradient_block/pallas_call | solution.py:29
  35.6 4.1 %collective-permute-done.13.refs_1_ = bf16[272,512]{1,0:T(8,128)(2,1)S(1)} collective-permute-done((bf16[272,512]{1,0:T(8,128)(2,1)S(1)}, bf16[272,512]{1,0:T(8,128)(2,1)S(1)}, u32[]{:S(2)}, u32[]{:S(2)}) %collective-permute-start.13) | collective-permute-done | bytes 278560 | tf_op jit(solution)/shard_map/ppermute | solution.py:61
  39.7 1.6 %collective-permute-start.16 = (bf16[256,512]{1,0:T(8,128)(2,1)S(1)}, bf16[256,512]{1,0:T(8,128)(2,1)S(1)}, u32[]{:S(2)}, u32[]{:S(2)}) collective-permute-start(bf16[256,512]{1,0:T(8,128)(2,1)S(1)} %get-tuple-element.111), channel_id=1, source_target_pairs={{0,4},{1,5},{2,6},{3,7},{4,0},{5,1},{6,2},{7,3},{8,12},{9,13},{10,... | collective-permute-start | bytes 786440 | tf_op jit(solution)/shard_map/ppermute | solution.py:61
  41.3 1.5 %collective-permute-done.message = bf16[256,1024]{1,0:T(8,128)(2,1)S(1)} collective-permute-done((bf16[256,1024]{1,0:T(8,128)(2,1)S(1)}, bf16[256,1024]{1,0:T(8,128)(2,1)S(1)}, u32[]{:S(2)}, u32[]{:S(2)}) %collective-permute-start) | collective-permute-done | bytes 524320 | tf_op jit(solution)/shard_map/ppermute | solution.py:61
  43.0 0.5 collective-permute-start.15
  43.5 1.5 %collective-permute-start.18 = (bf16[256,512]{1,0:T(8,128)(2,1)S(1)}, bf16[256,512]{1,0:T(8,128)(2,1)S(1)}, u32[]{:S(2)}, u32[]{:S(2)}) collective-permute-start(bf16[256,512]{1,0:T(8,128)(2,1)S(1)} %collective-permute-done.5.refs_4_), channel_id=1, source_target_pairs={{0,4},{1,5},{2,6},{3,7},{4,0},{5,1},{6,2},{7,3},{8,12},{9,13},{10,... | collective-permute-start | bytes 786440 | tf_op jit(solution)/shard_map/ppermute | solution.py:61
  45.0 0.8 %gradient_block.6 = (f32[256,512]{1,0:T(8,128)S(1)}, bf16[256,512]{1,0:T(8,128)(2,1)S(1)}) custom-call(bf16[256,2560]{1,0:T(8,128)(2,1)S(1)} %get-tuple-element.122.own, bf16[256,2560]{1,0:T(8,128)(2,1)S(1)} %collective-permute-done.2.sib, bf16[256,512]{1,0:T(8,128)(2,1)S(1)} %get-tuple-element.107.par.refs_2_, bf16[256,512]{1,0:T(8,128)(2,1)S(1)} %join_pieces.1.dia.refs_2_, ...), custom_call_target="tpu_custom_call" | custom-call | flops 1 | bytes 1 | tf_op jit(solution)/shard_map/gradient_block/pallas_call | solution.py:29
  45.9 1.3 %collective-permute-start.20 = (bf16[256,512]{1,0:T(8,128)(2,1)S(1)}, bf16[256,512]{1,0:T(8,128)(2,1)S(1)}, u32[]{:S(2)}, u32[]{:S(2)}) collective-permute-start(bf16[256,512]{1,0:T(8,128)(2,1)S(1)} %get-tuple-element.121), channel_id=1, source_target_pairs={{0,4},{1,5},{2,6},{3,7},{4,0},{5,1},{6,2},{7,3},{8,12},{9,13},{10,... | collective-permute-start | bytes 786440 | tf_op jit(solution)/shard_map/ppermute | solution.py:61
  47.3 0.6 collective-permute-done.17.refs_2_
  47.9 2.2 %collective-permute-start.24 = (bf16[256,512]{1,0:T(8,128)(2,1)S(1)}, bf16[256,512]{1,0:T(8,128)(2,1)S(1)}, u32[]{:S(2)}, u32[]{:S(2)}) collective-permute-start(bf16[256,512]{1,0:T(8,128)(2,1)S(1)} %add_blocks.4), channel_id=1, source_target_pairs={{0,16},{1,17},{2,18},{3,19},{4,20},{5,21},{6,22},{7,23},{8,24},{9,... | collective-permute-start | bytes 786440 | tf_op jit(solution)/shard_map/ppermute | solution.py:61
  50.2 2.5 %collective-permute-done.18.refs_5_ = bf16[256,512]{1,0:T(8,128)(2,1)S(1)} collective-permute-done((bf16[256,512]{1,0:T(8,128)(2,1)S(1)}, bf16[256,512]{1,0:T(8,128)(2,1)S(1)}, u32[]{:S(2)}, u32[]{:S(2)}) %collective-permute-start.18) | collective-permute-done | bytes 262176 | tf_op jit(solution)/shard_map/ppermute | solution.py:61
  52.8 0.7 far_features.2
  53.5 1.6 %collective-permute-start.21 = (bf16[256,512]{1,0:T(8,128)(2,1)S(1)}, bf16[256,512]{1,0:T(8,128)(2,1)S(1)}, u32[]{:S(2)}, u32[]{:S(2)}) collective-permute-start(bf16[256,512]{1,0:T(8,128)(2,1)S(1)} %far_features.2), channel_id=1, source_target_pairs={{0,1},{1,0},{2,3},{3,2},{4,5},{5,4},{6,7},{7,6},{8,9},{9,8},{10,11... | collective-permute-start | bytes 786440 | tf_op jit(solution)/shard_map/ppermute | solution.py:61
  55.1 0.8 %gradient_block.7 = (f32[256,512]{1,0:T(8,128)S(1)}, bf16[256,512]{1,0:T(8,128)(2,1)S(1)}) custom-call(bf16[256,2560]{1,0:T(8,128)(2,1)S(1)} %get-tuple-element.122.own, bf16[256,2560]{1,0:T(8,128)(2,1)S(1)} %collective-permute-done.2.sib, bf16[256,512]{1,0:T(8,128)(2,1)S(1)} %get-tuple-element.117.refs_3_.par, ...), custom_call_target="tpu_custom_call" | custom-call | flops 1 | bytes 1 | tf_op jit(solution)/shard_map/gradient_block/pallas_call | solution.py:29
  55.9 0.7 far_features.3
  56.7 1.6 %collective-permute-start.23 = (bf16[256,512]{1,0:T(8,128)(2,1)S(1)}, bf16[256,512]{1,0:T(8,128)(2,1)S(1)}, u32[]{:S(2)}, u32[]{:S(2)}) collective-permute-start(bf16[256,512]{1,0:T(8,128)(2,1)S(1)} %get-tuple-element.125), channel_id=1, source_target_pairs={{0,4},{1,5},{2,6},{3,7},{4,0},{5,1},{6,2},{7,3},{8,12},{9,13},{10,... | collective-permute-start | bytes 786440 | tf_op jit(solution)/shard_map/ppermute | solution.py:61
  58.3 1.8 %collective-permute-start.25 = (bf16[256,512]{1,0:T(8,128)(2,1)S(1)}, bf16[256,512]{1,0:T(8,128)(2,1)S(1)}, u32[]{:S(2)}, u32[]{:S(2)}) collective-permute-start(bf16[256,512]{1,0:T(8,128)(2,1)S(1)} %add_blocks.5), channel_id=1, source_target_pairs={{0,8},{1,9},{2,10},{3,11},{4,12},{5,13},{6,14},{7,15},{8,0},{9,1},... | collective-permute-start | bytes 786440 | tf_op jit(solution)/shard_map/ppermute | solution.py:61
  60.1 2.1 %collective-permute-done.24.refs_2_ = bf16[256,512]{1,0:T(8,128)(2,1)S(1)} collective-permute-done((bf16[256,512]{1,0:T(8,128)(2,1)S(1)}, bf16[256,512]{1,0:T(8,128)(2,1)S(1)}, u32[]{:S(2)}, u32[]{:S(2)}) %collective-permute-start.24) | collective-permute-done | bytes 262176 | tf_op jit(solution)/shard_map/ppermute | solution.py:61
  62.3 1.2 %near_features.1 = (bf16[256,512]{1,0:T(8,128)(2,1)S(1)}, bf16[256,512]{1,0:T(8,128)(2,1)S(1)}) custom-call(bf16[256,2560]{1,0:T(8,128)(2,1)S(1)} %get-tuple-element.122.own, bf16[256,2560]{1,0:T(8,128)(2,1)S(1)} %collective-permute-done.2.sib, bf16[2048,512]{1,0:T(8,128)(2,1)S(1)} %fill_teacher.1.refs_4_.full), custom_call_target="tpu_custom_call" | custom-call | flops 1 | bytes 1 | tf_op jit(solution)/shard_map/near_features/pallas_call | solution.py:29
  63.5 0.6 collective-permute-start.28
  64.1 1.3 %collective-permute-done.22.refs_3_ = bf16[256,512]{1,0:T(8,128)(2,1)S(1)} collective-permute-done((bf16[256,512]{1,0:T(8,128)(2,1)S(1)}, bf16[256,512]{1,0:T(8,128)(2,1)S(1)}, u32[]{:S(2)}, u32[]{:S(2)}) %collective-permute-start.22) | collective-permute-done | bytes 262176 | tf_op jit(solution)/shard_map/ppermute | solution.py:61
  65.6 2.2 %collective-permute-done.25.refs_3_ = bf16[256,512]{1,0:T(8,128)(2,1)S(1)} collective-permute-done((bf16[256,512]{1,0:T(8,128)(2,1)S(1)}, bf16[256,512]{1,0:T(8,128)(2,1)S(1)}, u32[]{:S(2)}, u32[]{:S(2)}) %collective-permute-start.25) | collective-permute-done | bytes 262176 | tf_op jit(solution)/shard_map/ppermute | solution.py:61
  68.0 1.6 %collective-permute-start.30 = (bf16[128,512]{1,0:T(8,128)(2,1)S(1)}, bf16[128,512]{1,0:T(8,128)(2,1)S(1)}, u32[]{:S(2)}, u32[]{:S(2)}) collective-permute-start(bf16[128,512]{1,0:T(8,128)(2,1)S(1)} %get-tuple-element.129.refs_0_), channel_id=1, source_target_pairs={{0,1},{1,0},{2,3},{3,2},{4,5},{5,4},{6,7},{7,6},{8,9},{9,8},{10,11... | collective-permute-start | bytes 393224 | tf_op jit(solution)/shard_map/ppermute | solution.py:61
  69.9 1.7 %update_near.1 = (f32[128,2048]{1,0:T(8,128)}, f32[128,2048]{1,0:T(8,128)}, f32[128,2048]{1,0:T(8,128)}, f32[128,2048]{1,0:T(8,128)}) custom-call(bf16[128,512]{1,0:T(8,128)(2,1)S(1)} %get-tuple-element.129.refs_0_, bf16[128,512]{1,0:T(8,128)(2,1)S(1)} %collective-permute-done.27.refs_1_, f32[128,2048]{1,0:T(8,128)S(1)} %copy-done.1, ...), custom_call_target="tpu_custom_call" | custom-call | flops 1 | bytes 1 | tf_op jit(solution)/shard_map/update_near/pallas_call | solution.py:401
  71.5 1.1 %place_features.1 = bf16[256,2048]{1,0:T(8,128)(2,1)} custom-call(bf16[256,512]{1,0:T(8,128)(2,1)S(1)} %get-tuple-element.132.refs_0_, bf16[256,512]{1,0:T(8,128)(2,1)S(1)} %collective-permute-done.28.refs_1_, bf16[256,512]{1,0:T(8,128)(2,1)S(1)} %collective-permute-done.21.refs_2_, bf16[256,512]{1,0:T(8,128)(2,1)S(1)} %collective-permute-done.22.refs_3_), custom_call_target="tpu_custom_call" | custom-call | flops 1 | bytes 1 | tf_op jit(solution)/shard_map/place_features/pallas_call | solution.py:29
  72.6 1.7 %collective-permute-done.30.refs_0_ = bf16[128,512]{1,0:T(8,128)(2,1)S(1)} collective-permute-done((bf16[128,512]{1,0:T(8,128)(2,1)S(1)}, bf16[128,512]{1,0:T(8,128)(2,1)S(1)}, u32[]{:S(2)}, u32[]{:S(2)}) %collective-permute-start.30) | collective-permute-done | bytes 131104 | tf_op jit(solution)/shard_map/ppermute | solution.py:61
  74.3 1.3 %update_partner.1 = (f32[128,2048]{1,0:T(8,128)}, f32[128,2048]{1,0:T(8,128)}, f32[128,2048]{1,0:T(8,128)}, f32[128,2048]{1,0:T(8,128)}) custom-call(bf16[128,512]{1,0:T(8,128)(2,1)S(1)} %collective-permute-done.30.refs_0_, f32[128,2048]{1,0:T(8,128)S(1)} %copy-done.1, ...), custom_call_target="tpu_custom_call", output_to_operand_aliasing={{0}: (5, {}), {1}: (6, {}), {2}: (7, {}), {3}: (8, {})} | custom-call | flops 1 | bytes 1 | tf_op jit(solution)/shard_map/update_partner/pallas_call | solution.py:401
  75.6 0.6 collective-permute-done.29.refs_0_
  76.2 1.3 %update_diagonal.1 = (f32[128,2048]{1,0:T(8,128)}, f32[128,2048]{1,0:T(8,128)}, f32[128,2048]{1,0:T(8,128)}, f32[128,2048]{1,0:T(8,128)}) custom-call(bf16[128,512]{1,0:T(8,128)(2,1)S(1)} %collective-permute-done.29.refs_0_, f32[128,2048]{1,0:T(8,128)S(1)} %copy-done.1, ...), custom_call_target="tpu_custom_call", output_to_operand_aliasing={{0}: (5, {}), {1}: (6, {}), {2}: (7, {}), {3}: (8, {})} | custom-call | flops 1 | bytes 1 | tf_op jit(solution)/shard_map/update_diagonal/pallas_call | solution.py:401
  (50 shorter events, 2.1 us)
Async XLA Ops:
  0.6 3.3 %copy-start = (f32[128,2048]{1,0:T(8,128)S(1)}, f32[128,2048]{1,0:T(8,128)}, u32[]{:S(2)}) copy-start(f32[128,2048]{1,0:T(8,128)} %refs_4_.5) | copy-start | bytes 3145732
  0.6 1.3 %copy-start.4 = (bf16[256,2048]{1,0:T(8,128)(2,1)S(1)}, bf16[256,2048]{1,0:T(8,128)(2,1)}, u32[]{:S(2)}) copy-start(bf16[256,2048]{1,0:T(8,128)(2,1)} %p.1) | copy-start | bytes 3145732
  2.0 1.2 %copy-start.5 = (bf16[256,2048]{1,0:T(8,128)(2,1)S(1)}, bf16[256,2048]{1,0:T(8,128)(2,1)}, u32[]{:S(2)}) copy-start(bf16[256,2048]{1,0:T(8,128)(2,1)} %c.1) | copy-start | bytes 3145732
  3.4 18.5 %collective-permute-start.2 = (bf16[256,2560]{1,0:T(8,128)(2,1)S(1)}, bf16[256,2560]{1,0:T(8,128)(2,1)S(1)}, u32[]{:S(2)}, u32[]{:S(2)}) collective-permute-start(bf16[256,2560]{1,0:T(8,128)(2,1)S(1)} %get-tuple-element.122.own), channel_id=1, source_target_pairs={{0,2},{1,3},{2,0},{3,1},{4,6},{5,7},{6,4},{7,5},{8,10},{9,11},{10,... | collective-permute-start | bytes 3932168 | tf_op jit(solution)/shard_map/ppermute | solution.py:61
  4.0 3.4 %collective-permute-start.1 = (bf16[544,512]{1,0:T(8,128)(2,1)S(1)}, bf16[544,512]{1,0:T(8,128)(2,1)S(1)}, u32[]{:S(2)}, u32[]{:S(2)}) collective-permute-start(bf16[544,512]{1,0:T(8,128)(2,1)S(1)} %get-tuple-element.82), channel_id=1, source_target_pairs={{0,2},{1,3},{2,0},{3,1},{4,6},{5,7},{6,4},{7,5},{8,10},{9,11},{10,... | collective-permute-start | bytes 1671176 | tf_op jit(solution)/shard_map/ppermute | solution.py:61
  4.1 21.3 %collective-permute-start.7 = (bf16[256,1536]{1,0:T(8,128)(2,1)S(1)}, bf16[256,1536]{1,0:T(8,128)(2,1)S(1)}, u32[]{:S(2)}, u32[]{:S(2)}) collective-permute-start(bf16[256,1536]{1,0:T(8,128)(2,1)S(1)} %get-tuple-element.78), channel_id=1, source_target_pairs={{0,1},{1,0},{2,3},{3,2},{4,5},{5,4},{6,7},{7,6},{8,9},{9,8},{10,11... | collective-permute-start | bytes 2359304 | tf_op jit(solution)/shard_map/ppermute | solution.py:61
  7.4 10.6 %collective-permute-start.4 = (bf16[256,512]{1,0:T(8,128)(2,1)S(1)}, bf16[256,512]{1,0:T(8,128)(2,1)S(1)}, u32[]{:S(2)}, u32[]{:S(2)}) collective-permute-start(bf16[256,512]{1,0:T(8,128)(2,1)S(1)} %join_teacher.1.refs_0_), channel_id=1, source_target_pairs={{0,8},{1,9},{2,10},{3,11},{4,12},{5,13},{6,14},{7,15},{8,24},{9,25... | collective-permute-start | bytes 786440 | tf_op jit(solution)/shard_map/ppermute | solution.py:61
  10.4 8.5 %collective-permute-start.3 = (bf16[256,512]{1,0:T(8,128)(2,1)S(1)}, bf16[256,512]{1,0:T(8,128)(2,1)S(1)}, u32[]{:S(2)}, u32[]{:S(2)}) collective-permute-start(bf16[256,512]{1,0:T(8,128)(2,1)S(1)} %join_teacher.1.refs_0_), channel_id=1, source_target_pairs={{0,4},{1,5},{2,6},{3,7},{4,0},{5,1},{6,2},{7,3},{8,12},{9,13},{10,... | collective-permute-start | bytes 786440 | tf_op jit(solution)/shard_map/ppermute | solution.py:61
  18.0 8.7 %collective-permute-start.5 = (bf16[256,512]{1,0:T(8,128)(2,1)S(1)}, bf16[256,512]{1,0:T(8,128)(2,1)S(1)}, u32[]{:S(2)}, u32[]{:S(2)}) collective-permute-start(bf16[256,512]{1,0:T(8,128)(2,1)S(1)} %collective-permute-done.4.refs_2_), channel_id=1, source_target_pairs={{0,8},{1,9},{2,10},{3,11},{4,12},{5,13},{6,14},{7,15},{8,24},{9,25... | collective-permute-start | bytes 786440 | tf_op jit(solution)/shard_map/ppermute | solution.py:61
  18.9 10.3 %collective-permute-start.8 = (bf16[256,512]{1,0:T(8,128)(2,1)S(1)}, bf16[256,512]{1,0:T(8,128)(2,1)S(1)}, u32[]{:S(2)}, u32[]{:S(2)}) collective-permute-start(bf16[256,512]{1,0:T(8,128)(2,1)S(1)} %collective-permute-done.4.refs_2_), channel_id=1, source_target_pairs={{0,4},{1,5},{2,6},{3,7},{4,0},{5,1},{6,2},{7,3},{8,12},{9,13},{10,... | collective-permute-start | bytes 786440 | tf_op jit(solution)/shard_map/ppermute | solution.py:61
  20.4 12.7 %collective-permute-start.11 = (bf16[288,512]{1,0:T(8,128)(2,1)S(1)}, bf16[288,512]{1,0:T(8,128)(2,1)S(1)}, u32[]{:S(2)}, u32[]{:S(2)}) collective-permute-start(bf16[288,512]{1,0:T(8,128)(2,1)S(1)} %get-tuple-element.96), channel_id=1, source_target_pairs={{0,1},{1,0},{2,3},{3,2},{4,5},{5,4},{6,7},{7,6},{8,9},{9,8},{10,11... | collective-permute-start | bytes 884744 | tf_op jit(solution)/shard_map/ppermute | solution.py:61
  25.4 5.2 %collective-permute-start.10 = (bf16[256,512]{1,0:T(8,128)(2,1)S(1)}, bf16[256,512]{1,0:T(8,128)(2,1)S(1)}, u32[]{:S(2)}, u32[]{:S(2)}) collective-permute-start(bf16[256,512]{1,0:T(8,128)(2,1)S(1)} %get-tuple-element.89), channel_id=1, source_target_pairs={{0,2},{1,3},{2,0},{3,1},{4,6},{5,7},{6,4},{7,5},{8,10},{9,11},{10,... | collective-permute-start | bytes 786440 | tf_op jit(solution)/shard_map/ppermute | solution.py:61
  25.5 5.2 %collective-permute-start.9 = (bf16[256,512]{1,0:T(8,128)(2,1)S(1)}, bf16[256,512]{1,0:T(8,128)(2,1)S(1)}, u32[]{:S(2)}, u32[]{:S(2)}) collective-permute-start(bf16[256,512]{1,0:T(8,128)(2,1)S(1)} %get-tuple-element.114.par.refs_0_), channel_id=1, source_target_pairs={{0,2},{1,3},{2,0},{3,1},{4,6},{5,7},{6,4},{7,5},{8,10},{9,11},{10,... | collective-permute-start | bytes 786440 | tf_op jit(solution)/shard_map/ppermute | solution.py:61
  26.8 16.0 %collective-permute-start.6 = (bf16[544,512]{1,0:T(8,128)(2,1)S(1)}, bf16[544,512]{1,0:T(8,128)(2,1)S(1)}, u32[]{:S(2)}, u32[]{:S(2)}) collective-permute-start(bf16[544,512]{1,0:T(8,128)(2,1)S(1)} %stack_teacher.1), channel_id=1, source_target_pairs={{0,16},{1,17},{2,18},{3,19},{4,20},{5,21},{6,22},{7,23},{8,0},{9,1... | collective-permute-start | bytes 1671176 | tf_op jit(solution)/shard_map/ppermute | solution.py:61
  29.2 13.6 %collective-permute-start = (bf16[256,1024]{1,0:T(8,128)(2,1)S(1)}, bf16[256,1024]{1,0:T(8,128)(2,1)S(1)}, u32[]{:S(2)}, u32[]{:S(2)}) collective-permute-start(bf16[256,1024]{1,0:T(8,128)(2,1)S(1)} %get-tuple-element.77), channel_id=1, source_target_pairs={{0,1},{1,0},{2,3},{3,2},{4,5},{5,4},{6,7},{7,6},{8,9},{9,8},{10,11... | collective-permute-start | bytes 1572872 | tf_op jit(solution)/shard_map/ppermute | solution.py:61
  31.5 8.1 %collective-permute-start.13 = (bf16[272,512]{1,0:T(8,128)(2,1)S(1)}, bf16[272,512]{1,0:T(8,128)(2,1)S(1)}, u32[]{:S(2)}, u32[]{:S(2)}) collective-permute-start(bf16[272,512]{1,0:T(8,128)(2,1)S(1)} %get-tuple-element.101), channel_id=1, source_target_pairs={{0,4},{1,5},{2,6},{3,7},{4,0},{5,1},{6,2},{7,3},{8,12},{9,13},{10,... | collective-permute-start | bytes 835592 | tf_op jit(solution)/shard_map/ppermute | solution.py:61
  33.1 1.6 %collective-permute-start.12 = (bf16[256,512]{1,0:T(8,128)(2,1)S(1)}, bf16[256,512]{1,0:T(8,128)(2,1)S(1)}, u32[]{:S(2)}, u32[]{:S(2)}) collective-permute-start(bf16[256,512]{1,0:T(8,128)(2,1)S(1)} %take_block.1.par.refs_1_), channel_id=1, source_target_pairs={{0,2},{1,3},{2,0},{3,1},{4,6},{5,7},{6,4},{7,5},{8,10},{9,11},{10,... | collective-permute-start | bytes 786440 | tf_op jit(solution)/shard_map/ppermute | solution.py:61
  39.7 7.5 %collective-permute-start.16 = (bf16[256,512]{1,0:T(8,128)(2,1)S(1)}, bf16[256,512]{1,0:T(8,128)(2,1)S(1)}, u32[]{:S(2)}, u32[]{:S(2)}) collective-permute-start(bf16[256,512]{1,0:T(8,128)(2,1)S(1)} %get-tuple-element.111), channel_id=1, source_target_pairs={{0,4},{1,5},{2,6},{3,7},{4,0},{5,1},{6,2},{7,3},{8,12},{9,13},{10,... | collective-permute-start | bytes 786440 | tf_op jit(solution)/shard_map/ppermute | solution.py:61
  41.3 6.5 %collective-permute-start.17 = (bf16[256,512]{1,0:T(8,128)(2,1)S(1)}, bf16[256,512]{1,0:T(8,128)(2,1)S(1)}, u32[]{:S(2)}, u32[]{:S(2)}) collective-permute-start(bf16[256,512]{1,0:T(8,128)(2,1)S(1)} %add_blocks.3), channel_id=1, source_target_pairs={{0,8},{1,9},{2,10},{3,11},{4,12},{5,13},{6,14},{7,15},{8,0},{9,1},... | collective-permute-start | bytes 786440 | tf_op jit(solution)/shard_map/ppermute | solution.py:61
  42.9 2.1 %collective-permute-start.14 = (bf16[128,512]{1,0:T(8,128)(2,1)S(1)}, bf16[128,512]{1,0:T(8,128)(2,1)S(1)}, u32[]{:S(2)}, u32[]{:S(2)}) collective-permute-start(bf16[128,512]{1,0:T(8,128)(2,1)S(1)} %get-tuple-element.103), channel_id=1, source_target_pairs={{0,2},{1,3},{2,0},{3,1},{4,6},{5,7},{6,4},{7,5},{8,10},{9,11},{10,... | collective-permute-start | bytes 393224 | tf_op jit(solution)/shard_map/ppermute | solution.py:61
  43.0 2.0 %collective-permute-start.15 = (bf16[128,512]{1,0:T(8,128)(2,1)S(1)}, bf16[128,512]{1,0:T(8,128)(2,1)S(1)}, u32[]{:S(2)}, u32[]{:S(2)}) collective-permute-start(bf16[128,512]{1,0:T(8,128)(2,1)S(1)} %get-tuple-element.105), channel_id=1, source_target_pairs={{0,2},{1,3},{2,0},{3,1},{4,6},{5,7},{6,4},{7,5},{8,10},{9,11},{10,... | collective-permute-start | bytes 393224 | tf_op jit(solution)/shard_map/ppermute | solution.py:61
  43.5 9.2 %collective-permute-start.18 = (bf16[256,512]{1,0:T(8,128)(2,1)S(1)}, bf16[256,512]{1,0:T(8,128)(2,1)S(1)}, u32[]{:S(2)}, u32[]{:S(2)}) collective-permute-start(bf16[256,512]{1,0:T(8,128)(2,1)S(1)} %collective-permute-done.5.refs_4_), channel_id=1, source_target_pairs={{0,4},{1,5},{2,6},{3,7},{4,0},{5,1},{6,2},{7,3},{8,12},{9,13},{10,... | collective-permute-start | bytes 786440 | tf_op jit(solution)/shard_map/ppermute | solution.py:61
  45.9 9.2 %collective-permute-start.19 = (bf16[256,512]{1,0:T(8,128)(2,1)S(1)}, bf16[256,512]{1,0:T(8,128)(2,1)S(1)}, u32[]{:S(2)}, u32[]{:S(2)}) collective-permute-start(bf16[256,512]{1,0:T(8,128)(2,1)S(1)} %get-tuple-element.117.refs_3_.par), channel_id=1, source_target_pairs={{0,2},{1,3},{2,0},{3,1},{4,6},{5,7},{6,4},{7,5},{8,10},{9,11},{10,... | collective-permute-start | bytes 786440 | tf_op jit(solution)/shard_map/ppermute | solution.py:61
  45.9 12.4 %collective-permute-start.20 = (bf16[256,512]{1,0:T(8,128)(2,1)S(1)}, bf16[256,512]{1,0:T(8,128)(2,1)S(1)}, u32[]{:S(2)}, u32[]{:S(2)}) collective-permute-start(bf16[256,512]{1,0:T(8,128)(2,1)S(1)} %get-tuple-element.121), channel_id=1, source_target_pairs={{0,4},{1,5},{2,6},{3,7},{4,0},{5,1},{6,2},{7,3},{8,12},{9,13},{10,... | collective-permute-start | bytes 786440 | tf_op jit(solution)/shard_map/ppermute | solution.py:61
  47.9 14.3 %collective-permute-start.24 = (bf16[256,512]{1,0:T(8,128)(2,1)S(1)}, bf16[256,512]{1,0:T(8,128)(2,1)S(1)}, u32[]{:S(2)}, u32[]{:S(2)}) collective-permute-start(bf16[256,512]{1,0:T(8,128)(2,1)S(1)} %add_blocks.4), channel_id=1, source_target_pairs={{0,16},{1,17},{2,18},{3,19},{4,20},{5,21},{6,22},{7,23},{8,24},{9,... | collective-permute-start | bytes 786440 | tf_op jit(solution)/shard_map/ppermute | solution.py:61
  53.5 10.0 %collective-permute-start.21 = (bf16[256,512]{1,0:T(8,128)(2,1)S(1)}, bf16[256,512]{1,0:T(8,128)(2,1)S(1)}, u32[]{:S(2)}, u32[]{:S(2)}) collective-permute-start(bf16[256,512]{1,0:T(8,128)(2,1)S(1)} %far_features.2), channel_id=1, source_target_pairs={{0,1},{1,0},{2,3},{3,2},{4,5},{5,4},{6,7},{7,6},{8,9},{9,8},{10,11... | collective-permute-start | bytes 786440 | tf_op jit(solution)/shard_map/ppermute | solution.py:61
  56.6 8.7 %collective-permute-start.22 = (bf16[256,512]{1,0:T(8,128)(2,1)S(1)}, bf16[256,512]{1,0:T(8,128)(2,1)S(1)}, u32[]{:S(2)}, u32[]{:S(2)}) collective-permute-start(bf16[256,512]{1,0:T(8,128)(2,1)S(1)} %far_features.3), channel_id=1, source_target_pairs={{0,3},{1,2},{2,1},{3,0},{4,7},{5,6},{6,5},{7,4},{8,11},{9,10},{10,... | collective-permute-start | bytes 786440 | tf_op jit(solution)/shard_map/ppermute | solution.py:61
  56.7 8.9 %collective-permute-start.23 = (bf16[256,512]{1,0:T(8,128)(2,1)S(1)}, bf16[256,512]{1,0:T(8,128)(2,1)S(1)}, u32[]{:S(2)}, u32[]{:S(2)}) collective-permute-start(bf16[256,512]{1,0:T(8,128)(2,1)S(1)} %get-tuple-element.125), channel_id=1, source_target_pairs={{0,4},{1,5},{2,6},{3,7},{4,0},{5,1},{6,2},{7,3},{8,12},{9,13},{10,... | collective-permute-start | bytes 786440 | tf_op jit(solution)/shard_map/ppermute | solution.py:61
  58.3 9.4 %collective-permute-start.25 = (bf16[256,512]{1,0:T(8,128)(2,1)S(1)}, bf16[256,512]{1,0:T(8,128)(2,1)S(1)}, u32[]{:S(2)}, u32[]{:S(2)}) collective-permute-start(bf16[256,512]{1,0:T(8,128)(2,1)S(1)} %add_blocks.5), channel_id=1, source_target_pairs={{0,8},{1,9},{2,10},{3,11},{4,12},{5,13},{6,14},{7,15},{8,0},{9,1},... | collective-permute-start | bytes 786440 | tf_op jit(solution)/shard_map/ppermute | solution.py:61
  62.2 5.5 %collective-permute-start.26 = (bf16[240,512]{1,0:T(8,128)(2,1)S(1)}, bf16[240,512]{1,0:T(8,128)(2,1)S(1)}, u32[]{:S(2)}, u32[]{:S(2)}) collective-permute-start(bf16[240,512]{1,0:T(8,128)(2,1)S(1)} %get-tuple-element.127), channel_id=1, source_target_pairs={{0,2},{1,3},{2,0},{3,1},{4,6},{5,7},{6,4},{7,5},{8,10},{9,11},{10,... | collective-permute-start | bytes 737288 | tf_op jit(solution)/shard_map/ppermute | solution.py:61
  62.2 7.6 %copy-start.2 = (f32[128,2048]{1,0:T(8,128)S(1)}, f32[128,2048]{1,0:T(8,128)}, u32[]{:S(2)}) copy-start(f32[128,2048]{1,0:T(8,128)} %refs_2_.5) | copy-start | bytes 3145732
  62.2 7.6 %copy-start.3 = (f32[128,2048]{1,0:T(8,128)S(1)}, f32[128,2048]{1,0:T(8,128)}, u32[]{:S(2)}) copy-start(f32[128,2048]{1,0:T(8,128)} %refs_3_.5) | copy-start | bytes 3145732
  63.5 6.3 %copy-start.1 = (f32[128,2048]{1,0:T(8,128)S(1)}, f32[128,2048]{1,0:T(8,128)}, u32[]{:S(2)}) copy-start(f32[128,2048]{1,0:T(8,128)} %refs_1_.3) | copy-start | bytes 3145732
  63.5 8.0 %collective-permute-start.28 = (bf16[256,512]{1,0:T(8,128)(2,1)S(1)}, bf16[256,512]{1,0:T(8,128)(2,1)S(1)}, u32[]{:S(2)}, u32[]{:S(2)}) collective-permute-start(bf16[256,512]{1,0:T(8,128)(2,1)S(1)} %get-tuple-element.133), channel_id=1, source_target_pairs={{0,2},{1,3},{2,0},{3,1},{4,6},{5,7},{6,4},{7,5},{8,10},{9,11},{10,... | collective-permute-start | bytes 786440 | tf_op jit(solution)/shard_map/ppermute | solution.py:61
  67.9 1.9 %collective-permute-start.27 = (bf16[128,512]{1,0:T(8,128)(2,1)S(1)}, bf16[128,512]{1,0:T(8,128)(2,1)S(1)}, u32[]{:S(2)}, u32[]{:S(2)}) collective-permute-start(bf16[128,512]{1,0:T(8,128)(2,1)S(1)} %get-tuple-element.130), channel_id=1, source_target_pairs={{0,2},{1,3},{2,0},{3,1},{4,6},{5,7},{6,4},{7,5},{8,10},{9,11},{10,... | collective-permute-start | bytes 393224 | tf_op jit(solution)/shard_map/ppermute | solution.py:61
  68.0 6.3 %collective-permute-start.30 = (bf16[128,512]{1,0:T(8,128)(2,1)S(1)}, bf16[128,512]{1,0:T(8,128)(2,1)S(1)}, u32[]{:S(2)}, u32[]{:S(2)}) collective-permute-start(bf16[128,512]{1,0:T(8,128)(2,1)S(1)} %get-tuple-element.129.refs_0_), channel_id=1, source_target_pairs={{0,1},{1,0},{2,3},{3,2},{4,5},{5,4},{6,7},{7,6},{8,9},{9,8},{10,11... | collective-permute-start | bytes 393224 | tf_op jit(solution)/shard_map/ppermute | solution.py:61
  69.6 6.7 %collective-permute-start.29 = (bf16[128,512]{1,0:T(8,128)(2,1)S(1)}, bf16[128,512]{1,0:T(8,128)(2,1)S(1)}, u32[]{:S(2)}, u32[]{:S(2)}) collective-permute-start(bf16[128,512]{1,0:T(8,128)(2,1)S(1)} %get-tuple-element.130), channel_id=1, source_target_pairs={{0,3},{1,2},{2,1},{3,0},{4,7},{5,6},{6,5},{7,4},{8,11},{9,10},{10,... | collective-permute-start | bytes 393224 | tf_op jit(solution)/shard_map/ppermute | solution.py:61

commit v7 on v6

--- a/solution.py
+++ b/solution.py
@@ -201,7 +201,7 @@
                 "gradient_block",
                 terms_body(k),
                 [((2 * rows, part), f32)]
-                + [((2 * rows + extra * (k == 0), part), bf16)] * (ny - 1),
+                + [((2 * rows + extra * (k < 2), part), bf16)] * (ny - 1),
                 [near_own, near_sib, far_par[k], far_dia[k], c_own, c_par, c_dia],
                 scratch=[pltpu.VMEM((span, part), f32)],
             )
@@ -216,10 +216,39 @@
         def add(values, dtype, more=0):
             return run("add_blocks", add_body, [((2 * rows + more, part), dtype)], values)[0]
 
-        def sum_body(*refs):
-            z, y, core, q = place()
-            for out, at in zip(refs[-2:], (aligned(core, rows), aligned(1 - core, rows))):
-                out[...] = sum(ref[at, :].astype(f32) for ref in refs[:-3]).astype(bf16)
+        def halves_sum_body(*refs):
+            z, y, core, q = place()
+            for out, owner in zip(refs[-2:], (1 - core, core)):
+                at = aligned(owner, rows)
+                out[...] = sum(ref[at, :].astype(f32) for ref in refs[:-2]).astype(bf16)
+
+        def rows_sum_body(mine, count):
+            def body(*refs):
+                z, y, core, q = place()
+                at = aligned(core if mine else 1 - core, rows)
+                total = sum(ref[at, :].astype(f32) for ref in refs[:count])
+                total = (total + refs[count][...].astype(f32)).astype(refs[-1].dtype)
+                refs[-1][:rows, :] = total
+                if refs[-1].shape[0] > rows:
+                    refs[-1][rows:, :] = total[: refs[-1].shape[0] - rows, :]
+
+            return body
+
+        def add_rows_body(*refs):
+            refs[-1][...] = sum(ref[...].astype(f32) for ref in refs[:-1]).astype(bf16)
+
+        def gradient_rows(mine, pieces, last, *unread):
+            kind = bf16 if pair_groups == 1 else f32
+            body = rows_sum_body(mine, len(pieces))
+            count = rows if mine else rows + extra
+            (total,) = run("sum_gradient", body, [((count, part), kind)], [*pieces, last, *unread])
+            if pair_groups > 1:
+                sent = total.astype(bf16)
+                others = [start(sent, along_g(dg)) for dg in range(1, pair_groups)]
+                (total,) = run(
+                    "add_groups", add_rows_body, [((count, part), bf16)], [total, *others]
+                )
+            return total
 
         def features_of(blocks, full, out):
             total = sum(
@@ -275,7 +304,7 @@
                 ((count, width), bf16)
                 for count, width in (
                     (tokens, lead + span), (tokens, feat + part), (tokens, part),
-                    (tokens + 2 * extra, span), (tokens, 2 * span), (tokens - extra, part),
+                    (tokens + 2 * extra, span), (tokens, 2 * span), (tokens, part),
                 )
             ],
             [patches, cotangent],
@@ -319,7 +348,7 @@
         (far_par[1],) = run("take_block", first_body, [((tokens, span), bf16)], [block])
         far_dia[1] = start(far_par[1], sibling)
         gradient_block(1)
-        onward = block_sum(3)
+        onward = block_sum(3, more=extra)
         block_y(2, onward)
         teacher_y(2, onward)
         onward = start(onward, across_z(1))
@@ -345,7 +374,10 @@
         gradient_block(3)
         block_y(0)
         f_dia = start(far_features(far_dia), diagonal)
-        back = start(block_sum(1), across_z(1))
+        back = run(
+            "add_halves", halves_sum_body, [((rows, part), bf16)] * 2, [terms[1][0], *moved_y[1]]
+        )
+        back_other, back_mine = [start(half, across_z(1)) for half in back]
         f_own, f_sib = run(
             "near_features",
             near_body,
@@ -354,16 +386,12 @@
         )
         f_sib = start(f_sib, sibling)
         wait(f_par, f_dia)
-        pieces = [terms[0][0], *moved_y[0], onward, back]
+        pieces = [terms[0][0], *moved_y[0], onward]
         spacer = start(mark, sibling, onward)
-        if pair_groups > 1:
-            total = add(pieces, f32)
-            sent = total.astype(bf16)
-            pieces = [total] + [start(sent, along_g(dg)) for dg in range(1, pair_groups)]
-        mine, other = run("sum_gradient", sum_body, [((rows, part), bf16)] * 2, [*pieces, spacer])
-        g_par, g_dia, g_sib = (
-            start(mine, partner), start(other, diagonal), start(other, sibling)
-        )
+        other = gradient_rows(False, pieces, back_other)
+        g_dia, g_sib = start(other, diagonal), start(other, sibling)
+        mine = gradient_rows(True, pieces, back_mine, spacer)
+        g_par = start(mine, partner)
         def update_body(quarters):
             def body(*refs):
                 z, y, core, q = place()
@@ -374,7 +402,7 @@
                 copies = []
                 for i, j in enumerate(quarters):
                     at = (slice(None), aligned(q ^ j, part))
-                    gradient = refs[i][...].astype(f32)
+                    gradient = refs[i][:rows, :].astype(f32)
                     new_first = beta_one * first[at] + (1.0 - beta_one) * gradient
                     new_second = beta_two * second[at] + (1.0 - beta_two) * gradient * gradient
                     direction = new_first / corr_one / (jnp.sqrt(new_second / corr_two) + adam_eps)

time: 77.7 us -> 80 us (1.030)
  starting transfers between devices: 32.9 us -> 35.4 us
    ppermute x31 -> x32, starting transfers between devices: 32.9 us -> 35.4 us  [send(): return lax.ppermute(value, ('fsdp', 'rep'), perm)]
    ppermute x31 -> x32, waiting for transfers between devices: 29 us -> 28.7 us  [send(): return lax.ppermute(value, ('fsdp', 'rep'), perm)]
    pallas_call x21 -> x22, Pallas kernels: 8.02 us -> 8.03 us  [call(): pl.pallas_call(body, out_shape=shapes, in_specs=[VMEM] * len(inputs), out...]
  transfers between devices with their start and end apart: 31 -> 32, of which waited for: 15 -> 13; matrix products, arithmetic and copies ran while one was open for 0% -> 0% of each run, Pallas kernels for 14% -> 13%
where the time goes in v7:
time: 80 us; the launch traced here: 79.9 us
  starting transfers between devices  35.4 us (44%)
  waiting for transfers between devices  28.7 us (36%)
  Pallas kernels  12.3 us (15%)
  local copies, waits for them, and re-layouts  2.54 us (3%)
  between operations  0.91 us (1%)
    ppermute x32, starting transfers between devices, send(): return lax.ppermute(value, ('fsdp', 'rep'), perm)  35.4 us
    ppermute x32, waiting for transfers between devices, send(): return lax.ppermute(value, ('fsdp', 'rep'), perm)  28.7 us
    pallas_call x22, Pallas kernels, call(): pl.pallas_call(body, out_shape=shapes, in_specs=[VMEM] * len(inputs), out...  8.03 us
    pallas_call x3, Pallas kernels, update(): pl.pallas_call(update_body(quarters), out_shape=[jax.ShapeDtypeStruct((ro...  4.24 us
    unnamed x12, local copies, waits for them, and re-layouts  2.54 us
  transfers between devices with their start and end apart: 32, of which 13 were waited for; matrix products, arithmetic and copies ran while one was open for 0% of the time, Pallas kernels for 13%

profile of v7, /device:TPU:0, one launch (start us, length us, event | category | flops | bytes accessed | tf_op | source)
XLA Modules:
  0.0 79.9 jit_solution(10423265854476650877)
XLA Ops:
  0.7 1.3 %copy-done.4 = bf16[256,2048]{1,0:T(8,128)(2,1)S(1)} copy-done((bf16[256,2048]{1,0:T(8,128)(2,1)S(1)}, bf16[256,2048]{1,0:T(8,128)(2,1)}, u32[]{:S(2)}) %copy-start.4) | copy-done | bytes 1048600
  2.0 1.2 %copy-done.5 = bf16[256,2048]{1,0:T(8,128)(2,1)S(1)} copy-done((bf16[256,2048]{1,0:T(8,128)(2,1)S(1)}, bf16[256,2048]{1,0:T(8,128)(2,1)}, u32[]{:S(2)}) %copy-start.5) | copy-done | bytes 1048600
  3.4 0.5 collective-permute-start.2
  4.1 2.9 %collective-permute-start.7 = (bf16[256,1536]{1,0:T(8,128)(2,1)S(1)}, bf16[256,1536]{1,0:T(8,128)(2,1)S(1)}, u32[]{:S(2)}, u32[]{:S(2)}) collective-permute-start(bf16[256,1536]{1,0:T(8,128)(2,1)S(1)} %get-tuple-element.79), channel_id=1, source_target_pairs={{0,1},{1,0},{2,3},{3,2},{4,5},{5,4},{6,7},{7,6},{8,9},{9,8},{10,11... | collective-permute-start | bytes 2359304 | tf_op jit(solution)/shard_map/ppermute | solution.py:61
  7.1 0.3 collective-permute-done.1.sib
  7.4 3.0 %collective-permute-start.4 = (bf16[256,512]{1,0:T(8,128)(2,1)S(1)}, bf16[256,512]{1,0:T(8,128)(2,1)S(1)}, u32[]{:S(2)}, u32[]{:S(2)}) collective-permute-start(bf16[256,512]{1,0:T(8,128)(2,1)S(1)} %join_teacher.1.refs_0_), channel_id=1, source_target_pairs={{0,8},{1,9},{2,10},{3,11},{4,12},{5,13},{6,14},{7,15},{8,24},{9,25... | collective-permute-start | bytes 786440 | tf_op jit(solution)/shard_map/ppermute | solution.py:61
  10.4 1.5 %collective-permute-start.3 = (bf16[256,512]{1,0:T(8,128)(2,1)S(1)}, bf16[256,512]{1,0:T(8,128)(2,1)S(1)}, u32[]{:S(2)}, u32[]{:S(2)}) collective-permute-start(bf16[256,512]{1,0:T(8,128)(2,1)S(1)} %join_teacher.1.refs_0_), channel_id=1, source_target_pairs={{0,4},{1,5},{2,6},{3,7},{4,0},{5,1},{6,2},{7,3},{8,12},{9,13},{10,... | collective-permute-start | bytes 786440 | tf_op jit(solution)/shard_map/ppermute | solution.py:61
  11.9 6.1 %collective-permute-done.4.refs_2_ = bf16[256,512]{1,0:T(8,128)(2,1)S(1)} collective-permute-done((bf16[256,512]{1,0:T(8,128)(2,1)S(1)}, bf16[256,512]{1,0:T(8,128)(2,1)S(1)}, u32[]{:S(2)}, u32[]{:S(2)}) %collective-permute-start.4) | collective-permute-done | bytes 262176 | tf_op jit(solution)/shard_map/ppermute | solution.py:61
  18.0 0.8 %collective-permute-start.5 = (bf16[256,512]{1,0:T(8,128)(2,1)S(1)}, bf16[256,512]{1,0:T(8,128)(2,1)S(1)}, u32[]{:S(2)}, u32[]{:S(2)}) collective-permute-start(bf16[256,512]{1,0:T(8,128)(2,1)S(1)} %collective-permute-done.4.refs_2_), channel_id=1, source_target_pairs={{0,8},{1,9},{2,10},{3,11},{4,12},{5,13},{6,14},{7,15},{8,24},{9,25... | collective-permute-start | bytes 786440 | tf_op jit(solution)/shard_map/ppermute | solution.py:61
  18.9 1.5 %collective-permute-start.8 = (bf16[256,512]{1,0:T(8,128)(2,1)S(1)}, bf16[256,512]{1,0:T(8,128)(2,1)S(1)}, u32[]{:S(2)}, u32[]{:S(2)}) collective-permute-start(bf16[256,512]{1,0:T(8,128)(2,1)S(1)} %collective-permute-done.4.refs_2_), channel_id=1, source_target_pairs={{0,4},{1,5},{2,6},{3,7},{4,0},{5,1},{6,2},{7,3},{8,12},{9,13},{10,... | collective-permute-start | bytes 786440 | tf_op jit(solution)/shard_map/ppermute | solution.py:61
  20.4 1.5 %collective-permute-start.11 = (bf16[288,512]{1,0:T(8,128)(2,1)S(1)}, bf16[288,512]{1,0:T(8,128)(2,1)S(1)}, u32[]{:S(2)}, u32[]{:S(2)}) collective-permute-start(bf16[288,512]{1,0:T(8,128)(2,1)S(1)} %get-tuple-element.97), channel_id=1, source_target_pairs={{0,1},{1,0},{2,3},{3,2},{4,5},{5,4},{6,7},{7,6},{8,9},{9,8},{10,11... | collective-permute-start | bytes 884744 | tf_op jit(solution)/shard_map/ppermute | solution.py:61
  21.9 4.8 %collective-permute-done.5.refs_4_ = bf16[256,512]{1,0:T(8,128)(2,1)S(1)} collective-permute-done((bf16[256,512]{1,0:T(8,128)(2,1)S(1)}, bf16[256,512]{1,0:T(8,128)(2,1)S(1)}, u32[]{:S(2)}, u32[]{:S(2)}) %collective-permute-start.5) | collective-permute-done | bytes 262176 | tf_op jit(solution)/shard_map/ppermute | solution.py:61
  26.8 1.3 %collective-permute-start.6 = (bf16[544,512]{1,0:T(8,128)(2,1)S(1)}, bf16[544,512]{1,0:T(8,128)(2,1)S(1)}, u32[]{:S(2)}, u32[]{:S(2)}) collective-permute-start(bf16[544,512]{1,0:T(8,128)(2,1)S(1)} %stack_teacher.1), channel_id=1, source_target_pairs={{0,16},{1,17},{2,18},{3,19},{4,20},{5,21},{6,22},{7,23},{8,0},{9,1... | collective-permute-start | bytes 1671176 | tf_op jit(solution)/shard_map/ppermute | solution.py:61
  28.2 0.5 collective-permute-start.9
  28.7 1.5 %collective-permute-start = (bf16[256,1024]{1,0:T(8,128)(2,1)S(1)}, bf16[256,1024]{1,0:T(8,128)(2,1)S(1)}, u32[]{:S(2)}, u32[]{:S(2)}) collective-permute-start(bf16[256,1024]{1,0:T(8,128)(2,1)S(1)} %get-tuple-element.78), channel_id=1, source_target_pairs={{0,1},{1,0},{2,3},{3,2},{4,5},{5,4},{6,7},{7,6},{8,9},{9,8},{10,11... | collective-permute-start | bytes 1572872 | tf_op jit(solution)/shard_map/ppermute | solution.py:61
  30.2 0.8 %gradient_block.4 = (f32[256,512]{1,0:T(8,128)S(1)}, bf16[272,512]{1,0:T(8,128)(2,1)S(1)}) custom-call(bf16[256,2560]{1,0:T(8,128)(2,1)S(1)} %get-tuple-element.124.own, bf16[256,2560]{1,0:T(8,128)(2,1)S(1)} %collective-permute-done.2.sib, bf16[256,512]{1,0:T(8,128)(2,1)S(1)} %get-tuple-element.115.par.refs_0_, ...), custom_call_target="tpu_custom_call" | custom-call | flops 1 | bytes 1 | tf_op jit(solution)/shard_map/gradient_block/pallas_call | solution.py:29
  31.0 1.6 %collective-permute-start.13 = (bf16[272,512]{1,0:T(8,128)(2,1)S(1)}, bf16[272,512]{1,0:T(8,128)(2,1)S(1)}, u32[]{:S(2)}, u32[]{:S(2)}) collective-permute-start(bf16[272,512]{1,0:T(8,128)(2,1)S(1)} %get-tuple-element.102), channel_id=1, source_target_pairs={{0,4},{1,5},{2,6},{3,7},{4,0},{5,1},{6,2},{7,3},{8,12},{9,13},{10,... | collective-permute-start | bytes 835592 | tf_op jit(solution)/shard_map/ppermute | solution.py:61
  32.7 1.5 %collective-permute-done.12.dia.refs_1_ = bf16[256,512]{1,0:T(8,128)(2,1)S(1)} collective-permute-done((bf16[256,512]{1,0:T(8,128)(2,1)S(1)}, bf16[256,512]{1,0:T(8,128)(2,1)S(1)}, u32[]{:S(2)}, u32[]{:S(2)}) %collective-permute-start.12) | collective-permute-done | bytes 262176 | tf_op jit(solution)/shard_map/ppermute | solution.py:61
  34.2 0.8 %gradient_block.5 = (f32[256,512]{1,0:T(8,128)S(1)}, bf16[272,512]{1,0:T(8,128)(2,1)S(1)}) custom-call(bf16[256,2560]{1,0:T(8,128)(2,1)S(1)} %get-tuple-element.124.own, bf16[256,2560]{1,0:T(8,128)(2,1)S(1)} %collective-permute-done.2.sib, bf16[256,512]{1,0:T(8,128)(2,1)S(1)} %take_block.1.par.refs_1_, ...), custom_call_target="tpu_custom_call" | custom-call | flops 1 | bytes 1 | tf_op jit(solution)/shard_map/gradient_block/pallas_call | solution.py:29
  35.1 4.6 %collective-permute-done.13.refs_1_ = bf16[272,512]{1,0:T(8,128)(2,1)S(1)} collective-permute-done((bf16[272,512]{1,0:T(8,128)(2,1)S(1)}, bf16[272,512]{1,0:T(8,128)(2,1)S(1)}, u32[]{:S(2)}, u32[]{:S(2)}) %collective-permute-start.13) | collective-permute-done | bytes 278560 | tf_op jit(solution)/shard_map/ppermute | solution.py:61
  39.7 1.6 %collective-permute-start.16 = (bf16[272,512]{1,0:T(8,128)(2,1)S(1)}, bf16[272,512]{1,0:T(8,128)(2,1)S(1)}, u32[]{:S(2)}, u32[]{:S(2)}) collective-permute-start(bf16[272,512]{1,0:T(8,128)(2,1)S(1)} %get-tuple-element.112), channel_id=1, source_target_pairs={{0,4},{1,5},{2,6},{3,7},{4,0},{5,1},{6,2},{7,3},{8,12},{9,13},{10,... | collective-permute-start | bytes 835592 | tf_op jit(solution)/shard_map/ppermute | solution.py:61
  41.3 0.5 collective-permute-start.17
  41.8 0.8 collective-permute-done.message
  42.7 0.5 collective-permute-start.15
  43.2 1.6 %collective-permute-start.18 = (bf16[256,512]{1,0:T(8,128)(2,1)S(1)}, bf16[256,512]{1,0:T(8,128)(2,1)S(1)}, u32[]{:S(2)}, u32[]{:S(2)}) collective-permute-start(bf16[256,512]{1,0:T(8,128)(2,1)S(1)} %collective-permute-done.5.refs_4_), channel_id=1, source_target_pairs={{0,4},{1,5},{2,6},{3,7},{4,0},{5,1},{6,2},{7,3},{8,12},{9,13},{10,... | collective-permute-start | bytes 786440 | tf_op jit(solution)/shard_map/ppermute | solution.py:61
  44.8 0.8 %gradient_block.6 = (f32[256,512]{1,0:T(8,128)S(1)}, bf16[256,512]{1,0:T(8,128)(2,1)S(1)}) custom-call(bf16[256,2560]{1,0:T(8,128)(2,1)S(1)} %get-tuple-element.124.own, bf16[256,2560]{1,0:T(8,128)(2,1)S(1)} %collective-permute-done.2.sib, bf16[256,512]{1,0:T(8,128)(2,1)S(1)} %get-tuple-element.108.par.refs_2_, bf16[256,512]{1,0:T(8,128)(2,1)S(1)} %join_pieces.1.dia.refs_2_, ...), custom_call_target="tpu_custom_call" | custom-call | flops 1 | bytes 1 | tf_op jit(solution)/shard_map/gradient_block/pallas_call | solution.py:29
  45.8 3.4 %collective-permute-done.16.refs_1_ = bf16[272,512]{1,0:T(8,128)(2,1)S(1)} collective-permute-done((bf16[272,512]{1,0:T(8,128)(2,1)S(1)}, bf16[272,512]{1,0:T(8,128)(2,1)S(1)}, u32[]{:S(2)}, u32[]{:S(2)}) %collective-permute-start.16) | collective-permute-done | bytes 278560 | tf_op jit(solution)/shard_map/ppermute | solution.py:61
  49.2 2.7 %collective-permute-start.24 = (bf16[256,512]{1,0:T(8,128)(2,1)S(1)}, bf16[256,512]{1,0:T(8,128)(2,1)S(1)}, u32[]{:S(2)}, u32[]{:S(2)}) collective-permute-start(bf16[256,512]{1,0:T(8,128)(2,1)S(1)} %add_blocks.3), channel_id=1, source_target_pairs={{0,16},{1,17},{2,18},{3,19},{4,20},{5,21},{6,22},{7,23},{8,24},{9,... | collective-permute-start | bytes 786440 | tf_op jit(solution)/shard_map/ppermute | solution.py:61
  51.9 1.5 %collective-permute-start.20 = (bf16[256,512]{1,0:T(8,128)(2,1)S(1)}, bf16[256,512]{1,0:T(8,128)(2,1)S(1)}, u32[]{:S(2)}, u32[]{:S(2)}) collective-permute-start(bf16[256,512]{1,0:T(8,128)(2,1)S(1)} %get-tuple-element.122), channel_id=1, source_target_pairs={{0,4},{1,5},{2,6},{3,7},{4,0},{5,1},{6,2},{7,3},{8,12},{9,13},{10,... | collective-permute-start | bytes 786440 | tf_op jit(solution)/shard_map/ppermute | solution.py:61
  53.4 0.9 %collective-permute-done.18.refs_5_ = bf16[256,512]{1,0:T(8,128)(2,1)S(1)} collective-permute-done((bf16[256,512]{1,0:T(8,128)(2,1)S(1)}, bf16[256,512]{1,0:T(8,128)(2,1)S(1)}, u32[]{:S(2)}, u32[]{:S(2)}) %collective-permute-start.18) | collective-permute-done | bytes 262176 | tf_op jit(solution)/shard_map/ppermute | solution.py:61
  54.6 0.7 far_features.2
  55.3 1.5 %collective-permute-start.21 = (bf16[256,512]{1,0:T(8,128)(2,1)S(1)}, bf16[256,512]{1,0:T(8,128)(2,1)S(1)}, u32[]{:S(2)}, u32[]{:S(2)}) collective-permute-start(bf16[256,512]{1,0:T(8,128)(2,1)S(1)} %far_features.2), channel_id=1, source_target_pairs={{0,1},{1,0},{2,3},{3,2},{4,5},{5,4},{6,7},{7,6},{8,9},{9,8},{10,11... | collective-permute-start | bytes 786440 | tf_op jit(solution)/shard_map/ppermute | solution.py:61
  56.8 0.8 %gradient_block.7 = (f32[256,512]{1,0:T(8,128)S(1)}, bf16[256,512]{1,0:T(8,128)(2,1)S(1)}) custom-call(bf16[256,2560]{1,0:T(8,128)(2,1)S(1)} %get-tuple-element.124.own, bf16[256,2560]{1,0:T(8,128)(2,1)S(1)} %collective-permute-done.2.sib, bf16[256,512]{1,0:T(8,128)(2,1)S(1)} %get-tuple-element.118.refs_3_.par, ...), custom_call_target="tpu_custom_call" | custom-call | flops 1 | bytes 1 | tf_op jit(solution)/shard_map/gradient_block/pallas_call | solution.py:29
  57.7 0.7 far_features.3
  58.5 2.2 %collective-permute-start.23 = (bf16[256,512]{1,0:T(8,128)(2,1)S(1)}, bf16[256,512]{1,0:T(8,128)(2,1)S(1)}, u32[]{:S(2)}, u32[]{:S(2)}) collective-permute-start(bf16[256,512]{1,0:T(8,128)(2,1)S(1)} %get-tuple-element.127), channel_id=1, source_target_pairs={{0,4},{1,5},{2,6},{3,7},{4,0},{5,1},{6,2},{7,3},{8,12},{9,13},{10,... | collective-permute-start | bytes 786440 | tf_op jit(solution)/shard_map/ppermute | solution.py:61
  60.6 1.0 %collective-permute-done.24.refs_2_ = bf16[256,512]{1,0:T(8,128)(2,1)S(1)} collective-permute-done((bf16[256,512]{1,0:T(8,128)(2,1)S(1)}, bf16[256,512]{1,0:T(8,128)(2,1)S(1)}, u32[]{:S(2)}, u32[]{:S(2)}) %collective-permute-start.24) | collective-permute-done | bytes 262176 | tf_op jit(solution)/shard_map/ppermute | solution.py:61
  62.0 1.2 %near_features.1 = (bf16[256,512]{1,0:T(8,128)(2,1)S(1)}, bf16[256,512]{1,0:T(8,128)(2,1)S(1)}) custom-call(bf16[256,2560]{1,0:T(8,128)(2,1)S(1)} %get-tuple-element.124.own, bf16[256,2560]{1,0:T(8,128)(2,1)S(1)} %collective-permute-done.2.sib, bf16[2048,512]{1,0:T(8,128)(2,1)S(1)} %fill_teacher.1.refs_4_.full), custom_call_target="tpu_custom_call" | custom-call | flops 1 | bytes 1 | tf_op jit(solution)/shard_map/near_features/pallas_call | solution.py:29
  63.3 1.8 %collective-permute-start.26 = (bf16[128,512]{1,0:T(8,128)(2,1)S(1)}, bf16[128,512]{1,0:T(8,128)(2,1)S(1)}, u32[]{:S(2)}, u32[]{:S(2)}) collective-permute-start(bf16[128,512]{1,0:T(8,128)(2,1)S(1)} %get-tuple-element.129), channel_id=1, source_target_pairs={{0,8},{1,9},{2,10},{3,11},{4,12},{5,13},{6,14},{7,15},{8,0},{9,1},... | collective-permute-start | bytes 393224 | tf_op jit(solution)/shard_map/ppermute | solution.py:61
  65.1 2.0 %collective-permute-done.22.refs_3_ = bf16[256,512]{1,0:T(8,128)(2,1)S(1)} collective-permute-done((bf16[256,512]{1,0:T(8,128)(2,1)S(1)}, bf16[256,512]{1,0:T(8,128)(2,1)S(1)}, u32[]{:S(2)}, u32[]{:S(2)}) %collective-permute-start.22) | collective-permute-done | bytes 262176 | tf_op jit(solution)/shard_map/ppermute | solution.py:61
  67.5 0.6 collective-permute-done.25.refs_3_
  68.2 1.9 %collective-permute-start.30 = (bf16[144,512]{1,0:T(8,128)(2,1)S(1)}, bf16[144,512]{1,0:T(8,128)(2,1)S(1)}, u32[]{:S(2)}, u32[]{:S(2)}) collective-permute-start(bf16[144,512]{1,0:T(8,128)(2,1)S(1)} %sum_gradient.2), channel_id=1, source_target_pairs={{0,3},{1,2},{2,1},{3,0},{4,7},{5,6},{6,5},{7,4},{8,11},{9,10},{10,... | collective-permute-start | bytes 442376 | tf_op jit(solution)/shard_map/ppermute | solution.py:61
  70.1 0.4 collective-permute-done.26.refs_3_
  70.6 1.8 %collective-permute-start.31 = (bf16[128,512]{1,0:T(8,128)(2,1)S(1)}, bf16[128,512]{1,0:T(8,128)(2,1)S(1)}, u32[]{:S(2)}, u32[]{:S(2)}) collective-permute-start(bf16[128,512]{1,0:T(8,128)(2,1)S(1)} %sum_gradient.3.refs_0_), channel_id=1, source_target_pairs={{0,1},{1,0},{2,3},{3,2},{4,5},{5,4},{6,7},{7,6},{8,9},{9,8},{10,11... | collective-permute-start | bytes 393224 | tf_op jit(solution)/shard_map/ppermute | solution.py:61
  72.4 1.7 %update_near.1 = (f32[128,2048]{1,0:T(8,128)}, f32[128,2048]{1,0:T(8,128)}, f32[128,2048]{1,0:T(8,128)}, f32[128,2048]{1,0:T(8,128)}) custom-call(bf16[128,512]{1,0:T(8,128)(2,1)S(1)} %sum_gradient.3.refs_0_, bf16[144,512]{1,0:T(8,128)(2,1)S(1)} %collective-permute-done.28.refs_1_, f32[128,2048]{1,0:T(8,128)S(1)} %copy-done.1, f32[128,2048]{1,0:T(8,128)S(1)} %copy-done.2, ...), custom_call_target="tpu_custom_call" | custom-call | flops 1 | bytes 1 | tf_op jit(solution)/shard_map/update_near/pallas_call | solution.py:429
  74.1 1.1 %place_features.1 = bf16[256,2048]{1,0:T(8,128)(2,1)} custom-call(bf16[256,512]{1,0:T(8,128)(2,1)S(1)} %get-tuple-element.134.refs_0_, bf16[256,512]{1,0:T(8,128)(2,1)S(1)} %collective-permute-done.29.refs_1_, bf16[256,512]{1,0:T(8,128)(2,1)S(1)} %collective-permute-done.21.refs_2_, bf16[256,512]{1,0:T(8,128)(2,1)S(1)} %collective-permute-done.22.refs_3_), custom_call_target="tpu_custom_call" | custom-call | flops 1 | bytes 1 | tf_op jit(solution)/shard_map/place_features/pallas_call | solution.py:29
  75.2 2.1 %collective-permute-done.31.refs_0_ = bf16[128,512]{1,0:T(8,128)(2,1)S(1)} collective-permute-done((bf16[128,512]{1,0:T(8,128)(2,1)S(1)}, bf16[128,512]{1,0:T(8,128)(2,1)S(1)}, u32[]{:S(2)}, u32[]{:S(2)}) %collective-permute-start.31) | collective-permute-done | bytes 131104 | tf_op jit(solution)/shard_map/ppermute | solution.py:61
  77.3 1.3 %update_partner.1 = (f32[128,2048]{1,0:T(8,128)}, f32[128,2048]{1,0:T(8,128)}, f32[128,2048]{1,0:T(8,128)}, f32[128,2048]{1,0:T(8,128)}) custom-call(bf16[128,512]{1,0:T(8,128)(2,1)S(1)} %collective-permute-done.31.refs_0_, f32[128,2048]{1,0:T(8,128)S(1)} %copy-done.1, ...), custom_call_target="tpu_custom_call", output_to_operand_aliasing={{0}: (5, {}), {1}: (6, {}), {2}: (7, {}), {3}: (8, {})} | custom-call | flops 1 | bytes 1 | tf_op jit(solution)/shard_map/update_partner/pallas_call | solution.py:429
  78.6 1.3 %update_diagonal.1 = (f32[128,2048]{1,0:T(8,128)}, f32[128,2048]{1,0:T(8,128)}, f32[128,2048]{1,0:T(8,128)}, f32[128,2048]{1,0:T(8,128)}) custom-call(bf16[144,512]{1,0:T(8,128)(2,1)S(1)} %collective-permute-done.30.refs_0_, f32[128,2048]{1,0:T(8,128)S(1)} %copy-done.1, ...), custom_call_target="tpu_custom_call", output_to_operand_aliasing={{0}: (5, {}), {1}: (6, {}), {2}: (7, {}), {3}: (8, {})} | custom-call | flops 1 | bytes 1 | tf_op jit(solution)/shard_map/update_diagonal/pallas_call | solution.py:429
  (53 shorter events, 2.3 us)
Async XLA Ops:
  0.6 3.3 %copy-start = (f32[128,2048]{1,0:T(8,128)S(1)}, f32[128,2048]{1,0:T(8,128)}, u32[]{:S(2)}) copy-start(f32[128,2048]{1,0:T(8,128)} %refs_4_.5) | copy-start | bytes 3145732
  0.6 1.3 %copy-start.4 = (bf16[256,2048]{1,0:T(8,128)(2,1)S(1)}, bf16[256,2048]{1,0:T(8,128)(2,1)}, u32[]{:S(2)}) copy-start(bf16[256,2048]{1,0:T(8,128)(2,1)} %p.1) | copy-start | bytes 3145732
  2.0 1.2 %copy-start.5 = (bf16[256,2048]{1,0:T(8,128)(2,1)S(1)}, bf16[256,2048]{1,0:T(8,128)(2,1)}, u32[]{:S(2)}) copy-start(bf16[256,2048]{1,0:T(8,128)(2,1)} %c.1) | copy-start | bytes 3145732
  3.4 18.5 %collective-permute-start.2 = (bf16[256,2560]{1,0:T(8,128)(2,1)S(1)}, bf16[256,2560]{1,0:T(8,128)(2,1)S(1)}, u32[]{:S(2)}, u32[]{:S(2)}) collective-permute-start(bf16[256,2560]{1,0:T(8,128)(2,1)S(1)} %get-tuple-element.124.own), channel_id=1, source_target_pairs={{0,2},{1,3},{2,0},{3,1},{4,6},{5,7},{6,4},{7,5},{8,10},{9,11},{10,... | collective-permute-start | bytes 3932168 | tf_op jit(solution)/shard_map/ppermute | solution.py:61
  4.0 3.4 %collective-permute-start.1 = (bf16[544,512]{1,0:T(8,128)(2,1)S(1)}, bf16[544,512]{1,0:T(8,128)(2,1)S(1)}, u32[]{:S(2)}, u32[]{:S(2)}) collective-permute-start(bf16[544,512]{1,0:T(8,128)(2,1)S(1)} %get-tuple-element.83), channel_id=1, source_target_pairs={{0,2},{1,3},{2,0},{3,1},{4,6},{5,7},{6,4},{7,5},{8,10},{9,11},{10,... | collective-permute-start | bytes 1671176 | tf_op jit(solution)/shard_map/ppermute | solution.py:61
  4.1 23.9 %collective-permute-start.7 = (bf16[256,1536]{1,0:T(8,128)(2,1)S(1)}, bf16[256,1536]{1,0:T(8,128)(2,1)S(1)}, u32[]{:S(2)}, u32[]{:S(2)}) collective-permute-start(bf16[256,1536]{1,0:T(8,128)(2,1)S(1)} %get-tuple-element.79), channel_id=1, source_target_pairs={{0,1},{1,0},{2,3},{3,2},{4,5},{5,4},{6,7},{7,6},{8,9},{9,8},{10,11... | collective-permute-start | bytes 2359304 | tf_op jit(solution)/shard_map/ppermute | solution.py:61
  7.4 10.6 %collective-permute-start.4 = (bf16[256,512]{1,0:T(8,128)(2,1)S(1)}, bf16[256,512]{1,0:T(8,128)(2,1)S(1)}, u32[]{:S(2)}, u32[]{:S(2)}) collective-permute-start(bf16[256,512]{1,0:T(8,128)(2,1)S(1)} %join_teacher.1.refs_0_), channel_id=1, source_target_pairs={{0,8},{1,9},{2,10},{3,11},{4,12},{5,13},{6,14},{7,15},{8,24},{9,25... | collective-permute-start | bytes 786440 | tf_op jit(solution)/shard_map/ppermute | solution.py:61
  10.4 8.5 %collective-permute-start.3 = (bf16[256,512]{1,0:T(8,128)(2,1)S(1)}, bf16[256,512]{1,0:T(8,128)(2,1)S(1)}, u32[]{:S(2)}, u32[]{:S(2)}) collective-permute-start(bf16[256,512]{1,0:T(8,128)(2,1)S(1)} %join_teacher.1.refs_0_), channel_id=1, source_target_pairs={{0,4},{1,5},{2,6},{3,7},{4,0},{5,1},{6,2},{7,3},{8,12},{9,13},{10,... | collective-permute-start | bytes 786440 | tf_op jit(solution)/shard_map/ppermute | solution.py:61
  18.0 8.7 %collective-permute-start.5 = (bf16[256,512]{1,0:T(8,128)(2,1)S(1)}, bf16[256,512]{1,0:T(8,128)(2,1)S(1)}, u32[]{:S(2)}, u32[]{:S(2)}) collective-permute-start(bf16[256,512]{1,0:T(8,128)(2,1)S(1)} %collective-permute-done.4.refs_2_), channel_id=1, source_target_pairs={{0,8},{1,9},{2,10},{3,11},{4,12},{5,13},{6,14},{7,15},{8,24},{9,25... | collective-permute-start | bytes 786440 | tf_op jit(solution)/shard_map/ppermute | solution.py:61
  18.9 9.8 %collective-permute-start.8 = (bf16[256,512]{1,0:T(8,128)(2,1)S(1)}, bf16[256,512]{1,0:T(8,128)(2,1)S(1)}, u32[]{:S(2)}, u32[]{:S(2)}) collective-permute-start(bf16[256,512]{1,0:T(8,128)(2,1)S(1)} %collective-permute-done.4.refs_2_), channel_id=1, source_target_pairs={{0,4},{1,5},{2,6},{3,7},{4,0},{5,1},{6,2},{7,3},{8,12},{9,13},{10,... | collective-permute-start | bytes 786440 | tf_op jit(solution)/shard_map/ppermute | solution.py:61
  20.4 12.2 %collective-permute-start.11 = (bf16[288,512]{1,0:T(8,128)(2,1)S(1)}, bf16[288,512]{1,0:T(8,128)(2,1)S(1)}, u32[]{:S(2)}, u32[]{:S(2)}) collective-permute-start(bf16[288,512]{1,0:T(8,128)(2,1)S(1)} %get-tuple-element.97), channel_id=1, source_target_pairs={{0,1},{1,0},{2,3},{3,2},{4,5},{5,4},{6,7},{7,6},{8,9},{9,8},{10,11... | collective-permute-start | bytes 884744 | tf_op jit(solution)/shard_map/ppermute | solution.py:61
  26.8 15.8 %collective-permute-start.6 = (bf16[544,512]{1,0:T(8,128)(2,1)S(1)}, bf16[544,512]{1,0:T(8,128)(2,1)S(1)}, u32[]{:S(2)}, u32[]{:S(2)}) collective-permute-start(bf16[544,512]{1,0:T(8,128)(2,1)S(1)} %stack_teacher.1), channel_id=1, source_target_pairs={{0,16},{1,17},{2,18},{3,19},{4,20},{5,21},{6,22},{7,23},{8,0},{9,1... | collective-permute-start | bytes 1671176 | tf_op jit(solution)/shard_map/ppermute | solution.py:61
  28.1 2.1 %collective-permute-start.10 = (bf16[256,512]{1,0:T(8,128)(2,1)S(1)}, bf16[256,512]{1,0:T(8,128)(2,1)S(1)}, u32[]{:S(2)}, u32[]{:S(2)}) collective-permute-start(bf16[256,512]{1,0:T(8,128)(2,1)S(1)} %get-tuple-element.90), channel_id=1, source_target_pairs={{0,2},{1,3},{2,0},{3,1},{4,6},{5,7},{6,4},{7,5},{8,10},{9,11},{10,... | collective-permute-start | bytes 786440 | tf_op jit(solution)/shard_map/ppermute | solution.py:61
  28.2 2.0 %collective-permute-start.9 = (bf16[256,512]{1,0:T(8,128)(2,1)S(1)}, bf16[256,512]{1,0:T(8,128)(2,1)S(1)}, u32[]{:S(2)}, u32[]{:S(2)}) collective-permute-start(bf16[256,512]{1,0:T(8,128)(2,1)S(1)} %get-tuple-element.115.par.refs_0_), channel_id=1, source_target_pairs={{0,2},{1,3},{2,0},{3,1},{4,6},{5,7},{6,4},{7,5},{8,10},{9,11},{10,... | collective-permute-start | bytes 786440 | tf_op jit(solution)/shard_map/ppermute | solution.py:61
  28.7 13.9 %collective-permute-start = (bf16[256,1024]{1,0:T(8,128)(2,1)S(1)}, bf16[256,1024]{1,0:T(8,128)(2,1)S(1)}, u32[]{:S(2)}, u32[]{:S(2)}) collective-permute-start(bf16[256,1024]{1,0:T(8,128)(2,1)S(1)} %get-tuple-element.78), channel_id=1, source_target_pairs={{0,1},{1,0},{2,3},{3,2},{4,5},{5,4},{6,7},{7,6},{8,9},{9,8},{10,11... | collective-permute-start | bytes 1572872 | tf_op jit(solution)/shard_map/ppermute | solution.py:61
  31.0 8.7 %collective-permute-start.13 = (bf16[272,512]{1,0:T(8,128)(2,1)S(1)}, bf16[272,512]{1,0:T(8,128)(2,1)S(1)}, u32[]{:S(2)}, u32[]{:S(2)}) collective-permute-start(bf16[272,512]{1,0:T(8,128)(2,1)S(1)} %get-tuple-element.102), channel_id=1, source_target_pairs={{0,4},{1,5},{2,6},{3,7},{4,0},{5,1},{6,2},{7,3},{8,12},{9,13},{10,... | collective-permute-start | bytes 835592 | tf_op jit(solution)/shard_map/ppermute | solution.py:61
  32.6 1.6 %collective-permute-start.12 = (bf16[256,512]{1,0:T(8,128)(2,1)S(1)}, bf16[256,512]{1,0:T(8,128)(2,1)S(1)}, u32[]{:S(2)}, u32[]{:S(2)}) collective-permute-start(bf16[256,512]{1,0:T(8,128)(2,1)S(1)} %take_block.1.par.refs_1_), channel_id=1, source_target_pairs={{0,2},{1,3},{2,0},{3,1},{4,6},{5,7},{6,4},{7,5},{8,10},{9,11},{10,... | collective-permute-start | bytes 786440 | tf_op jit(solution)/shard_map/ppermute | solution.py:61
  39.7 9.4 %collective-permute-start.16 = (bf16[272,512]{1,0:T(8,128)(2,1)S(1)}, bf16[272,512]{1,0:T(8,128)(2,1)S(1)}, u32[]{:S(2)}, u32[]{:S(2)}) collective-permute-start(bf16[272,512]{1,0:T(8,128)(2,1)S(1)} %get-tuple-element.112), channel_id=1, source_target_pairs={{0,4},{1,5},{2,6},{3,7},{4,0},{5,1},{6,2},{7,3},{8,12},{9,13},{10,... | collective-permute-start | bytes 835592 | tf_op jit(solution)/shard_map/ppermute | solution.py:61
  41.3 7.8 %collective-permute-start.17 = (bf16[272,512]{1,0:T(8,128)(2,1)S(1)}, bf16[272,512]{1,0:T(8,128)(2,1)S(1)}, u32[]{:S(2)}, u32[]{:S(2)}) collective-permute-start(bf16[272,512]{1,0:T(8,128)(2,1)S(1)} %add_blocks.2), channel_id=1, source_target_pairs={{0,8},{1,9},{2,10},{3,11},{4,12},{5,13},{6,14},{7,15},{8,0},{9,1},... | collective-permute-start | bytes 835592 | tf_op jit(solution)/shard_map/ppermute | solution.py:61
  42.6 2.2 %collective-permute-start.14 = (bf16[128,512]{1,0:T(8,128)(2,1)S(1)}, bf16[128,512]{1,0:T(8,128)(2,1)S(1)}, u32[]{:S(2)}, u32[]{:S(2)}) collective-permute-start(bf16[128,512]{1,0:T(8,128)(2,1)S(1)} %get-tuple-element.104), channel_id=1, source_target_pairs={{0,2},{1,3},{2,0},{3,1},{4,6},{5,7},{6,4},{7,5},{8,10},{9,11},{10,... | collective-permute-start | bytes 393224 | tf_op jit(solution)/shard_map/ppermute | solution.py:61
  42.7 2.1 %collective-permute-start.15 = (bf16[128,512]{1,0:T(8,128)(2,1)S(1)}, bf16[128,512]{1,0:T(8,128)(2,1)S(1)}, u32[]{:S(2)}, u32[]{:S(2)}) collective-permute-start(bf16[128,512]{1,0:T(8,128)(2,1)S(1)} %get-tuple-element.106), channel_id=1, source_target_pairs={{0,2},{1,3},{2,0},{3,1},{4,6},{5,7},{6,4},{7,5},{8,10},{9,11},{10,... | collective-permute-start | bytes 393224 | tf_op jit(solution)/shard_map/ppermute | solution.py:61
  43.2 11.2 %collective-permute-start.18 = (bf16[256,512]{1,0:T(8,128)(2,1)S(1)}, bf16[256,512]{1,0:T(8,128)(2,1)S(1)}, u32[]{:S(2)}, u32[]{:S(2)}) collective-permute-start(bf16[256,512]{1,0:T(8,128)(2,1)S(1)} %collective-permute-done.5.refs_4_), channel_id=1, source_target_pairs={{0,4},{1,5},{2,6},{3,7},{4,0},{5,1},{6,2},{7,3},{8,12},{9,13},{10,... | collective-permute-start | bytes 786440 | tf_op jit(solution)/shard_map/ppermute | solution.py:61
  45.7 11.1 %collective-permute-start.19 = (bf16[256,512]{1,0:T(8,128)(2,1)S(1)}, bf16[256,512]{1,0:T(8,128)(2,1)S(1)}, u32[]{:S(2)}, u32[]{:S(2)}) collective-permute-start(bf16[256,512]{1,0:T(8,128)(2,1)S(1)} %get-tuple-element.118.refs_3_.par), channel_id=1, source_target_pairs={{0,2},{1,3},{2,0},{3,1},{4,6},{5,7},{6,4},{7,5},{8,10},{9,11},{10,... | collective-permute-start | bytes 786440 | tf_op jit(solution)/shard_map/ppermute | solution.py:61
  49.2 12.4 %collective-permute-start.24 = (bf16[256,512]{1,0:T(8,128)(2,1)S(1)}, bf16[256,512]{1,0:T(8,128)(2,1)S(1)}, u32[]{:S(2)}, u32[]{:S(2)}) collective-permute-start(bf16[256,512]{1,0:T(8,128)(2,1)S(1)} %add_blocks.3), channel_id=1, source_target_pairs={{0,16},{1,17},{2,18},{3,19},{4,20},{5,21},{6,22},{7,23},{8,24},{9,... | collective-permute-start | bytes 786440 | tf_op jit(solution)/shard_map/ppermute | solution.py:61
  51.9 9.7 %collective-permute-start.20 = (bf16[256,512]{1,0:T(8,128)(2,1)S(1)}, bf16[256,512]{1,0:T(8,128)(2,1)S(1)}, u32[]{:S(2)}, u32[]{:S(2)}) collective-permute-start(bf16[256,512]{1,0:T(8,128)(2,1)S(1)} %get-tuple-element.122), channel_id=1, source_target_pairs={{0,4},{1,5},{2,6},{3,7},{4,0},{5,1},{6,2},{7,3},{8,12},{9,13},{10,... | collective-permute-start | bytes 786440 | tf_op jit(solution)/shard_map/ppermute | solution.py:61
  55.3 8.0 %collective-permute-start.21 = (bf16[256,512]{1,0:T(8,128)(2,1)S(1)}, bf16[256,512]{1,0:T(8,128)(2,1)S(1)}, u32[]{:S(2)}, u32[]{:S(2)}) collective-permute-start(bf16[256,512]{1,0:T(8,128)(2,1)S(1)} %far_features.2), channel_id=1, source_target_pairs={{0,1},{1,0},{2,3},{3,2},{4,5},{5,4},{6,7},{7,6},{8,9},{9,8},{10,11... | collective-permute-start | bytes 786440 | tf_op jit(solution)/shard_map/ppermute | solution.py:61
  58.4 8.7 %collective-permute-start.22 = (bf16[256,512]{1,0:T(8,128)(2,1)S(1)}, bf16[256,512]{1,0:T(8,128)(2,1)S(1)}, u32[]{:S(2)}, u32[]{:S(2)}) collective-permute-start(bf16[256,512]{1,0:T(8,128)(2,1)S(1)} %far_features.3), channel_id=1, source_target_pairs={{0,3},{1,2},{2,1},{3,0},{4,7},{5,6},{6,5},{7,4},{8,11},{9,10},{10,... | collective-permute-start | bytes 786440 | tf_op jit(solution)/shard_map/ppermute | solution.py:61
  58.5 9.6 %collective-permute-start.23 = (bf16[256,512]{1,0:T(8,128)(2,1)S(1)}, bf16[256,512]{1,0:T(8,128)(2,1)S(1)}, u32[]{:S(2)}, u32[]{:S(2)}) collective-permute-start(bf16[256,512]{1,0:T(8,128)(2,1)S(1)} %get-tuple-element.127), channel_id=1, source_target_pairs={{0,4},{1,5},{2,6},{3,7},{4,0},{5,1},{6,2},{7,3},{8,12},{9,13},{10,... | collective-permute-start | bytes 786440 | tf_op jit(solution)/shard_map/ppermute | solution.py:61
  61.7 8.8 %collective-permute-start.27 = (bf16[256,512]{1,0:T(8,128)(2,1)S(1)}, bf16[256,512]{1,0:T(8,128)(2,1)S(1)}, u32[]{:S(2)}, u32[]{:S(2)}) collective-permute-start(bf16[256,512]{1,0:T(8,128)(2,1)S(1)} %get-tuple-element.131), channel_id=1, source_target_pairs={{0,2},{1,3},{2,0},{3,1},{4,6},{5,7},{6,4},{7,5},{8,10},{9,11},{10,... | collective-permute-start | bytes 786440 | tf_op jit(solution)/shard_map/ppermute | solution.py:61
  61.7 6.4 %collective-permute-start.25 = (bf16[128,512]{1,0:T(8,128)(2,1)S(1)}, bf16[128,512]{1,0:T(8,128)(2,1)S(1)}, u32[]{:S(2)}, u32[]{:S(2)}) collective-permute-start(bf16[128,512]{1,0:T(8,128)(2,1)S(1)} %get-tuple-element.123), channel_id=1, source_target_pairs={{0,8},{1,9},{2,10},{3,11},{4,12},{5,13},{6,14},{7,15},{8,0},{9,1},... | collective-permute-start | bytes 393224 | tf_op jit(solution)/shard_map/ppermute | solution.py:61
  62.0 10.3 %copy-start.3 = (f32[128,2048]{1,0:T(8,128)S(1)}, f32[128,2048]{1,0:T(8,128)}, u32[]{:S(2)}) copy-start(f32[128,2048]{1,0:T(8,128)} %refs_3_.5) | copy-start | bytes 3145732
  63.3 7.2 %collective-permute-start.26 = (bf16[128,512]{1,0:T(8,128)(2,1)S(1)}, bf16[128,512]{1,0:T(8,128)(2,1)S(1)}, u32[]{:S(2)}, u32[]{:S(2)}) collective-permute-start(bf16[128,512]{1,0:T(8,128)(2,1)S(1)} %get-tuple-element.129), channel_id=1, source_target_pairs={{0,8},{1,9},{2,10},{3,11},{4,12},{5,13},{6,14},{7,15},{8,0},{9,1},... | collective-permute-start | bytes 393224 | tf_op jit(solution)/shard_map/ppermute | solution.py:61
  67.1 7.0 %collective-permute-start.29 = (bf16[256,512]{1,0:T(8,128)(2,1)S(1)}, bf16[256,512]{1,0:T(8,128)(2,1)S(1)}, u32[]{:S(2)}, u32[]{:S(2)}) collective-permute-start(bf16[256,512]{1,0:T(8,128)(2,1)S(1)} %get-tuple-element.135), channel_id=1, source_target_pairs={{0,2},{1,3},{2,0},{3,1},{4,6},{5,7},{6,4},{7,5},{8,10},{9,11},{10,... | collective-permute-start | bytes 786440 | tf_op jit(solution)/shard_map/ppermute | solution.py:61
  67.4 4.9 %copy-start.1 = (f32[128,2048]{1,0:T(8,128)S(1)}, f32[128,2048]{1,0:T(8,128)}, u32[]{:S(2)}) copy-start(f32[128,2048]{1,0:T(8,128)} %refs_1_.3) | copy-start | bytes 3145732
  67.5 4.9 %copy-start.2 = (f32[128,2048]{1,0:T(8,128)S(1)}, f32[128,2048]{1,0:T(8,128)}, u32[]{:S(2)}) copy-start(f32[128,2048]{1,0:T(8,128)} %refs_2_.5) | copy-start | bytes 3145732
  68.1 4.2 %collective-permute-start.28 = (bf16[144,512]{1,0:T(8,128)(2,1)S(1)}, bf16[144,512]{1,0:T(8,128)(2,1)S(1)}, u32[]{:S(2)}, u32[]{:S(2)}) collective-permute-start(bf16[144,512]{1,0:T(8,128)(2,1)S(1)} %sum_gradient.2), channel_id=1, source_target_pairs={{0,2},{1,3},{2,0},{3,1},{4,6},{5,7},{6,4},{7,5},{8,10},{9,11},{10,... | collective-permute-start | bytes 442376 | tf_op jit(solution)/shard_map/ppermute | solution.py:61
  68.2 10.3 %collective-permute-start.30 = (bf16[144,512]{1,0:T(8,128)(2,1)S(1)}, bf16[144,512]{1,0:T(8,128)(2,1)S(1)}, u32[]{:S(2)}, u32[]{:S(2)}) collective-permute-start(bf16[144,512]{1,0:T(8,128)(2,1)S(1)} %sum_gradient.2), channel_id=1, source_target_pairs={{0,3},{1,2},{2,1},{3,0},{4,7},{5,6},{6,5},{7,4},{8,11},{9,10},{10,... | collective-permute-start | bytes 442376 | tf_op jit(solution)/shard_map/ppermute | solution.py:61
  70.6 6.7 %collective-permute-start.31 = (bf16[128,512]{1,0:T(8,128)(2,1)S(1)}, bf16[128,512]{1,0:T(8,128)(2,1)S(1)}, u32[]{:S(2)}, u32[]{:S(2)}) collective-permute-start(bf16[128,512]{1,0:T(8,128)(2,1)S(1)} %sum_gradient.3.refs_0_), channel_id=1, source_target_pairs={{0,1},{1,0},{2,3},{3,2},{4,5},{5,4},{6,7},{7,6},{8,9},{9,8},{10,11... | collective-permute-start | bytes 393224 | tf_op jit(solution)/shard_map/ppermute | solution.py:61

commit v8 on v6

--- a/solution.py
+++ b/solution.py
@@ -319,7 +319,7 @@
         (far_par[1],) = run("take_block", first_body, [((tokens, span), bf16)], [block])
         far_dia[1] = start(far_par[1], sibling)
         gradient_block(1)
-        onward = block_sum(3)
+        onward = block_sum(3, more=extra)
         block_y(2, onward)
         teacher_y(2, onward)
         onward = start(onward, across_z(1))

time: 77.7 us -> 77.7 us (level)
  transfers between devices with their start and end apart: 31 -> 31, of which waited for: 15 -> 14; matrix products, arithmetic and copies ran while one was open for 0% -> 0% of each run, Pallas kernels for 14% -> 14%
where the time goes in v8:
time: 77.7 us; the launch traced here: 77.5 us
  starting transfers between devices  33.3 us (43%)
  waiting for transfers between devices  28.5 us (37%)
  Pallas kernels  12.2 us (16%)
  local copies, waits for them, and re-layouts  2.55 us (3%)
  between operations  0.89 us (1%)
    ppermute x31, starting transfers between devices, send(): return lax.ppermute(value, ('fsdp', 'rep'), perm)  33.3 us
    ppermute x31, waiting for transfers between devices, send(): return lax.ppermute(value, ('fsdp', 'rep'), perm)  28.5 us
    pallas_call x21, Pallas kernels, call(): pl.pallas_call(body, out_shape=shapes, in_specs=[VMEM] * len(inputs), out...  8.02 us
    pallas_call x3, Pallas kernels, update(): pl.pallas_call(update_body(quarters), out_shape=[jax.ShapeDtypeStruct((ro...  4.22 us
    unnamed x12, local copies, waits for them, and re-layouts  2.55 us
  transfers between devices with their start and end apart: 31, of which 14 were waited for; matrix products, arithmetic and copies ran while one was open for 0% of the time, Pallas kernels for 14%

profile of v8, /device:TPU:0, one launch (start us, length us, event | category | flops | bytes accessed | tf_op | source)
XLA Modules:
  0.0 77.5 jit_solution(14306891328780191203)
XLA Ops:
  0.7 1.3 %copy-done.4 = bf16[256,2048]{1,0:T(8,128)(2,1)S(1)} copy-done((bf16[256,2048]{1,0:T(8,128)(2,1)S(1)}, bf16[256,2048]{1,0:T(8,128)(2,1)}, u32[]{:S(2)}) %copy-start.4) | copy-done | bytes 1048600
  2.0 1.2 %copy-done.5 = bf16[256,2048]{1,0:T(8,128)(2,1)S(1)} copy-done((bf16[256,2048]{1,0:T(8,128)(2,1)S(1)}, bf16[256,2048]{1,0:T(8,128)(2,1)}, u32[]{:S(2)}) %copy-start.5) | copy-done | bytes 1048600
  3.4 0.5 collective-permute-start.2
  4.1 2.9 %collective-permute-start.7 = (bf16[256,1536]{1,0:T(8,128)(2,1)S(1)}, bf16[256,1536]{1,0:T(8,128)(2,1)S(1)}, u32[]{:S(2)}, u32[]{:S(2)}) collective-permute-start(bf16[256,1536]{1,0:T(8,128)(2,1)S(1)} %get-tuple-element.78), channel_id=1, source_target_pairs={{0,1},{1,0},{2,3},{3,2},{4,5},{5,4},{6,7},{7,6},{8,9},{9,8},{10,11... | collective-permute-start | bytes 2359304 | tf_op jit(solution)/shard_map/ppermute | solution.py:61
  7.1 0.3 collective-permute-done.1.sib
  7.4 3.0 %collective-permute-start.4 = (bf16[256,512]{1,0:T(8,128)(2,1)S(1)}, bf16[256,512]{1,0:T(8,128)(2,1)S(1)}, u32[]{:S(2)}, u32[]{:S(2)}) collective-permute-start(bf16[256,512]{1,0:T(8,128)(2,1)S(1)} %join_teacher.1.refs_0_), channel_id=1, source_target_pairs={{0,8},{1,9},{2,10},{3,11},{4,12},{5,13},{6,14},{7,15},{8,24},{9,25... | collective-permute-start | bytes 786440 | tf_op jit(solution)/shard_map/ppermute | solution.py:61
  10.4 1.5 %collective-permute-start.3 = (bf16[256,512]{1,0:T(8,128)(2,1)S(1)}, bf16[256,512]{1,0:T(8,128)(2,1)S(1)}, u32[]{:S(2)}, u32[]{:S(2)}) collective-permute-start(bf16[256,512]{1,0:T(8,128)(2,1)S(1)} %join_teacher.1.refs_0_), channel_id=1, source_target_pairs={{0,4},{1,5},{2,6},{3,7},{4,0},{5,1},{6,2},{7,3},{8,12},{9,13},{10,... | collective-permute-start | bytes 786440 | tf_op jit(solution)/shard_map/ppermute | solution.py:61
  11.9 6.1 %collective-permute-done.4.refs_2_ = bf16[256,512]{1,0:T(8,128)(2,1)S(1)} collective-permute-done((bf16[256,512]{1,0:T(8,128)(2,1)S(1)}, bf16[256,512]{1,0:T(8,128)(2,1)S(1)}, u32[]{:S(2)}, u32[]{:S(2)}) %collective-permute-start.4) | collective-permute-done | bytes 262176 | tf_op jit(solution)/shard_map/ppermute | solution.py:61
  18.0 0.8 %collective-permute-start.5 = (bf16[256,512]{1,0:T(8,128)(2,1)S(1)}, bf16[256,512]{1,0:T(8,128)(2,1)S(1)}, u32[]{:S(2)}, u32[]{:S(2)}) collective-permute-start(bf16[256,512]{1,0:T(8,128)(2,1)S(1)} %collective-permute-done.4.refs_2_), channel_id=1, source_target_pairs={{0,8},{1,9},{2,10},{3,11},{4,12},{5,13},{6,14},{7,15},{8,24},{9,25... | collective-permute-start | bytes 786440 | tf_op jit(solution)/shard_map/ppermute | solution.py:61
  18.9 1.5 %collective-permute-start.8 = (bf16[256,512]{1,0:T(8,128)(2,1)S(1)}, bf16[256,512]{1,0:T(8,128)(2,1)S(1)}, u32[]{:S(2)}, u32[]{:S(2)}) collective-permute-start(bf16[256,512]{1,0:T(8,128)(2,1)S(1)} %collective-permute-done.4.refs_2_), channel_id=1, source_target_pairs={{0,4},{1,5},{2,6},{3,7},{4,0},{5,1},{6,2},{7,3},{8,12},{9,13},{10,... | collective-permute-start | bytes 786440 | tf_op jit(solution)/shard_map/ppermute | solution.py:61
  20.4 1.5 %collective-permute-start.11 = (bf16[288,512]{1,0:T(8,128)(2,1)S(1)}, bf16[288,512]{1,0:T(8,128)(2,1)S(1)}, u32[]{:S(2)}, u32[]{:S(2)}) collective-permute-start(bf16[288,512]{1,0:T(8,128)(2,1)S(1)} %get-tuple-element.96), channel_id=1, source_target_pairs={{0,1},{1,0},{2,3},{3,2},{4,5},{5,4},{6,7},{7,6},{8,9},{9,8},{10,11... | collective-permute-start | bytes 884744 | tf_op jit(solution)/shard_map/ppermute | solution.py:61
  21.9 3.4 %collective-permute-done.7.message = bf16[256,1536]{1,0:T(8,128)(2,1)S(1)} collective-permute-done((bf16[256,1536]{1,0:T(8,128)(2,1)S(1)}, bf16[256,1536]{1,0:T(8,128)(2,1)S(1)}, u32[]{:S(2)}, u32[]{:S(2)}) %collective-permute-start.7) | collective-permute-done | bytes 786464 | tf_op jit(solution)/shard_map/ppermute | solution.py:61
  25.5 0.5 collective-permute-start.9
  26.0 0.8 collective-permute-done.5.refs_4_
  26.8 2.4 %collective-permute-start.6 = (bf16[544,512]{1,0:T(8,128)(2,1)S(1)}, bf16[544,512]{1,0:T(8,128)(2,1)S(1)}, u32[]{:S(2)}, u32[]{:S(2)}) collective-permute-start(bf16[544,512]{1,0:T(8,128)(2,1)S(1)} %stack_teacher.1), channel_id=1, source_target_pairs={{0,16},{1,17},{2,18},{3,19},{4,20},{5,21},{6,22},{7,23},{8,0},{9,1... | collective-permute-start | bytes 1671176 | tf_op jit(solution)/shard_map/ppermute | solution.py:61
  29.2 1.5 %collective-permute-start = (bf16[256,1024]{1,0:T(8,128)(2,1)S(1)}, bf16[256,1024]{1,0:T(8,128)(2,1)S(1)}, u32[]{:S(2)}, u32[]{:S(2)}) collective-permute-start(bf16[256,1024]{1,0:T(8,128)(2,1)S(1)} %get-tuple-element.77), channel_id=1, source_target_pairs={{0,1},{1,0},{2,3},{3,2},{4,5},{5,4},{6,7},{7,6},{8,9},{9,8},{10,11... | collective-permute-start | bytes 1572872 | tf_op jit(solution)/shard_map/ppermute | solution.py:61
  30.7 0.8 %gradient_block.4 = (f32[256,512]{1,0:T(8,128)S(1)}, bf16[272,512]{1,0:T(8,128)(2,1)S(1)}) custom-call(bf16[256,2560]{1,0:T(8,128)(2,1)S(1)} %get-tuple-element.122.own, bf16[256,2560]{1,0:T(8,128)(2,1)S(1)} %collective-permute-done.2.sib, bf16[256,512]{1,0:T(8,128)(2,1)S(1)} %get-tuple-element.114.par.refs_0_, ...), custom_call_target="tpu_custom_call" | custom-call | flops 1 | bytes 1 | tf_op jit(solution)/shard_map/gradient_block/pallas_call | solution.py:29
  31.5 1.6 %collective-permute-start.13 = (bf16[272,512]{1,0:T(8,128)(2,1)S(1)}, bf16[272,512]{1,0:T(8,128)(2,1)S(1)}, u32[]{:S(2)}, u32[]{:S(2)}) collective-permute-start(bf16[272,512]{1,0:T(8,128)(2,1)S(1)} %get-tuple-element.101), channel_id=1, source_target_pairs={{0,4},{1,5},{2,6},{3,7},{4,0},{5,1},{6,2},{7,3},{8,12},{9,13},{10,... | collective-permute-start | bytes 835592 | tf_op jit(solution)/shard_map/ppermute | solution.py:61
  33.2 1.5 %collective-permute-done.12.dia.refs_1_ = bf16[256,512]{1,0:T(8,128)(2,1)S(1)} collective-permute-done((bf16[256,512]{1,0:T(8,128)(2,1)S(1)}, bf16[256,512]{1,0:T(8,128)(2,1)S(1)}, u32[]{:S(2)}, u32[]{:S(2)}) %collective-permute-start.12) | collective-permute-done | bytes 262176 | tf_op jit(solution)/shard_map/ppermute | solution.py:61
  34.7 0.8 %gradient_block.5 = (f32[256,512]{1,0:T(8,128)S(1)}, bf16[256,512]{1,0:T(8,128)(2,1)S(1)}) custom-call(bf16[256,2560]{1,0:T(8,128)(2,1)S(1)} %get-tuple-element.122.own, bf16[256,2560]{1,0:T(8,128)(2,1)S(1)} %collective-permute-done.2.sib, bf16[256,512]{1,0:T(8,128)(2,1)S(1)} %take_block.1.par.refs_1_, ...), custom_call_target="tpu_custom_call" | custom-call | flops 1 | bytes 1 | tf_op jit(solution)/shard_map/gradient_block/pallas_call | solution.py:29
  35.6 4.1 %collective-permute-done.13.refs_1_ = bf16[272,512]{1,0:T(8,128)(2,1)S(1)} collective-permute-done((bf16[272,512]{1,0:T(8,128)(2,1)S(1)}, bf16[272,512]{1,0:T(8,128)(2,1)S(1)}, u32[]{:S(2)}, u32[]{:S(2)}) %collective-permute-start.13) | collective-permute-done | bytes 278560 | tf_op jit(solution)/shard_map/ppermute | solution.py:61
  39.8 1.6 %collective-permute-start.16 = (bf16[256,512]{1,0:T(8,128)(2,1)S(1)}, bf16[256,512]{1,0:T(8,128)(2,1)S(1)}, u32[]{:S(2)}, u32[]{:S(2)}) collective-permute-start(bf16[256,512]{1,0:T(8,128)(2,1)S(1)} %get-tuple-element.111), channel_id=1, source_target_pairs={{0,4},{1,5},{2,6},{3,7},{4,0},{5,1},{6,2},{7,3},{8,12},{9,13},{10,... | collective-permute-start | bytes 786440 | tf_op jit(solution)/shard_map/ppermute | solution.py:61
  41.4 1.4 %collective-permute-done.message = bf16[256,1024]{1,0:T(8,128)(2,1)S(1)} collective-permute-done((bf16[256,1024]{1,0:T(8,128)(2,1)S(1)}, bf16[256,1024]{1,0:T(8,128)(2,1)S(1)}, u32[]{:S(2)}, u32[]{:S(2)}) %collective-permute-start) | collective-permute-done | bytes 524320 | tf_op jit(solution)/shard_map/ppermute | solution.py:61
  43.0 0.5 collective-permute-start.15
  43.5 1.5 %collective-permute-start.18 = (bf16[256,512]{1,0:T(8,128)(2,1)S(1)}, bf16[256,512]{1,0:T(8,128)(2,1)S(1)}, u32[]{:S(2)}, u32[]{:S(2)}) collective-permute-start(bf16[256,512]{1,0:T(8,128)(2,1)S(1)} %collective-permute-done.5.refs_4_), channel_id=1, source_target_pairs={{0,4},{1,5},{2,6},{3,7},{4,0},{5,1},{6,2},{7,3},{8,12},{9,13},{10,... | collective-permute-start | bytes 786440 | tf_op jit(solution)/shard_map/ppermute | solution.py:61
  45.0 0.8 %gradient_block.6 = (f32[256,512]{1,0:T(8,128)S(1)}, bf16[256,512]{1,0:T(8,128)(2,1)S(1)}) custom-call(bf16[256,2560]{1,0:T(8,128)(2,1)S(1)} %get-tuple-element.122.own, bf16[256,2560]{1,0:T(8,128)(2,1)S(1)} %collective-permute-done.2.sib, bf16[256,512]{1,0:T(8,128)(2,1)S(1)} %get-tuple-element.107.par.refs_2_, bf16[256,512]{1,0:T(8,128)(2,1)S(1)} %join_pieces.1.dia.refs_2_, ...), custom_call_target="tpu_custom_call" | custom-call | flops 1 | bytes 1 | tf_op jit(solution)/shard_map/gradient_block/pallas_call | solution.py:29
  45.9 1.3 %collective-permute-start.20 = (bf16[256,512]{1,0:T(8,128)(2,1)S(1)}, bf16[256,512]{1,0:T(8,128)(2,1)S(1)}, u32[]{:S(2)}, u32[]{:S(2)}) collective-permute-start(bf16[256,512]{1,0:T(8,128)(2,1)S(1)} %get-tuple-element.121), channel_id=1, source_target_pairs={{0,4},{1,5},{2,6},{3,7},{4,0},{5,1},{6,2},{7,3},{8,12},{9,13},{10,... | collective-permute-start | bytes 786440 | tf_op jit(solution)/shard_map/ppermute | solution.py:61
  47.4 2.8 %collective-permute-start.24 = (bf16[256,512]{1,0:T(8,128)(2,1)S(1)}, bf16[256,512]{1,0:T(8,128)(2,1)S(1)}, u32[]{:S(2)}, u32[]{:S(2)}) collective-permute-start(bf16[256,512]{1,0:T(8,128)(2,1)S(1)} %add_blocks.4), channel_id=1, source_target_pairs={{0,16},{1,17},{2,18},{3,19},{4,20},{5,21},{6,22},{7,23},{8,24},{9,... | collective-permute-start | bytes 786440 | tf_op jit(solution)/shard_map/ppermute | solution.py:61
  50.2 2.6 %collective-permute-done.18.refs_5_ = bf16[256,512]{1,0:T(8,128)(2,1)S(1)} collective-permute-done((bf16[256,512]{1,0:T(8,128)(2,1)S(1)}, bf16[256,512]{1,0:T(8,128)(2,1)S(1)}, u32[]{:S(2)}, u32[]{:S(2)}) %collective-permute-start.18) | collective-permute-done | bytes 262176 | tf_op jit(solution)/shard_map/ppermute | solution.py:61
  53.0 0.7 far_features.2
  53.7 1.4 %collective-permute-start.21 = (bf16[256,512]{1,0:T(8,128)(2,1)S(1)}, bf16[256,512]{1,0:T(8,128)(2,1)S(1)}, u32[]{:S(2)}, u32[]{:S(2)}) collective-permute-start(bf16[256,512]{1,0:T(8,128)(2,1)S(1)} %far_features.2), channel_id=1, source_target_pairs={{0,1},{1,0},{2,3},{3,2},{4,5},{5,4},{6,7},{7,6},{8,9},{9,8},{10,11... | collective-permute-start | bytes 786440 | tf_op jit(solution)/shard_map/ppermute | solution.py:61
  55.1 0.8 %gradient_block.7 = (f32[256,512]{1,0:T(8,128)S(1)}, bf16[256,512]{1,0:T(8,128)(2,1)S(1)}) custom-call(bf16[256,2560]{1,0:T(8,128)(2,1)S(1)} %get-tuple-element.122.own, bf16[256,2560]{1,0:T(8,128)(2,1)S(1)} %collective-permute-done.2.sib, bf16[256,512]{1,0:T(8,128)(2,1)S(1)} %get-tuple-element.117.refs_3_.par, ...), custom_call_target="tpu_custom_call" | custom-call | flops 1 | bytes 1 | tf_op jit(solution)/shard_map/gradient_block/pallas_call | solution.py:29
  55.9 0.7 far_features.3
  56.7 1.6 %collective-permute-start.23 = (bf16[256,512]{1,0:T(8,128)(2,1)S(1)}, bf16[256,512]{1,0:T(8,128)(2,1)S(1)}, u32[]{:S(2)}, u32[]{:S(2)}) collective-permute-start(bf16[256,512]{1,0:T(8,128)(2,1)S(1)} %get-tuple-element.125), channel_id=1, source_target_pairs={{0,4},{1,5},{2,6},{3,7},{4,0},{5,1},{6,2},{7,3},{8,12},{9,13},{10,... | collective-permute-start | bytes 786440 | tf_op jit(solution)/shard_map/ppermute | solution.py:61
  58.3 1.8 %collective-permute-start.25 = (bf16[256,512]{1,0:T(8,128)(2,1)S(1)}, bf16[256,512]{1,0:T(8,128)(2,1)S(1)}, u32[]{:S(2)}, u32[]{:S(2)}) collective-permute-start(bf16[256,512]{1,0:T(8,128)(2,1)S(1)} %add_blocks.5), channel_id=1, source_target_pairs={{0,8},{1,9},{2,10},{3,11},{4,12},{5,13},{6,14},{7,15},{8,0},{9,1},... | collective-permute-start | bytes 786440 | tf_op jit(solution)/shard_map/ppermute | solution.py:61
  60.1 2.1 %collective-permute-done.24.refs_2_ = bf16[256,512]{1,0:T(8,128)(2,1)S(1)} collective-permute-done((bf16[256,512]{1,0:T(8,128)(2,1)S(1)}, bf16[256,512]{1,0:T(8,128)(2,1)S(1)}, u32[]{:S(2)}, u32[]{:S(2)}) %collective-permute-start.24) | collective-permute-done | bytes 262176 | tf_op jit(solution)/shard_map/ppermute | solution.py:61
  62.2 1.2 %near_features.1 = (bf16[256,512]{1,0:T(8,128)(2,1)S(1)}, bf16[256,512]{1,0:T(8,128)(2,1)S(1)}) custom-call(bf16[256,2560]{1,0:T(8,128)(2,1)S(1)} %get-tuple-element.122.own, bf16[256,2560]{1,0:T(8,128)(2,1)S(1)} %collective-permute-done.2.sib, bf16[2048,512]{1,0:T(8,128)(2,1)S(1)} %fill_teacher.1.refs_4_.full), custom_call_target="tpu_custom_call" | custom-call | flops 1 | bytes 1 | tf_op jit(solution)/shard_map/near_features/pallas_call | solution.py:29
  63.5 0.6 collective-permute-start.28
  64.1 1.3 %collective-permute-done.22.refs_3_ = bf16[256,512]{1,0:T(8,128)(2,1)S(1)} collective-permute-done((bf16[256,512]{1,0:T(8,128)(2,1)S(1)}, bf16[256,512]{1,0:T(8,128)(2,1)S(1)}, u32[]{:S(2)}, u32[]{:S(2)}) %collective-permute-start.22) | collective-permute-done | bytes 262176 | tf_op jit(solution)/shard_map/ppermute | solution.py:61
  65.4 0.4 collective-permute-done.23.refs_1_
  65.7 2.1 %collective-permute-done.25.refs_3_ = bf16[256,512]{1,0:T(8,128)(2,1)S(1)} collective-permute-done((bf16[256,512]{1,0:T(8,128)(2,1)S(1)}, bf16[256,512]{1,0:T(8,128)(2,1)S(1)}, u32[]{:S(2)}, u32[]{:S(2)}) %collective-permute-start.25) | collective-permute-done | bytes 262176 | tf_op jit(solution)/shard_map/ppermute | solution.py:61
  68.0 1.6 %collective-permute-start.30 = (bf16[128,512]{1,0:T(8,128)(2,1)S(1)}, bf16[128,512]{1,0:T(8,128)(2,1)S(1)}, u32[]{:S(2)}, u32[]{:S(2)}) collective-permute-start(bf16[128,512]{1,0:T(8,128)(2,1)S(1)} %get-tuple-element.129.refs_0_), channel_id=1, source_target_pairs={{0,1},{1,0},{2,3},{3,2},{4,5},{5,4},{6,7},{7,6},{8,9},{9,8},{10,11... | collective-permute-start | bytes 393224 | tf_op jit(solution)/shard_map/ppermute | solution.py:61
  69.9 1.7 %update_near.1 = (f32[128,2048]{1,0:T(8,128)}, f32[128,2048]{1,0:T(8,128)}, f32[128,2048]{1,0:T(8,128)}, f32[128,2048]{1,0:T(8,128)}) custom-call(bf16[128,512]{1,0:T(8,128)(2,1)S(1)} %get-tuple-element.129.refs_0_, bf16[128,512]{1,0:T(8,128)(2,1)S(1)} %collective-permute-done.27.refs_1_, f32[128,2048]{1,0:T(8,128)S(1)} %copy-done.1, ...), custom_call_target="tpu_custom_call" | custom-call | flops 1 | bytes 1 | tf_op jit(solution)/shard_map/update_near/pallas_call | solution.py:401
  71.5 1.1 %place_features.1 = bf16[256,2048]{1,0:T(8,128)(2,1)} custom-call(bf16[256,512]{1,0:T(8,128)(2,1)S(1)} %get-tuple-element.132.refs_0_, bf16[256,512]{1,0:T(8,128)(2,1)S(1)} %collective-permute-done.28.refs_1_, bf16[256,512]{1,0:T(8,128)(2,1)S(1)} %collective-permute-done.21.refs_2_, bf16[256,512]{1,0:T(8,128)(2,1)S(1)} %collective-permute-done.22.refs_3_), custom_call_target="tpu_custom_call" | custom-call | flops 1 | bytes 1 | tf_op jit(solution)/shard_map/place_features/pallas_call | solution.py:29
  72.6 1.7 %collective-permute-done.30.refs_0_ = bf16[128,512]{1,0:T(8,128)(2,1)S(1)} collective-permute-done((bf16[128,512]{1,0:T(8,128)(2,1)S(1)}, bf16[128,512]{1,0:T(8,128)(2,1)S(1)}, u32[]{:S(2)}, u32[]{:S(2)}) %collective-permute-start.30) | collective-permute-done | bytes 131104 | tf_op jit(solution)/shard_map/ppermute | solution.py:61
  74.3 1.3 %update_partner.1 = (f32[128,2048]{1,0:T(8,128)}, f32[128,2048]{1,0:T(8,128)}, f32[128,2048]{1,0:T(8,128)}, f32[128,2048]{1,0:T(8,128)}) custom-call(bf16[128,512]{1,0:T(8,128)(2,1)S(1)} %collective-permute-done.30.refs_0_, f32[128,2048]{1,0:T(8,128)S(1)} %copy-done.1, ...), custom_call_target="tpu_custom_call", output_to_operand_aliasing={{0}: (5, {}), {1}: (6, {}), {2}: (7, {}), {3}: (8, {})} | custom-call | flops 1 | bytes 1 | tf_op jit(solution)/shard_map/update_partner/pallas_call | solution.py:401
  75.6 0.6 collective-permute-done.29.refs_0_
  76.2 1.3 %update_diagonal.1 = (f32[128,2048]{1,0:T(8,128)}, f32[128,2048]{1,0:T(8,128)}, f32[128,2048]{1,0:T(8,128)}, f32[128,2048]{1,0:T(8,128)}) custom-call(bf16[128,512]{1,0:T(8,128)(2,1)S(1)} %collective-permute-done.29.refs_0_, f32[128,2048]{1,0:T(8,128)S(1)} %copy-done.1, ...), custom_call_target="tpu_custom_call", output_to_operand_aliasing={{0}: (5, {}), {1}: (6, {}), {2}: (7, {}), {3}: (8, {})} | custom-call | flops 1 | bytes 1 | tf_op jit(solution)/shard_map/update_diagonal/pallas_call | solution.py:401
  (50 shorter events, 2.0 us)
Async XLA Ops:
  0.6 3.3 %copy-start = (f32[128,2048]{1,0:T(8,128)S(1)}, f32[128,2048]{1,0:T(8,128)}, u32[]{:S(2)}) copy-start(f32[128,2048]{1,0:T(8,128)} %refs_4_.5) | copy-start | bytes 3145732
  0.6 1.3 %copy-start.4 = (bf16[256,2048]{1,0:T(8,128)(2,1)S(1)}, bf16[256,2048]{1,0:T(8,128)(2,1)}, u32[]{:S(2)}) copy-start(bf16[256,2048]{1,0:T(8,128)(2,1)} %p.1) | copy-start | bytes 3145732
  2.0 1.2 %copy-start.5 = (bf16[256,2048]{1,0:T(8,128)(2,1)S(1)}, bf16[256,2048]{1,0:T(8,128)(2,1)}, u32[]{:S(2)}) copy-start(bf16[256,2048]{1,0:T(8,128)(2,1)} %c.1) | copy-start | bytes 3145732
  3.4 18.5 %collective-permute-start.2 = (bf16[256,2560]{1,0:T(8,128)(2,1)S(1)}, bf16[256,2560]{1,0:T(8,128)(2,1)S(1)}, u32[]{:S(2)}, u32[]{:S(2)}) collective-permute-start(bf16[256,2560]{1,0:T(8,128)(2,1)S(1)} %get-tuple-element.122.own), channel_id=1, source_target_pairs={{0,2},{1,3},{2,0},{3,1},{4,6},{5,7},{6,4},{7,5},{8,10},{9,11},{10,... | collective-permute-start | bytes 3932168 | tf_op jit(solution)/shard_map/ppermute | solution.py:61
  4.0 3.4 %collective-permute-start.1 = (bf16[544,512]{1,0:T(8,128)(2,1)S(1)}, bf16[544,512]{1,0:T(8,128)(2,1)S(1)}, u32[]{:S(2)}, u32[]{:S(2)}) collective-permute-start(bf16[544,512]{1,0:T(8,128)(2,1)S(1)} %get-tuple-element.82), channel_id=1, source_target_pairs={{0,2},{1,3},{2,0},{3,1},{4,6},{5,7},{6,4},{7,5},{8,10},{9,11},{10,... | collective-permute-start | bytes 1671176 | tf_op jit(solution)/shard_map/ppermute | solution.py:61
  4.1 21.3 %collective-permute-start.7 = (bf16[256,1536]{1,0:T(8,128)(2,1)S(1)}, bf16[256,1536]{1,0:T(8,128)(2,1)S(1)}, u32[]{:S(2)}, u32[]{:S(2)}) collective-permute-start(bf16[256,1536]{1,0:T(8,128)(2,1)S(1)} %get-tuple-element.78), channel_id=1, source_target_pairs={{0,1},{1,0},{2,3},{3,2},{4,5},{5,4},{6,7},{7,6},{8,9},{9,8},{10,11... | collective-permute-start | bytes 2359304 | tf_op jit(solution)/shard_map/ppermute | solution.py:61
  7.4 10.6 %collective-permute-start.4 = (bf16[256,512]{1,0:T(8,128)(2,1)S(1)}, bf16[256,512]{1,0:T(8,128)(2,1)S(1)}, u32[]{:S(2)}, u32[]{:S(2)}) collective-permute-start(bf16[256,512]{1,0:T(8,128)(2,1)S(1)} %join_teacher.1.refs_0_), channel_id=1, source_target_pairs={{0,8},{1,9},{2,10},{3,11},{4,12},{5,13},{6,14},{7,15},{8,24},{9,25... | collective-permute-start | bytes 786440 | tf_op jit(solution)/shard_map/ppermute | solution.py:61
  10.4 8.5 %collective-permute-start.3 = (bf16[256,512]{1,0:T(8,128)(2,1)S(1)}, bf16[256,512]{1,0:T(8,128)(2,1)S(1)}, u32[]{:S(2)}, u32[]{:S(2)}) collective-permute-start(bf16[256,512]{1,0:T(8,128)(2,1)S(1)} %join_teacher.1.refs_0_), channel_id=1, source_target_pairs={{0,4},{1,5},{2,6},{3,7},{4,0},{5,1},{6,2},{7,3},{8,12},{9,13},{10,... | collective-permute-start | bytes 786440 | tf_op jit(solution)/shard_map/ppermute | solution.py:61
  18.0 8.7 %collective-permute-start.5 = (bf16[256,512]{1,0:T(8,128)(2,1)S(1)}, bf16[256,512]{1,0:T(8,128)(2,1)S(1)}, u32[]{:S(2)}, u32[]{:S(2)}) collective-permute-start(bf16[256,512]{1,0:T(8,128)(2,1)S(1)} %collective-permute-done.4.refs_2_), channel_id=1, source_target_pairs={{0,8},{1,9},{2,10},{3,11},{4,12},{5,13},{6,14},{7,15},{8,24},{9,25... | collective-permute-start | bytes 786440 | tf_op jit(solution)/shard_map/ppermute | solution.py:61
  18.9 10.3 %collective-permute-start.8 = (bf16[256,512]{1,0:T(8,128)(2,1)S(1)}, bf16[256,512]{1,0:T(8,128)(2,1)S(1)}, u32[]{:S(2)}, u32[]{:S(2)}) collective-permute-start(bf16[256,512]{1,0:T(8,128)(2,1)S(1)} %collective-permute-done.4.refs_2_), channel_id=1, source_target_pairs={{0,4},{1,5},{2,6},{3,7},{4,0},{5,1},{6,2},{7,3},{8,12},{9,13},{10,... | collective-permute-start | bytes 786440 | tf_op jit(solution)/shard_map/ppermute | solution.py:61
  20.4 12.7 %collective-permute-start.11 = (bf16[288,512]{1,0:T(8,128)(2,1)S(1)}, bf16[288,512]{1,0:T(8,128)(2,1)S(1)}, u32[]{:S(2)}, u32[]{:S(2)}) collective-permute-start(bf16[288,512]{1,0:T(8,128)(2,1)S(1)} %get-tuple-element.96), channel_id=1, source_target_pairs={{0,1},{1,0},{2,3},{3,2},{4,5},{5,4},{6,7},{7,6},{8,9},{9,8},{10,11... | collective-permute-start | bytes 884744 | tf_op jit(solution)/shard_map/ppermute | solution.py:61
  25.4 5.2 %collective-permute-start.10 = (bf16[256,512]{1,0:T(8,128)(2,1)S(1)}, bf16[256,512]{1,0:T(8,128)(2,1)S(1)}, u32[]{:S(2)}, u32[]{:S(2)}) collective-permute-start(bf16[256,512]{1,0:T(8,128)(2,1)S(1)} %get-tuple-element.89), channel_id=1, source_target_pairs={{0,2},{1,3},{2,0},{3,1},{4,6},{5,7},{6,4},{7,5},{8,10},{9,11},{10,... | collective-permute-start | bytes 786440 | tf_op jit(solution)/shard_map/ppermute | solution.py:61
  25.5 5.2 %collective-permute-start.9 = (bf16[256,512]{1,0:T(8,128)(2,1)S(1)}, bf16[256,512]{1,0:T(8,128)(2,1)S(1)}, u32[]{:S(2)}, u32[]{:S(2)}) collective-permute-start(bf16[256,512]{1,0:T(8,128)(2,1)S(1)} %get-tuple-element.114.par.refs_0_), channel_id=1, source_target_pairs={{0,2},{1,3},{2,0},{3,1},{4,6},{5,7},{6,4},{7,5},{8,10},{9,11},{10,... | collective-permute-start | bytes 786440 | tf_op jit(solution)/shard_map/ppermute | solution.py:61
  26.8 16.0 %collective-permute-start.6 = (bf16[544,512]{1,0:T(8,128)(2,1)S(1)}, bf16[544,512]{1,0:T(8,128)(2,1)S(1)}, u32[]{:S(2)}, u32[]{:S(2)}) collective-permute-start(bf16[544,512]{1,0:T(8,128)(2,1)S(1)} %stack_teacher.1), channel_id=1, source_target_pairs={{0,16},{1,17},{2,18},{3,19},{4,20},{5,21},{6,22},{7,23},{8,0},{9,1... | collective-permute-start | bytes 1671176 | tf_op jit(solution)/shard_map/ppermute | solution.py:61
  29.2 13.6 %collective-permute-start = (bf16[256,1024]{1,0:T(8,128)(2,1)S(1)}, bf16[256,1024]{1,0:T(8,128)(2,1)S(1)}, u32[]{:S(2)}, u32[]{:S(2)}) collective-permute-start(bf16[256,1024]{1,0:T(8,128)(2,1)S(1)} %get-tuple-element.77), channel_id=1, source_target_pairs={{0,1},{1,0},{2,3},{3,2},{4,5},{5,4},{6,7},{7,6},{8,9},{9,8},{10,11... | collective-permute-start | bytes 1572872 | tf_op jit(solution)/shard_map/ppermute | solution.py:61
  31.5 8.1 %collective-permute-start.13 = (bf16[272,512]{1,0:T(8,128)(2,1)S(1)}, bf16[272,512]{1,0:T(8,128)(2,1)S(1)}, u32[]{:S(2)}, u32[]{:S(2)}) collective-permute-start(bf16[272,512]{1,0:T(8,128)(2,1)S(1)} %get-tuple-element.101), channel_id=1, source_target_pairs={{0,4},{1,5},{2,6},{3,7},{4,0},{5,1},{6,2},{7,3},{8,12},{9,13},{10,... | collective-permute-start | bytes 835592 | tf_op jit(solution)/shard_map/ppermute | solution.py:61
  33.1 1.6 %collective-permute-start.12 = (bf16[256,512]{1,0:T(8,128)(2,1)S(1)}, bf16[256,512]{1,0:T(8,128)(2,1)S(1)}, u32[]{:S(2)}, u32[]{:S(2)}) collective-permute-start(bf16[256,512]{1,0:T(8,128)(2,1)S(1)} %take_block.1.par.refs_1_), channel_id=1, source_target_pairs={{0,2},{1,3},{2,0},{3,1},{4,6},{5,7},{6,4},{7,5},{8,10},{9,11},{10,... | collective-permute-start | bytes 786440 | tf_op jit(solution)/shard_map/ppermute | solution.py:61
  39.7 7.6 %collective-permute-start.17 = (bf16[272,512]{1,0:T(8,128)(2,1)S(1)}, bf16[272,512]{1,0:T(8,128)(2,1)S(1)}, u32[]{:S(2)}, u32[]{:S(2)}) collective-permute-start(bf16[272,512]{1,0:T(8,128)(2,1)S(1)} %add_blocks.3), channel_id=1, source_target_pairs={{0,8},{1,9},{2,10},{3,11},{4,12},{5,13},{6,14},{7,15},{8,0},{9,1},... | collective-permute-start | bytes 835592 | tf_op jit(solution)/shard_map/ppermute | solution.py:61
  39.8 7.4 %collective-permute-start.16 = (bf16[256,512]{1,0:T(8,128)(2,1)S(1)}, bf16[256,512]{1,0:T(8,128)(2,1)S(1)}, u32[]{:S(2)}, u32[]{:S(2)}) collective-permute-start(bf16[256,512]{1,0:T(8,128)(2,1)S(1)} %get-tuple-element.111), channel_id=1, source_target_pairs={{0,4},{1,5},{2,6},{3,7},{4,0},{5,1},{6,2},{7,3},{8,12},{9,13},{10,... | collective-permute-start | bytes 786440 | tf_op jit(solution)/shard_map/ppermute | solution.py:61
  42.9 2.1 %collective-permute-start.14 = (bf16[128,512]{1,0:T(8,128)(2,1)S(1)}, bf16[128,512]{1,0:T(8,128)(2,1)S(1)}, u32[]{:S(2)}, u32[]{:S(2)}) collective-permute-start(bf16[128,512]{1,0:T(8,128)(2,1)S(1)} %get-tuple-element.103), channel_id=1, source_target_pairs={{0,2},{1,3},{2,0},{3,1},{4,6},{5,7},{6,4},{7,5},{8,10},{9,11},{10,... | collective-permute-start | bytes 393224 | tf_op jit(solution)/shard_map/ppermute | solution.py:61
  43.0 2.0 %collective-permute-start.15 = (bf16[128,512]{1,0:T(8,128)(2,1)S(1)}, bf16[128,512]{1,0:T(8,128)(2,1)S(1)}, u32[]{:S(2)}, u32[]{:S(2)}) collective-permute-start(bf16[128,512]{1,0:T(8,128)(2,1)S(1)} %get-tuple-element.105), channel_id=1, source_target_pairs={{0,2},{1,3},{2,0},{3,1},{4,6},{5,7},{6,4},{7,5},{8,10},{9,11},{10,... | collective-permute-start | bytes 393224 | tf_op jit(solution)/shard_map/ppermute | solution.py:61
  43.5 9.3 %collective-permute-start.18 = (bf16[256,512]{1,0:T(8,128)(2,1)S(1)}, bf16[256,512]{1,0:T(8,128)(2,1)S(1)}, u32[]{:S(2)}, u32[]{:S(2)}) collective-permute-start(bf16[256,512]{1,0:T(8,128)(2,1)S(1)} %collective-permute-done.5.refs_4_), channel_id=1, source_target_pairs={{0,4},{1,5},{2,6},{3,7},{4,0},{5,1},{6,2},{7,3},{8,12},{9,13},{10,... | collective-permute-start | bytes 786440 | tf_op jit(solution)/shard_map/ppermute | solution.py:61
  45.9 9.2 %collective-permute-start.19 = (bf16[256,512]{1,0:T(8,128)(2,1)S(1)}, bf16[256,512]{1,0:T(8,128)(2,1)S(1)}, u32[]{:S(2)}, u32[]{:S(2)}) collective-permute-start(bf16[256,512]{1,0:T(8,128)(2,1)S(1)} %get-tuple-element.117.refs_3_.par), channel_id=1, source_target_pairs={{0,2},{1,3},{2,0},{3,1},{4,6},{5,7},{6,4},{7,5},{8,10},{9,11},{10,... | collective-permute-start | bytes 786440 | tf_op jit(solution)/shard_map/ppermute | solution.py:61
  45.9 12.4 %collective-permute-start.20 = (bf16[256,512]{1,0:T(8,128)(2,1)S(1)}, bf16[256,512]{1,0:T(8,128)(2,1)S(1)}, u32[]{:S(2)}, u32[]{:S(2)}) collective-permute-start(bf16[256,512]{1,0:T(8,128)(2,1)S(1)} %get-tuple-element.121), channel_id=1, source_target_pairs={{0,4},{1,5},{2,6},{3,7},{4,0},{5,1},{6,2},{7,3},{8,12},{9,13},{10,... | collective-permute-start | bytes 786440 | tf_op jit(solution)/shard_map/ppermute | solution.py:61
  47.4 14.9 %collective-permute-start.24 = (bf16[256,512]{1,0:T(8,128)(2,1)S(1)}, bf16[256,512]{1,0:T(8,128)(2,1)S(1)}, u32[]{:S(2)}, u32[]{:S(2)}) collective-permute-start(bf16[256,512]{1,0:T(8,128)(2,1)S(1)} %add_blocks.4), channel_id=1, source_target_pairs={{0,16},{1,17},{2,18},{3,19},{4,20},{5,21},{6,22},{7,23},{8,24},{9,... | collective-permute-start | bytes 786440 | tf_op jit(solution)/shard_map/ppermute | solution.py:61
  53.7 9.8 %collective-permute-start.21 = (bf16[256,512]{1,0:T(8,128)(2,1)S(1)}, bf16[256,512]{1,0:T(8,128)(2,1)S(1)}, u32[]{:S(2)}, u32[]{:S(2)}) collective-permute-start(bf16[256,512]{1,0:T(8,128)(2,1)S(1)} %far_features.2), channel_id=1, source_target_pairs={{0,1},{1,0},{2,3},{3,2},{4,5},{5,4},{6,7},{7,6},{8,9},{9,8},{10,11... | collective-permute-start | bytes 786440 | tf_op jit(solution)/shard_map/ppermute | solution.py:61
  56.6 8.7 %collective-permute-start.22 = (bf16[256,512]{1,0:T(8,128)(2,1)S(1)}, bf16[256,512]{1,0:T(8,128)(2,1)S(1)}, u32[]{:S(2)}, u32[]{:S(2)}) collective-permute-start(bf16[256,512]{1,0:T(8,128)(2,1)S(1)} %far_features.3), channel_id=1, source_target_pairs={{0,3},{1,2},{2,1},{3,0},{4,7},{5,6},{6,5},{7,4},{8,11},{9,10},{10,... | collective-permute-start | bytes 786440 | tf_op jit(solution)/shard_map/ppermute | solution.py:61
  56.7 9.0 %collective-permute-start.23 = (bf16[256,512]{1,0:T(8,128)(2,1)S(1)}, bf16[256,512]{1,0:T(8,128)(2,1)S(1)}, u32[]{:S(2)}, u32[]{:S(2)}) collective-permute-start(bf16[256,512]{1,0:T(8,128)(2,1)S(1)} %get-tuple-element.125), channel_id=1, source_target_pairs={{0,4},{1,5},{2,6},{3,7},{4,0},{5,1},{6,2},{7,3},{8,12},{9,13},{10,... | collective-permute-start | bytes 786440 | tf_op jit(solution)/shard_map/ppermute | solution.py:61
  58.3 9.4 %collective-permute-start.25 = (bf16[256,512]{1,0:T(8,128)(2,1)S(1)}, bf16[256,512]{1,0:T(8,128)(2,1)S(1)}, u32[]{:S(2)}, u32[]{:S(2)}) collective-permute-start(bf16[256,512]{1,0:T(8,128)(2,1)S(1)} %add_blocks.5), channel_id=1, source_target_pairs={{0,8},{1,9},{2,10},{3,11},{4,12},{5,13},{6,14},{7,15},{8,0},{9,1},... | collective-permute-start | bytes 786440 | tf_op jit(solution)/shard_map/ppermute | solution.py:61
  62.2 5.5 %collective-permute-start.26 = (bf16[240,512]{1,0:T(8,128)(2,1)S(1)}, bf16[240,512]{1,0:T(8,128)(2,1)S(1)}, u32[]{:S(2)}, u32[]{:S(2)}) collective-permute-start(bf16[240,512]{1,0:T(8,128)(2,1)S(1)} %get-tuple-element.127), channel_id=1, source_target_pairs={{0,2},{1,3},{2,0},{3,1},{4,6},{5,7},{6,4},{7,5},{8,10},{9,11},{10,... | collective-permute-start | bytes 737288 | tf_op jit(solution)/shard_map/ppermute | solution.py:61
  62.2 7.6 %copy-start.2 = (f32[128,2048]{1,0:T(8,128)S(1)}, f32[128,2048]{1,0:T(8,128)}, u32[]{:S(2)}) copy-start(f32[128,2048]{1,0:T(8,128)} %refs_2_.5) | copy-start | bytes 3145732
  62.2 7.6 %copy-start.3 = (f32[128,2048]{1,0:T(8,128)S(1)}, f32[128,2048]{1,0:T(8,128)}, u32[]{:S(2)}) copy-start(f32[128,2048]{1,0:T(8,128)} %refs_3_.5) | copy-start | bytes 3145732
  63.5 6.4 %copy-start.1 = (f32[128,2048]{1,0:T(8,128)S(1)}, f32[128,2048]{1,0:T(8,128)}, u32[]{:S(2)}) copy-start(f32[128,2048]{1,0:T(8,128)} %refs_1_.3) | copy-start | bytes 3145732
  63.5 8.0 %collective-permute-start.28 = (bf16[256,512]{1,0:T(8,128)(2,1)S(1)}, bf16[256,512]{1,0:T(8,128)(2,1)S(1)}, u32[]{:S(2)}, u32[]{:S(2)}) collective-permute-start(bf16[256,512]{1,0:T(8,128)(2,1)S(1)} %get-tuple-element.133), channel_id=1, source_target_pairs={{0,2},{1,3},{2,0},{3,1},{4,6},{5,7},{6,4},{7,5},{8,10},{9,11},{10,... | collective-permute-start | bytes 786440 | tf_op jit(solution)/shard_map/ppermute | solution.py:61
  67.9 1.9 %collective-permute-start.27 = (bf16[128,512]{1,0:T(8,128)(2,1)S(1)}, bf16[128,512]{1,0:T(8,128)(2,1)S(1)}, u32[]{:S(2)}, u32[]{:S(2)}) collective-permute-start(bf16[128,512]{1,0:T(8,128)(2,1)S(1)} %get-tuple-element.130), channel_id=1, source_target_pairs={{0,2},{1,3},{2,0},{3,1},{4,6},{5,7},{6,4},{7,5},{8,10},{9,11},{10,... | collective-permute-start | bytes 393224 | tf_op jit(solution)/shard_map/ppermute | solution.py:61
  68.0 6.3 %collective-permute-start.30 = (bf16[128,512]{1,0:T(8,128)(2,1)S(1)}, bf16[128,512]{1,0:T(8,128)(2,1)S(1)}, u32[]{:S(2)}, u32[]{:S(2)}) collective-permute-start(bf16[128,512]{1,0:T(8,128)(2,1)S(1)} %get-tuple-element.129.refs_0_), channel_id=1, source_target_pairs={{0,1},{1,0},{2,3},{3,2},{4,5},{5,4},{6,7},{7,6},{8,9},{9,8},{10,11... | collective-permute-start | bytes 393224 | tf_op jit(solution)/shard_map/ppermute | solution.py:61
  69.6 6.6 %collective-permute-start.29 = (bf16[128,512]{1,0:T(8,128)(2,1)S(1)}, bf16[128,512]{1,0:T(8,128)(2,1)S(1)}, u32[]{:S(2)}, u32[]{:S(2)}) collective-permute-start(bf16[128,512]{1,0:T(8,128)(2,1)S(1)} %get-tuple-element.130), channel_id=1, source_target_pairs={{0,3},{1,2},{2,1},{3,0},{4,7},{5,6},{6,5},{7,4},{8,11},{9,10},{10,... | collective-permute-start | bytes 393224 | tf_op jit(solution)/shard_map/ppermute | solution.py:61
